TPU v7x, 32 devices: a whole 2x2x4 slice. The times are simulated.
32 devices in a mesh: dp: 8 (over z, x), ctx: 4 (over y, core).
Axes of the slice: x: 2, y: 2, z: 4, core: 2. Of those that a mesh axis runs over, the one named last changes fastest.
Arguments:
- tokens: bfloat16 [16, 1024, 1024], P('dp', 'ctx'), may hold values from -6 to 6
- cotangent: bfloat16 [16, 1024, 1024], P('dp', 'ctx'), may hold values from -6 to 6
- adapter_ids: int32 [16], replicated, may hold values from 0 to 7
- attend_weight: bfloat16 [2, 1024, 3072], P(None, ('dp', 'ctx')), may hold values from -0.1875 to 0.1875
- output_weight: bfloat16 [2, 1024, 1024], P(None, ('dp', 'ctx')), may hold values from -4 to 4
- expand_weight: bfloat16 [2, 1024, 4096], P(None, ('dp', 'ctx')), may hold values from -0.1875 to 0.1875
- reduce_weight: bfloat16 [2, 4096, 1024], P(None, ('dp', 'ctx')), may hold values from -0.09375 to 0.09375
- attend_bias: float32 [2, 2048], replicated, may hold values from -3 to 3
- output_bias: float32 [2, 1024], replicated, may hold values from -3 to 3
- expand_bias: float32 [2, 4096], replicated, may hold values from -3 to 3
- reduce_bias: float32 [2, 1024], replicated, may hold values from -3 to 3
- first_gain: float32 [2, 1024], replicated, may hold values from 0.1 to 1.9
- first_shift: float32 [2, 1024], replicated, may hold values from -3 to 3
- second_gain: float32 [2, 1024], replicated, may hold values from 0.1 to 1.9
- second_shift: float32 [2, 1024], replicated, may hold values from -3 to 3
- attend_left: bfloat16 [2, 8, 1024, 16], P(None, None, ('dp', 'ctx')), may hold values from -0.1875 to 0.1875
- attend_right: bfloat16 [2, 8, 3072, 16], P(None, None, ('dp', 'ctx')), may hold values from -0.75 to 0.75
- output_left: bfloat16 [2, 8, 1024, 16], P(None, None, ('dp', 'ctx')), may hold values from -4 to 4
- output_right: bfloat16 [2, 8, 1024, 16], P(None, None, ('dp', 'ctx')), may hold values from -0.75 to 0.75
- expand_left: bfloat16 [2, 8, 1024, 16], P(None, None, ('dp', 'ctx')), may hold values from -0.1875 to 0.1875
- expand_right: bfloat16 [2, 8, 4096, 16], P(None, None, ('dp', 'ctx')), may hold values from -0.75 to 0.75
- reduce_left: bfloat16 [2, 8, 4096, 16], P(None, None, ('dp', 'ctx')), may hold values from -0.09375 to 0.09375
- reduce_right: bfloat16 [2, 8, 1024, 16], P(None, None, ('dp', 'ctx')), may hold values from -0.75 to 0.75
Outputs:
- output: bfloat16 [16, 1024, 1024], P('dp', 'ctx')
- input_grad: float32 [16, 1024, 1024], P('dp', 'ctx')
- attend_left_grad: float32 [2, 8, 1024, 16], P(None, None, ('dp', 'ctx'))
- attend_right_grad: float32 [2, 8, 3072, 16], P(None, None, ('dp', 'ctx'))
- output_left_grad: float32 [2, 8, 1024, 16], P(None, None, ('dp', 'ctx'))
- output_right_grad: float32 [2, 8, 1024, 16], P(None, None, ('dp', 'ctx'))
- expand_left_grad: float32 [2, 8, 1024, 16], P(None, None, ('dp', 'ctx'))
- expand_right_grad: float32 [2, 8, 4096, 16], P(None, None, ('dp', 'ctx'))
- reduce_left_grad: float32 [2, 8, 4096, 16], P(None, None, ('dp', 'ctx'))
- reduce_right_grad: float32 [2, 8, 1024, 16], P(None, None, ('dp', 'ctx'))
Inputs may be any that keep to these rules, and one draw needn't show every extreme that they name: adapter_ids[s] is the adapter that sequence s uses in every layer.
All inputs are finite; a program needn't handle non-finite values.
Results may differ from a plain program's by a relative error of at most 0.018.
Values may be sent and summed in bfloat16 or wider, within the bound.
No kernel may reach another device: no remote copies, remote signals or barrier semaphores. Data moves between devices by JAX's collectives and lax.ppermute only.
A program may use at most 384 MiB of HBM per device.

v0:
```python
import jax
import jax.numpy as jnp
from jax import lax
from jax.sharding import PartitionSpec as P

HEADS = 16
HEAD_DIM = 64
RANK = 16
ADAPTERS = 8
LAYERS = 2
BLK = 256
KEYBLK = 512
TOK_DEV = 256


epsilon = 1e-05
masked_score = -1e30
root_factor = 0.7978845608028654


def as_sent(x):

    def short(part):
        return part.astype(jnp.bfloat16) if part.dtype == jnp.float32 else part

    return jax.tree.map(short, x)


def normalize(values, gain_vector, shift_vector):
    center = jnp.mean(values, axis=-1, keepdims=True)
    spread = values - center
    variance = jnp.mean(spread * spread, axis=-1, keepdims=True)
    return spread * lax.rsqrt(variance + epsilon) * gain_vector + shift_vector


def gelu_tanh(values):
    return (
        0.5
        * values
        * (1.0 + jnp.tanh(root_factor * (values + 0.044715 * values * values * values)))
    )


def matmul(left_side, right_side):
    return jnp.dot(left_side, right_side, preferred_element_type=jnp.float32)


def matmul_last(left_side, right_side):
    return lax.dot_general(
        left_side, right_side, (((1,), (1,)), ((), ())), preferred_element_type=jnp.float32
    )


def matmul_first(left_side, right_side):
    return lax.dot_general(
        left_side, right_side, (((0,), (0,)), ((), ())), preferred_element_type=jnp.float32
    )


def adapt_forward(inputs, weight, left_factor, right_factor):
    low_rank = matmul(inputs, left_factor).astype(jnp.bfloat16)
    return (matmul(inputs, weight) + matmul_last(low_rank, right_factor), low_rank)


def adapt_backward(grad_output, inputs, low_rank, weight, left_factor, right_factor):
    grad_rank = matmul(grad_output, right_factor).astype(jnp.bfloat16)
    grad_inputs = matmul_last(grad_output, weight) + matmul_last(grad_rank, left_factor)
    return (grad_inputs, matmul_first(inputs, grad_rank), matmul_first(grad_output, low_rank))


def block_scores(queries, key_all, offset, row_first):
    key_rows = lax.dynamic_slice_in_dim(key_all, offset, KEYBLK, 0).reshape(KEYBLK, HEADS, HEAD_DIM)
    scores = jnp.einsum(
        "qhd,khd->hqk", queries, key_rows, preferred_element_type=jnp.float32
    ) * HEAD_DIM ** (-0.5)
    key_block = (offset + lax.iota(jnp.int32, KEYBLK)) // BLK
    query_block = (row_first + lax.iota(jnp.int32, queries.shape[0])) // BLK
    visible = key_block[None, :] <= query_block[:, None]
    return (jnp.where(visible[None], scores, masked_score), key_rows)


def attend_forward(queries_low, key_all, value_all, row_first, block_count):
    row_count = queries_low.shape[0]
    queries = queries_low.reshape(row_count, HEADS, HEAD_DIM)

    def stats_step(block_index, carried):
        row_peak, row_total = carried
        scores, key_rows = block_scores(queries, key_all, block_index * KEYBLK, row_first)
        newest = jnp.maximum(row_peak, jnp.max(scores, axis=-1))
        row_total = row_total * jnp.exp(row_peak - newest) + jnp.sum(
            jnp.exp(scores - newest[..., None]), axis=-1
        )
        return (newest, row_total)

    start_peak = jnp.full((HEADS, row_count), masked_score, jnp.float32)
    start_total = jnp.zeros((HEADS, row_count), jnp.float32)
    row_peak, row_total = lax.fori_loop(0, block_count, stats_step, (start_peak, start_total))
    logsum = row_peak + jnp.log(row_total)

    def value_step(block_index, accumulated):
        offset = block_index * KEYBLK
        scores, key_rows = block_scores(queries, key_all, offset, row_first)
        weights = jnp.exp(scores - logsum[..., None]).astype(jnp.bfloat16)
        value_rows = lax.dynamic_slice_in_dim(value_all, offset, KEYBLK, 0).reshape(
            KEYBLK, HEADS, HEAD_DIM
        )
        return accumulated + jnp.einsum(
            "hqk,khd->qhd", weights, value_rows, preferred_element_type=jnp.float32
        )

    accumulated = lax.fori_loop(
        0, block_count, value_step, jnp.zeros((row_count, HEADS, HEAD_DIM), jnp.float32)
    )
    return (accumulated.reshape(row_count, HEADS * HEAD_DIM), logsum)


def attend_backward(
    queries_low, key_all, value_all, grad_low, logsum, delta, row_first, block_count
):
    row_count = queries_low.shape[0]
    queries = queries_low.reshape(row_count, HEADS, HEAD_DIM)
    grad_heads = grad_low.reshape(row_count, HEADS, HEAD_DIM)
    scale = HEAD_DIM ** (-0.5)

    def grad_step(block_index, carried):
        offset = block_index * KEYBLK
        scores, key_rows = block_scores(queries, key_all, offset, row_first)
        value_rows = lax.dynamic_slice_in_dim(value_all, offset, KEYBLK, 0).reshape(
            KEYBLK, HEADS, HEAD_DIM
        )
        probability = jnp.exp(scores - logsum[..., None])
        grad_probs = jnp.einsum(
            "qhd,khd->hqk", grad_heads, value_rows, preferred_element_type=jnp.float32
        )
        grad_scores = (probability * (grad_probs - delta[..., None])).astype(jnp.bfloat16)
        grad_query = (
            carried[0]
            + jnp.einsum("hqk,khd->qhd", grad_scores, key_rows, preferred_element_type=jnp.float32)
            * scale
        )
        key_term = (
            jnp.einsum("hqk,qhd->khd", grad_scores, queries, preferred_element_type=jnp.float32)
            * scale
        )
        value_term = jnp.einsum(
            "hqk,qhd->khd",
            probability.astype(jnp.bfloat16),
            grad_heads,
            preferred_element_type=jnp.float32,
        )
        grad_key = lax.dynamic_update_slice_in_dim(
            carried[1], key_term.reshape(KEYBLK, HEADS * HEAD_DIM), offset, 0
        )
        grad_value = lax.dynamic_update_slice_in_dim(
            carried[2], value_term.reshape(KEYBLK, HEADS * HEAD_DIM), offset, 0
        )
        return (grad_query, grad_key, grad_value)

    start_query = jnp.zeros((row_count, HEADS, HEAD_DIM), jnp.float32)
    empty_keys = jnp.zeros(key_all.shape, jnp.float32)
    start = (start_query, empty_keys, empty_keys)
    carried = lax.fori_loop(0, block_count, grad_step, start)
    grad_query = carried[0].reshape(row_count, HEADS * HEAD_DIM)
    return (grad_query, carried[1], carried[2])


def layer_forward(current, frozen, picked, extras, row_first, block_count):
    attend_weight, output_weight, expand_weight, reduce_weight = frozen
    (
        attend_left,
        attend_right,
        output_left,
        output_right,
        expand_left,
        expand_right,
        reduce_left,
        reduce_right,
    ) = picked
    (
        attend_bias,
        output_bias,
        expand_bias,
        reduce_bias,
        first_gain,
        first_shift,
        second_gain,
        second_shift,
    ) = extras
    columns = current.shape[1]
    normed_one = normalize(current, first_gain, first_shift).astype(jnp.bfloat16)
    joined_rows, rank_attend = adapt_forward(normed_one, attend_weight, attend_left, attend_right)
    bias_full = jnp.concatenate(
        [attend_bias[:columns], jnp.zeros((columns,), jnp.float32), attend_bias[columns:]]
    )
    joined_rows = (joined_rows + bias_full).astype(jnp.bfloat16)
    queries_low = joined_rows[:, :columns]
    keys_low = joined_rows[:, columns : 2 * columns]
    values_low = joined_rows[:, 2 * columns :]
    key_all, value_all = (
        lax.all_gather(keys_low, "ctx", axis=0, tiled=True),
        lax.all_gather(values_low, "ctx", axis=0, tiled=True),
    )
    attended, logsum = attend_forward(queries_low, key_all, value_all, row_first, block_count)
    attended_low = attended.astype(jnp.bfloat16)
    projected, rank_output = adapt_forward(attended_low, output_weight, output_left, output_right)
    middle = current + projected + output_bias
    normed_two = normalize(middle, second_gain, second_shift).astype(jnp.bfloat16)
    expanded, rank_expand = adapt_forward(normed_two, expand_weight, expand_left, expand_right)
    expanded = expanded + expand_bias
    active = gelu_tanh(expanded).astype(jnp.bfloat16)
    reduced, rank_reduce = adapt_forward(active, reduce_weight, reduce_left, reduce_right)
    result = middle + reduced + reduce_bias
    kept_values = (
        current,
        normed_one,
        rank_attend,
        queries_low,
        keys_low,
        values_low,
        attended,
        attended_low,
        logsum,
        rank_output,
        middle,
        normed_two,
        rank_expand,
        expanded,
        active,
        rank_reduce,
    )
    return (result, kept_values)


def layer_backward(grad_result, kept_values, frozen, picked, extras, row_first, block_count):
    attend_weight, output_weight, expand_weight, reduce_weight = frozen
    (
        attend_left,
        attend_right,
        output_left,
        output_right,
        expand_left,
        expand_right,
        reduce_left,
        reduce_right,
    ) = picked
    (
        attend_bias,
        output_bias,
        expand_bias,
        reduce_bias,
        first_gain,
        first_shift,
        second_gain,
        second_shift,
    ) = extras
    (
        current,
        normed_one,
        rank_attend,
        queries_low,
        keys_low,
        values_low,
        attended,
        attended_low,
        logsum,
        rank_output,
        middle,
        normed_two,
        rank_expand,
        expanded,
        active,
        rank_reduce,
    ) = kept_values
    row_count = current.shape[0]
    grad_reduce = grad_result.astype(jnp.bfloat16)
    grad_active, reduce_left_g, reduce_right_g = adapt_backward(
        grad_reduce, active, rank_reduce, reduce_weight, reduce_left, reduce_right
    )
    grad_expand = jax.vjp(gelu_tanh, expanded)[1](grad_active)[0].astype(jnp.bfloat16)
    grad_second, expand_left_g, expand_right_g = adapt_backward(
        grad_expand, normed_two, rank_expand, expand_weight, expand_left, expand_right
    )
    second_pull = jax.vjp(lambda values: normalize(values, second_gain, second_shift), middle)[1]
    grad_middle = grad_result + second_pull(grad_second)[0]
    grad_project = grad_middle.astype(jnp.bfloat16)
    grad_attended, output_left_g, output_right_g = adapt_backward(
        grad_project, attended_low, rank_output, output_weight, output_left, output_right
    )
    grad_attended_low = grad_attended.astype(jnp.bfloat16)
    key_all, value_all = (
        lax.all_gather(as_sent(keys_low), "ctx", axis=0, tiled=True).astype(keys_low.dtype),
        lax.all_gather(as_sent(values_low), "ctx", axis=0, tiled=True).astype(values_low.dtype),
    )
    grad_heads = grad_attended_low.astype(jnp.float32).reshape(row_count, HEADS, HEAD_DIM)
    delta = jnp.sum(grad_heads * attended.reshape(row_count, HEADS, HEAD_DIM), axis=-1).T
    grad_query, grad_key_all, grad_value_all = attend_backward(
        queries_low, key_all, value_all, grad_attended_low, logsum, delta, row_first, block_count
    )
    key_own, value_own = (
        lax.psum_scatter(
            grad_key_all.astype(jnp.bfloat16), "ctx", scatter_dimension=0, tiled=True
        ).astype(jnp.float32),
        lax.psum_scatter(
            grad_value_all.astype(jnp.bfloat16), "ctx", scatter_dimension=0, tiled=True
        ).astype(jnp.float32),
    )
    grad_joined = jnp.concatenate([grad_query, key_own, value_own], axis=1).astype(jnp.bfloat16)
    grad_first, attend_left_g, attend_right_g = adapt_backward(
        grad_joined, normed_one, rank_attend, attend_weight, attend_left, attend_right
    )
    first_pull = jax.vjp(lambda values: normalize(values, first_gain, first_shift), current)[1]
    grad_current = grad_middle + first_pull(grad_first)[0]
    return (
        grad_current,
        (
            attend_left_g,
            attend_right_g,
            output_left_g,
            output_right_g,
            expand_left_g,
            expand_right_g,
            reduce_left_g,
            reduce_right_g,
        ),
    )


def local(
    tokens,
    cotangent,
    adapter_ids,
    attend_weight,
    output_weight,
    expand_weight,
    reduce_weight,
    attend_bias,
    output_bias,
    expand_bias,
    reduce_bias,
    first_gain,
    first_shift,
    second_gain,
    second_shift,
    attend_left,
    attend_right,
    output_left,
    output_right,
    expand_left,
    expand_right,
    reduce_left,
    reduce_right,
):
    data_rank = lax.axis_index("dp")
    context_rank = lax.axis_index("ctx")
    data_count = lax.axis_size("dp")
    context_count = lax.axis_size("ctx")
    batches = tokens.shape[0]
    row_first = context_rank * TOK_DEV
    block_count = ((context_rank + 1) * TOK_DEV + KEYBLK - 1) // KEYBLK

    def fetch_forward(layer_index):
        return (
            lax.all_gather(attend_weight[layer_index], ("dp", "ctx"), axis=0, tiled=True),
            lax.all_gather(output_weight[layer_index], ("dp", "ctx"), axis=0, tiled=True),
            lax.all_gather(expand_weight[layer_index], ("dp", "ctx"), axis=0, tiled=True),
            lax.all_gather(reduce_weight[layer_index], ("dp", "ctx"), axis=0, tiled=True),
            lax.all_gather(attend_left[layer_index], ("dp", "ctx"), axis=1, tiled=True),
            lax.all_gather(attend_right[layer_index], ("dp", "ctx"), axis=1, tiled=True),
            lax.all_gather(output_left[layer_index], ("dp", "ctx"), axis=1, tiled=True),
            lax.all_gather(output_right[layer_index], ("dp", "ctx"), axis=1, tiled=True),
            lax.all_gather(expand_left[layer_index], ("dp", "ctx"), axis=1, tiled=True),
            lax.all_gather(expand_right[layer_index], ("dp", "ctx"), axis=1, tiled=True),
            lax.all_gather(reduce_left[layer_index], ("dp", "ctx"), axis=1, tiled=True),
            lax.all_gather(reduce_right[layer_index], ("dp", "ctx"), axis=1, tiled=True),
        )

    def fetch_backward(layer_index):
        return (
            lax.all_gather(attend_weight[layer_index], ("dp", "ctx"), axis=0, tiled=True),
            lax.all_gather(output_weight[layer_index], ("dp", "ctx"), axis=0, tiled=True),
            lax.all_gather(expand_weight[layer_index], ("dp", "ctx"), axis=0, tiled=True),
            lax.all_gather(reduce_weight[layer_index], ("dp", "ctx"), axis=0, tiled=True),
            lax.all_gather(attend_left[layer_index], ("dp", "ctx"), axis=1, tiled=True),
            lax.all_gather(attend_right[layer_index], ("dp", "ctx"), axis=1, tiled=True),
            lax.all_gather(output_left[layer_index], ("dp", "ctx"), axis=1, tiled=True),
            lax.all_gather(output_right[layer_index], ("dp", "ctx"), axis=1, tiled=True),
            lax.all_gather(expand_left[layer_index], ("dp", "ctx"), axis=1, tiled=True),
            lax.all_gather(expand_right[layer_index], ("dp", "ctx"), axis=1, tiled=True),
            lax.all_gather(reduce_left[layer_index], ("dp", "ctx"), axis=1, tiled=True),
            lax.all_gather(reduce_right[layer_index], ("dp", "ctx"), axis=1, tiled=True),
        )

    def layer_extras(layer_index):
        return tuple(
            (
                member[layer_index]
                for member in (
                    attend_bias,
                    output_bias,
                    expand_bias,
                    reduce_bias,
                    first_gain,
                    first_shift,
                    second_gain,
                    second_shift,
                )
            )
        )

    def split_gathered(gathered, adapter_pick):
        picked = tuple(
            (
                lax.dynamic_index_in_dim(member, adapter_pick, 0, keepdims=False)
                for member in gathered[4:]
            )
        )
        return (gathered[:4], picked)

    def micro_step(counter, inputs):
        batch_tokens, batch_cotangent, batch_index = inputs
        adapter_pick = lax.dynamic_index_in_dim(
            adapter_ids, data_rank * batches + batch_index, 0, keepdims=False
        )
        current = batch_tokens.astype(jnp.float32)
        kept_list = []
        fetched_list = []
        for layer_index in range(LAYERS):
            gathered = fetch_forward(layer_index)
            frozen, picked = split_gathered(gathered, adapter_pick)
            current, kept_values = layer_forward(
                current, frozen, picked, layer_extras(layer_index), row_first, block_count
            )
            kept_list.append(kept_values)
            fetched_list.append(gathered)
        grad_current = batch_cotangent.astype(jnp.float32)
        layer_grads = [None] * LAYERS
        for layer_index in reversed(range(LAYERS)):
            gathered = fetch_backward(layer_index)
            frozen, picked = split_gathered(gathered, adapter_pick)
            grad_current, layer_grads[layer_index] = layer_backward(
                grad_current,
                kept_list[layer_index],
                frozen,
                picked,
                layer_extras(layer_index),
                row_first,
                block_count,
            )
        stacked = tuple(
            (
                jnp.stack([layer_grads[layer_index][kind_index] for layer_index in range(LAYERS)])
                for kind_index in range(8)
            )
        )
        return (counter, (current.astype(jnp.bfloat16), grad_current, stacked))

    unused, (outputs, input_grads, adapter_terms) = lax.scan(
        micro_step, jnp.zeros((), jnp.int32), (tokens, cotangent, lax.iota(jnp.int32, batches))
    )

    def split_rows(grad_term):
        shape = grad_term.shape
        return grad_term.reshape(
            shape[0],
            shape[1],
            data_count,
            context_count,
            shape[2] // (data_count * context_count),
            shape[3],
        )

    split_terms = tuple((split_rows(grad_term) for grad_term in adapter_terms))
    summed = (
        lax.psum_scatter(
            split_terms[0].astype(jnp.bfloat16), "ctx", scatter_dimension=3, tiled=True
        ).astype(jnp.float32),
        lax.psum_scatter(
            split_terms[1].astype(jnp.bfloat16), "ctx", scatter_dimension=3, tiled=True
        ).astype(jnp.float32),
        lax.psum_scatter(
            split_terms[2].astype(jnp.bfloat16), "ctx", scatter_dimension=3, tiled=True
        ).astype(jnp.float32),
        lax.psum_scatter(
            split_terms[3].astype(jnp.bfloat16), "ctx", scatter_dimension=3, tiled=True
        ).astype(jnp.float32),
        lax.psum_scatter(
            split_terms[4].astype(jnp.bfloat16), "ctx", scatter_dimension=3, tiled=True
        ).astype(jnp.float32),
        lax.psum_scatter(
            split_terms[5].astype(jnp.bfloat16), "ctx", scatter_dimension=3, tiled=True
        ).astype(jnp.float32),
        lax.psum_scatter(
            split_terms[6].astype(jnp.bfloat16), "ctx", scatter_dimension=3, tiled=True
        ).astype(jnp.float32),
        lax.psum_scatter(
            split_terms[7].astype(jnp.bfloat16), "ctx", scatter_dimension=3, tiled=True
        ).astype(jnp.float32),
    )
    flattened = tuple(
        (
            member.reshape(
                member.shape[0], member.shape[1], data_count, member.shape[4] * member.shape[5]
            )
            for member in summed
        )
    )
    received = (
        lax.all_to_all(as_sent(flattened[0]), "dp", split_axis=2, concat_axis=2, tiled=True),
        lax.all_to_all(as_sent(flattened[1]), "dp", split_axis=2, concat_axis=2, tiled=True),
        lax.all_to_all(as_sent(flattened[2]), "dp", split_axis=2, concat_axis=2, tiled=True),
        lax.all_to_all(as_sent(flattened[3]), "dp", split_axis=2, concat_axis=2, tiled=True),
        lax.all_to_all(as_sent(flattened[4]), "dp", split_axis=2, concat_axis=2, tiled=True),
        lax.all_to_all(as_sent(flattened[5]), "dp", split_axis=2, concat_axis=2, tiled=True),
        lax.all_to_all(as_sent(flattened[6]), "dp", split_axis=2, concat_axis=2, tiled=True),
        lax.all_to_all(as_sent(flattened[7]), "dp", split_axis=2, concat_axis=2, tiled=True),
    )
    owners = adapter_ids.reshape(data_count, batches)
    one_hot = (owners[:, :, None] == lax.iota(jnp.int32, ADAPTERS)[None, None, :]).astype(
        jnp.float32
    )
    results = []
    for kind_index in range(8):
        combined = jnp.einsum(
            "sma,mlsp->lap", one_hot, received[kind_index], precision=lax.Precision.HIGHEST
        )
        row_part = split_terms[kind_index].shape[4]
        results.append(combined.reshape(LAYERS, ADAPTERS, row_part, RANK))
    return (
        outputs,
        input_grads,
        results[0],
        results[1],
        results[2],
        results[3],
        results[4],
        results[5],
        results[6],
        results[7],
    )


def solution(mesh):
    in_specs = (
        P("dp", "ctx", None),
        P("dp", "ctx", None),
        P(),
        P(None, ("dp", "ctx"), None),
        P(None, ("dp", "ctx"), None),
        P(None, ("dp", "ctx"), None),
        P(None, ("dp", "ctx"), None),
        P(),
        P(),
        P(),
        P(),
        P(),
        P(),
        P(),
        P(),
        P(None, None, ("dp", "ctx"), None),
        P(None, None, ("dp", "ctx"), None),
        P(None, None, ("dp", "ctx"), None),
        P(None, None, ("dp", "ctx"), None),
        P(None, None, ("dp", "ctx"), None),
        P(None, None, ("dp", "ctx"), None),
        P(None, None, ("dp", "ctx"), None),
        P(None, None, ("dp", "ctx"), None),
    )
    out_specs = (
        P("dp", "ctx", None),
        P("dp", "ctx", None),
        P(None, None, ("dp", "ctx"), None),
        P(None, None, ("dp", "ctx"), None),
        P(None, None, ("dp", "ctx"), None),
        P(None, None, ("dp", "ctx"), None),
        P(None, None, ("dp", "ctx"), None),
        P(None, None, ("dp", "ctx"), None),
        P(None, None, ("dp", "ctx"), None),
        P(None, None, ("dp", "ctx"), None),
    )
    return jax.shard_map(local, mesh=mesh, in_specs=in_specs, out_specs=out_specs, check_vma=False)
```

profile of v0, /device:TPU:0, one launch (start us, length us, event | category | flops | bytes accessed | tf_op | source)
XLA Modules:
  0.0 2931.0 jit_solution(529307163369642570)
XLA Ops:
  16.9 2616.5 %while.199 = (s32[]{:T(128)}, bf16[2,256,1024]{2,1,0:T(8,128)(2,1)}, f32[2,256,1024]{2,1,0:T(8,128)}, bf16[2,2,1024,16]{2,3,1,0:T(8,128)(2,1)}, bf16[2,2,3072,16...) while((s32[]{:T(128)}, bf16[2,256,1024]{2,1,0:T(8,128)(2,1)}, ...), condition=%wide.region_39.40_spmd, body=%wide.region_0.39_spmd.sunk | while | flops 31112736768 | bytes 1178589056 | solution.py:457
  23.1 51.7 %all-gather.49 = bf16[1,8,1024,16]{3,1,0,2:T(8,128)(2,1)S(1)} all-gather(bf16[1,8,32,16]{3,1,0,2:T(8,128)(2,1)S(1)} %get-tuple-element.2779), channel_id=3, replica_groups=mesh['dp'=8,'ctx'=4] {'dp','ctx'}, dimensions={2}, use_global_device_ids=true | all-gather | bytes 270336 | tf_op jit(solution)/shard_map/while/body/eval_jaxpr/all_gather | solution.py:367
  75.7 84.4 %all-gather.50 = bf16[1,8,3072,16]{3,1,0,2:T(8,128)(2,1)S(1)} all-gather(bf16[1,8,96,16]{3,1,0,2:T(8,128)(2,1)S(1)} %get-tuple-element.2785), channel_id=4, replica_groups=mesh['dp'=8,'ctx'=4] {'dp','ctx'}, dimensions={2}, use_global_device_ids=true | all-gather | bytes 811008 | tf_op jit(solution)/shard_map/while/body/eval_jaxpr/all_gather | solution.py:368
  178.9 46.6 %all-gather.52 = bf16[1,8,1024,16]{3,1,0,2:T(8,128)(2,1)S(1)} all-gather(bf16[1,8,32,16]{3,1,0,2:T(8,128)(2,1)S(1)} %get-tuple-element.2793), channel_id=6, replica_groups=mesh['dp'=8,'ctx'=4] {'dp','ctx'}, dimensions={2}, use_global_device_ids=true | all-gather | bytes 270336 | tf_op jit(solution)/shard_map/while/body/eval_jaxpr/all_gather | solution.py:369
  227.3 47.1 %all-gather.53 = bf16[1,8,1024,16]{3,1,0,2:T(8,128)(2,1)S(1)} all-gather(bf16[1,8,32,16]{3,1,0,2:T(8,128)(2,1)S(1)} %get-tuple-element.2794), channel_id=7, replica_groups=mesh['dp'=8,'ctx'=4] {'dp','ctx'}, dimensions={2}, use_global_device_ids=true | all-gather | bytes 270336 | tf_op jit(solution)/shard_map/while/body/eval_jaxpr/all_gather | solution.py:370
  278.5 46.0 %all-gather.55 = bf16[1,8,1024,16]{3,1,0,2:T(8,128)(2,1)S(1)} all-gather(bf16[1,8,32,16]{3,1,0,2:T(8,128)(2,1)S(1)} %get-tuple-element.2801), channel_id=9, replica_groups=mesh['dp'=8,'ctx'=4] {'dp','ctx'}, dimensions={2}, use_global_device_ids=true | all-gather | bytes 270336 | tf_op jit(solution)/shard_map/while/body/eval_jaxpr/all_gather | solution.py:371
  327.5 49.7 %all-gather.59 = bf16[1,8,1024,16]{3,1,0,2:T(8,128)(2,1)S(1)} all-gather(bf16[1,8,32,16]{3,1,0,2:T(8,128)(2,1)S(1)} %get-tuple-element.2806), channel_id=13, replica_groups=mesh['dp'=8,'ctx'=4] {'dp','ctx'}, dimensions={2}, use_global_device_ids=true | all-gather | bytes 270336 | tf_op jit(solution)/shard_map/while/body/eval_jaxpr/all_gather | solution.py:374
  378.6 46.8 %all-gather.61 = bf16[1,8,1024,16]{3,1,0,2:T(8,128)(2,1)S(1)} all-gather(bf16[1,8,32,16]{3,1,0,2:T(8,128)(2,1)S(1)} %get-tuple-element.2812), channel_id=15, replica_groups=mesh['dp'=8,'ctx'=4] {'dp','ctx'}, dimensions={2}, use_global_device_ids=true | all-gather | bytes 270336 | tf_op jit(solution)/shard_map/while/body/eval_jaxpr/all_gather | solution.py:367
  426.2 89.3 %all-gather.62 = bf16[1,8,3072,16]{3,1,0,2:T(8,128)(2,1)S(1)} all-gather(bf16[1,8,96,16]{3,1,0,2:T(8,128)(2,1)S(1)} %get-tuple-element.2814), channel_id=16, replica_groups=mesh['dp'=8,'ctx'=4] {'dp','ctx'}, dimensions={2}, use_global_device_ids=true | all-gather | bytes 811008 | tf_op jit(solution)/shard_map/while/body/eval_jaxpr/all_gather | solution.py:368
  530.3 9.0 while.201
  548.3 7.7 fusion.756
  564.9 22.0 all-gather.101.cloned.1.call-done
  594.6 63.4 %all-gather.105.cloned.1.call-done = bf16[1,1024,3072]{2,1,0:T(8,128)(2,1)} async-done(((bf16[1,32,3072]{2,1,0:T(8,128)(2,1)}), bf16[1,1024,3072]{2,1,0:T(8,128)(2,1)}) %all-gather.105.cloned.1.call-update) | async-done | bytes 6291472 | tf_op jit(solution)/shard_map/while/body/eval_jaxpr/all_gather | solution.py:363
  667.5 48.8 %all-gather.64 = bf16[1,8,1024,16]{3,1,0,2:T(8,128)(2,1)S(1)} all-gather(bf16[1,8,32,16]{3,1,0,2:T(8,128)(2,1)S(1)} %get-tuple-element.2822), channel_id=18, replica_groups=mesh['dp'=8,'ctx'=4] {'dp','ctx'}, dimensions={2}, use_global_device_ids=true | all-gather | bytes 270336 | tf_op jit(solution)/shard_map/while/body/eval_jaxpr/all_gather | solution.py:369
  717.1 50.8 %all-gather.65 = bf16[1,8,1024,16]{3,1,0,2:T(8,128)(2,1)S(1)} all-gather(bf16[1,8,32,16]{3,1,0,2:T(8,128)(2,1)S(1)} %get-tuple-element.2823), channel_id=19, replica_groups=mesh['dp'=8,'ctx'=4] {'dp','ctx'}, dimensions={2}, use_global_device_ids=true | all-gather | bytes 270336 | tf_op jit(solution)/shard_map/while/body/eval_jaxpr/all_gather | solution.py:370
  768.7 45.9 %all-gather.67 = bf16[1,8,1024,16]{3,1,0,2:T(8,128)(2,1)S(1)} all-gather(bf16[1,8,32,16]{3,1,0,2:T(8,128)(2,1)S(1)} %copy-done.77), channel_id=21, replica_groups=mesh['dp'=8,'ctx'=4] {'dp','ctx'}, dimensions={2}, use_global_device_ids=true | all-gather | bytes 270336 | tf_op jit(solution)/shard_map/while/body/eval_jaxpr/all_gather | solution.py:371
  815.4 50.0 %all-gather.71 = bf16[1,8,1024,16]{3,1,0,2:T(8,128)(2,1)S(1)} all-gather(bf16[1,8,32,16]{3,1,0,2:T(8,128)(2,1)S(1)} %copy-done.78), channel_id=25, replica_groups=mesh['dp'=8,'ctx'=4] {'dp','ctx'}, dimensions={2}, use_global_device_ids=true | all-gather | bytes 270336 | tf_op jit(solution)/shard_map/while/body/eval_jaxpr/all_gather | solution.py:374
  866.7 7.8 fusion.774
  886.1 8.8 while.203
  900.8 57.0 %all-gather.113.cloned.1.call-done = bf16[1,1024,4096]{2,1,0:T(8,128)(2,1)} async-done(((bf16[1,32,4096]{2,1,0:T(8,128)(2,1)}), bf16[1,1024,4096]{2,1,0:T(8,128)(2,1)}) %all-gather.113.cloned.1.call-update) | async-done | bytes 8388624 | tf_op jit(solution)/shard_map/while/body/eval_jaxpr/all_gather | solution.py:365
  957.7 7.6 fusion.771
  965.4 42.3 %all-gather.115.cloned.1.call-done = bf16[1,8,4096,16]{2,3,1,0:T(8,128)(2,1)} async-done(((bf16[1,8,128,16]{2,3,1,0:T(8,128)(2,1)}), bf16[1,8,4096,16]{2,3,1,0:T(8,128)(2,1)}) %all-gather.115.cloned.1.call-update) | async-done | bytes 1048592 | tf_op jit(solution)/shard_map/while/body/eval_jaxpr/all_gather | solution.py:372
  1014.4 44.1 %all-gather.119.cloned.1.call-done = bf16[1,8,4096,16]{2,3,1,0:T(8,128)(2,1)} async-done(((bf16[1,8,128,16]{2,3,1,0:T(8,128)(2,1)}), bf16[1,8,4096,16]{2,3,1,0:T(8,128)(2,1)}) %all-gather.119.cloned.1.call-update) | async-done | bytes 1048592 | tf_op jit(solution)/shard_map/while/body/eval_jaxpr/all_gather | solution.py:373
  1084.6 14.5 while.204
  1101.0 43.5 %reduce-scatter.29.cloned.1.call-done = bf16[256,1024]{0,1:T(8,128)(2,1)} async-done(((bf16[1024,1024]{0,1:T(8,128)(2,1)}), bf16[256,1024]{0,1:T(8,128)(2,1)}) %reduce-scatter.29.cloned.1.call-update) | async-done | bytes 524304 | tf_op jit(solution)/shard_map/while/body/eval_jaxpr/reduce_scatter | solution.py:303
  1144.5 34.0 %reduce-scatter.31.cloned.1.call-done = bf16[256,1024]{0,1:T(8,128)(2,1)} async-done(((bf16[1024,1024]{0,1:T(8,128)(2,1)}), bf16[256,1024]{0,1:T(8,128)(2,1)}) %reduce-scatter.31.cloned.1.call-update) | async-done | bytes 524304 | tf_op jit(solution)/shard_map/while/body/eval_jaxpr/reduce_scatter | solution.py:300
  1211.3 14.8 while.205
  1247.3 24.9 reduce-scatter.33.cloned.1.call-done
  1272.2 34.0 %reduce-scatter.35.cloned.1.call-done = bf16[256,1024]{0,1:T(8,128)(2,1)} async-done(((bf16[1024,1024]{0,1:T(8,128)(2,1)}), bf16[256,1024]{0,1:T(8,128)(2,1)}) %reduce-scatter.35.cloned.1.call-update) | async-done | bytes 524304 | tf_op jit(solution)/shard_map/while/body/eval_jaxpr/reduce_scatter | solution.py:300
  1323.3 49.9 %all-gather.49 = bf16[1,8,1024,16]{3,1,0,2:T(8,128)(2,1)S(1)} all-gather(bf16[1,8,32,16]{3,1,0,2:T(8,128)(2,1)S(1)} %get-tuple-element.2779), channel_id=3, replica_groups=mesh['dp'=8,'ctx'=4] {'dp','ctx'}, dimensions={2}, use_global_device_ids=true | all-gather | bytes 270336 | tf_op jit(solution)/shard_map/while/body/eval_jaxpr/all_gather | solution.py:367
  1374.0 87.3 %all-gather.50 = bf16[1,8,3072,16]{3,1,0,2:T(8,128)(2,1)S(1)} all-gather(bf16[1,8,96,16]{3,1,0,2:T(8,128)(2,1)S(1)} %get-tuple-element.2785), channel_id=4, replica_groups=mesh['dp'=8,'ctx'=4] {'dp','ctx'}, dimensions={2}, use_global_device_ids=true | all-gather | bytes 811008 | tf_op jit(solution)/shard_map/while/body/eval_jaxpr/all_gather | solution.py:368
  1480.1 52.5 %all-gather.52 = bf16[1,8,1024,16]{3,1,0,2:T(8,128)(2,1)S(1)} all-gather(bf16[1,8,32,16]{3,1,0,2:T(8,128)(2,1)S(1)} %get-tuple-element.2793), channel_id=6, replica_groups=mesh['dp'=8,'ctx'=4] {'dp','ctx'}, dimensions={2}, use_global_device_ids=true | all-gather | bytes 270336 | tf_op jit(solution)/shard_map/while/body/eval_jaxpr/all_gather | solution.py:369
  1534.3 46.2 %all-gather.53 = bf16[1,8,1024,16]{3,1,0,2:T(8,128)(2,1)S(1)} all-gather(bf16[1,8,32,16]{3,1,0,2:T(8,128)(2,1)S(1)} %get-tuple-element.2794), channel_id=7, replica_groups=mesh['dp'=8,'ctx'=4] {'dp','ctx'}, dimensions={2}, use_global_device_ids=true | all-gather | bytes 270336 | tf_op jit(solution)/shard_map/while/body/eval_jaxpr/all_gather | solution.py:370
  1584.7 46.3 %all-gather.55 = bf16[1,8,1024,16]{3,1,0,2:T(8,128)(2,1)S(1)} all-gather(bf16[1,8,32,16]{3,1,0,2:T(8,128)(2,1)S(1)} %get-tuple-element.2801), channel_id=9, replica_groups=mesh['dp'=8,'ctx'=4] {'dp','ctx'}, dimensions={2}, use_global_device_ids=true | all-gather | bytes 270336 | tf_op jit(solution)/shard_map/while/body/eval_jaxpr/all_gather | solution.py:371
  1634.0 49.2 %all-gather.59 = bf16[1,8,1024,16]{3,1,0,2:T(8,128)(2,1)S(1)} all-gather(bf16[1,8,32,16]{3,1,0,2:T(8,128)(2,1)S(1)} %get-tuple-element.2806), channel_id=13, replica_groups=mesh['dp'=8,'ctx'=4] {'dp','ctx'}, dimensions={2}, use_global_device_ids=true | all-gather | bytes 270336 | tf_op jit(solution)/shard_map/while/body/eval_jaxpr/all_gather | solution.py:374
  1684.6 46.8 %all-gather.61 = bf16[1,8,1024,16]{3,1,0,2:T(8,128)(2,1)S(1)} all-gather(bf16[1,8,32,16]{3,1,0,2:T(8,128)(2,1)S(1)} %get-tuple-element.2812), channel_id=15, replica_groups=mesh['dp'=8,'ctx'=4] {'dp','ctx'}, dimensions={2}, use_global_device_ids=true | all-gather | bytes 270336 | tf_op jit(solution)/shard_map/while/body/eval_jaxpr/all_gather | solution.py:367
  1732.2 82.3 %all-gather.62 = bf16[1,8,3072,16]{3,1,0,2:T(8,128)(2,1)S(1)} all-gather(bf16[1,8,96,16]{3,1,0,2:T(8,128)(2,1)S(1)} %get-tuple-element.2814), channel_id=16, replica_groups=mesh['dp'=8,'ctx'=4] {'dp','ctx'}, dimensions={2}, use_global_device_ids=true | all-gather | bytes 811008 | tf_op jit(solution)/shard_map/while/body/eval_jaxpr/all_gather | solution.py:368
  1829.3 9.0 while.201
  1847.3 7.7 fusion.756
  1862.8 32.1 %all-gather.101.cloned.1.call-done = bf16[1,4096,1024]{2,1,0:T(8,128)(2,1)} async-done(((bf16[1,128,1024]{2,1,0:T(8,128)(2,1)}), bf16[1,4096,1024]{2,1,0:T(8,128)(2,1)}) %all-gather.101.cloned.1.call-update) | async-done | bytes 8388624 | tf_op jit(solution)/shard_map/while/body/eval_jaxpr/all_gather | solution.py:366
  1902.6 63.4 %all-gather.105.cloned.1.call-done = bf16[1,1024,3072]{2,1,0:T(8,128)(2,1)} async-done(((bf16[1,32,3072]{2,1,0:T(8,128)(2,1)}), bf16[1,1024,3072]{2,1,0:T(8,128)(2,1)}) %all-gather.105.cloned.1.call-update) | async-done | bytes 6291472 | tf_op jit(solution)/shard_map/while/body/eval_jaxpr/all_gather | solution.py:363
  1975.8 48.2 %all-gather.64 = bf16[1,8,1024,16]{3,1,0,2:T(8,128)(2,1)S(1)} all-gather(bf16[1,8,32,16]{3,1,0,2:T(8,128)(2,1)S(1)} %get-tuple-element.2822), channel_id=18, replica_groups=mesh['dp'=8,'ctx'=4] {'dp','ctx'}, dimensions={2}, use_global_device_ids=true | all-gather | bytes 270336 | tf_op jit(solution)/shard_map/while/body/eval_jaxpr/all_gather | solution.py:369
  2024.8 51.2 %all-gather.65 = bf16[1,8,1024,16]{3,1,0,2:T(8,128)(2,1)S(1)} all-gather(bf16[1,8,32,16]{3,1,0,2:T(8,128)(2,1)S(1)} %get-tuple-element.2823), channel_id=19, replica_groups=mesh['dp'=8,'ctx'=4] {'dp','ctx'}, dimensions={2}, use_global_device_ids=true | all-gather | bytes 270336 | tf_op jit(solution)/shard_map/while/body/eval_jaxpr/all_gather | solution.py:370
  2076.8 48.2 %all-gather.67 = bf16[1,8,1024,16]{3,1,0,2:T(8,128)(2,1)S(1)} all-gather(bf16[1,8,32,16]{3,1,0,2:T(8,128)(2,1)S(1)} %copy-done.77), channel_id=21, replica_groups=mesh['dp'=8,'ctx'=4] {'dp','ctx'}, dimensions={2}, use_global_device_ids=true | all-gather | bytes 270336 | tf_op jit(solution)/shard_map/while/body/eval_jaxpr/all_gather | solution.py:371
  2125.9 49.9 %all-gather.71 = bf16[1,8,1024,16]{3,1,0,2:T(8,128)(2,1)S(1)} all-gather(bf16[1,8,32,16]{3,1,0,2:T(8,128)(2,1)S(1)} %copy-done.78), channel_id=25, replica_groups=mesh['dp'=8,'ctx'=4] {'dp','ctx'}, dimensions={2}, use_global_device_ids=true | all-gather | bytes 270336 | tf_op jit(solution)/shard_map/while/body/eval_jaxpr/all_gather | solution.py:374
  2177.1 7.8 fusion.774
  2196.4 8.8 while.203
  2211.2 55.1 %all-gather.113.cloned.1.call-done = bf16[1,1024,4096]{2,1,0:T(8,128)(2,1)} async-done(((bf16[1,32,4096]{2,1,0:T(8,128)(2,1)}), bf16[1,1024,4096]{2,1,0:T(8,128)(2,1)}) %all-gather.113.cloned.1.call-update) | async-done | bytes 8388624 | tf_op jit(solution)/shard_map/while/body/eval_jaxpr/all_gather | solution.py:365
  2266.3 7.6 fusion.771
  2273.9 42.5 %all-gather.115.cloned.1.call-done = bf16[1,8,4096,16]{2,3,1,0:T(8,128)(2,1)} async-done(((bf16[1,8,128,16]{2,3,1,0:T(8,128)(2,1)}), bf16[1,8,4096,16]{2,3,1,0:T(8,128)(2,1)}) %all-gather.115.cloned.1.call-update) | async-done | bytes 1048592 | tf_op jit(solution)/shard_map/while/body/eval_jaxpr/all_gather | solution.py:372
  2323.1 44.1 %all-gather.119.cloned.1.call-done = bf16[1,8,4096,16]{2,3,1,0:T(8,128)(2,1)} async-done(((bf16[1,8,128,16]{2,3,1,0:T(8,128)(2,1)}), bf16[1,8,4096,16]{2,3,1,0:T(8,128)(2,1)}) %all-gather.119.cloned.1.call-update) | async-done | bytes 1048592 | tf_op jit(solution)/shard_map/while/body/eval_jaxpr/all_gather | solution.py:373
  2393.2 14.5 while.204
  2409.9 43.3 %reduce-scatter.29.cloned.1.call-done = bf16[256,1024]{0,1:T(8,128)(2,1)} async-done(((bf16[1024,1024]{0,1:T(8,128)(2,1)}), bf16[256,1024]{0,1:T(8,128)(2,1)}) %reduce-scatter.29.cloned.1.call-update) | async-done | bytes 524304 | tf_op jit(solution)/shard_map/while/body/eval_jaxpr/reduce_scatter | solution.py:303
  2453.2 34.2 %reduce-scatter.31.cloned.1.call-done = bf16[256,1024]{0,1:T(8,128)(2,1)} async-done(((bf16[1024,1024]{0,1:T(8,128)(2,1)}), bf16[256,1024]{0,1:T(8,128)(2,1)}) %reduce-scatter.31.cloned.1.call-update) | async-done | bytes 524304 | tf_op jit(solution)/shard_map/while/body/eval_jaxpr/reduce_scatter | solution.py:300
  2520.2 14.8 while.205
  2556.2 24.9 reduce-scatter.33.cloned.1.call-done
  2581.1 34.2 %reduce-scatter.35.cloned.1.call-done = bf16[256,1024]{0,1:T(8,128)(2,1)} async-done(((bf16[1024,1024]{0,1:T(8,128)(2,1)}), bf16[256,1024]{0,1:T(8,128)(2,1)}) %reduce-scatter.35.cloned.1.call-update) | async-done | bytes 524304 | tf_op jit(solution)/shard_map/while/body/eval_jaxpr/reduce_scatter | solution.py:300
  2668.6 20.0 reduce-scatter.17.cloned.1.call-done
  2696.0 19.8 reduce-scatter.19.cloned.1.call-done
  2723.3 20.1 reduce-scatter.21.cloned.1.call-done
  2750.8 19.9 reduce-scatter.27.cloned.1.call-done
  2778.3 32.9 %reduce-scatter.15.cloned.1.call-done = bf16[2,2,8,1,96,16]{5,4,2,1,0,3:T(8,128)(2,1)} async-done(((bf16[2,2,8,4,96,16]{5,4,2,1,0,3:T(8,128)(2,1)}), bf16[2,2,8,1,96,16]{5,4,2,1,0,3:T(8,128)(2,1)}) %reduce-scatter.15.cloned.1.call-update) | async-done | bytes 98320 | tf_op jit(solution)/shard_map/reduce_scatter | solution.py:477
  2820.6 37.6 %reduce-scatter.23.cloned.1.call-done = bf16[2,2,8,1,128,16]{5,4,2,1,0,3:T(8,128)(2,1)} async-done(((bf16[2,2,8,4,128,16]{5,4,2,1,0,3:T(8,128)(2,1)}), bf16[2,2,8,1,128,16]{5,4,2,1,0,3:T(8,128)(2,1)}) %reduce-scatter.23.cloned.1.call-update) | async-done | bytes 131088 | tf_op jit(solution)/shard_map/reduce_scatter | solution.py:489
  2872.6 32.6 %reduce-scatter.25.cloned.1.call-done = bf16[2,2,8,1,128,16]{5,4,2,1,0,3:T(8,128)(2,1)} async-done(((bf16[2,2,8,4,128,16]{5,4,2,1,0,3:T(8,128)(2,1)}), bf16[2,2,8,1,128,16]{5,4,2,1,0,3:T(8,128)(2,1)}) %reduce-scatter.25.cloned.1.call-update) | async-done | bytes 131088 | tf_op jit(solution)/shard_map/reduce_scatter | solution.py:492
  (1374 shorter events, 625.4 us)
Async XLA Ops:
  16.9 148.3 %all-gather.89.cloned.1.call-start = ((), (), s32[]{:S(2)}) async-start(), calls=%async_computation.28 | async-start | bytes 6488064 | tf_op jit(solution)/shard_map/while/body/eval_jaxpr/all_gather | solution.py:363
  18.9 499.8 %all-gather.93.cloned.1.call-start = ((), (), s32[]{:S(2)}) async-start(), calls=%async_computation.30 | async-start | bytes 2621440 | tf_op jit(solution)/shard_map/while/body/eval_jaxpr/all_gather | solution.py:200
  164.2 429.1 %copy-start.97 = (f32[1,1024]{1,0:T(1,128)}, f32[1,1024]{1,0:T(1,128)S(1)}, u32[]{:S(2)}) copy-start(f32[1,1024]{1,0:T(1,128)S(1)} %get-tuple-element.2809) | copy-start | bytes 12292 | tf_op jit(solution)/shard_map/while
  171.8 349.8 %all-gather.91.cloned.1.call-start = ((), (), s32[]{:S(2)}) async-start(), calls=%async_computation.29 | async-start | bytes 2621440 | tf_op jit(solution)/shard_map/while/body/eval_jaxpr/all_gather | solution.py:201
  172.6 369.6 %all-gather.95.cloned.1.call-start = ((), (), s32[]{:S(2)}) async-start(), calls=%async_computation.31 | async-start | bytes 2162688 | tf_op jit(solution)/shard_map/while/body/eval_jaxpr/all_gather | solution.py:364
  173.3 375.0 %all-gather.97.cloned.1.call-start = ((), (), s32[]{:S(2)}) async-start(), calls=%async_computation.32 | async-start | bytes 8650752 | tf_op jit(solution)/shard_map/while/body/eval_jaxpr/all_gather | solution.py:365
  174.2 381.7 %all-gather.99.cloned.1.call-start = ((), (), s32[]{:S(2)}) async-start(), calls=%async_computation.33 | async-start | bytes 1081344 | tf_op jit(solution)/shard_map/while/body/eval_jaxpr/all_gather | solution.py:372
  175.0 388.2 %all-gather.103.cloned.1.call-start = ((), (), s32[]{:S(2)}) async-start(), calls=%async_computation.35 | async-start | bytes 1081344 | tf_op jit(solution)/shard_map/while/body/eval_jaxpr/all_gather | solution.py:373
  175.7 411.2 %all-gather.101.cloned.1.call-start = ((), (), s32[]{:S(2)}) async-start(), calls=%async_computation.34 | async-start | bytes 8650752 | tf_op jit(solution)/shard_map/while/body/eval_jaxpr/all_gather | solution.py:366
  176.6 481.3 %all-gather.105.cloned.1.call-start = ((), (), s32[]{:S(2)}) async-start(), calls=%async_computation.36 | async-start | bytes 6488064 | tf_op jit(solution)/shard_map/while/body/eval_jaxpr/all_gather | solution.py:363
  177.4 689.3 %all-gather.117.cloned.1.call-start = ((), (), s32[]{:S(2)}) async-start(), calls=%async_computation.42 | async-start | bytes 8650752 | tf_op jit(solution)/shard_map/while/body/eval_jaxpr/all_gather | solution.py:366
  178.0 696.5 %all-gather.109.cloned.1.call-start = ((), (), s32[]{:S(2)}) async-start(), calls=%async_computation.38 | async-start | bytes 2621440 | tf_op jit(solution)/shard_map/while/body/eval_jaxpr/all_gather | solution.py:200
  226.3 315.7 %copy-start.75 = (bf16[1,1,1024,16]{2,3,1,0:T(8,128)(2,1)}, bf16[1,1,1024,16]{2,3,1,0:T(8,128)(2,1)S(1)}, u32[]{:S(2)}) copy-start(bf16[1,1,1024,16]{2,3,1,0:T(8,128)(2,1)S(1)} %copy.322) | copy-start | bytes 98308 | tf_op jit(solution)/shard_map/while
  275.1 269.4 %copy-start.65 = (bf16[1,1,1024,16]{2,3,1,0:T(8,128)(2,1)}, bf16[1,1,1024,16]{2,3,1,0:T(8,128)(2,1)S(1)}, u32[]{:S(2)}) copy-start(bf16[1,1,1024,16]{2,3,1,0:T(8,128)(2,1)S(1)} %copy.323) | copy-start | bytes 98308 | tf_op jit(solution)/shard_map/while
  276.4 270.0 %copy-start.99 = (f32[1,1024]{1,0:T(1,128)}, f32[1,1024]{1,0:T(1,128)S(1)}, u32[]{:S(2)}) copy-start(f32[1,1024]{1,0:T(1,128)S(1)} %get-tuple-element.2798) | copy-start | bytes 12292 | tf_op jit(solution)/shard_map/while
  664.4 216.7 %all-gather.107.cloned.1.call-start = ((), (), s32[]{:S(2)}) async-start(), calls=%async_computation.37 | async-start | bytes 2621440 | tf_op jit(solution)/shard_map/while/body/eval_jaxpr/all_gather | solution.py:201
  664.9 231.5 %all-gather.111.cloned.1.call-start = ((), (), s32[]{:S(2)}) async-start(), calls=%async_computation.39 | async-start | bytes 2162688 | tf_op jit(solution)/shard_map/while/body/eval_jaxpr/all_gather | solution.py:364
  665.7 292.1 %all-gather.113.cloned.1.call-start = ((), (), s32[]{:S(2)}) async-start(), calls=%async_computation.40 | async-start | bytes 8650752 | tf_op jit(solution)/shard_map/while/body/eval_jaxpr/all_gather | solution.py:365
  666.3 341.4 %all-gather.115.cloned.1.call-start = ((), (), s32[]{:S(2)}) async-start(), calls=%async_computation.41 | async-start | bytes 1081344 | tf_op jit(solution)/shard_map/while/body/eval_jaxpr/all_gather | solution.py:372
  666.9 391.7 %all-gather.119.cloned.1.call-start = ((), (), s32[]{:S(2)}) async-start(), calls=%async_computation.43 | async-start | bytes 1081344 | tf_op jit(solution)/shard_map/while/body/eval_jaxpr/all_gather | solution.py:373
  667.4 477.1 %reduce-scatter.29.cloned.1.call-start = ((), (), s32[]{:S(2)}) async-start(), calls=%async_computation.44 | async-start | bytes 2621440 | tf_op jit(solution)/shard_map/while/body/eval_jaxpr/reduce_scatter | solution.py:303
  1099.1 79.4 %reduce-scatter.31.cloned.1.call-start = ((), (), s32[]{:S(2)}) async-start(), calls=%async_computation.45 | async-start | bytes 2621440 | tf_op jit(solution)/shard_map/while/body/eval_jaxpr/reduce_scatter | solution.py:300
  1099.7 172.5 %reduce-scatter.33.cloned.1.call-start = ((), (), s32[]{:S(2)}) async-start(), calls=%async_computation.46 | async-start | bytes 2621440 | tf_op jit(solution)/shard_map/while/body/eval_jaxpr/reduce_scatter | solution.py:303
  1226.2 80.0 %reduce-scatter.35.cloned.1.call-start = ((), (), s32[]{:S(2)}) async-start(), calls=%async_computation.47 | async-start | bytes 2621440 | tf_op jit(solution)/shard_map/while/body/eval_jaxpr/reduce_scatter | solution.py:300
  1317.1 149.4 %all-gather.89.cloned.1.call-start = ((), (), s32[]{:S(2)}) async-start(), calls=%async_computation.28 | async-start | bytes 6488064 | tf_op jit(solution)/shard_map/while/body/eval_jaxpr/all_gather | solution.py:363
  1319.1 498.6 %all-gather.93.cloned.1.call-start = ((), (), s32[]{:S(2)}) async-start(), calls=%async_computation.30 | async-start | bytes 2621440 | tf_op jit(solution)/shard_map/while/body/eval_jaxpr/all_gather | solution.py:200
  1465.5 435.9 %copy-start.97 = (f32[1,1024]{1,0:T(1,128)}, f32[1,1024]{1,0:T(1,128)S(1)}, u32[]{:S(2)}) copy-start(f32[1,1024]{1,0:T(1,128)S(1)} %get-tuple-element.2809) | copy-start | bytes 12292 | tf_op jit(solution)/shard_map/while
  1473.1 347.5 %all-gather.91.cloned.1.call-start = ((), (), s32[]{:S(2)}) async-start(), calls=%async_computation.29 | async-start | bytes 2621440 | tf_op jit(solution)/shard_map/while/body/eval_jaxpr/all_gather | solution.py:201
  1473.8 367.3 %all-gather.95.cloned.1.call-start = ((), (), s32[]{:S(2)}) async-start(), calls=%async_computation.31 | async-start | bytes 2162688 | tf_op jit(solution)/shard_map/while/body/eval_jaxpr/all_gather | solution.py:364
  1474.6 372.7 %all-gather.97.cloned.1.call-start = ((), (), s32[]{:S(2)}) async-start(), calls=%async_computation.32 | async-start | bytes 8650752 | tf_op jit(solution)/shard_map/while/body/eval_jaxpr/all_gather | solution.py:365
  1475.5 379.5 %all-gather.99.cloned.1.call-start = ((), (), s32[]{:S(2)}) async-start(), calls=%async_computation.33 | async-start | bytes 1081344 | tf_op jit(solution)/shard_map/while/body/eval_jaxpr/all_gather | solution.py:372
  1476.2 384.9 %all-gather.103.cloned.1.call-start = ((), (), s32[]{:S(2)}) async-start(), calls=%async_computation.35 | async-start | bytes 1081344 | tf_op jit(solution)/shard_map/while/body/eval_jaxpr/all_gather | solution.py:373
  1476.9 417.9 %all-gather.101.cloned.1.call-start = ((), (), s32[]{:S(2)}) async-start(), calls=%async_computation.34 | async-start | bytes 8650752 | tf_op jit(solution)/shard_map/while/body/eval_jaxpr/all_gather | solution.py:366
  1477.8 488.2 %all-gather.105.cloned.1.call-start = ((), (), s32[]{:S(2)}) async-start(), calls=%async_computation.36 | async-start | bytes 6488064 | tf_op jit(solution)/shard_map/while/body/eval_jaxpr/all_gather | solution.py:363
  1478.6 698.5 %all-gather.117.cloned.1.call-start = ((), (), s32[]{:S(2)}) async-start(), calls=%async_computation.42 | async-start | bytes 8650752 | tf_op jit(solution)/shard_map/while/body/eval_jaxpr/all_gather | solution.py:366
  1479.2 705.6 %all-gather.109.cloned.1.call-start = ((), (), s32[]{:S(2)}) async-start(), calls=%async_computation.38 | async-start | bytes 2621440 | tf_op jit(solution)/shard_map/while/body/eval_jaxpr/all_gather | solution.py:200
  1533.4 307.6 %copy-start.75 = (bf16[1,1,1024,16]{2,3,1,0:T(8,128)(2,1)}, bf16[1,1,1024,16]{2,3,1,0:T(8,128)(2,1)S(1)}, u32[]{:S(2)}) copy-start(bf16[1,1,1024,16]{2,3,1,0:T(8,128)(2,1)S(1)} %copy.322) | copy-start | bytes 98308 | tf_op jit(solution)/shard_map/while
  1581.4 262.1 %copy-start.65 = (bf16[1,1,1024,16]{2,3,1,0:T(8,128)(2,1)}, bf16[1,1,1024,16]{2,3,1,0:T(8,128)(2,1)S(1)}, u32[]{:S(2)}) copy-start(bf16[1,1,1024,16]{2,3,1,0:T(8,128)(2,1)S(1)} %copy.323) | copy-start | bytes 98308 | tf_op jit(solution)/shard_map/while
  1582.6 262.7 %copy-start.99 = (f32[1,1024]{1,0:T(1,128)}, f32[1,1024]{1,0:T(1,128)S(1)}, u32[]{:S(2)}) copy-start(f32[1,1024]{1,0:T(1,128)S(1)} %get-tuple-element.2798) | copy-start | bytes 12292 | tf_op jit(solution)/shard_map/while
  1972.4 219.0 %all-gather.107.cloned.1.call-start = ((), (), s32[]{:S(2)}) async-start(), calls=%async_computation.37 | async-start | bytes 2621440 | tf_op jit(solution)/shard_map/while/body/eval_jaxpr/all_gather | solution.py:201
  1973.1 233.6 %all-gather.111.cloned.1.call-start = ((), (), s32[]{:S(2)}) async-start(), calls=%async_computation.39 | async-start | bytes 2162688 | tf_op jit(solution)/shard_map/while/body/eval_jaxpr/all_gather | solution.py:364
  1973.7 292.6 %all-gather.113.cloned.1.call-start = ((), (), s32[]{:S(2)}) async-start(), calls=%async_computation.40 | async-start | bytes 8650752 | tf_op jit(solution)/shard_map/while/body/eval_jaxpr/all_gather | solution.py:365
  1974.4 341.9 %all-gather.115.cloned.1.call-start = ((), (), s32[]{:S(2)}) async-start(), calls=%async_computation.41 | async-start | bytes 1081344 | tf_op jit(solution)/shard_map/while/body/eval_jaxpr/all_gather | solution.py:372
  1975.2 392.0 %all-gather.119.cloned.1.call-start = ((), (), s32[]{:S(2)}) async-start(), calls=%async_computation.43 | async-start | bytes 1081344 | tf_op jit(solution)/shard_map/while/body/eval_jaxpr/all_gather | solution.py:373
  1975.8 477.4 %reduce-scatter.29.cloned.1.call-start = ((), (), s32[]{:S(2)}) async-start(), calls=%async_computation.44 | async-start | bytes 2621440 | tf_op jit(solution)/shard_map/while/body/eval_jaxpr/reduce_scatter | solution.py:303
  2407.7 79.6 %reduce-scatter.31.cloned.1.call-start = ((), (), s32[]{:S(2)}) async-start(), calls=%async_computation.45 | async-start | bytes 2621440 | tf_op jit(solution)/shard_map/while/body/eval_jaxpr/reduce_scatter | solution.py:300
  2408.5 172.5 %reduce-scatter.33.cloned.1.call-start = ((), (), s32[]{:S(2)}) async-start(), calls=%async_computation.46 | async-start | bytes 2621440 | tf_op jit(solution)/shard_map/while/body/eval_jaxpr/reduce_scatter | solution.py:303
  2535.1 80.2 %reduce-scatter.35.cloned.1.call-start = ((), (), s32[]{:S(2)}) async-start(), calls=%async_computation.47 | async-start | bytes 2621440 | tf_op jit(solution)/shard_map/while/body/eval_jaxpr/reduce_scatter | solution.py:300
  2633.3 27.8 reduce-scatter.13.cloned.1.call-start
  2636.2 52.3 %reduce-scatter.17.cloned.1.call-start = ((), (), s32[]{:S(2)}) async-start(), calls=%async_computation.22 | async-start | bytes 1310720 | tf_op jit(solution)/shard_map/reduce_scatter | solution.py:480
  2639.1 76.7 %reduce-scatter.19.cloned.1.call-start = ((), (), s32[]{:S(2)}) async-start(), calls=%async_computation.23 | async-start | bytes 1310720 | tf_op jit(solution)/shard_map/reduce_scatter | solution.py:483
  2642.0 101.3 %reduce-scatter.21.cloned.1.call-start = ((), (), s32[]{:S(2)}) async-start(), calls=%async_computation.24 | async-start | bytes 1310720 | tf_op jit(solution)/shard_map/reduce_scatter | solution.py:486
  2643.9 126.8 %reduce-scatter.27.cloned.1.call-start = ((), (), s32[]{:S(2)}) async-start(), calls=%async_computation.27 | async-start | bytes 1310720 | tf_op jit(solution)/shard_map/reduce_scatter | solution.py:495
  2645.9 165.4 %reduce-scatter.15.cloned.1.call-start = ((), (), s32[]{:S(2)}) async-start(), calls=%async_computation.21 | async-start | bytes 3932160 | tf_op jit(solution)/shard_map/reduce_scatter | solution.py:477
  2649.5 208.6 %reduce-scatter.23.cloned.1.call-start = ((), (), s32[]{:S(2)}) async-start(), calls=%async_computation.25 | async-start | bytes 5242880 | tf_op jit(solution)/shard_map/reduce_scatter | solution.py:489
  2654.1 251.0 %reduce-scatter.25.cloned.1.call-start = ((), (), s32[]{:S(2)}) async-start(), calls=%async_computation.26 | async-start | bytes 5242880 | tf_op jit(solution)/shard_map/reduce_scatter | solution.py:492
  2663.1 27.4 all-to-all-start
  2690.5 27.3 all-to-all-start.2
  2717.8 27.5 all-to-all-start.3
  2745.3 27.4 all-to-all-start.4
  2772.7 41.7 %all-to-all-start.7 = ((bf16[2,2,8,512]{3,0,1,2:T(2,128)(2,1)}), bf16[2,2,8,512]{3,0,1,2:T(2,128)(2,1)S(1)}, u32[]{:S(2)}, u32[]{:S(2)}) async-start(bf16[2,2,8,512]{3,0,1,2:T(2,128)(2,1)} %copy.243), calls=%async_computation.19 | async-start | bytes 65536 | tf_op jit(solution)/shard_map/all_to_all | solution.py:515
  2814.4 47.5 %all-to-all-start.1 = ((bf16[2,2,8,1536]{3,0,1,2:T(2,128)(2,1)}), bf16[2,2,8,1536]{3,0,1,2:T(2,128)(2,1)S(1)}, u32[]{:S(2)}, u32[]{:S(2)}) async-start(bf16[2,2,8,1536]{3,0,1,2:T(2,128)(2,1)} %copy.225), calls=%async_computation.7 | async-start | bytes 196608 | tf_op jit(solution)/shard_map/all_to_all | solution.py:509
  2861.9 47.0 %all-to-all-start.5 = ((bf16[2,2,8,2048]{3,0,1,2:T(2,128)(2,1)}), bf16[2,2,8,2048]{3,0,1,2:T(2,128)(2,1)S(1)}, u32[]{:S(2)}, u32[]{:S(2)}) async-start(bf16[2,2,8,2048]{3,0,1,2:T(2,128)(2,1)} %copy.237), calls=%async_computation.15 | async-start | bytes 262144 | tf_op jit(solution)/shard_map/all_to_all | solution.py:513
  2908.9 12.8 all-to-all-start.6
  (344 other events, 7719.7 us)
Sparse Core Ops, SparseCore 0:
  20.6 94.1 all-gather.88
  172.0 27.1 all-gather.92
  200.7 29.7 all-gather.90
  233.3 61.0 all-gather.94
  297.1 88.5 all-gather.96
  388.4 56.9 all-gather.98
  448.1 57.4 all-gather.102
  508.5 78.3 all-gather.100
  589.8 68.1 all-gather.104
  660.7 95.8 all-gather.116
  758.1 26.7 all-gather.108
  786.3 32.0 all-gather.106
  821.3 57.2 all-gather.110
  881.3 76.4 all-gather.112
  960.4 47.2 all-gather.114
  1010.4 48.1 all-gather.118
  1099.2 45.2 reduce-scatter.28
  1147.0 31.3 reduce-scatter.30
  1226.3 45.8 reduce-scatter.32
  1274.7 31.4 reduce-scatter.34
  1320.8 92.5 all-gather.88
  1473.2 37.3 all-gather.92
  1512.1 23.6 all-gather.90
  1538.6 62.4 all-gather.94
  1603.9 87.6 all-gather.96
  1694.2 58.9 all-gather.98
  1755.9 56.9 all-gather.102
  1815.8 79.0 all-gather.100
  1897.7 68.1 all-gather.104
  1968.7 94.4 all-gather.116
  2064.8 27.8 all-gather.108
  2094.3 32.2 all-gather.106
  2129.3 57.6 all-gather.110
  2189.9 76.3 all-gather.112
  2269.1 47.2 all-gather.114
  2319.0 48.1 all-gather.118
  2407.9 45.2 reduce-scatter.28
  2455.9 31.4 reduce-scatter.30
  2535.2 45.8 reduce-scatter.32
  2583.7 31.4 reduce-scatter.34
Sparse Core Ops, SparseCore 1:
  2636.3 24.8 reduce-scatter.12
  2663.7 24.8 reduce-scatter.16
  2691.0 24.8 reduce-scatter.18
  2718.5 24.8 reduce-scatter.20
  2745.9 24.8 reduce-scatter.26
  2773.5 37.8 reduce-scatter.14
  2813.7 44.4 reduce-scatter.22
  2860.7 44.4 reduce-scatter.24
where the time goes:
time: 2940 us; the launch traced here: 2930 us
  blocking collectives  1310 us (45%)
  waiting for transfers between devices  942 us (32%)
  matrix products  321 us (11%)
  local copies, waits for them, and re-layouts  226 us (8%)
  starting transfers between devices  46.4 us (2%)
  other arithmetic  44.5 us (2%)
    all_gather x4, blocking collectives, fetch_forward(): lax.all_gather(attend_right[layer_index], ('dp', 'ctx'), axis=1, tiled=True)  343 us
    all_gather x4, blocking collectives, fetch_forward(): lax.all_gather(reduce_right[layer_index], ('dp', 'ctx'), axis=1, tiled=True)  199 us
    all_gather x4, blocking collectives, fetch_forward(): lax.all_gather(output_left[layer_index], ('dp', 'ctx'), axis=1, tiled=True)  196 us
    all_gather x4, blocking collectives, fetch_forward(): lax.all_gather(output_right[layer_index], ('dp', 'ctx'), axis=1, tiled=True)  195 us
    all_gather x4, blocking collectives, fetch_forward(): lax.all_gather(attend_left[layer_index], ('dp', 'ctx'), axis=1, tiled=True)  195 us
    all_gather x4, blocking collectives, fetch_forward(): lax.all_gather(expand_left[layer_index], ('dp', 'ctx'), axis=1, tiled=True)  186 us
    reduce_scatter x4, waiting for transfers between devices, layer_backward(): lax.psum_scatter(grad_value_all.astype(jnp.bfloat16), 'ctx', scatter_dime...  137 us
    reduce_scatter x4, waiting for transfers between devices, layer_backward(): lax.psum_scatter(grad_key_all.astype(jnp.bfloat16), 'ctx', scatter_dimens...  136 us
  transfers between devices with their start and end apart: 56, of which 27 were waited for; matrix products, arithmetic and copies ran while one was open for 12% of the time, Pallas kernels for 0%

commit v1 on v0

v1 whole, which is shorter than its diff:
```python
import functools

import jax
import jax.numpy as jnp
from jax import lax
from jax.experimental import pallas as pl
from jax.experimental.pallas import tpu as pltpu
from jax.sharding import Mesh
from jax.sharding import PartitionSpec as P

HEADS = 16
HEAD_DIM = 64
RANK = 16
ADAPTERS = 8
LAYERS = 2
BLK = 256

epsilon = 1e-05
root_factor = 0.7978845608028654
low_type = jnp.bfloat16
wide = jnp.float32

ROWS_BY_ROWS = (((1,), (1,)), ((), ()))
COLS_BY_COLS = (((0,), (0,)), ((), ()))
PLAIN = (((1,), (0,)), ((), ()))
EVERY = ("dp", "chip", "core")
LANE = ("dp", "chip")
CTX = ("chip", "core")


def times(left_side, right_side, dims=PLAIN):
    return lax.dot_general(left_side, right_side, dims, preferred_element_type=wide)


def normalize(values, gain_vector, shift_vector):
    center = jnp.mean(values, axis=-1, keepdims=True)
    spread = values - center
    variance = jnp.mean(spread * spread, axis=-1, keepdims=True)
    return spread * lax.rsqrt(variance + epsilon) * gain_vector + shift_vector


def gelu_tanh(values):
    return (
        0.5
        * values
        * (1.0 + jnp.tanh(root_factor * (values + 0.044715 * values * values * values)))
    )


def block_pair(step, place, blocks):
    half = blocks // 2
    late = step > place
    slot = jnp.where(late, 1, 0)
    key_block = jnp.where(late, step - place - 1, step)
    owner = jnp.where(key_block < half, key_block, blocks - 1 - key_block)
    owner_slot = jnp.where(key_block < half, 0, 1)
    piece = lax.rem(place - owner + half, half)
    return slot, pl.multiple_of((piece * 2 + owner_slot) * BLK, BLK)


def stack_heads(rows, mask):
    zero = jnp.zeros_like(rows)
    return jnp.concatenate([jnp.where(mask, rows, zero), jnp.where(mask, zero, rows)], axis=0)


def attend_forward_kernel(blocks, place_ref, q_ref, k_ref, v_ref, o_ref, stat_ref, queries, scores, total):
    place = place_ref[0]
    mask = lax.broadcasted_iota(jnp.int32, (BLK, 2 * HEAD_DIM), 1) < HEAD_DIM
    for slot in range(2):
        queries[slot] = stack_heads(q_ref[slot * BLK : (slot + 1) * BLK, :] * HEAD_DIM**-0.5, mask)
    steps = [block_pair(step, place, blocks) for step in range(blocks + 1)]
    peaks = [jnp.full((1, 2 * BLK), -1e30, wide)] * 2
    for step, (slot, row) in enumerate(steps):
        block = times(k_ref[pl.ds(row, BLK), :], queries[slot], ROWS_BY_ROWS)
        scores[step] = block
        top = jnp.max(block, axis=0, keepdims=True)
        peaks = [
            jnp.where(slot == which, jnp.maximum(peaks[which], top), peaks[which])
            for which in range(2)
        ]
    total[...] = jnp.zeros_like(total)
    sums = [jnp.zeros((1, 2 * BLK), wide)] * 2
    for step, (slot, row) in enumerate(steps):
        weights = jnp.exp(scores[step] - jnp.where(slot == 0, peaks[0], peaks[1]))
        part = jnp.sum(weights, axis=0, keepdims=True)
        sums = [sums[which] + jnp.where(slot == which, part, 0.0) for which in range(2)]
        weights = weights.astype(low_type)
        turned = v_ref[pl.ds(row, BLK), :].T
        total[slot] = total[slot] + jnp.concatenate(
            [
                times(turned[:HEAD_DIM], weights[:, :BLK]),
                times(turned[HEAD_DIM:], weights[:, BLK:]),
            ],
            axis=0,
        )
    for slot in range(2):
        share = 1.0 / sums[slot]
        held = total[slot]
        held = jnp.concatenate(
            [held[:HEAD_DIM] * share[:, :BLK], held[HEAD_DIM:] * share[:, BLK:]], axis=0
        )
        o_ref[slot * BLK : (slot + 1) * BLK, :] = held.T
        stat_ref[0, slot : slot + 1, :] = peaks[slot] + jnp.log(sums[slot])


def attend_backward_kernel(
    blocks, place_ref, q_ref, k_ref, v_ref, g_ref, o_ref, stat_ref,
    dq_ref, dk_ref, dv_ref, queries, grads, key_sum, value_sum, query_sum, inner,
):
    place = place_ref[0]
    mask = lax.broadcasted_iota(jnp.int32, (BLK, 2 * HEAD_DIM), 1) < HEAD_DIM
    for slot in range(2):
        rows = slice(slot * BLK, (slot + 1) * BLK)
        queries[slot] = stack_heads(q_ref[rows, :] * HEAD_DIM**-0.5, mask)
        grad = g_ref[rows, :]
        grads[slot] = stack_heads(grad, mask)
        both = (grad.astype(wide) * o_ref[rows, :]).T
        inner[slot] = jnp.concatenate(
            [
                jnp.sum(both[:HEAD_DIM], axis=0, keepdims=True),
                jnp.sum(both[HEAD_DIM:], axis=0, keepdims=True),
            ],
            axis=1,
        )
    key_sum[...] = jnp.zeros_like(key_sum)
    value_sum[...] = jnp.zeros_like(value_sum)
    query_sum[...] = jnp.zeros_like(query_sum)
    for step in range(blocks + 1):
        slot, row = block_pair(step, place, blocks)
        at = pl.ds(row, BLK)
        keys, values = k_ref[at, :], v_ref[at, :]
        own, grad = queries[slot], grads[slot]
        probs = jnp.exp(times(keys, own, ROWS_BY_ROWS) - stat_ref[0, pl.ds(slot, 1), :])
        dscores = probs * (times(values, grad, ROWS_BY_ROWS) - inner[slot])
        dscores = dscores.astype(low_type)
        value_sum[at, :] = value_sum[at, :] + times(probs.astype(low_type), grad)
        key_sum[at, :] = key_sum[at, :] + times(dscores, own)
        turned = keys.T
        query_sum[slot] = query_sum[slot] + jnp.concatenate(
            [
                times(turned[:HEAD_DIM], dscores[:, :BLK]),
                times(turned[HEAD_DIM:], dscores[:, BLK:]),
            ],
            axis=0,
        )
    for slot in range(2):
        dq_ref[slot * BLK : (slot + 1) * BLK, :] = (query_sum[slot].T * HEAD_DIM**-0.5).astype(
            low_type
        )
    dk_ref[...] = key_sum[...].astype(low_type)
    dv_ref[...] = value_sum[...].astype(low_type)


def attention_specs(blocks):
    own = pl.BlockSpec((2 * BLK, 2 * HEAD_DIM), lambda pair, place: (0, pair))
    every = pl.BlockSpec((blocks * BLK, 2 * HEAD_DIM), lambda pair, place: (0, pair))
    stats = pl.BlockSpec((1, 2, 2 * BLK), lambda pair, place: (pair, 0, 0))
    return own, every, stats


def attend_forward(place, queries, keys, values):
    blocks, columns = keys.shape[0] // BLK, queries.shape[1]
    pairs = columns // (2 * HEAD_DIM)
    own, every, stats = attention_specs(blocks)
    return pl.pallas_call(
        functools.partial(attend_forward_kernel, blocks),
        out_shape=(
            jax.ShapeDtypeStruct(queries.shape, wide),
            jax.ShapeDtypeStruct((pairs, 2, 2 * BLK), wide),
        ),
        grid_spec=pltpu.PrefetchScalarGridSpec(
            num_scalar_prefetch=1,
            grid=(pairs,),
            in_specs=[own, every, every],
            out_specs=[own, stats],
            scratch_shapes=[
                pltpu.VMEM((2, 2 * BLK, 2 * HEAD_DIM), low_type),
                pltpu.VMEM((blocks + 1, BLK, 2 * BLK), wide),
                pltpu.VMEM((2, 2 * HEAD_DIM, BLK), wide),
            ],
        ),
        compiler_params=pltpu.CompilerParams(vmem_limit_bytes=48 * 2**20),
        name="attend_forward",
    )(place, queries, keys, values)


def attend_backward(place, queries, keys, values, grads, attended, stat):
    blocks, columns = keys.shape[0] // BLK, queries.shape[1]
    pairs = columns // (2 * HEAD_DIM)
    own, every, stats = attention_specs(blocks)
    return pl.pallas_call(
        functools.partial(attend_backward_kernel, blocks),
        out_shape=(
            jax.ShapeDtypeStruct(queries.shape, low_type),
            jax.ShapeDtypeStruct(keys.shape, low_type),
            jax.ShapeDtypeStruct(keys.shape, low_type),
        ),
        grid_spec=pltpu.PrefetchScalarGridSpec(
            num_scalar_prefetch=1,
            grid=(pairs,),
            in_specs=[own, every, every, own, own, stats],
            out_specs=[own, every, every],
            scratch_shapes=[
                pltpu.VMEM((2, 2 * BLK, 2 * HEAD_DIM), low_type),
                pltpu.VMEM((2, 2 * BLK, 2 * HEAD_DIM), low_type),
                pltpu.VMEM((blocks * BLK, 2 * HEAD_DIM), wide),
                pltpu.VMEM((blocks * BLK, 2 * HEAD_DIM), wide),
                pltpu.VMEM((2, 2 * HEAD_DIM, BLK), wide),
                pltpu.VMEM((2, 1, 2 * BLK), wide),
            ],
        ),
        compiler_params=pltpu.CompilerParams(vmem_limit_bytes=48 * 2**20),
        name="attend_backward",
    )(place, queries, keys, values, grads, attended, stat)


def spread_tokens(pair, below, count):
    half = count // 2
    across = [(b, half + b if b < half else count - 1 - b) for b in range(count)]
    inside = [(b, half + count - 1 - b) for b in range(half, count)]
    got = lax.ppermute(jnp.where(below, pair[1], pair[0]), CTX, across)
    other = lax.ppermute(pair[1], CTX, inside)
    return jnp.concatenate(
        [jnp.where(below, pair[0], got), jnp.where(below, got, other)], axis=0
    )


def collect_tokens(rows, below, count):
    half = count // 2
    across = [(half + b if b < half else count - 1 - b, b) for b in range(count)]
    inside = [(half + count - 1 - b, b) for b in range(half, count)]
    early, late = rows[:BLK], rows[BLK:]
    got = lax.ppermute(jnp.where(below, late, early), CTX, across)
    other = lax.ppermute(late, CTX, inside)
    return jnp.stack([jnp.where(below, early, got), jnp.where(below, got, other)])


def ring_gather(rows, count):
    half = count // 2
    pieces = [rows]
    for step in range(1, half):
        pairs = [
            (side * half + b, side * half + (b + step) % half)
            for side in range(2)
            for b in range(half)
        ]
        pieces.append(lax.ppermute(rows, CTX, pairs))
    return jnp.concatenate(pieces, axis=0)


def ring_scatter(rows, count):
    half = count // 2
    size = rows.shape[0] // half
    total = rows[:size].astype(wide)
    for step in range(1, half):
        pairs = [
            (side * half + b, side * half + (b - step) % half)
            for side in range(2)
            for b in range(half)
        ]
        part = rows[step * size : (step + 1) * size]
        total = total + lax.ppermute(part, CTX, pairs).astype(wide)
    return total


def layer_forward(current, frozen, picked, extras, place, count):
    attend_weight, output_weight, expand_weight, reduce_weight = frozen
    (
        attend_left, attend_right, output_left, output_right,
        expand_left, expand_right, reduce_left, reduce_right,
    ) = picked
    (
        attend_bias, output_bias, expand_bias, reduce_bias,
        first_gain, first_shift, second_gain, second_shift,
    ) = extras
    columns = current.shape[1]
    normed_one = normalize(current, first_gain, first_shift).astype(low_type)
    rank_attend = times(normed_one, attend_left, ROWS_BY_ROWS).astype(low_type)
    biases = [attend_bias[:columns], jnp.zeros((columns,), wide), attend_bias[columns:]]
    queries, keys, values = (
        (
            times(normed_one, attend_weight[part])
            + times(rank_attend, attend_right[:, part * columns : (part + 1) * columns])
            + biases[part]
        ).astype(low_type)
        for part in range(3)
    )
    key_all, value_all = ring_gather(keys, count), ring_gather(values, count)
    attended, stat = attend_forward(place, queries, key_all, value_all)
    attended_low = attended.astype(low_type)
    rank_output = times(attended_low, output_left, ROWS_BY_ROWS).astype(low_type)
    middle = (
        current + times(attended_low, output_weight) + times(rank_output, output_right) + output_bias
    )
    normed_two = normalize(middle, second_gain, second_shift).astype(low_type)
    rank_expand = times(normed_two, expand_left, ROWS_BY_ROWS).astype(low_type)
    parts = len(expand_weight)
    expanded = [
        times(normed_two, expand_weight[part])
        + times(rank_expand, expand_right[:, part * columns : (part + 1) * columns])
        + expand_bias[part * columns : (part + 1) * columns]
        for part in range(parts)
    ]
    active = [gelu_tanh(member).astype(low_type) for member in expanded]
    rank_reduce = sum(
        times(active[part], reduce_left[:, part * columns : (part + 1) * columns], ROWS_BY_ROWS)
        for part in range(parts)
    ).astype(low_type)
    result = (
        middle
        + sum(times(active[part], reduce_weight[part]) for part in range(parts))
        + times(rank_reduce, reduce_right)
        + reduce_bias
    )
    kept = (
        current, normed_one, rank_attend, queries, key_all, value_all, attended, attended_low, stat,
        rank_output, middle, normed_two, rank_expand, expanded, active, rank_reduce,
    )
    return result, kept


def layer_backward(grad_result, kept, frozen, picked, extras, place, count):
    attend_weight, output_weight, expand_weight, reduce_weight = frozen
    (
        attend_left, attend_right, output_left, output_right,
        expand_left, expand_right, reduce_left, reduce_right,
    ) = picked
    first_gain, first_shift, second_gain, second_shift = extras[4:]
    (
        current, normed_one, rank_attend, queries, key_all, value_all, attended, attended_low, stat,
        rank_output, middle, normed_two, rank_expand, expanded, active, rank_reduce,
    ) = kept
    columns = current.shape[1]
    parts = len(expand_weight)

    def piece(member, part):
        return member[:, part * columns : (part + 1) * columns]

    grad_reduce = grad_result.astype(low_type)
    turn_reduce = times(grad_reduce, reduce_right, ROWS_BY_ROWS).astype(low_type)
    grad_expand = []
    for part in range(parts):
        grad_active = times(grad_reduce, reduce_weight[part], ROWS_BY_ROWS) + times(
            turn_reduce, piece(reduce_left, part)
        )
        grad_expand.append(jax.vjp(gelu_tanh, expanded[part])[1](grad_active)[0].astype(low_type))
    reduce_left_g = jnp.concatenate(
        [times(turn_reduce, active[part], COLS_BY_COLS) for part in range(parts)], axis=1
    )
    reduce_right_g = times(rank_reduce, grad_reduce, COLS_BY_COLS)
    turn_expand = sum(
        times(grad_expand[part], piece(expand_right, part), ROWS_BY_ROWS) for part in range(parts)
    ).astype(low_type)
    grad_second = sum(
        times(grad_expand[part], expand_weight[part], ROWS_BY_ROWS) for part in range(parts)
    ) + times(turn_expand, expand_left)
    expand_left_g = times(turn_expand, normed_two, COLS_BY_COLS)
    expand_right_g = jnp.concatenate(
        [times(rank_expand, grad_expand[part], COLS_BY_COLS) for part in range(parts)], axis=1
    )
    pull = jax.vjp(lambda rows: normalize(rows, second_gain, second_shift), middle)[1]
    grad_middle = grad_result + pull(grad_second)[0]
    grad_project = grad_middle.astype(low_type)
    turn_output = times(grad_project, output_right, ROWS_BY_ROWS).astype(low_type)
    grad_attended = (
        times(grad_project, output_weight, ROWS_BY_ROWS) + times(turn_output, output_left)
    ).astype(low_type)
    output_left_g = times(turn_output, attended_low, COLS_BY_COLS)
    output_right_g = times(rank_output, grad_project, COLS_BY_COLS)
    grad_query, grad_keys, grad_values = attend_backward(
        place, queries, key_all, value_all, grad_attended, attended, stat
    )
    joined = (
        grad_query,
        ring_scatter(grad_keys, count).astype(low_type),
        ring_scatter(grad_values, count).astype(low_type),
    )
    turn_attend = sum(
        times(joined[part], piece(attend_right, part), ROWS_BY_ROWS) for part in range(3)
    ).astype(low_type)
    grad_first = sum(
        times(joined[part], attend_weight[part], ROWS_BY_ROWS) for part in range(3)
    ) + times(turn_attend, attend_left)
    attend_left_g = times(turn_attend, normed_one, COLS_BY_COLS)
    attend_right_g = jnp.concatenate(
        [times(rank_attend, joined[part], COLS_BY_COLS) for part in range(3)], axis=1
    )
    pull = jax.vjp(lambda rows: normalize(rows, first_gain, first_shift), current)[1]
    grad_current = grad_middle + pull(grad_first)[0]
    return grad_current, (
        attend_left_g, attend_right_g, output_left_g, output_right_g,
        expand_left_g, expand_right_g, reduce_left_g, reduce_right_g,
    )


def local(
    tokens, cotangent, adapter_ids, attend_weight, output_weight, expand_weight, reduce_weight,
    attend_bias, output_bias, expand_bias, reduce_bias, first_gain, first_shift, second_gain, second_shift,
    *adapters,
):
    data_count, chips = lax.axis_size("dp"), lax.axis_size("chip")
    count = chips * lax.axis_size("core")
    half = count // 2
    devices = data_count * count
    data_rank, core = lax.axis_index("dp"), lax.axis_index("core")
    rank = lax.axis_index("chip") * 2 + core
    below = rank < half
    place = jnp.reshape(lax.rem(rank, half), (1,)).astype(jnp.int32)
    columns = tokens.shape[2]

    lane_chip = jnp.arange(data_count * chips, dtype=jnp.int32)
    lane_sequence = (lane_chip // chips) * 2 + (lane_chip % chips) // (chips // 2)
    lane_adapter = jnp.take(adapter_ids, lane_sequence)

    current = spread_tokens(tokens, below, count).astype(wide)
    grad_current = spread_tokens(cotangent, below, count).astype(wide)

    sizes = [member.shape[2] for member in adapters]
    packed = jnp.concatenate([jnp.swapaxes(member, 2, 3) for member in adapters], axis=3)
    chosen = jnp.moveaxis(jnp.take(packed, lane_adapter, axis=1), 1, 0)
    mine = lax.all_to_all(chosen, LANE, split_axis=0, concat_axis=0, tiled=True)
    theirs = lax.ppermute(mine, "core", [(0, 1), (1, 0)])
    both = jnp.stack(
        [jnp.where(core == 0, mine, theirs), jnp.where(core == 0, theirs, mine)], axis=1
    )

    def factors(layer_index):
        found, first = [], 0
        for size in sizes:
            part = both[:, :, layer_index, :, first : first + size]
            found.append(jnp.transpose(part, (2, 0, 1, 3)).reshape(RANK, devices * size))
            first += size
        return tuple(found)

    def shards(layer_index):
        lists = [attend_weight[layer_index], output_weight[layer_index], expand_weight[layer_index]]
        blocks = [
            member[:, first : first + columns]
            for member in lists
            for first in range(0, member.shape[1], columns)
        ]
        return jnp.concatenate(blocks + [reduce_weight[layer_index]], axis=0)

    def frozen_of(whole):
        rows = columns // devices
        blocks = [
            whole[:, part * rows : (part + 1) * rows, :].reshape(columns, columns)
            for part in range(8)
        ]
        members = devices // 4
        reduce_blocks = [
            whole[part * members : (part + 1) * members, 8 * rows :, :].reshape(columns, columns)
            for part in range(4)
        ]
        return blocks[:3], blocks[3], blocks[4:8], reduce_blocks

    extras = [
        tuple(
            member[layer_index]
            for member in (
                attend_bias, output_bias, expand_bias, reduce_bias,
                first_gain, first_shift, second_gain, second_shift,
            )
        )
        for layer_index in range(LAYERS)
    ]
    gathered = [
        lax.all_gather(shards(layer_index), EVERY, axis=0) for layer_index in range(LAYERS)
    ]
    frozen = [frozen_of(member) for member in gathered]
    picked = [factors(layer_index) for layer_index in range(LAYERS)]
    kept = []
    for layer_index in range(LAYERS):
        current, keep = layer_forward(
            current, frozen[layer_index], picked[layer_index], extras[layer_index], place, count
        )
        kept.append(keep)

    owner_adapter = (lane_adapter[:, None] == jnp.arange(ADAPTERS)[None, :]).astype(wide)
    summed = [None] * LAYERS
    for layer_index in reversed(range(LAYERS)):
        grad_current, terms = layer_backward(
            grad_current,
            kept[layer_index],
            frozen[layer_index],
            picked[layer_index],
            extras[layer_index],
            place,
            count,
        )
        owned = jnp.concatenate(
            [
                jnp.transpose(
                    term.astype(low_type).reshape(RANK, data_count * chips, 2, size), (2, 1, 0, 3)
                )
                for term, size in zip(terms, sizes)
            ],
            axis=3,
        )
        sent = lax.ppermute(jnp.where(core == 0, owned[1], owned[0]), "core", [(0, 1), (1, 0)])
        total = jnp.where(core == 0, owned[0], owned[1]).astype(wide) + sent.astype(wide)
        received = lax.all_to_all(
            total.astype(low_type), LANE, split_axis=0, concat_axis=0, tiled=True
        )
        summed[layer_index] = jnp.einsum(
            "sa,srp->arp", owner_adapter, received.astype(wide), precision=lax.Precision.HIGHEST
        )
    results, first = [], 0
    for size in sizes:
        member = jnp.stack([layer[:, :, first : first + size] for layer in summed])
        results.append(jnp.swapaxes(member, 2, 3))
        first += size
    outputs = collect_tokens(current.astype(low_type), below, count)
    early_late = grad_current
    moved = collect_tokens(early_late, below, count)
    return (outputs, moved, *results)


def solution(mesh):
    count = mesh.shape["ctx"]
    inner = Mesh(mesh.devices.reshape(mesh.shape["dp"], count // 2, 2), EVERY)
    token_spec, factor_spec = P("dp", CTX, None), P(None, None, EVERY, None)
    in_specs = (
        (token_spec,) * 2 + (P(),) + (P(None, EVERY, None),) * 4 + (P(),) * 8 + (factor_spec,) * 8
    )
    out_specs = (token_spec,) * 2 + (factor_spec,) * 8
    return jax.shard_map(local, mesh=inner, in_specs=in_specs, out_specs=out_specs, check_vma=False)
```

time: 2940 us -> 778 us (0.26)
  blocking collectives: 1310 us -> 0 us
  waiting for transfers between devices: 942 us -> 236 us
  matrix products: 321 us -> 190 us
  Pallas kernels: 0 us -> 71.5 us
  local copies, waits for them, and re-layouts: 226 us -> 175 us
    all_gather x24 -> x0, blocking collectives: 1310 us -> none  [the longest x4 343 us: fetch_forward(): lax.all_gather(attend_right[layer_index], ('dp', 'ctx'), axis=1, tiled=True)]
    reduce_scatter x16 -> x0, waiting for transfers between devices: 458 us -> none  [the longest x4 137 us: layer_backward(): lax.psum_scatter(grad_value_all.astype(jnp.bfloat16), 'ctx', scatter_dime...]
    all_gather x32 -> x2, waiting for transfers between devices: 466 us -> 187 us  [local(): lax.all_gather(shards(layer_index), EVERY, axis=0)]
    dot_general x164 -> x146, matrix products: 321 us -> 190 us  [the longest x144 187 us: times(): lax.dot_general(left_side, right_side, dims, preferred_element_type=wide)]
    while x738 -> x0, local copies, waits for them, and re-layouts: 75.7 us -> none
    pallas_call x0 -> x4, Pallas kernels: none -> 71.5 us  [the longest x2 43 us: attend_backward(): pl.pallas_call(functools.partial(attend_backward_kernel, blocks), out_sha...]
    convert_element_type x36 -> x4, local copies, waits for them, and re-layouts: 51.8 us -> 1.09 us  [local(): term.astype(low_type).reshape(RANK, data_count * chips, 2, size)]
    ppermute x0 -> x19, waiting for transfers between devices: none -> 41.7 us  [the longest x2 24.8 us: spread_tokens(): got = lax.ppermute(jnp.where(below, pair[1], pair[0]), CTX, across)]
  transfers between devices with their start and end apart: 56 -> 24, of which waited for: 27 -> 5; matrix products, arithmetic and copies ran while one was open for 12% -> 33% of each run, Pallas kernels for 0% -> 6%
where the time goes in v1:
time: 778 us; the launch traced here: 765 us
  waiting for transfers between devices  236 us (30%)
  matrix products  190 us (24%)
  local copies, waits for them, and re-layouts  175 us (22%)
  Pallas kernels  71.5 us (9%)
  other arithmetic  39.8 us (5%)
  starting transfers between devices  35.4 us (5%)
  between operations  17.2 us (2%)
    dot_general x144, matrix products, times(): lax.dot_general(left_side, right_side, dims, preferred_element_type=wide)  187 us
    all_gather x2, waiting for transfers between devices, local(): lax.all_gather(shards(layer_index), EVERY, axis=0)  187 us
    pallas_call x2, Pallas kernels, attend_backward(): pl.pallas_call(functools.partial(attend_backward_kernel, blocks), out_sha...  43 us
    unnamed x478, local copies, waits for them, and re-layouts  32.1 us
    pallas_call x2, Pallas kernels, attend_forward(): pl.pallas_call(functools.partial(attend_forward_kernel, blocks), out_shap...  28.5 us
    ppermute x2, waiting for transfers between devices, spread_tokens(): got = lax.ppermute(jnp.where(below, pair[1], pair[0]), CTX, across)  24.8 us
    slice x2, local copies, waits for them, and re-layouts, frozen_of(): whole[:, part * rows:(part + 1) * rows, :].reshape(columns, columns)  22.4 us
    transpose x16, local copies, waits for them, and re-layouts, factors(): jnp.transpose(part, (2, 0, 1, 3)).reshape(RANK, devices * size)  21.4 us
  transfers between devices with their start and end apart: 24, of which 5 were waited for; matrix products, arithmetic and copies ran while one was open for 33% of the time, Pallas kernels for 6%

profile of v1, /device:TPU:0, one launch (start us, length us, event | category | flops | bytes accessed | tf_op | source)
XLA Modules:
  0.0 764.8 jit_solution(10686515189505893160)
XLA Ops:
  15.5 8.5 %all-to-all-start = ((bf16[16,2,16,512]{3,2,1,0:T(8,128)(2,1)}), bf16[16,2,16,512]{3,2,1,0:T(8,128)(2,1)}, u32[]{:S(2)}, u32[]{:S(2)}) async-start(bf16[16,2,16,512]{3,2,1,0:T(8,128)(2,1)} %broadcast_select_fusion), calls=%async_computation | async-start | bytes 1048576 | tf_op jit(solution)/shard_map/all_to_all | solution.py:421
  24.9 1.9 collective-permute-start.9
  34.7 24.8 %collective-permute-done = bf16[256,1024]{1,0:T(8,128)(2,1)} collective-permute-done((bf16[256,1024]{1,0:T(8,128)(2,1)S(1)}, bf16[256,1024]{1,0:T(8,128)(2,1)}, u32[]{:S(2)}, u32[]{:S(2)}) %collective-permute-start) | collective-permute-done | bytes 524320 | tf_op jit(solution)/shard_map/ppermute | solution.py:221
  62.2 2.6 bitcast_select_fusion
  72.7 1.7 copy.205
  85.8 1.7 copy.200
  103.3 1.8 reshape.474
  105.0 1.8 copy.210
  112.0 1.8 fusion.156
  113.8 1.8 fusion.160
  115.6 1.8 fusion.163
  117.4 1.8 fusion.106
  119.2 1.8 fusion.109
  121.0 1.8 fusion.112
  122.8 1.8 fusion.115
  124.6 55.5 %all-gather.5.cloned.1.call-done = bf16[12288,1024]{1,0:T(8,128)(2,1)} async-done(((bf16[384,1024]{1,0:T(8,128)(2,1)}), bf16[12288,1024]{1,0:T(8,128)(2,1)}) %all-gather.5.cloned.1.call-update) | async-done | bytes 25165840 | tf_op jit(solution)/shard_map/all_gather | solution.py:468
  180.1 10.8 %fusion.196 = (bf16[32,32,1024]{2,1,0:T(8,128)(2,1)}, bf16[32,32,1024]{2,1,0:T(8,128)(2,1)}, bf16[32,32,1024]{2,1,0:T(8,128)(2,1)}, bf16[32,32,1024]{2,1,0:T(8,1...) fusion(bf16[32,384,1024]{2,1,0:T(8,128)(2,1)} %bitcast.501), kind=kLoop, calls=%fused_computation.499 | loop fusion | bytes 33554432 | tf_op jit(solution)/shard_map/slice | solution.py:447
  190.9 2.3 add_convert_fusion.13
  194.1 2.2 add_convert_fusion.14
  196.6 6.2 fusion.195
  204.1 131.7 %all-gather.7.cloned.1.call-done = bf16[12288,1024]{1,0:T(8,128)(2,1)} async-done(((bf16[384,1024]{1,0:T(8,128)(2,1)}), bf16[12288,1024]{1,0:T(8,128)(2,1)}) %all-gather.7.cloned.1.call-update) | async-done | bytes 25165840 | tf_op jit(solution)/shard_map/all_gather | solution.py:468
  335.8 11.6 %fusion.194 = (bf16[32,32,1024]{2,1,0:T(8,128)(2,1)}, bf16[32,32,1024]{2,1,0:T(8,128)(2,1)}, bf16[32,32,1024]{2,1,0:T(8,128)(2,1)}, bf16[32,32,1024]{2,1,0:T(8,1...) fusion(bf16[32,384,1024]{2,1,0:T(8,128)(2,1)} %bitcast.499), kind=kLoop, calls=%fused_computation.497 | loop fusion | bytes 33554432 | tf_op jit(solution)/shard_map/slice | solution.py:447
  347.4 3.8 pad_maximum_fusion.1.v_ref
  351.2 1.7 pad_maximum_fusion.k_ref
  352.9 14.3 %attend_forward.2 = (f32[512,1024]{1,0:T(8,128)S(1)}, f32[8,2,512]{2,1,0:T(2,128)S(1)}) custom-call(s32[1]{0:T(128)} %bitcast.2.place_ref, bf16[512,1024]{1,0:T(8,128)(2,1)S(1)} %add_convert_fusion.15.q_ref, bf16[1024,1024]{1,0:T(8,128)(2,1)S(1)} %pad_maximum_fusion.k_ref, bf16[1024,1024]{1,0:T(8,128)(2,1)} %pad_maximum_fusion.1.v_ref), custom_call_target="tpu_custom_call" | custom-call | tf_op jit(solution)/shard_map/attend_forward/pallas_call | solution.py:165
  379.9 2.4 multiply_convert_fusion.6
  383.5 2.3 multiply_convert_fusion.7
  386.7 2.3 multiply_convert_fusion.5
  390.6 2.7 multiply_convert_fusion.4
  404.1 6.2 fusion.193
  413.8 14.2 %attend_forward.3 = (f32[512,1024]{1,0:T(8,128)S(1)}, f32[8,2,512]{2,1,0:T(2,128)S(1)}) custom-call(s32[1]{0:T(128)} %bitcast.2.place_ref, bf16[512,1024]{1,0:T(8,128)(2,1)S(1)} %add_convert_fusion.10.q_ref, bf16[1024,1024]{1,0:T(8,128)(2,1)S(1)} %pad_maximum_fusion.2.k_ref, bf16[1024,1024]{1,0:T(8,128)(2,1)} %pad_maximum_fusion.3.v_ref), custom_call_target="tpu_custom_call" | custom-call | tf_op jit(solution)/shard_map/attend_forward/pallas_call | solution.py:165
  437.3 3.4 fusion.35
  442.8 2.6 fusion.228
  450.2 3.8 fusion.31
  456.2 2.6 fusion.226
  463.6 3.4 fusion.27
  469.1 2.6 fusion.224
  476.1 3.6 fusion.23
  482.2 2.6 fusion.222
  492.1 2.6 fusion.233
  511.1 4.3 add_convert_fusion.6
  518.9 21.5 %attend_backward.2 = (bf16[512,1024]{1,0:T(8,128)(2,1)S(1)}, bf16[1024,1024]{1,0:T(8,128)(2,1)S(1)}, bf16[1024,1024]{1,0:T(8,128)(2,1)}) custom-call(s32[1]{0:T(128)} %bitcast.2.place_ref, bf16[512,1024]{1,0:T(8,128)(2,1)S(1)} %add_convert_fusion.10.q_ref, bf16[1024,1024]{1,0:T(8,128)(2,1)} %copy-done.6, bf16[1024,1024]{1,0:T(8,128)(2,1)} %pad_maximum_fusion.3.v_ref, ...), custom_call_target="tpu_custom_call" | custom-call | tf_op jit(solution)/shard_map/attend_backward/pallas_call | solution.py:191
  556.8 3.0 fusion.234
  569.0 2.9 multiply_reduce_fusion.1
  585.6 2.5 fusion.7
  591.1 2.1 fusion.11
  595.4 2.1 fusion.15
  599.7 2.3 fusion.19
  610.5 2.6 fusion.244
  620.9 21.5 %attend_backward.3 = (bf16[512,1024]{1,0:T(8,128)(2,1)S(1)}, bf16[1024,1024]{1,0:T(8,128)(2,1)S(1)}, bf16[1024,1024]{1,0:T(8,128)(2,1)}) custom-call(s32[1]{0:T(128)} %bitcast.2.place_ref, bf16[512,1024]{1,0:T(8,128)(2,1)S(1)} %copy-done.8, bf16[1024,1024]{1,0:T(8,128)(2,1)} %copy-done.3, bf16[1024,1024]{1,0:T(8,128)(2,1)} %pad_maximum_fusion.1.v_ref, ...), custom_call_target="tpu_custom_call" | custom-call | tf_op jit(solution)/shard_map/attend_backward/pallas_call | solution.py:191
  642.5 2.4 slice.611
  646.1 2.6 fusion.245
  648.7 1.9 select_bitcast_fusion.2
  651.5 5.9 all-to-all-start.2
  657.5 2.3 pad_maximum_fusion.6
  688.9 1.9 fusion.154
  690.9 1.8 fusion.158
  693.3 1.8 fusion.246
  696.8 1.7 convolution_convert_fusion.29
  702.4 3.6 fusion.187
  706.0 3.6 fusion.40
  713.4 7.1 all-to-all-start.1
  724.3 6.6 all-to-all-done.1
  732.3 16.8 %collective-permute-done.15 = f32[256,1024]{1,0:T(8,128)S(1)} collective-permute-done((f32[256,1024]{1,0:T(8,128)}, f32[256,1024]{1,0:T(8,128)S(1)}, u32[]{:S(2)}, u32[]{:S(2)}) %collective-permute-start.15) | collective-permute-done | bytes 1048608 | tf_op jit(solution)/shard_map/ppermute | solution.py:233
  (812 shorter events, 268.0 us)
Async XLA Ops:
  7.2 172.8 %all-gather.5.cloned.1.call-start = ((), (), s32[]{:S(2)}) async-start(), calls=%async_computation.3 | async-start | bytes 25952256 | tf_op jit(solution)/shard_map/all_gather | solution.py:468
  10.7 325.1 %all-gather.7.cloned.1.call-start = ((), (), s32[]{:S(2)}) async-start(), calls=%async_computation.4 | async-start | bytes 25952256 | tf_op jit(solution)/shard_map/all_gather | solution.py:468
  12.1 11.9 %copy-start.66 = (bf16[2,256,1024]{2,1,0:T(8,128)(2,1)S(1)}, bf16[2,256,1024]{2,1,0:T(8,128)(2,1)}, u32[]{:S(2)}) copy-start(bf16[2,256,1024]{2,1,0:T(8,128)(2,1)} %param.24) | copy-start | bytes 3145732
  15.5 13.7 %copy-start.65 = (bf16[2,256,1024]{2,1,0:T(8,128)(2,1)S(1)}, bf16[2,256,1024]{2,1,0:T(8,128)(2,1)}, u32[]{:S(2)}) copy-start(bf16[2,256,1024]{2,1,0:T(8,128)(2,1)} %param.23) | copy-start | bytes 3145732
  15.5 46.1 %all-to-all-start = ((bf16[16,2,16,512]{3,2,1,0:T(8,128)(2,1)}), bf16[16,2,16,512]{3,2,1,0:T(8,128)(2,1)}, u32[]{:S(2)}, u32[]{:S(2)}) async-start(bf16[16,2,16,512]{3,2,1,0:T(8,128)(2,1)} %broadcast_select_fusion), calls=%async_computation | async-start | bytes 1048576 | tf_op jit(solution)/shard_map/all_to_all | solution.py:421
  24.9 37.3 %collective-permute-start.9 = (bf16[256,1024]{1,0:T(8,128)(2,1)}, bf16[256,1024]{1,0:T(8,128)(2,1)}, u32[]{:S(2)}, u32[]{:S(2)}) collective-permute-start(bf16[256,1024]{1,0:T(8,128)(2,1)} %bitcast_select_fusion.1), channel_id=1, source_target_pairs={{0,2},{1,3},{2,1},{3,0},{4,6},{5,7},{6,5},{7,4},{8,10},{9,11},{10,... | collective-permute-start | bytes 1572872 | tf_op jit(solution)/shard_map/ppermute | solution.py:221
  27.7 34.5 %collective-permute-start.10 = (bf16[256,1024]{1,0:T(8,128)(2,1)}, bf16[256,1024]{1,0:T(8,128)(2,1)}, u32[]{:S(2)}, u32[]{:S(2)}) collective-permute-start(bf16[256,1024]{1,0:T(8,128)(2,1)} %slice_bitcast_fusion), channel_id=1, source_target_pairs={{2,3},{3,2},{6,7},{7,6},{10,11},{11,10},{14,15},{15,14},{18,19},{1... | collective-permute-start | bytes 1572872 | tf_op jit(solution)/shard_map/ppermute | solution.py:222
  29.2 30.3 %collective-permute-start = (bf16[256,1024]{1,0:T(8,128)(2,1)S(1)}, bf16[256,1024]{1,0:T(8,128)(2,1)}, u32[]{:S(2)}, u32[]{:S(2)}) collective-permute-start(bf16[256,1024]{1,0:T(8,128)(2,1)S(1)} %bitcast_select_fusion.3), channel_id=1, source_target_pairs={{0,2},{1,3},{2,1},{3,0},{4,6},{5,7},{6,5},{7,4},{8,10},{9,11},{10,... | collective-permute-start | bytes 1572872 | tf_op jit(solution)/shard_map/ppermute | solution.py:221
  30.1 29.5 %collective-permute-start.1 = (bf16[256,1024]{1,0:T(8,128)(2,1)S(1)}, bf16[256,1024]{1,0:T(8,128)(2,1)}, u32[]{:S(2)}, u32[]{:S(2)}) collective-permute-start(bf16[256,1024]{1,0:T(8,128)(2,1)S(1)} %slice_bitcast_fusion.1), channel_id=1, source_target_pairs={{2,3},{3,2},{6,7},{7,6},{10,11},{11,10},{14,15},{15,14},{18,19},{1... | collective-permute-start | bytes 1572872 | tf_op jit(solution)/shard_map/ppermute | solution.py:222
  32.8 29.0 %copy-start.188 = (f32[1,1024]{1,0:T(1,128)}, f32[1,1024]{1,0:T(1,128)S(1)}, u32[]{:S(2)}) copy-start(f32[1,1024]{1,0:T(1,128)S(1)} %get-tuple-element.182) | copy-start | bytes 12292
  34.0 337.4 %copy-start.190 = (f32[1,1024]{1,0:T(1,128)}, f32[1,1024]{1,0:T(1,128)S(1)}, u32[]{:S(2)}) copy-start(f32[1,1024]{1,0:T(1,128)S(1)} %get-tuple-element.176) | copy-start | bytes 12292
  60.9 307.6 %copy-start.17 = (bf16[256,1024]{1,0:T(8,128)(2,1)}, bf16[256,1024]{1,0:T(8,128)(2,1)S(1)}, u32[]{:S(2)}) copy-start(bf16[256,1024]{1,0:T(8,128)(2,1)S(1)} %get-tuple-element.141) | copy-start | bytes 1572868
  60.9 307.6 %copy-start.19 = (bf16[256,1024]{1,0:T(8,128)(2,1)}, bf16[256,1024]{1,0:T(8,128)(2,1)S(1)}, u32[]{:S(2)}) copy-start(bf16[256,1024]{1,0:T(8,128)(2,1)S(1)} %get-tuple-element.142) | copy-start | bytes 1572868
  61.6 3.2 collective-permute-start.2
  62.2 140.6 %copy-start.29 = (bf16[512,1024]{1,0:T(8,128)(2,1)}, bf16[512,1024]{1,0:T(8,128)(2,1)S(1)}, u32[]{:S(2)}) copy-start(bf16[512,1024]{1,0:T(8,128)(2,1)S(1)} %fusion.39) | copy-start | bytes 3145732
  70.0 45.7 %copy-start.115 = (bf16[16,3072]{1,0:T(8,128)(2,1)}, bf16[16,3072]{1,0:T(8,128)(2,1)S(1)}, u32[]{:S(2)}) copy-start(bf16[16,3072]{1,0:T(8,128)(2,1)S(1)} %reshape.455) | copy-start | bytes 294916
  72.7 50.0 %copy-start.108 = (bf16[16,4096]{1,0:T(8,128)(2,1)}, bf16[16,4096]{1,0:T(8,128)(2,1)S(1)}, u32[]{:S(2)}) copy-start(bf16[16,4096]{1,0:T(8,128)(2,1)S(1)} %reshape.491) | copy-start | bytes 393220
  83.9 27.3 %copy-start.48 = (bf16[256,1024]{1,0:T(8,128)(2,1)S(1)}, bf16[256,1024]{1,0:T(8,128)(2,1)}, u32[]{:S(2)}) copy-start(bf16[256,1024]{1,0:T(8,128)(2,1)} %get-tuple-element.135) | copy-start | bytes 1572868
  83.9 27.3 %copy-start.51 = (bf16[256,1024]{1,0:T(8,128)(2,1)S(1)}, bf16[256,1024]{1,0:T(8,128)(2,1)}, u32[]{:S(2)}) copy-start(bf16[256,1024]{1,0:T(8,128)(2,1)} %get-tuple-element.136) | copy-start | bytes 1572868
  85.8 25.5 %copy-start.155 = (bf16[16,1024]{1,0:T(8,128)(2,1)}, bf16[16,1024]{1,0:T(8,128)(2,1)S(1)}, u32[]{:S(2)}) copy-start(bf16[16,1024]{1,0:T(8,128)(2,1)S(1)} %reshape.492) | copy-start | bytes 98308
  88.6 23.0 %copy-start.134 = (bf16[16,1024]{1,0:T(8,128)(2,1)}, bf16[16,1024]{1,0:T(8,128)(2,1)S(1)}, u32[]{:S(2)}) copy-start(bf16[16,1024]{1,0:T(8,128)(2,1)S(1)} %reshape.454) | copy-start | bytes 98308
  91.4 275.8 %copy-start.132 = (bf16[16,1024]{1,0:T(8,128)(2,1)}, bf16[16,1024]{1,0:T(8,128)(2,1)S(1)}, u32[]{:S(2)}) copy-start(bf16[16,1024]{1,0:T(8,128)(2,1)S(1)} %reshape.459) | copy-start | bytes 98308
  180.1 10.8 %copy-start.95 = (f32[512,1024]{1,0:T(8,128)S(1)}, f32[512,1024]{1,0:T(8,128)}, u32[]{:S(2)}) copy-start(f32[512,1024]{1,0:T(8,128)} %fusion.156) | copy-start | bytes 6291460
  180.1 10.8 %copy-start.222 = (f32[1,1024]{1,0:T(1,128)S(1)}, f32[1,1024]{1,0:T(1,128)}, u32[]{:S(2)}) copy-start(f32[1,1024]{1,0:T(1,128)} %get-tuple-element.170) | copy-start | bytes 12292
  190.9 11.9 %copy-start.68 = (bf16[32,32,1024]{2,1,0:T(8,128)(2,1)}, bf16[32,32,1024]{2,1,0:T(8,128)(2,1)S(1)}, u32[]{:S(2)}) copy-start(bf16[32,32,1024]{2,1,0:T(8,128)(2,1)S(1)} %get-tuple-element.113) | copy-start | bytes 6291460
  193.2 154.2 %collective-permute-start.4 = (bf16[512,1024]{1,0:T(8,128)(2,1)}, bf16[512,1024]{1,0:T(8,128)(2,1)}, u32[]{:S(2)}, u32[]{:S(2)}) collective-permute-start(bf16[512,1024]{1,0:T(8,128)(2,1)} %add_convert_fusion.13), channel_id=1, source_target_pairs={{0,1},{1,0},{2,3},{3,2},{4,5},{5,4},{6,7},{7,6},{8,9},{9,8},{10,11... | collective-permute-start | bytes 3145736 | tf_op jit(solution)/shard_map/ppermute | solution.py:247
  196.3 154.9 %collective-permute-start.3 = (bf16[512,1024]{1,0:T(8,128)(2,1)}, bf16[512,1024]{1,0:T(8,128)(2,1)}, u32[]{:S(2)}, u32[]{:S(2)}) collective-permute-start(bf16[512,1024]{1,0:T(8,128)(2,1)} %add_convert_fusion.14), channel_id=1, source_target_pairs={{0,1},{1,0},{2,3},{3,2},{4,5},{5,4},{6,7},{7,6},{8,9},{9,8},{10,11... | collective-permute-start | bytes 3145736 | tf_op jit(solution)/shard_map/ppermute | solution.py:247
  204.1 148.8 %copy-start.7 = (bf16[512,1024]{1,0:T(8,128)(2,1)}, bf16[512,1024]{1,0:T(8,128)(2,1)S(1)}, u32[]{:S(2)}) copy-start(bf16[512,1024]{1,0:T(8,128)(2,1)S(1)} %add_convert_fusion.15.q_ref) | copy-start | bytes 3145732
  347.4 51.8 %copy-start.37 = (bf16[32,32,1024]{2,1,0:T(8,128)(2,1)}, bf16[32,32,1024]{2,1,0:T(8,128)(2,1)S(1)}, u32[]{:S(2)}) copy-start(bf16[32,32,1024]{2,1,0:T(8,128)(2,1)S(1)} %get-tuple-element.99) | copy-start | bytes 6291460
  352.9 14.3 %copy-start.3 = (bf16[1024,1024]{1,0:T(8,128)(2,1)}, bf16[1024,1024]{1,0:T(8,128)(2,1)S(1)}, u32[]{:S(2)}) copy-start(bf16[1024,1024]{1,0:T(8,128)(2,1)S(1)} %pad_maximum_fusion.k_ref) | copy-start | bytes 6291460
  371.1 25.5 %copy-start.15 = (f32[512,1024]{1,0:T(8,128)}, f32[512,1024]{1,0:T(8,128)S(1)}, u32[]{:S(2)}) copy-start(f32[512,1024]{1,0:T(8,128)S(1)} %get-tuple-element.186) | copy-start | bytes 6291460
  372.7 17.9 %copy-start.130 = (bf16[512,16]{0,1:T(8,128)(2,1)}, bf16[512,16]{0,1:T(8,128)(2,1)S(1)}, u32[]{:S(2)}) copy-start(bf16[512,16]{0,1:T(8,128)(2,1)S(1)} %convolution_convert_fusion.39) | copy-start | bytes 49156
  397.6 31.6 %copy-start.11 = (f32[512,1024]{1,0:T(8,128)}, f32[512,1024]{1,0:T(8,128)S(1)}, u32[]{:S(2)}) copy-start(f32[512,1024]{1,0:T(8,128)S(1)} %get-tuple-element.196) | copy-start | bytes 6291460
  398.8 11.5 %copy-start.33 = (bf16[512,1024]{1,0:T(8,128)(2,1)}, bf16[512,1024]{1,0:T(8,128)(2,1)S(1)}, u32[]{:S(2)}) copy-start(bf16[512,1024]{1,0:T(8,128)(2,1)S(1)} %add_convert_fusion.11) | copy-start | bytes 3145732
  401.0 11.1 %collective-permute-start.6 = (bf16[512,1024]{1,0:T(8,128)(2,1)S(1)}, bf16[512,1024]{1,0:T(8,128)(2,1)S(1)}, u32[]{:S(2)}, u32[]{:S(2)}) collective-permute-start(bf16[512,1024]{1,0:T(8,128)(2,1)S(1)} %add_convert_fusion.8), channel_id=1, source_target_pairs={{0,1},{1,0},{2,3},{3,2},{4,5},{5,4},{6,7},{7,6},{8,9},{9,8},{10,11... | collective-permute-start | bytes 3145736 | tf_op jit(solution)/shard_map/ppermute | solution.py:247
  403.8 9.8 %collective-permute-start.5 = (bf16[512,1024]{1,0:T(8,128)(2,1)S(1)}, bf16[512,1024]{1,0:T(8,128)(2,1)S(1)}, u32[]{:S(2)}, u32[]{:S(2)}) collective-permute-start(bf16[512,1024]{1,0:T(8,128)(2,1)S(1)} %add_convert_fusion.9), channel_id=1, source_target_pairs={{0,1},{1,0},{2,3},{3,2},{4,5},{5,4},{6,7},{7,6},{8,9},{9,8},{10,11... | collective-permute-start | bytes 3145736 | tf_op jit(solution)/shard_map/ppermute | solution.py:247
  413.8 14.2 %copy-start.6 = (bf16[1024,1024]{1,0:T(8,128)(2,1)}, bf16[1024,1024]{1,0:T(8,128)(2,1)S(1)}, u32[]{:S(2)}) copy-start(bf16[1024,1024]{1,0:T(8,128)(2,1)S(1)} %pad_maximum_fusion.2.k_ref) | copy-start | bytes 6291460
  428.0 89.6 %copy-start.2 = (f32[512,1024]{1,0:T(8,128)}, f32[512,1024]{1,0:T(8,128)S(1)}, u32[]{:S(2)}) copy-start(f32[512,1024]{1,0:T(8,128)S(1)} %get-tuple-element.21.o_ref) | copy-start | bytes 6291460
  430.7 59.1 %copy-start.13 = (f32[512,1024]{1,0:T(8,128)}, f32[512,1024]{1,0:T(8,128)S(1)}, u32[]{:S(2)}) copy-start(f32[512,1024]{1,0:T(8,128)S(1)} %get-tuple-element.198) | copy-start | bytes 6291460
  495.6 15.4 %copy-start.201 = (f32[1,1024]{1,0:T(1,128)S(1)}, f32[1,1024]{1,0:T(1,128)}, u32[]{:S(2)}) copy-start(f32[1,1024]{1,0:T(1,128)} %get-tuple-element.173) | copy-start | bytes 12292
  516.3 43.6 %collective-permute-start.7 = (bf16[256,1024]{1,0:T(8,128)(2,1)}, bf16[256,1024]{1,0:T(8,128)(2,1)}, u32[]{:S(2)}, u32[]{:S(2)}) collective-permute-start(bf16[256,1024]{1,0:T(8,128)(2,1)} %broadcast_select_fusion.2), channel_id=1, source_target_pairs={{2,0},{3,1},{1,2},{0,3},{6,4},{7,5},{5,6},{4,7},{10,8},{11,9},{9,1... | collective-permute-start | bytes 1572872 | tf_op jit(solution)/shard_map/ppermute | solution.py:233
  544.3 18.3 %collective-permute-start.12 = (bf16[512,1024]{1,0:T(8,128)(2,1)}, bf16[512,1024]{1,0:T(8,128)(2,1)}, u32[]{:S(2)}, u32[]{:S(2)}) collective-permute-start(bf16[512,1024]{1,0:T(8,128)(2,1)} %slice.607), channel_id=1, source_target_pairs={{0,1},{1,0},{2,3},{3,2},{4,5},{5,4},{6,7},{7,6},{8,9},{9,8},{10,11... | collective-permute-start | bytes 3145736 | tf_op jit(solution)/shard_map/ppermute | solution.py:262
  544.6 19.6 %collective-permute-start.11 = (bf16[512,1024]{1,0:T(8,128)(2,1)}, bf16[512,1024]{1,0:T(8,128)(2,1)S(1)}, u32[]{:S(2)}, u32[]{:S(2)}) collective-permute-start(bf16[512,1024]{1,0:T(8,128)(2,1)} %slice.605), channel_id=1, source_target_pairs={{0,1},{1,0},{2,3},{3,2},{4,5},{5,4},{6,7},{7,6},{8,9},{9,8},{10,11... | collective-permute-start | bytes 3145736 | tf_op jit(solution)/shard_map/ppermute | solution.py:262
  561.0 87.7 %collective-permute-start.8 = (bf16[256,1024]{1,0:T(8,128)(2,1)}, bf16[256,1024]{1,0:T(8,128)(2,1)}, u32[]{:S(2)}, u32[]{:S(2)}) collective-permute-start(bf16[256,1024]{1,0:T(8,128)(2,1)} %get-tuple-element.117), channel_id=1, source_target_pairs={{3,2},{2,3},{7,6},{6,7},{11,10},{10,11},{15,14},{14,15},{19,18},{1... | collective-permute-start | bytes 1572872 | tf_op jit(solution)/shard_map/ppermute | solution.py:234
  574.0 34.0 %copy-start.23 = (f32[512,1024]{1,0:T(8,128)}, f32[512,1024]{1,0:T(8,128)S(1)}, u32[]{:S(2)}) copy-start(f32[512,1024]{1,0:T(8,128)S(1)} %get-tuple-element.83) | copy-start | bytes 6291460
  618.0 32.7 %collective-permute-start.18 = (bf16[16,16,512]{2,1,0:T(8,128)(2,1)S(1)}, bf16[16,16,512]{2,1,0:T(8,128)(2,1)S(1)}, u32[]{:S(2)}, u32[]{:S(2)}) collective-permute-start(bf16[16,16,512]{2,1,0:T(8,128)(2,1)S(1)} %select_bitcast_fusion.6), channel_id=1, source_target_pairs={{0,1},{1,0},{2,3},{3,2},{4,5},{5,4},{6,7},{7,6},{8,9},{9,8},{10,11... | collective-permute-start | bytes 786440 | tf_op jit(solution)/shard_map/ppermute | solution.py:500
  620.9 24.2 %copy-start.154 = (bf16[512,16]{0,1:T(8,128)(2,1)S(1)}, bf16[512,16]{0,1:T(8,128)(2,1)}, u32[]{:S(2)}) copy-start(bf16[512,16]{0,1:T(8,128)(2,1)} %copy-done.153) | copy-start | bytes 49156
  644.9 44.1 %collective-permute-start.14 = (bf16[512,1024]{1,0:T(8,128)(2,1)}, bf16[512,1024]{1,0:T(8,128)(2,1)}, u32[]{:S(2)}, u32[]{:S(2)}) collective-permute-start(bf16[512,1024]{1,0:T(8,128)(2,1)} %slice.611), channel_id=1, source_target_pairs={{0,1},{1,0},{2,3},{3,2},{4,5},{5,4},{6,7},{7,6},{8,9},{9,8},{10,11... | collective-permute-start | bytes 3145736 | tf_op jit(solution)/shard_map/ppermute | solution.py:262
  650.6 11.9 %copy-start.161 = (bf16[16,1024]{1,0:T(8,128)(2,1)S(1)}, bf16[16,1024]{1,0:T(8,128)(2,1)}, u32[]{:S(2)}) copy-start(bf16[16,1024]{1,0:T(8,128)(2,1)} %convolution_convert_fusion.19) | copy-start | bytes 98308
  650.6 13.9 %copy-start.159 = (bf16[16,1024]{1,0:T(8,128)(2,1)S(1)}, bf16[16,1024]{1,0:T(8,128)(2,1)}, u32[]{:S(2)}) copy-start(bf16[16,1024]{1,0:T(8,128)(2,1)} %convolution_convert_fusion.18) | copy-start | bytes 98308
  650.6 14.5 %copy-start.158 = (bf16[16,1024]{1,0:T(8,128)(2,1)S(1)}, bf16[16,1024]{1,0:T(8,128)(2,1)}, u32[]{:S(2)}) copy-start(bf16[16,1024]{1,0:T(8,128)(2,1)} %convolution_convert_fusion.17) | copy-start | bytes 98308
  650.6 19.4 %copy-start.160 = (bf16[16,1024]{1,0:T(8,128)(2,1)S(1)}, bf16[16,1024]{1,0:T(8,128)(2,1)}, u32[]{:S(2)}) copy-start(bf16[16,1024]{1,0:T(8,128)(2,1)} %convolution_convert_fusion.24) | copy-start | bytes 98308
  651.5 34.7 %all-to-all-start.2 = ((bf16[16,16,512]{2,1,0:T(8,128)(2,1)}), bf16[16,16,512]{2,1,0:T(8,128)(2,1)S(1)}, u32[]{:S(2)}, u32[]{:S(2)}) async-start(bf16[16,16,512]{2,1,0:T(8,128)(2,1)} %fusion.68), calls=%async_computation.2 | async-start | bytes 524288 | tf_op jit(solution)/shard_map/all_to_all | solution.py:502
  670.1 15.2 %copy-start.114 = (bf16[512,16]{0,1:T(8,128)(2,1)S(1)}, bf16[512,16]{0,1:T(8,128)(2,1)}, u32[]{:S(2)}) copy-start(bf16[512,16]{0,1:T(8,128)(2,1)} %copy-done.113) | copy-start | bytes 49156
  671.2 15.8 %copy-start.223 = (s32[16]{0:T(128)S(1)}, s32[16]{0:T(128)}, u32[]{:S(2)}) copy-start(s32[16]{0:T(128)} %get-tuple-element.89) | copy-start | bytes 196
  671.2 17.8 %copy-start.116 = (bf16[16,3072]{1,0:T(8,128)(2,1)S(1)}, bf16[16,3072]{1,0:T(8,128)(2,1)}, u32[]{:S(2)}) copy-start(bf16[16,3072]{1,0:T(8,128)(2,1)} %copy-done.115) | copy-start | bytes 294916
  671.2 19.7 %collective-permute-start.13 = (bf16[512,1024]{1,0:T(8,128)(2,1)}, bf16[512,1024]{1,0:T(8,128)(2,1)}, u32[]{:S(2)}, u32[]{:S(2)}) collective-permute-start(bf16[512,1024]{1,0:T(8,128)(2,1)} %slice.609), channel_id=1, source_target_pairs={{0,1},{1,0},{2,3},{3,2},{4,5},{5,4},{6,7},{7,6},{8,9},{9,8},{10,11... | collective-permute-start | bytes 3145736 | tf_op jit(solution)/shard_map/ppermute | solution.py:262
  701.8 10.7 %collective-permute-start.17 = (bf16[16,16,512]{2,1,0:T(8,128)(2,1)S(1)}, bf16[16,16,512]{2,1,0:T(8,128)(2,1)S(1)}, u32[]{:S(2)}, u32[]{:S(2)}) collective-permute-start(bf16[16,16,512]{2,1,0:T(8,128)(2,1)S(1)} %select_bitcast_fusion.7), channel_id=1, source_target_pairs={{0,1},{1,0},{2,3},{3,2},{4,5},{5,4},{6,7},{7,6},{8,9},{9,8},{10,11... | collective-permute-start | bytes 786440 | tf_op jit(solution)/shard_map/ppermute | solution.py:500
  713.4 17.5 %all-to-all-start.1 = ((bf16[16,16,512]{2,1,0:T(8,128)(2,1)}), bf16[16,16,512]{2,1,0:T(8,128)(2,1)}, u32[]{:S(2)}, u32[]{:S(2)}) async-start(bf16[16,16,512]{2,1,0:T(8,128)(2,1)} %fusion.69), calls=%async_computation.1 | async-start | bytes 524288 | tf_op jit(solution)/shard_map/all_to_all | solution.py:502
  721.6 27.6 %collective-permute-start.15 = (f32[256,1024]{1,0:T(8,128)}, f32[256,1024]{1,0:T(8,128)S(1)}, u32[]{:S(2)}, u32[]{:S(2)}) collective-permute-start(f32[256,1024]{1,0:T(8,128)} %slice_select_fusion), channel_id=1, source_target_pairs={{2,0},{3,1},{1,2},{0,3},{6,4},{7,5},{5,6},{4,7},{10,8},{11,9},{9,1... | collective-permute-start | bytes 3145736 | tf_op jit(solution)/shard_map/ppermute | solution.py:233
  732.3 18.0 %copy-start.150 = (f32[1,8,16,96]{3,1,2,0:T(8,128)S(1)}, f32[1,8,16,96]{3,1,2,0:T(8,128)}, u32[]{:S(2)}) copy-start(f32[1,8,16,96]{3,1,2,0:T(8,128)} %slice_bitcast_fusion.18) | copy-start | bytes 147460
  732.3 18.7 %copy-start.152 = (f32[1,8,16,128]{3,1,2,0:T(8,128)S(1)}, f32[1,8,16,128]{3,1,2,0:T(8,128)}, u32[]{:S(2)}) copy-start(f32[1,8,16,128]{3,1,2,0:T(8,128)} %get-tuple-element.157) | copy-start | bytes 196612
  732.3 19.4 %copy-start.151 = (f32[1,8,16,128]{3,1,2,0:T(8,128)S(1)}, f32[1,8,16,128]{3,1,2,0:T(8,128)}, u32[]{:S(2)}) copy-start(f32[1,8,16,128]{3,1,2,0:T(8,128)} %get-tuple-element.158) | copy-start | bytes 196612
  749.5 6.6 collective-permute-start.16
  (188 other events, 564.8 us)
Sparse Core Ops, SparseCore 0:
  11.5 168.4 all-gather.4
  182.9 152.8 all-gather.6

commit v2 on v1

--- a/solution.py
+++ b/solution.py
@@ -30,21 +30,6 @@
 
 def times(left_side, right_side, dims=PLAIN):
     return lax.dot_general(left_side, right_side, dims, preferred_element_type=wide)
-
-
-def normalize(values, gain_vector, shift_vector):
-    center = jnp.mean(values, axis=-1, keepdims=True)
-    spread = values - center
-    variance = jnp.mean(spread * spread, axis=-1, keepdims=True)
-    return spread * lax.rsqrt(variance + epsilon) * gain_vector + shift_vector
-
-
-def gelu_tanh(values):
-    return (
-        0.5
-        * values
-        * (1.0 + jnp.tanh(root_factor * (values + 0.044715 * values * values * values)))
-    )
 
 
 def block_pair(step, place, blocks):
@@ -263,8 +248,392 @@
     return total
 
 
-def layer_forward(current, frozen, picked, extras, place, count):
-    attend_weight, output_weight, expand_weight, reduce_weight = frozen
+def ring_position(z):
+    return jnp.where(z == 2, 3, jnp.where(z == 3, 2, z))
+
+
+SWAP = [(0, 1), (1, 0)]
+RING = [(z * 2 + x, after * 2 + x) for z, after in enumerate((1, 3, 0, 2)) for x in range(2)]
+ACROSS_X = [(d, d ^ 1) for d in range(8)]
+
+
+def along_z(rows):
+    return lax.ppermute(rows, "dp", RING)
+
+
+def along_x(rows):
+    return lax.ppermute(rows, "dp", ACROSS_X)
+
+
+def along_y(rows):
+    return lax.ppermute(rows, "chip", SWAP)
+
+
+def on_chip(rows):
+    return lax.ppermute(rows, "core", SWAP)
+
+
+def join(*members):
+    return jnp.concatenate(members, axis=0)
+
+
+def after(members, earlier):
+    return lax.optimization_barrier(tuple(members) + tuple(earlier))[: len(members)]
+
+
+def over_z(rows):
+    members = [rows]
+    for _ in range(3):
+        members.append(along_z(members[-1]))
+    return members
+
+
+def by_z(ring, first, rows, position):
+    parts = [member[first : first + rows] for member in ring]
+    placed = []
+    for spot in (0, 1, 3, 2):
+        step = lax.rem(position + 4 - spot, 4)
+        chosen = parts[3]
+        for index in (2, 1, 0):
+            chosen = jnp.where(step == index, parts[index], chosen)
+        placed.append(chosen)
+    return jnp.stack(placed)
+
+
+def gather_chunks(plan, position):
+    started = []
+    for rows, z_first in plan:
+        if not z_first:
+            size = rows.shape[0] // 2
+            one, two = rows[:size], rows[size:]
+            rows = join(one, along_x(one), two, along_y(two))
+        started.append(rows)
+    rings = []
+    for rows in started:
+        rings.append(over_z(after((rows,), rings[-1][3:])[0] if rings else rows))
+    found, far = [], ()
+    for ring, (rows, z_first) in zip(rings, plan):
+        size = ring[0].shape[0] // 2
+        near = [by_z(ring, part * size, size, position) for part in range(2)]
+        if z_first:
+            near = after(near, far)
+            near = [
+                jnp.stack([near[0], along_x(near[0])]),
+                jnp.stack([near[1], along_y(near[1])]),
+            ]
+        else:
+            near = [member.reshape(4, 2, size // 2, member.shape[2]) for member in near]
+        near = after(near, far)
+        far = (along_y(near[0]), along_x(near[1]))
+        own = [near[0], far[0], near[1], far[1]]
+        found.append(tuple(own + [on_chip(member) for member in own]))
+    return found
+
+
+SQUARE = (4, 2, 2, 2, 32, 1024)
+TALL = (4, 2, 2, 2, 128, 1024)
+QKVO_UNITS = ((0, 0), (0, 32), (1, 0), (1, 32))
+EXPAND_UNITS = ((0, 0), (0, 32), (0, 64), (0, 96))
+REDUCE_UNIT = (1, 0)
+
+
+def fetch(form, at_ref, sources, unit, rows, held, arrived, by_quarter=None):
+    if form == "whole":
+        source = sources[unit]
+        if by_quarter is None:
+            pltpu.make_async_copy(source, held, arrived).start()
+        else:
+            pltpu.make_async_copy(source.at[by_quarter], held.at[by_quarter], arrived).start()
+        return
+    part, first = unit
+    x, y, core = at_ref[1], at_ref[2], at_ref[3]
+    spread_z = slice(None) if by_quarter is None else by_quarter
+    for other in range(2):
+        for far in range(2):
+            source = sources[other * 4 + part * 2 + far]
+            for over in range(2):
+                over_x, over_y = (over, far) if part == 0 else (far, over)
+                where = (over, spread_z) if form == "z first" else (spread_z, over)
+                pltpu.make_async_copy(
+                    source.at[(*where, pl.ds(first, rows), slice(None))],
+                    held.at[
+                        spread_z,
+                        lax.rem(x + over_x, 2),
+                        lax.rem(y + over_y, 2),
+                        lax.rem(core + other, 2),
+                    ],
+                    arrived,
+                ).start()
+
+
+def wait_for(held, arrived):
+    pltpu.make_async_copy(held, held, arrived).wait()
+
+
+def square(held):
+    return held[...].reshape(1024, 1024)
+
+
+TILE = 256
+STRIP = 32
+COLUMNS = 1024
+
+
+def strips(count, body):
+    def step(index, carry):
+        body(pl.ds(pl.multiple_of(index * STRIP, STRIP), STRIP))
+        return carry
+
+    lax.fori_loop(0, count // STRIP, step, 0)
+
+
+def normalize_rows(values, gain, shift):
+    center = jnp.mean(values, axis=-1, keepdims=True)
+    spread = values - center
+    scale = lax.rsqrt(jnp.mean(spread * spread, axis=-1, keepdims=True) + epsilon)
+    unit = spread * scale
+    return unit, scale, unit * gain + shift
+
+
+def normalize_pull(grad, unit, scale, gain):
+    scaled = grad * gain
+    first = jnp.mean(scaled, axis=-1, keepdims=True)
+    second = jnp.mean(scaled * unit, axis=-1, keepdims=True)
+    return scale * (scaled - first - unit * second)
+
+
+def qkv_kernel(form, at_ref, x_ref, gain_ref, shift_ref, left_ref, right_ref, bias_ref, *refs):
+    sources, (normed_ref, unit_ref, scale_ref, rank_ref, *outs) = refs[:-9], refs[-9:-2]
+    held, arrived = refs[-2:]
+    for part in range(3):
+        unit = part if form == "whole" else QKVO_UNITS[part]
+        fetch(form, at_ref, sources, unit, 32, held.at[part], arrived.at[part])
+
+    def norm(rows):
+        unit, scale, normed = normalize_rows(x_ref[rows, :], gain_ref[...], shift_ref[...])
+        normed_ref[rows, :] = normed.astype(low_type)
+        unit_ref[rows, :] = unit.astype(low_type)
+        scale_ref[rows, :] = jnp.broadcast_to(scale, (STRIP, 128))
+
+    strips(x_ref.shape[0], norm)
+    rank_ref[...] = times(normed_ref[...], left_ref[...], ROWS_BY_ROWS).astype(low_type)
+    for part, out in enumerate(outs):
+        wait_for(held.at[part], arrived.at[part])
+        columns = slice(part * COLUMNS, (part + 1) * COLUMNS)
+        for first in range(0, x_ref.shape[0], TILE):
+            rows = slice(first, first + TILE)
+            out[rows, :] = (
+                times(normed_ref[rows, :], square(held.at[part]))
+                + times(rank_ref[rows, :], right_ref[:, columns])
+                + bias_ref[:, columns]
+            ).astype(low_type)
+
+
+def output_kernel(form, at_ref, x_ref, attended_ref, left_ref, right_ref, bias_ref, gain_ref, shift_ref, *refs):
+    sources, (low_ref, middle_ref, normed_ref, unit_ref, scale_ref, rank_ref) = refs[:-8], refs[-8:-2]
+    held, arrived = refs[-2:]
+    fetch(form, at_ref, sources, 3 if form == "whole" else QKVO_UNITS[3], 32, held, arrived)
+    low_ref[...] = attended_ref[...].astype(low_type)
+    rank_ref[...] = times(low_ref[...], left_ref[...], ROWS_BY_ROWS).astype(low_type)
+    wait_for(held, arrived)
+    for first in range(0, x_ref.shape[0], TILE):
+        rows = slice(first, first + TILE)
+        middle_ref[rows, :] = (
+            x_ref[rows, :]
+            + times(low_ref[rows, :], square(held))
+            + times(rank_ref[rows, :], right_ref[...])
+            + bias_ref[...]
+        )
+
+    def norm(rows):
+        unit, scale, normed = normalize_rows(middle_ref[rows, :], gain_ref[...], shift_ref[...])
+        normed_ref[rows, :] = normed.astype(low_type)
+        unit_ref[rows, :] = unit.astype(low_type)
+        scale_ref[rows, :] = jnp.broadcast_to(scale, (STRIP, 128))
+
+    strips(x_ref.shape[0], norm)
+
+
+def fetch_feed_forward(form, at_ref, sources, expand, reduce, arrived, reduce_first):
+    for part in range(4):
+        whole = form == "whole"
+        jobs = [
+            (part if whole else EXPAND_UNITS[part], 32, expand.at[part], arrived.at[0, part], None),
+            (4 if whole else REDUCE_UNIT, 128, reduce, arrived.at[1, part], part),
+        ]
+        for unit, rows, held, semaphore, quarter in jobs[::-1] if reduce_first else jobs:
+            fetch(form, at_ref, sources, unit, rows, held, semaphore, quarter)
+
+
+def feed_forward_kernel(
+    form, at_ref, normed_ref, middle_ref, expand_left_ref, expand_right_ref, expand_bias_ref,
+    reduce_left_ref, reduce_right_ref, reduce_bias_ref, *refs,
+):
+    sources, (result_ref, slope_ref, active_ref, rank_expand_ref, rank_reduce_ref) = refs[:-9], refs[-9:-4]
+    expand, reduce, rank_sum, arrived = refs[-4:]
+    fetch_feed_forward(form, at_ref, sources, expand, reduce, arrived, False)
+    count = normed_ref.shape[0]
+    rank_expand_ref[...] = times(normed_ref[...], expand_left_ref[...], ROWS_BY_ROWS).astype(low_type)
+    result_ref[...] = middle_ref[...] + reduce_bias_ref[...]
+    rank_sum[...] = jnp.zeros_like(rank_sum)
+
+    def part_step(part, carry):
+        columns = pl.ds(pl.multiple_of(part * COLUMNS, COLUMNS), COLUMNS)
+        wait_for(expand.at[part], arrived.at[0, part])
+        wait_for(reduce.at[part], arrived.at[1, part])
+        for first in range(0, count, TILE):
+            rows = slice(first, first + TILE)
+            value = (
+                times(normed_ref[rows, :], square(expand.at[part]))
+                + times(rank_expand_ref[rows, :], expand_right_ref[:, columns])
+                + expand_bias_ref[:, columns]
+            )
+            squared = value * value
+            bent = jnp.tanh(root_factor * value * (1.0 + 0.044715 * squared))
+            half = 0.5 * (1.0 + bent)
+            slope_ref[rows, columns] = (
+                half
+                + 0.5 * value * (1.0 - bent * bent) * (root_factor + 3 * 0.044715 * root_factor * squared)
+            ).astype(low_type)
+            active = (value * half).astype(low_type)
+            active_ref[rows, columns] = active
+            result_ref[rows, :] = result_ref[rows, :] + times(active, square(reduce.at[part]))
+            rank_sum[rows, :] = rank_sum[rows, :] + times(
+                active, reduce_left_ref[:, columns], ROWS_BY_ROWS
+            )
+        return carry
+
+    lax.fori_loop(0, 4, part_step, 0)
+    rank_reduce_ref[...] = rank_sum[...].astype(low_type)
+    result_ref[...] = result_ref[...] + times(rank_reduce_ref[...], reduce_right_ref[...])
+
+
+def feed_backward_kernel(
+    form, at_ref, grad_ref, slope_ref, active_ref, normed_ref, unit_ref, scale_ref, rank_expand_ref, rank_reduce_ref,
+    gain_ref, expand_left_ref, expand_right_ref, reduce_left_ref, reduce_right_ref, *refs,
+):
+    sources, (out_ref, expand_left_g, expand_right_g, reduce_left_g, reduce_right_g) = refs[:-13], refs[-13:-8]
+    expand, reduce, arrived, low_grad, turned, bent, total, turn_sum = refs[-8:]
+    fetch_feed_forward(form, at_ref, sources, expand, reduce, arrived, True)
+    count = grad_ref.shape[0]
+    low_grad[...] = grad_ref[...].astype(low_type)
+    turned[...] = times(low_grad[...], reduce_right_ref[...], ROWS_BY_ROWS).astype(low_type)
+    reduce_right_g[...] = times(rank_reduce_ref[...], low_grad[...], COLS_BY_COLS).astype(low_type)
+    total[...] = jnp.zeros_like(total)
+    turn_sum[...] = jnp.zeros_like(turn_sum)
+
+    def part_step(part, carry):
+        columns = pl.ds(pl.multiple_of(part * COLUMNS, COLUMNS), COLUMNS)
+        wait_for(reduce.at[part], arrived.at[1, part])
+        wait_for(expand.at[part], arrived.at[0, part])
+        for first in range(0, count, TILE):
+            rows = slice(first, first + TILE)
+            grad_active = times(low_grad[rows, :], square(reduce.at[part]), ROWS_BY_ROWS) + times(
+                turned[rows, :], reduce_left_ref[:, columns]
+            )
+            grad_expand = (grad_active * slope_ref[rows, columns].astype(wide)).astype(low_type)
+            bent[rows, :] = grad_expand
+            total[rows, :] = total[rows, :] + times(grad_expand, square(expand.at[part]), ROWS_BY_ROWS)
+            turn_sum[rows, :] = turn_sum[rows, :] + times(
+                grad_expand, expand_right_ref[:, columns], ROWS_BY_ROWS
+            )
+        reduce_left_g[:, columns] = times(turned[...], active_ref[:, columns], COLS_BY_COLS).astype(
+            low_type
+        )
+        expand_right_g[:, columns] = times(rank_expand_ref[...], bent[...], COLS_BY_COLS).astype(low_type)
+        return carry
+
+    lax.fori_loop(0, 4, part_step, 0)
+    turned[...] = turn_sum[...].astype(low_type)
+    expand_left_g[...] = times(turned[...], normed_ref[...], COLS_BY_COLS).astype(low_type)
+    total[...] = total[...] + times(turned[...], expand_left_ref[...])
+
+    def pull(rows):
+        out_ref[rows, :] = grad_ref[rows, :] + normalize_pull(
+            total[rows, :], unit_ref[rows, :].astype(wide), scale_ref[rows, :1], gain_ref[...]
+        )
+
+    strips(count, pull)
+
+
+def output_backward_kernel(form, at_ref, grad_ref, attended_ref, rank_ref, left_ref, right_ref, *refs):
+    sources, (out_ref, left_g, right_g) = refs[:-7], refs[-7:-4]
+    held, arrived, low_grad, turned = refs[-4:]
+    fetch(form, at_ref, sources, 3 if form == "whole" else QKVO_UNITS[3], 32, held, arrived)
+    low_grad[...] = grad_ref[...].astype(low_type)
+    turned[...] = times(low_grad[...], right_ref[...], ROWS_BY_ROWS).astype(low_type)
+    right_g[...] = times(rank_ref[...], low_grad[...], COLS_BY_COLS).astype(low_type)
+    left_g[...] = times(turned[...], attended_ref[...], COLS_BY_COLS).astype(low_type)
+    wait_for(held, arrived)
+    for first in range(0, grad_ref.shape[0], TILE):
+        rows = slice(first, first + TILE)
+        out_ref[rows, :] = (
+            times(low_grad[rows, :], square(held), ROWS_BY_ROWS) + times(turned[rows, :], left_ref[...])
+        ).astype(low_type)
+
+
+def qkv_backward_kernel(
+    form, at_ref, dq_ref, dk_ref, dv_ref, grad_ref, normed_ref, unit_ref, scale_ref, rank_ref,
+    gain_ref, left_ref, right_ref, *refs,
+):
+    sources, (out_ref, left_g, right_g) = refs[:-7], refs[-7:-4]
+    held, arrived, turned, total = refs[-4:]
+    count = grad_ref.shape[0]
+    for part in range(3):
+        unit = part if form == "whole" else QKVO_UNITS[part]
+        fetch(form, at_ref, sources, unit, 32, held.at[part], arrived.at[part])
+    grads = (dq_ref, dk_ref, dv_ref)
+    spans = [slice(part * COLUMNS, (part + 1) * COLUMNS) for part in range(3)]
+    turned[...] = sum(
+        times(grads[part][...], right_ref[:, spans[part]], ROWS_BY_ROWS) for part in range(3)
+    ).astype(low_type)
+    for part in range(3):
+        right_g[:, spans[part]] = times(rank_ref[...], grads[part][...], COLS_BY_COLS).astype(low_type)
+    left_g[...] = times(turned[...], normed_ref[...], COLS_BY_COLS).astype(low_type)
+    for part in range(3):
+        wait_for(held.at[part], arrived.at[part])
+        for first in range(0, count, TILE):
+            rows = slice(first, first + TILE)
+            value = times(grads[part][rows, :], square(held.at[part]), ROWS_BY_ROWS)
+            if part == 0:
+                total[rows, :] = value + times(turned[rows, :], left_ref[...])
+            else:
+                total[rows, :] = total[rows, :] + value
+
+    def pull(rows):
+        out_ref[rows, :] = grad_ref[rows, :] + normalize_pull(
+            total[rows, :], unit_ref[rows, :].astype(wide), scale_ref[rows, :1], gain_ref[...]
+        )
+
+    strips(count, pull)
+
+
+def frozen_call(kernel, name, at, weights, members, outs, scratch, cost):
+    form, sources = weights
+    local_spec = pl.BlockSpec(memory_space=pltpu.VMEM)
+    return pl.pallas_call(
+        functools.partial(kernel, form),
+        out_shape=tuple(jax.ShapeDtypeStruct(shape, kind) for shape, kind in outs),
+        in_specs=[pl.BlockSpec(memory_space=pltpu.SMEM)]
+        + [local_spec] * len(members)
+        + [pl.BlockSpec(memory_space=pl.ANY)] * len(sources),
+        out_specs=(local_spec,) * len(outs),
+        scratch_shapes=scratch,
+        compiler_params=pltpu.CompilerParams(vmem_limit_bytes=56 * 2**20),
+        cost_estimate=pl.CostEstimate(flops=cost, bytes_accessed=0, transcendentals=0),
+        name=name,
+    )(at, *members, *sources)
+
+
+def row(vector):
+    return vector.reshape(1, -1)
+
+
+DMA = pltpu.SemaphoreType.DMA
+
+
+def layer_forward(current, frozen, picked, extras, at, place, count):
+    first_weights, second_weights = frozen
     (
         attend_left, attend_right, output_left, output_right,
         expand_left, expand_right, reduce_left, reduce_right,
@@ -273,120 +642,98 @@
         attend_bias, output_bias, expand_bias, reduce_bias,
         first_gain, first_shift, second_gain, second_shift,
     ) = extras
-    columns = current.shape[1]
-    normed_one = normalize(current, first_gain, first_shift).astype(low_type)
-    rank_attend = times(normed_one, attend_left, ROWS_BY_ROWS).astype(low_type)
-    biases = [attend_bias[:columns], jnp.zeros((columns,), wide), attend_bias[columns:]]
-    queries, keys, values = (
-        (
-            times(normed_one, attend_weight[part])
-            + times(rank_attend, attend_right[:, part * columns : (part + 1) * columns])
-            + biases[part]
-        ).astype(low_type)
-        for part in range(3)
+    rows, columns = current.shape
+    full, full_low = ((rows, columns), wide), ((rows, columns), low_type)
+    scales, ranks = ((rows, 128), wide), ((rows, RANK), low_type)
+    bias = jnp.concatenate([attend_bias[:columns], jnp.zeros((columns,), wide), attend_bias[columns:]])
+    normed_one, unit_one, scale_one, rank_attend, queries, keys, values = frozen_call(
+        qkv_kernel, "qkv_forward", at, first_weights,
+        (current, row(first_gain), row(first_shift), attend_left, attend_right, row(bias)),
+        (full_low, full_low, scales, ranks, full_low, full_low, full_low),
+        [pltpu.VMEM((3, *SQUARE), low_type), DMA((3,))], 10**6,
     )
     key_all, value_all = ring_gather(keys, count), ring_gather(values, count)
     attended, stat = attend_forward(place, queries, key_all, value_all)
-    attended_low = attended.astype(low_type)
-    rank_output = times(attended_low, output_left, ROWS_BY_ROWS).astype(low_type)
-    middle = (
-        current + times(attended_low, output_weight) + times(rank_output, output_right) + output_bias
-    )
-    normed_two = normalize(middle, second_gain, second_shift).astype(low_type)
-    rank_expand = times(normed_two, expand_left, ROWS_BY_ROWS).astype(low_type)
-    parts = len(expand_weight)
-    expanded = [
-        times(normed_two, expand_weight[part])
-        + times(rank_expand, expand_right[:, part * columns : (part + 1) * columns])
-        + expand_bias[part * columns : (part + 1) * columns]
-        for part in range(parts)
-    ]
-    active = [gelu_tanh(member).astype(low_type) for member in expanded]
-    rank_reduce = sum(
-        times(active[part], reduce_left[:, part * columns : (part + 1) * columns], ROWS_BY_ROWS)
-        for part in range(parts)
-    ).astype(low_type)
-    result = (
-        middle
-        + sum(times(active[part], reduce_weight[part]) for part in range(parts))
-        + times(rank_reduce, reduce_right)
-        + reduce_bias
+    attended_low, middle, normed_two, unit_two, scale_two, rank_output = frozen_call(
+        output_kernel, "output_forward", at, first_weights,
+        (current, attended, output_left, output_right, row(output_bias), row(second_gain), row(second_shift)),
+        (full_low, full, full_low, full_low, scales, ranks),
+        [pltpu.VMEM(SQUARE, low_type), DMA], 10**6,
+    )
+    tall = ((rows, expand_right.shape[1]), low_type)
+    result, slope, active, rank_expand, rank_reduce = frozen_call(
+        feed_forward_kernel, "feed_forward", at, second_weights,
+        (normed_two, middle, expand_left, expand_right, row(expand_bias), reduce_left, reduce_right, row(reduce_bias)),
+        (full, tall, tall, ranks, ranks),
+        [
+            pltpu.VMEM((4, *SQUARE), low_type), pltpu.VMEM(TALL, low_type),
+            pltpu.VMEM((rows, RANK), wide), DMA((2, 4)),
+        ], 10**6,
     )
     kept = (
-        current, normed_one, rank_attend, queries, key_all, value_all, attended, attended_low, stat,
-        rank_output, middle, normed_two, rank_expand, expanded, active, rank_reduce,
+        normed_one, unit_one, scale_one, rank_attend, queries, key_all, value_all, attended, attended_low, stat,
+        rank_output, normed_two, unit_two, scale_two, rank_expand, slope, active, rank_reduce,
     )
     return result, kept
 
 
-def layer_backward(grad_result, kept, frozen, picked, extras, place, count):
-    attend_weight, output_weight, expand_weight, reduce_weight = frozen
+def layer_backward(grad_result, kept, frozen, picked, extras, at, place, count):
+    first_weights, second_weights = frozen
     (
         attend_left, attend_right, output_left, output_right,
         expand_left, expand_right, reduce_left, reduce_right,
     ) = picked
-    first_gain, first_shift, second_gain, second_shift = extras[4:]
+    first_gain, second_gain = extras[4], extras[6]
     (
-        current, normed_one, rank_attend, queries, key_all, value_all, attended, attended_low, stat,
-        rank_output, middle, normed_two, rank_expand, expanded, active, rank_reduce,
+        normed_one, unit_one, scale_one, rank_attend, queries, key_all, value_all, attended, attended_low, stat,
+        rank_output, normed_two, unit_two, scale_two, rank_expand, slope, active, rank_reduce,
     ) = kept
-    columns = current.shape[1]
-    parts = len(expand_weight)
-
-    def piece(member, part):
-        return member[:, part * columns : (part + 1) * columns]
-
-    grad_reduce = grad_result.astype(low_type)
-    turn_reduce = times(grad_reduce, reduce_right, ROWS_BY_ROWS).astype(low_type)
-    grad_expand = []
-    for part in range(parts):
-        grad_active = times(grad_reduce, reduce_weight[part], ROWS_BY_ROWS) + times(
-            turn_reduce, piece(reduce_left, part)
-        )
-        grad_expand.append(jax.vjp(gelu_tanh, expanded[part])[1](grad_active)[0].astype(low_type))
-    reduce_left_g = jnp.concatenate(
-        [times(turn_reduce, active[part], COLS_BY_COLS) for part in range(parts)], axis=1
-    )
-    reduce_right_g = times(rank_reduce, grad_reduce, COLS_BY_COLS)
-    turn_expand = sum(
-        times(grad_expand[part], piece(expand_right, part), ROWS_BY_ROWS) for part in range(parts)
-    ).astype(low_type)
-    grad_second = sum(
-        times(grad_expand[part], expand_weight[part], ROWS_BY_ROWS) for part in range(parts)
-    ) + times(turn_expand, expand_left)
-    expand_left_g = times(turn_expand, normed_two, COLS_BY_COLS)
-    expand_right_g = jnp.concatenate(
-        [times(rank_expand, grad_expand[part], COLS_BY_COLS) for part in range(parts)], axis=1
-    )
-    pull = jax.vjp(lambda rows: normalize(rows, second_gain, second_shift), middle)[1]
-    grad_middle = grad_result + pull(grad_second)[0]
-    grad_project = grad_middle.astype(low_type)
-    turn_output = times(grad_project, output_right, ROWS_BY_ROWS).astype(low_type)
-    grad_attended = (
-        times(grad_project, output_weight, ROWS_BY_ROWS) + times(turn_output, output_left)
-    ).astype(low_type)
-    output_left_g = times(turn_output, attended_low, COLS_BY_COLS)
-    output_right_g = times(rank_output, grad_project, COLS_BY_COLS)
+    rows, columns = grad_result.shape
+    full, full_low = ((rows, columns), wide), ((rows, columns), low_type)
+
+    def like(member):
+        return (member.shape, low_type)
+
+    grad_middle, expand_left_g, expand_right_g, reduce_left_g, reduce_right_g = frozen_call(
+        feed_backward_kernel, "feed_backward", at, second_weights,
+        (
+            grad_result, slope, active, normed_two, unit_two, scale_two, rank_expand, rank_reduce,
+            row(second_gain), expand_left, expand_right, reduce_left, reduce_right,
+        ),
+        (full, like(expand_left), like(expand_right), like(reduce_left), like(reduce_right)),
+        [
+            pltpu.VMEM((4, *SQUARE), low_type), pltpu.VMEM(TALL, low_type), DMA((2, 4)),
+            pltpu.VMEM((rows, columns), low_type), pltpu.VMEM((rows, RANK), low_type),
+            pltpu.VMEM((rows, columns), low_type), pltpu.VMEM((rows, columns), wide),
+            pltpu.VMEM((rows, RANK), wide),
+        ], 10**6,
+    )
+    grad_attended, output_left_g, output_right_g = frozen_call(
+        output_backward_kernel, "output_backward", at, first_weights,
+        (grad_middle, attended_low, rank_output, output_left, output_right),
+        (full_low, like(output_left), like(output_right)),
+        [
+            pltpu.VMEM(SQUARE, low_type), DMA,
+            pltpu.VMEM((rows, columns), low_type), pltpu.VMEM((rows, RANK), low_type),
+        ], 10**6,
+    )
     grad_query, grad_keys, grad_values = attend_backward(
         place, queries, key_all, value_all, grad_attended, attended, stat
     )
-    joined = (
-        grad_query,
-        ring_scatter(grad_keys, count).astype(low_type),
-        ring_scatter(grad_values, count).astype(low_type),
-    )
-    turn_attend = sum(
-        times(joined[part], piece(attend_right, part), ROWS_BY_ROWS) for part in range(3)
-    ).astype(low_type)
-    grad_first = sum(
-        times(joined[part], attend_weight[part], ROWS_BY_ROWS) for part in range(3)
-    ) + times(turn_attend, attend_left)
-    attend_left_g = times(turn_attend, normed_one, COLS_BY_COLS)
-    attend_right_g = jnp.concatenate(
-        [times(rank_attend, joined[part], COLS_BY_COLS) for part in range(3)], axis=1
-    )
-    pull = jax.vjp(lambda rows: normalize(rows, first_gain, first_shift), current)[1]
-    grad_current = grad_middle + pull(grad_first)[0]
+    grad_current, attend_left_g, attend_right_g = frozen_call(
+        qkv_backward_kernel, "qkv_backward", at, first_weights,
+        (
+            grad_query,
+            ring_scatter(grad_keys, count).astype(low_type),
+            ring_scatter(grad_values, count).astype(low_type),
+            grad_middle, normed_one, unit_one, scale_one, rank_attend, row(first_gain), attend_left, attend_right,
+        ),
+        (full, like(attend_left), like(attend_right)),
+        [
+            pltpu.VMEM((3, *SQUARE), low_type), DMA((3,)),
+            pltpu.VMEM((rows, RANK), low_type), pltpu.VMEM((rows, columns), wide),
+        ], 10**6,
+    )
     return grad_current, (
         attend_left_g, attend_right_g, output_left_g, output_right_g,
         expand_left_g, expand_right_g, reduce_left_g, reduce_right_g,
@@ -407,6 +754,7 @@
     below = rank < half
     place = jnp.reshape(lax.rem(rank, half), (1,)).astype(jnp.int32)
     columns = tokens.shape[2]
+    linked = (data_count, chips, columns) == (8, 2, 1024)
 
     lane_chip = jnp.arange(data_count * chips, dtype=jnp.int32)
     lane_sequence = (lane_chip // chips) * 2 + (lane_chip % chips) // (chips // 2)
@@ -443,16 +791,11 @@
 
     def frozen_of(whole):
         rows = columns // devices
-        blocks = [
-            whole[:, part * rows : (part + 1) * rows, :].reshape(columns, columns)
-            for part in range(8)
+        squares = [
+            whole[:, part * rows : (part + 1) * rows, :].reshape(SQUARE) for part in range(8)
         ]
-        members = devices // 4
-        reduce_blocks = [
-            whole[part * members : (part + 1) * members, 8 * rows :, :].reshape(columns, columns)
-            for part in range(4)
-        ]
-        return blocks[:3], blocks[3], blocks[4:8], reduce_blocks
+        tall = whole[:, 8 * rows :, :].reshape(TALL)
+        return ("whole", tuple(squares[:4])), ("whole", (*squares[4:], tall))
 
     extras = [
         tuple(
@@ -464,15 +807,28 @@
         )
         for layer_index in range(LAYERS)
     ]
-    gathered = [
-        lax.all_gather(shards(layer_index), EVERY, axis=0) for layer_index in range(LAYERS)
-    ]
-    frozen = [frozen_of(member) for member in gathered]
+    position = ring_position(data_rank // 2)
+    at = jnp.stack([position, data_rank % 2, lax.axis_index("chip"), core]).astype(jnp.int32)
+    if linked:
+        first, second = shards(0), shards(1)
+        found = gather_chunks(
+            ((first[:128], True), (first[128:], True), (second[:128], False), (second[128:], False)),
+            position,
+        )
+        frozen = [
+            (("z first", found[0]), ("z first", found[1])),
+            (("z between", found[2]), ("z between", found[3])),
+        ]
+    else:
+        gathered = [
+            lax.all_gather(shards(layer_index), EVERY, axis=0) for layer_index in range(LAYERS)
+        ]
+        frozen = [frozen_of(member) for member in gathered]
     picked = [factors(layer_index) for layer_index in range(LAYERS)]
     kept = []
     for layer_index in range(LAYERS):
         current, keep = layer_forward(
-            current, frozen[layer_index], picked[layer_index], extras[layer_index], place, count
+            current, frozen[layer_index], picked[layer_index], extras[layer_index], at, place, count
         )
         kept.append(keep)
 
@@ -485,6 +841,7 @@
             frozen[layer_index],
             picked[layer_index],
             extras[layer_index],
+            at,
             place,
             count,
         )

time: 778 us -> 640 us (0.82)
  matrix products: 190 us -> 2.42 us
  Pallas kernels: 71.5 us -> 247 us
  waiting for transfers between devices: 236 us -> 139 us
  local copies, waits for them, and re-layouts: 175 us -> 103 us
  starting transfers between devices: 35.4 us -> 76.5 us
  other arithmetic: 39.8 us -> 58.6 us
  between operations: 17.2 us -> 2.77 us
    dot_general x144 -> x0, matrix products: 187 us -> none  [times(): lax.dot_general(left_side, right_side, dims, preferred_element_type=wide)]
    all_gather x2 -> x0, waiting for transfers between devices: 187 us -> none  [local(): lax.all_gather(shards(layer_index), EVERY, axis=0)]
    pallas_call x0 -> x12, Pallas kernels: none -> 177 us  [frozen_call(): pl.pallas_call(functools.partial(kernel, form), out_shape=tuple((jax.Shap...]
    ppermute x0 -> x44, waiting for transfers between devices: none -> 101 us  [the longest x12 75.3 us: along_z(): return lax.ppermute(rows, 'dp', RING)]
    ppermute x0 -> x44, starting transfers between devices: none -> 43.9 us  [the longest x12 19.8 us: along_z(): return lax.ppermute(rows, 'dp', RING)]
    slice x6 -> x3, local copies, waits for them, and re-layouts: 36.1 us -> 0.7 us  [the longest x2 0.69 us: shards(): member[:, first:first + columns]]
    ppermute x2, waiting for transfers between devices: 24.8 us -> 0.01 us  [spread_tokens(): got = lax.ppermute(jnp.where(below, pair[1], pair[0]), CTX, across)]
    concatenate x33 -> x6, local copies, waits for them, and re-layouts: 24.8 us -> 7.23 us  [the longest x4 5.6 us: ring_gather(): return jnp.concatenate(pieces, axis=0)]
  transfers between devices with their start and end apart: 24 -> 66, of which waited for: 5 -> 18; matrix products, arithmetic and copies ran while one was open for 33% -> 22% of each run, Pallas kernels for 6% -> 27%
where the time goes in v2:
time: 640 us; the launch traced here: 630 us
  Pallas kernels  247 us (39%)
  waiting for transfers between devices  139 us (22%)
  local copies, waits for them, and re-layouts  103 us (16%)
  starting transfers between devices  76.5 us (12%)
  other arithmetic  58.6 us (9%)
    pallas_call x12, Pallas kernels, frozen_call(): pl.pallas_call(functools.partial(kernel, form), out_shape=tuple((jax.Shap...  177 us
    ppermute x12, waiting for transfers between devices, along_z(): return lax.ppermute(rows, 'dp', RING)  75.3 us
    pallas_call x2, Pallas kernels, attend_backward(): pl.pallas_call(functools.partial(attend_backward_kernel, blocks), out_sha...  43 us
    ppermute x2, waiting for transfers between devices, collect_tokens(): got = lax.ppermute(jnp.where(below, late, early), CTX, across)  29.4 us
    unnamed x208, local copies, waits for them, and re-layouts  28.3 us
    pallas_call x2, Pallas kernels, attend_forward(): pl.pallas_call(functools.partial(attend_forward_kernel, blocks), out_shap...  27.6 us
    ppermute x8, waiting for transfers between devices, along_y(): return lax.ppermute(rows, 'chip', SWAP)  21.2 us
    ppermute x12, starting transfers between devices, along_z(): return lax.ppermute(rows, 'dp', RING)  19.8 us
  transfers between devices with their start and end apart: 66, of which 18 were waited for; matrix products, arithmetic and copies ran while one was open for 22% of the time, Pallas kernels for 27%

profile of v2, /device:TPU:0, one launch (start us, length us, event | category | flops | bytes accessed | tf_op | source)
XLA Modules:
  0.0 629.6 jit_solution(15546489740685091602)
XLA Ops:
  3.4 3.0 collective-permute-start.3
  14.3 2.6 collective-permute-start.4
  18.8 3.5 collective-permute-done.4
  25.2 4.4 collective-permute-done.5
  30.6 11.1 %collective-permute-done.16 = bf16[256,1024]{1,0:T(8,128)(2,1)S(1)} collective-permute-done((bf16[256,1024]{1,0:T(8,128)(2,1)S(1)}, bf16[256,1024]{1,0:T(8,128)(2,1)S(1)}, u32[]{:S(2)}, u32[]{:S(2)}) %collective-permute-start.16) | collective-permute-done | bytes 524320 | tf_op jit(solution)/shard_map/ppermute | solution.py:261
  45.6 8.2 %collective-permute-done.17 = bf16[256,1024]{1,0:T(8,128)(2,1)S(1)} collective-permute-done((bf16[256,1024]{1,0:T(8,128)(2,1)S(1)}, bf16[256,1024]{1,0:T(8,128)(2,1)S(1)}, u32[]{:S(2)}, u32[]{:S(2)}) %collective-permute-start.17) | collective-permute-done | bytes 524320 | tf_op jit(solution)/shard_map/ppermute | solution.py:261
  59.3 6.8 %collective-permute-done.18 = bf16[256,1024]{1,0:T(8,128)(2,1)S(1)} collective-permute-done((bf16[256,1024]{1,0:T(8,128)(2,1)S(1)}, bf16[256,1024]{1,0:T(8,128)(2,1)S(1)}, u32[]{:S(2)}, u32[]{:S(2)}) %collective-permute-start.18) | collective-permute-done | bytes 524320 | tf_op jit(solution)/shard_map/ppermute | solution.py:261
  69.2 6.7 %collective-permute-done.8.refs_1_ = bf16[2,4,64,1024]{3,2,1,0:T(8,128)(2,1)S(1)} collective-permute-done((bf16[2,4,64,1024]{3,2,1,0:T(8,128)(2,1)S(1)}, bf16[2,4,64,1024]{3,2,1,0:T(8,128)(2,1)S(1)}, u32[]{:S(2)}, u32[]{:S(2)}) %collective-permute-start.8) | collective-permute-done | bytes 1048608 | tf_op jit(solution)/shard_map/ppermute | solution.py:269
  75.8 3.1 collective-permute-done.9.refs_3_
  79.9 2.5 collective-permute-start.19
  85.1 2.0 broadcast_select_fusion
  87.0 6.2 all-to-all-start
  93.2 1.9 collective-permute-start.30
  95.1 1.7 slice_bitcast_fusion.2
  98.3 2.1 bitcast_select_fusion.3
  100.9 14.5 %collective-permute-done.41 = bf16[128,1024]{1,0:T(8,128)(2,1)S(1)} collective-permute-done((bf16[128,1024]{1,0:T(8,128)(2,1)}, bf16[128,1024]{1,0:T(8,128)(2,1)S(1)}, u32[]{:S(2)}, u32[]{:S(2)}) %collective-permute-start.41) | collective-permute-done | bytes 262176 | tf_op jit(solution)/shard_map/ppermute | solution.py:269
  115.4 3.5 collective-permute-start.31
  118.9 1.9 slice_bitcast_fusion.1
  123.1 3.2 pad_maximum_fusion.refs_0_
  126.3 4.7 collective-permute-done.31
  131.1 2.8 pad_maximum_fusion.1.refs_2_
  135.1 2.5 collective-permute-start.42
  137.6 1.8 collective-permute-start.22
  143.0 18.6 %collective-permute-done.42 = bf16[512,1024]{1,0:T(8,128)(2,1)} collective-permute-done((bf16[512,1024]{1,0:T(8,128)(2,1)}, bf16[512,1024]{1,0:T(8,128)(2,1)}, u32[]{:S(2)}, u32[]{:S(2)}) %collective-permute-start.42) | collective-permute-done | bytes 1048608 | tf_op jit(solution)/shard_map/ppermute | solution.py:261
  172.5 10.9 %qkv_forward.2 = (bf16[512,1024]{1,0:T(8,128)(2,1)}, bf16[512,1024]{1,0:T(8,128)(2,1)}, f32[512,128]{1,0:T(8,128)}, bf16[512,16]{1,0:T(8,128)(2,1)}, bf16[512,10...) custom-call(s32[4]{0:T(128)} %pad_add_fusion.at_ref, f32[512,1024]{1,0:T(8,128)} %maximum_convert_fusion.x_ref, ...), custom_call_target="tpu_custom_call" | custom-call | flops 1000000 | tf_op jit(solution)/shard_map/qkv_forward/pallas_call | solution.py:614
  185.5 1.7 collective-permute-done.43
  192.7 2.0 bitcast_select_fusion.1
  196.2 16.2 %collective-permute-done.44 = bf16[512,1024]{1,0:T(8,128)(2,1)} collective-permute-done((bf16[512,1024]{1,0:T(8,128)(2,1)}, bf16[512,1024]{1,0:T(8,128)(2,1)}, u32[]{:S(2)}, u32[]{:S(2)}) %collective-permute-start.44) | collective-permute-done | bytes 1048608 | tf_op jit(solution)/shard_map/ppermute | solution.py:261
  212.4 2.4 select_select_fusion.1
  214.8 2.4 select_select_fusion.3
  217.9 1.9 select_select_fusion.7
  230.7 1.7 copy.117
  232.4 1.8 reshape.288.expand_left_ref
  248.3 2.1 constant_dynamic-update-slice_fusion.2.v_ref
  251.7 13.8 %attend_forward.2 = (f32[512,1024]{1,0:T(8,128)S(1)}, f32[8,2,512]{2,1,0:T(2,128)S(1)}) custom-call(s32[1]{0:T(128)} %bitcast.6.place_ref, bf16[512,1024]{1,0:T(8,128)(2,1)S(1)} %copy-done.6, bf16[1024,1024]{1,0:T(8,128)(2,1)S(1)} %constant_dynamic-update-slice_fusion.k_ref, bf16[1024,1024]{1,0:T(8,128)(2,1)} %copy-done.32), custom_call_target="tpu_custom_call" | custom-call | tf_op jit(solution)/shard_map/attend_forward/pallas_call | solution.py:150
  266.8 11.1 %output_forward.2 = (bf16[512,1024]{1,0:T(8,128)(2,1)}, f32[512,1024]{1,0:T(8,128)}, bf16[512,1024]{1,0:T(8,128)(2,1)}, bf16[512,1024]{1,0:T(8,128)(2,1)}, f32[512,128]{1,0:T(8,128)}, /*index=5*/bf16[512,16]{1,0:T(8,128)(2,1)}) custom-call(s32[4]{0:T(128)} %pad_add_fusion.at_ref, f32[512,1024]{1,0:T(8,128)} %maximum_convert_fusion.x_ref, ...), custom_call_target="tpu_custom_call" | custom-call | flops 1000000 | tf_op jit(solution)/shard_map/output_forward/pallas_call | solution.py:614
  277.9 24.0 %feed_forward.2 = (f32[512,1024]{1,0:T(8,128)}, bf16[512,4096]{1,0:T(8,128)(2,1)}, bf16[512,4096]{1,0:T(8,128)(2,1)}, bf16[512,16]{1,0:T(8,128)(2,1)}, bf16[512,16]{1,0:T(8,128)(2,1)}) custom-call(s32[4]{0:T(128)} %pad_add_fusion.at_ref, bf16[512,1024]{1,0:T(8,128)(2,1)} %get-tuple-element.101.normed_ref, f32[512,1024]{1,0:T(8,128)} %get-tuple-element.102.middle_ref, ...), custom_call_target="tpu_custom_call" | custom-call | flops 1000000 | tf_op jit(solution)/shard_map/feed_forward/pallas_call | solution.py:614
  302.9 11.3 %qkv_forward.3 = (bf16[512,1024]{1,0:T(8,128)(2,1)}, bf16[512,1024]{1,0:T(8,128)(2,1)}, f32[512,128]{1,0:T(8,128)}, bf16[512,16]{1,0:T(8,128)(2,1)}, bf16[512,10...) custom-call(s32[4]{0:T(128)} %pad_add_fusion.at_ref, f32[512,1024]{1,0:T(8,128)} %get-tuple-element.108.x_ref, ...), custom_call_target="tpu_custom_call" | custom-call | flops 1000000 | tf_op jit(solution)/shard_map/qkv_forward/pallas_call | solution.py:614
  315.4 2.4 collective-permute-done.38
  321.4 1.7 reshape.295.left_ref
  323.9 1.7 reshape.296.right_ref
  326.6 1.7 reshape.297.expand_left_ref
  328.2 1.7 copy.126
  336.2 2.1 constant_dynamic-update-slice_fusion.12.v_ref
  339.7 13.8 %attend_forward.3 = (f32[512,1024]{1,0:T(8,128)S(1)}, f32[8,2,512]{2,1,0:T(2,128)S(1)}) custom-call(s32[1]{0:T(128)} %bitcast.6.place_ref, bf16[512,1024]{1,0:T(8,128)(2,1)S(1)} %copy-done.7, bf16[1024,1024]{1,0:T(8,128)(2,1)S(1)} %constant_dynamic-update-slice_fusion.10.k_ref, bf16[1024,1024]{1,0:T(8,128)(2,1)} %copy-done.31), custom_call_target="tpu_custom_call" | custom-call | tf_op jit(solution)/shard_map/attend_forward/pallas_call | solution.py:150
  354.8 11.0 %output_forward.3 = (bf16[512,1024]{1,0:T(8,128)(2,1)}, f32[512,1024]{1,0:T(8,128)}, bf16[512,1024]{1,0:T(8,128)(2,1)}, bf16[512,1024]{1,0:T(8,128)(2,1)}, f32[512,128]{1,0:T(8,128)}, /*index=5*/bf16[512,16]{1,0:T(8,128)(2,1)}) custom-call(s32[4]{0:T(128)} %pad_add_fusion.at_ref, f32[512,1024]{1,0:T(8,128)} %get-tuple-element.108.x_ref, ...), custom_call_target="tpu_custom_call" | custom-call | flops 1000000 | tf_op jit(solution)/shard_map/output_forward/pallas_call | solution.py:614
  365.9 24.0 %feed_forward.3 = (f32[512,1024]{1,0:T(8,128)}, bf16[512,4096]{1,0:T(8,128)(2,1)}, bf16[512,4096]{1,0:T(8,128)(2,1)}, bf16[512,16]{1,0:T(8,128)(2,1)}, bf16[512,16]{1,0:T(8,128)(2,1)}) custom-call(s32[4]{0:T(128)} %pad_add_fusion.at_ref, bf16[512,1024]{1,0:T(8,128)(2,1)} %get-tuple-element.116.normed_ref, f32[512,1024]{1,0:T(8,128)} %get-tuple-element.117.middle_ref, ...), custom_call_target="tpu_custom_call" | custom-call | flops 1000000 | tf_op jit(solution)/shard_map/feed_forward/pallas_call | solution.py:614
  389.9 23.7 %feed_backward.2 = (f32[512,1024]{1,0:T(8,128)}, bf16[16,1024]{1,0:T(8,128)(2,1)}, bf16[16,4096]{1,0:T(8,128)(2,1)}, bf16[16,4096]{1,0:T(8,128)(2,1)}, bf16[16,1024]{1,0:T(8,128)(2,1)}) custom-call(s32[4]{0:T(128)} %pad_add_fusion.at_ref, f32[512,1024]{1,0:T(8,128)} %maximum_convert_fusion.1.grad_ref, bf16[512,4096]{1,0:T(8,128)(2,1)} %get-tuple-element.122.slope_ref, ...), custom_call_target="tpu_custom_call" | custom-call | flops 1000000 | tf_op jit(solution)/shard_map/feed_backward/pallas_call | solution.py:614
  413.6 6.0 output_backward.2
  420.8 21.5 %attend_backward.2 = (bf16[512,1024]{1,0:T(8,128)(2,1)S(1)}, bf16[1024,1024]{1,0:T(8,128)(2,1)S(1)}, bf16[1024,1024]{1,0:T(8,128)(2,1)}) custom-call(s32[1]{0:T(128)} %bitcast.6.place_ref, bf16[512,1024]{1,0:T(8,128)(2,1)S(1)} %copy-done.7, bf16[1024,1024]{1,0:T(8,128)(2,1)} %copy-done.3, bf16[1024,1024]{1,0:T(8,128)(2,1)} %copy-done.31, ...), custom_call_target="tpu_custom_call" | custom-call | tf_op jit(solution)/shard_map/attend_backward/pallas_call | solution.py:176
  446.4 12.6 %collective-permute-done.51 = bf16[256,1024]{1,0:T(8,128)(2,1)S(1)} collective-permute-done((bf16[256,1024]{1,0:T(8,128)(2,1)S(1)}, bf16[256,1024]{1,0:T(8,128)(2,1)S(1)}, u32[]{:S(2)}, u32[]{:S(2)}) %collective-permute-start.51) | collective-permute-done | bytes 524320 | tf_op jit(solution)/shard_map/ppermute | solution.py:218
  464.5 12.3 %qkv_backward.2 = (f32[512,1024]{1,0:T(8,128)}, bf16[16,1024]{1,0:T(8,128)(2,1)}, bf16[16,3072]{1,0:T(8,128)(2,1)}) custom-call(s32[4]{0:T(128)} %pad_add_fusion.at_ref, bf16[512,1024]{1,0:T(8,128)(2,1)} %copy-done.11, bf16[512,1024]{1,0:T(8,128)(2,1)} %add_convert_fusion.3.dk_ref, bf16[512,1024]{1,0:T(8,128)(2,1)} %add_convert_fusion.2.dv_ref, ...), custom_call_target="tpu_custom_call" | custom-call | flops 1000000 | tf_op jit(solution)/shard_map/qkv_backward/pallas_call | solution.py:614
  476.9 24.0 %feed_backward.3 = (f32[512,1024]{1,0:T(8,128)}, bf16[16,1024]{1,0:T(8,128)(2,1)}, bf16[16,4096]{1,0:T(8,128)(2,1)}, bf16[16,4096]{1,0:T(8,128)(2,1)}, bf16[16,1024]{1,0:T(8,128)(2,1)}) custom-call(s32[4]{0:T(128)} %pad_add_fusion.at_ref, f32[512,1024]{1,0:T(8,128)} %get-tuple-element.140.grad_ref, bf16[512,4096]{1,0:T(8,128)(2,1)} %get-tuple-element.141.slope_ref, ...), custom_call_target="tpu_custom_call" | custom-call | flops 1000000 | tf_op jit(solution)/shard_map/feed_backward/pallas_call | solution.py:614
  500.9 5.9 output_backward.3
  508.1 21.5 %attend_backward.3 = (bf16[512,1024]{1,0:T(8,128)(2,1)S(1)}, bf16[1024,1024]{1,0:T(8,128)(2,1)S(1)}, bf16[1024,1024]{1,0:T(8,128)(2,1)}) custom-call(s32[1]{0:T(128)} %bitcast.6.place_ref, bf16[512,1024]{1,0:T(8,128)(2,1)S(1)} %copy-done.6, bf16[1024,1024]{1,0:T(8,128)(2,1)} %copy-done.2, bf16[1024,1024]{1,0:T(8,128)(2,1)} %copy-done.32, ...), custom_call_target="tpu_custom_call" | custom-call | tf_op jit(solution)/shard_map/attend_backward/pallas_call | solution.py:176
  532.8 2.4 slice.517
  548.6 1.8 fusion
  550.4 7.9 %all-to-all-start.2 = ((bf16[16,16,512]{2,1,0:T(8,128)(2,1)}), bf16[16,16,512]{2,1,0:T(8,128)(2,1)S(1)}, u32[]{:S(2)}, u32[]{:S(2)}) async-start(bf16[16,16,512]{2,1,0:T(8,128)(2,1)} %fusion), calls=%async_computation.2 | async-start | bytes 524288 | tf_op jit(solution)/shard_map/all_to_all | solution.py:859
  558.3 2.8 add_convert_fusion.1.dk_ref
  561.1 2.5 add_convert_fusion.dv_ref
  563.6 12.4 %qkv_backward.3 = (f32[512,1024]{1,0:T(8,128)}, bf16[16,1024]{1,0:T(8,128)(2,1)}, bf16[16,3072]{1,0:T(8,128)(2,1)}) custom-call(s32[4]{0:T(128)} %pad_add_fusion.at_ref, bf16[512,1024]{1,0:T(8,128)(2,1)} %copy-done.10, bf16[512,1024]{1,0:T(8,128)(2,1)} %add_convert_fusion.1.dk_ref, bf16[512,1024]{1,0:T(8,128)(2,1)} %add_convert_fusion.dv_ref, ...), custom_call_target="tpu_custom_call" | custom-call | flops 1000000 | tf_op jit(solution)/shard_map/qkv_backward/pallas_call | solution.py:614
  584.7 7.1 %all-to-all-start.1 = ((bf16[16,16,512]{2,1,0:T(8,128)(2,1)}), bf16[16,16,512]{2,1,0:T(8,128)(2,1)}, u32[]{:S(2)}, u32[]{:S(2)}) async-start(bf16[16,16,512]{2,1,0:T(8,128)(2,1)} %fusion.1), calls=%async_computation.1 | async-start | bytes 524288 | tf_op jit(solution)/shard_map/all_to_all | solution.py:859
  595.7 6.6 %all-to-all-done.1 = bf16[16,16,512]{2,1,0:T(8,128)(2,1)} async-done(((bf16[16,16,512]{2,1,0:T(8,128)(2,1)}), bf16[16,16,512]{2,1,0:T(8,128)(2,1)}, u32[]{:S(2)}, u32[]{:S(2)}) %all-to-all-start.1) | async-done | bytes 262176 | tf_op jit(solution)/shard_map/all_to_all | solution.py:859
  603.8 16.8 %collective-permute-done.59 = f32[256,1024]{1,0:T(8,128)S(1)} collective-permute-done((f32[256,1024]{1,0:T(8,128)}, f32[256,1024]{1,0:T(8,128)S(1)}, u32[]{:S(2)}, u32[]{:S(2)}) %collective-permute-start.59) | collective-permute-done | bytes 1048608 | tf_op jit(solution)/shard_map/ppermute | solution.py:218
  (468 shorter events, 156.7 us)
Async XLA Ops:
  3.4 10.8 %collective-permute-start.3 = (bf16[128,1024]{1,0:T(8,128)(2,1)}, bf16[128,1024]{1,0:T(8,128)(2,1)S(1)}, u32[]{:S(2)}, u32[]{:S(2)}) collective-permute-start(bf16[128,1024]{1,0:T(8,128)(2,1)} %pad_maximum_fusion.14), channel_id=1, source_target_pairs={{0,8},{4,12},{8,24},{12,28},{16,0},{20,4},{24,16},{28,20},{1,9},{5... | collective-permute-start | bytes 786440 | tf_op jit(solution)/shard_map/ppermute | solution.py:261
  7.2 16.6 %collective-permute-start.40 = (bf16[128,1024]{1,0:T(8,128)(2,1)S(1)}, bf16[128,1024]{1,0:T(8,128)(2,1)S(1)}, u32[]{:S(2)}, u32[]{:S(2)}) collective-permute-start(bf16[128,1024]{1,0:T(8,128)(2,1)S(1)} %pad_maximum_fusion.15), channel_id=1, source_target_pairs={{0,4},{4,0},{8,12},{12,8},{16,20},{20,16},{24,28},{28,24},{1,5},{5... | collective-permute-start | bytes 786440 | tf_op jit(solution)/shard_map/ppermute | solution.py:265
  9.4 8.5 %collective-permute-start.27 = (bf16[64,1024]{1,0:T(8,128)(2,1)}, bf16[64,1024]{1,0:T(8,128)(2,1)}, u32[]{:S(2)}, u32[]{:S(2)}) collective-permute-start(bf16[64,1024]{1,0:T(8,128)(2,1)} %pad_maximum_fusion.19), channel_id=1, source_target_pairs={{0,4},{4,0},{8,12},{12,8},{16,20},{20,16},{24,28},{28,24},{1,5},{5... | collective-permute-start | bytes 393224 | tf_op jit(solution)/shard_map/ppermute | solution.py:265
  10.0 44.5 %collective-permute-start.28 = (bf16[64,1024]{1,0:T(8,128)(2,1)S(1)}, bf16[64,1024]{1,0:T(8,128)(2,1)}, u32[]{:S(2)}, u32[]{:S(2)}) collective-permute-start(bf16[64,1024]{1,0:T(8,128)(2,1)S(1)} %pad_maximum_fusion.20), channel_id=1, source_target_pairs={{0,2},{2,0},{1,3},{3,1},{4,6},{6,4},{5,7},{7,5},{8,10},{10,8},{9,1... | collective-permute-start | bytes 393224 | tf_op jit(solution)/shard_map/ppermute | solution.py:269
  14.3 8.1 %collective-permute-start.4 = (bf16[128,1024]{1,0:T(8,128)(2,1)S(1)}, bf16[128,1024]{1,0:T(8,128)(2,1)S(1)}, u32[]{:S(2)}, u32[]{:S(2)}) collective-permute-start(bf16[128,1024]{1,0:T(8,128)(2,1)S(1)} %collective-permute-done.3), channel_id=1, source_target_pairs={{0,8},{4,12},{8,24},{12,28},{16,0},{20,4},{24,16},{28,20},{1,9},{5... | collective-permute-start | bytes 786440 | tf_op jit(solution)/shard_map/ppermute | solution.py:261
  22.4 7.3 %collective-permute-start.5 = (bf16[128,1024]{1,0:T(8,128)(2,1)S(1)}, bf16[128,1024]{1,0:T(8,128)(2,1)S(1)}, u32[]{:S(2)}, u32[]{:S(2)}) collective-permute-start(bf16[128,1024]{1,0:T(8,128)(2,1)S(1)} %collective-permute-done.4), channel_id=1, source_target_pairs={{0,8},{4,12},{8,24},{12,28},{16,0},{20,4},{24,16},{28,20},{1,9},{5... | collective-permute-start | bytes 786440 | tf_op jit(solution)/shard_map/ppermute | solution.py:261
  29.6 12.1 %collective-permute-start.16 = (bf16[256,1024]{1,0:T(8,128)(2,1)S(1)}, bf16[256,1024]{1,0:T(8,128)(2,1)S(1)}, u32[]{:S(2)}, u32[]{:S(2)}) collective-permute-start(bf16[256,1024]{1,0:T(8,128)(2,1)S(1)} %get-tuple-element.103), channel_id=1, source_target_pairs={{0,8},{4,12},{8,24},{12,28},{16,0},{20,4},{24,16},{28,20},{1,9},{5... | collective-permute-start | bytes 1572872 | tf_op jit(solution)/shard_map/ppermute | solution.py:261
  41.7 12.1 %collective-permute-start.17 = (bf16[256,1024]{1,0:T(8,128)(2,1)S(1)}, bf16[256,1024]{1,0:T(8,128)(2,1)S(1)}, u32[]{:S(2)}, u32[]{:S(2)}) collective-permute-start(bf16[256,1024]{1,0:T(8,128)(2,1)S(1)} %collective-permute-done.16), channel_id=1, source_target_pairs={{0,8},{4,12},{8,24},{12,28},{16,0},{20,4},{24,16},{28,20},{1,9},{5... | collective-permute-start | bytes 1572872 | tf_op jit(solution)/shard_map/ppermute | solution.py:261
  42.6 12.8 %collective-permute-start.6 = (bf16[4,64,1024]{2,1,0:T(8,128)(2,1)S(1)}, bf16[4,64,1024]{2,1,0:T(8,128)(2,1)S(1)}, u32[]{:S(2)}, u32[]{:S(2)}) collective-permute-start(bf16[4,64,1024]{2,1,0:T(8,128)(2,1)S(1)} %pad_maximum_fusion.12), channel_id=1, source_target_pairs={{0,4},{4,0},{8,12},{12,8},{16,20},{20,16},{24,28},{28,24},{1,5},{5... | collective-permute-start | bytes 1572872 | tf_op jit(solution)/shard_map/ppermute | solution.py:265
  44.2 11.4 %collective-permute-start.7 = (bf16[4,64,1024]{2,1,0:T(8,128)(2,1)S(1)}, bf16[4,64,1024]{2,1,0:T(8,128)(2,1)S(1)}, u32[]{:S(2)}, u32[]{:S(2)}) collective-permute-start(bf16[4,64,1024]{2,1,0:T(8,128)(2,1)S(1)} %pad_maximum_fusion.13), channel_id=1, source_target_pairs={{0,2},{2,0},{1,3},{3,1},{4,6},{6,4},{5,7},{7,5},{8,10},{10,8},{9,1... | collective-permute-start | bytes 1572872 | tf_op jit(solution)/shard_map/ppermute | solution.py:269
  53.8 12.2 %collective-permute-start.18 = (bf16[256,1024]{1,0:T(8,128)(2,1)S(1)}, bf16[256,1024]{1,0:T(8,128)(2,1)S(1)}, u32[]{:S(2)}, u32[]{:S(2)}) collective-permute-start(bf16[256,1024]{1,0:T(8,128)(2,1)S(1)} %collective-permute-done.17), channel_id=1, source_target_pairs={{0,8},{4,12},{8,24},{12,28},{16,0},{20,4},{24,16},{28,20},{1,9},{5... | collective-permute-start | bytes 1572872 | tf_op jit(solution)/shard_map/ppermute | solution.py:261
  56.3 19.5 %collective-permute-start.8 = (bf16[2,4,64,1024]{3,2,1,0:T(8,128)(2,1)S(1)}, bf16[2,4,64,1024]{3,2,1,0:T(8,128)(2,1)S(1)}, u32[]{:S(2)}, u32[]{:S(2)}) collective-permute-start(bf16[2,4,64,1024]{3,2,1,0:T(8,128)(2,1)S(1)} %pad_maximum_fusion.5.refs_0_), channel_id=1, source_target_pairs={{0,2},{2,0},{1,3},{3,1},{4,6},{6,4},{5,7},{7,5},{8,10},{10,8},{9,1... | collective-permute-start | bytes 3145736 | tf_op jit(solution)/shard_map/ppermute | solution.py:269
  57.8 21.2 %collective-permute-start.9 = (bf16[2,4,64,1024]{3,2,1,0:T(8,128)(2,1)S(1)}, bf16[2,4,64,1024]{3,2,1,0:T(8,128)(2,1)S(1)}, u32[]{:S(2)}, u32[]{:S(2)}) collective-permute-start(bf16[2,4,64,1024]{3,2,1,0:T(8,128)(2,1)S(1)} %pad_maximum_fusion.6.refs_2_), channel_id=1, source_target_pairs={{0,4},{4,0},{8,12},{12,8},{16,20},{20,16},{24,28},{28,24},{1,5},{5... | collective-permute-start | bytes 3145736 | tf_op jit(solution)/shard_map/ppermute | solution.py:265
  66.1 27.1 %collective-permute-start.29 = (bf16[256,1024]{1,0:T(8,128)(2,1)}, bf16[256,1024]{1,0:T(8,128)(2,1)}, u32[]{:S(2)}, u32[]{:S(2)}) collective-permute-start(bf16[256,1024]{1,0:T(8,128)(2,1)} %copy-done.39), channel_id=1, source_target_pairs={{0,8},{4,12},{8,24},{12,28},{16,0},{20,4},{24,16},{28,20},{1,9},{5... | collective-permute-start | bytes 1572872 | tf_op jit(solution)/shard_map/ppermute | solution.py:261
  79.9 40.8 %collective-permute-start.19 = (bf16[4,128,1024]{2,1,0:T(8,128)(2,1)}, bf16[4,128,1024]{2,1,0:T(8,128)(2,1)}, u32[]{:S(2)}, u32[]{:S(2)}) collective-permute-start(bf16[4,128,1024]{2,1,0:T(8,128)(2,1)} %pad_maximum_fusion.7), channel_id=1, source_target_pairs={{0,4},{4,0},{8,12},{12,8},{16,20},{20,16},{24,28},{28,24},{1,5},{5... | collective-permute-start | bytes 3145736 | tf_op jit(solution)/shard_map/ppermute | solution.py:265
  85.0 37.9 %collective-permute-start.20 = (bf16[4,128,1024]{2,1,0:T(8,128)(2,1)}, bf16[4,128,1024]{2,1,0:T(8,128)(2,1)}, u32[]{:S(2)}, u32[]{:S(2)}) collective-permute-start(bf16[4,128,1024]{2,1,0:T(8,128)(2,1)} %pad_maximum_fusion.8), channel_id=1, source_target_pairs={{0,2},{2,0},{1,3},{3,1},{4,6},{6,4},{5,7},{7,5},{8,10},{10,8},{9,1... | collective-permute-start | bytes 3145736 | tf_op jit(solution)/shard_map/ppermute | solution.py:269
  87.0 35.9 %all-to-all-start = ((bf16[16,2,16,512]{3,2,1,0:T(8,128)(2,1)}), bf16[16,2,16,512]{3,2,1,0:T(8,128)(2,1)}, u32[]{:S(2)}, u32[]{:S(2)}) async-start(bf16[16,2,16,512]{3,2,1,0:T(8,128)(2,1)} %broadcast_select_fusion), calls=%async_computation | async-start | bytes 1048576 | tf_op jit(solution)/shard_map/all_to_all | solution.py:769
  93.2 22.2 %collective-permute-start.30 = (bf16[256,1024]{1,0:T(8,128)(2,1)}, bf16[256,1024]{1,0:T(8,128)(2,1)}, u32[]{:S(2)}, u32[]{:S(2)}) collective-permute-start(bf16[256,1024]{1,0:T(8,128)(2,1)} %collective-permute-done.29), channel_id=1, source_target_pairs={{0,8},{4,12},{8,24},{12,28},{16,0},{20,4},{24,16},{28,20},{1,9},{5... | collective-permute-start | bytes 1572872 | tf_op jit(solution)/shard_map/ppermute | solution.py:261
  96.8 18.6 %collective-permute-start.41 = (bf16[128,1024]{1,0:T(8,128)(2,1)}, bf16[128,1024]{1,0:T(8,128)(2,1)S(1)}, u32[]{:S(2)}, u32[]{:S(2)}) collective-permute-start(bf16[128,1024]{1,0:T(8,128)(2,1)} %slice_bitcast_fusion.2), channel_id=1, source_target_pairs={{0,2},{2,0},{1,3},{3,1},{4,6},{6,4},{5,7},{7,5},{8,10},{10,8},{9,1... | collective-permute-start | bytes 786440 | tf_op jit(solution)/shard_map/ppermute | solution.py:269
  100.3 33.5 %collective-permute-start = (bf16[256,1024]{1,0:T(8,128)(2,1)}, bf16[256,1024]{1,0:T(8,128)(2,1)}, u32[]{:S(2)}, u32[]{:S(2)}) collective-permute-start(bf16[256,1024]{1,0:T(8,128)(2,1)} %bitcast_select_fusion.3), channel_id=1, source_target_pairs={{0,2},{1,3},{2,1},{3,0},{4,6},{5,7},{6,5},{7,4},{8,10},{9,11},{10,... | collective-permute-start | bytes 1572872 | tf_op jit(solution)/shard_map/ppermute | solution.py:206
  115.4 24.6 %collective-permute-start.10 = (bf16[2,4,64,1024]{3,2,1,0:T(8,128)(2,1)S(1)}, bf16[2,4,64,1024]{3,2,1,0:T(8,128)(2,1)}, u32[]{:S(2)}, u32[]{:S(2)}) collective-permute-start(bf16[2,4,64,1024]{3,2,1,0:T(8,128)(2,1)S(1)} %pad_maximum_fusion.5.refs_0_), channel_id=1, source_target_pairs={{0,1},{1,0},{2,3},{3,2},{4,5},{5,4},{6,7},{7,6},{8,9},{9,8},{10,11... | collective-permute-start | bytes 3145736 | tf_op jit(solution)/shard_map/ppermute | solution.py:273
  115.4 15.7 %collective-permute-start.31 = (bf16[256,1024]{1,0:T(8,128)(2,1)}, bf16[256,1024]{1,0:T(8,128)(2,1)}, u32[]{:S(2)}, u32[]{:S(2)}) collective-permute-start(bf16[256,1024]{1,0:T(8,128)(2,1)} %collective-permute-done.30), channel_id=1, source_target_pairs={{0,8},{4,12},{8,24},{12,28},{16,0},{20,4},{24,16},{28,20},{1,9},{5... | collective-permute-start | bytes 1572872 | tf_op jit(solution)/shard_map/ppermute | solution.py:261
  120.8 14.3 %collective-permute-start.1 = (bf16[256,1024]{1,0:T(8,128)(2,1)}, bf16[256,1024]{1,0:T(8,128)(2,1)}, u32[]{:S(2)}, u32[]{:S(2)}) collective-permute-start(bf16[256,1024]{1,0:T(8,128)(2,1)} %slice_bitcast_fusion.1), channel_id=1, source_target_pairs={{2,3},{3,2},{6,7},{7,6},{10,11},{11,10},{14,15},{15,14},{18,19},{1... | collective-permute-start | bytes 1572872 | tf_op jit(solution)/shard_map/ppermute | solution.py:207
  123.0 14.6 %collective-permute-start.2 = (bf16[16,2,16,512]{3,2,1,0:T(8,128)(2,1)}, bf16[16,2,16,512]{3,2,1,0:T(8,128)(2,1)S(1)}, u32[]{:S(2)}, u32[]{:S(2)}) collective-permute-start(bf16[16,2,16,512]{3,2,1,0:T(8,128)(2,1)} %all-to-all-done), channel_id=1, source_target_pairs={{0,1},{1,0},{2,3},{3,2},{4,5},{5,4},{6,7},{7,6},{8,9},{9,8},{10,11... | collective-permute-start | bytes 1572872 | tf_op jit(solution)/shard_map/ppermute | solution.py:770
  131.0 10.8 %collective-permute-start.12 = (bf16[2,4,64,1024]{3,2,1,0:T(8,128)(2,1)S(1)}, bf16[2,4,64,1024]{3,2,1,0:T(8,128)(2,1)}, u32[]{:S(2)}, u32[]{:S(2)}) collective-permute-start(bf16[2,4,64,1024]{3,2,1,0:T(8,128)(2,1)S(1)} %pad_maximum_fusion.6.refs_2_), channel_id=1, source_target_pairs={{0,1},{1,0},{2,3},{3,2},{4,5},{5,4},{6,7},{7,6},{8,9},{9,8},{10,11... | collective-permute-start | bytes 3145736 | tf_op jit(solution)/shard_map/ppermute | solution.py:273
  133.9 49.5 %collective-permute-start.21 = (bf16[2,4,128,1024]{3,2,1,0:T(8,128)(2,1)}, bf16[2,4,128,1024]{3,2,1,0:T(8,128)(2,1)}, u32[]{:S(2)}, u32[]{:S(2)}) collective-permute-start(bf16[2,4,128,1024]{3,2,1,0:T(8,128)(2,1)} %pad_maximum_fusion.refs_0_), channel_id=1, source_target_pairs={{0,2},{2,0},{1,3},{3,1},{4,6},{6,4},{5,7},{7,5},{8,10},{10,8},{9,1... | collective-permute-start | bytes 6291464 | tf_op jit(solution)/shard_map/ppermute | solution.py:269
  135.1 26.5 %collective-permute-start.42 = (bf16[512,1024]{1,0:T(8,128)(2,1)}, bf16[512,1024]{1,0:T(8,128)(2,1)}, u32[]{:S(2)}, u32[]{:S(2)}) collective-permute-start(bf16[512,1024]{1,0:T(8,128)(2,1)} %constant_dynamic-update-slice_fusion.14), channel_id=1, source_target_pairs={{0,8},{4,12},{8,24},{12,28},{16,0},{20,4},{24,16},{28,20},{1,9},{5... | collective-permute-start | bytes 3145736 | tf_op jit(solution)/shard_map/ppermute | solution.py:261
  137.6 47.9 %collective-permute-start.22 = (bf16[2,4,128,1024]{3,2,1,0:T(8,128)(2,1)}, bf16[2,4,128,1024]{3,2,1,0:T(8,128)(2,1)}, u32[]{:S(2)}, u32[]{:S(2)}) collective-permute-start(bf16[2,4,128,1024]{3,2,1,0:T(8,128)(2,1)} %pad_maximum_fusion.1.refs_2_), channel_id=1, source_target_pairs={{0,4},{4,0},{8,12},{12,8},{16,20},{20,16},{24,28},{28,24},{1,5},{5... | collective-permute-start | bytes 6291464 | tf_op jit(solution)/shard_map/ppermute | solution.py:265
  140.0 26.0 %collective-permute-start.11 = (bf16[2,4,64,1024]{3,2,1,0:T(8,128)(2,1)S(1)}, bf16[2,4,64,1024]{3,2,1,0:T(8,128)(2,1)S(1)}, u32[]{:S(2)}, u32[]{:S(2)}) collective-permute-start(bf16[2,4,64,1024]{3,2,1,0:T(8,128)(2,1)S(1)} %collective-permute-done.8.refs_1_), channel_id=1, source_target_pairs={{0,1},{1,0},{2,3},{3,2},{4,5},{5,4},{6,7},{7,6},{8,9},{9,8},{10,11... | collective-permute-start | bytes 3145736 | tf_op jit(solution)/shard_map/ppermute | solution.py:273
  141.9 29.6 %collective-permute-start.13 = (bf16[2,4,64,1024]{3,2,1,0:T(8,128)(2,1)}, bf16[2,4,64,1024]{3,2,1,0:T(8,128)(2,1)S(1)}, u32[]{:S(2)}, u32[]{:S(2)}) collective-permute-start(bf16[2,4,64,1024]{3,2,1,0:T(8,128)(2,1)} %copy-done.17), channel_id=1, source_target_pairs={{0,1},{1,0},{2,3},{3,2},{4,5},{5,4},{6,7},{7,6},{8,9},{9,8},{10,11... | collective-permute-start | bytes 3145736 | tf_op jit(solution)/shard_map/ppermute | solution.py:273
  161.6 25.7 %collective-permute-start.43 = (bf16[512,1024]{1,0:T(8,128)(2,1)}, bf16[512,1024]{1,0:T(8,128)(2,1)}, u32[]{:S(2)}, u32[]{:S(2)}) collective-permute-start(bf16[512,1024]{1,0:T(8,128)(2,1)} %collective-permute-done.42), channel_id=1, source_target_pairs={{0,8},{4,12},{8,24},{12,28},{16,0},{20,4},{24,16},{28,20},{1,9},{5... | collective-permute-start | bytes 3145736 | tf_op jit(solution)/shard_map/ppermute | solution.py:261
  166.0 28.7 %collective-permute-start.23 = (bf16[2,4,128,1024]{3,2,1,0:T(8,128)(2,1)}, bf16[2,4,128,1024]{3,2,1,0:T(8,128)(2,1)}, u32[]{:S(2)}, u32[]{:S(2)}) collective-permute-start(bf16[2,4,128,1024]{3,2,1,0:T(8,128)(2,1)} %pad_maximum_fusion.refs_0_), channel_id=1, source_target_pairs={{0,1},{1,0},{2,3},{3,2},{4,5},{5,4},{6,7},{7,6},{8,9},{9,8},{10,11... | collective-permute-start | bytes 6291464 | tf_op jit(solution)/shard_map/ppermute | solution.py:273
  171.5 45.7 %collective-permute-start.25 = (bf16[2,4,128,1024]{3,2,1,0:T(8,128)(2,1)}, bf16[2,4,128,1024]{3,2,1,0:T(8,128)(2,1)}, u32[]{:S(2)}, u32[]{:S(2)}) collective-permute-start(bf16[2,4,128,1024]{3,2,1,0:T(8,128)(2,1)} %pad_maximum_fusion.1.refs_2_), channel_id=1, source_target_pairs={{0,1},{1,0},{2,3},{3,2},{4,5},{5,4},{6,7},{7,6},{8,9},{9,8},{10,11... | collective-permute-start | bytes 6291464 | tf_op jit(solution)/shard_map/ppermute | solution.py:273
  183.4 7.8 %collective-permute-start.14 = (bf16[512,1024]{1,0:T(8,128)(2,1)}, bf16[512,1024]{1,0:T(8,128)(2,1)}, u32[]{:S(2)}, u32[]{:S(2)}) collective-permute-start(bf16[512,1024]{1,0:T(8,128)(2,1)} %get-tuple-element.98), channel_id=1, source_target_pairs={{0,1},{1,0},{2,3},{3,2},{4,5},{5,4},{6,7},{7,6},{8,9},{9,8},{10,11... | collective-permute-start | bytes 3145736 | tf_op jit(solution)/shard_map/ppermute | solution.py:232
  185.4 9.3 %collective-permute-start.15 = (bf16[512,1024]{1,0:T(8,128)(2,1)}, bf16[512,1024]{1,0:T(8,128)(2,1)}, u32[]{:S(2)}, u32[]{:S(2)}) collective-permute-start(bf16[512,1024]{1,0:T(8,128)(2,1)} %get-tuple-element.99), channel_id=1, source_target_pairs={{0,1},{1,0},{2,3},{3,2},{4,5},{5,4},{6,7},{7,6},{8,9},{9,8},{10,11... | collective-permute-start | bytes 3145736 | tf_op jit(solution)/shard_map/ppermute | solution.py:232
  187.3 25.2 %collective-permute-start.44 = (bf16[512,1024]{1,0:T(8,128)(2,1)}, bf16[512,1024]{1,0:T(8,128)(2,1)}, u32[]{:S(2)}, u32[]{:S(2)}) collective-permute-start(bf16[512,1024]{1,0:T(8,128)(2,1)} %collective-permute-done.43), channel_id=1, source_target_pairs={{0,8},{4,12},{8,24},{12,28},{16,0},{20,4},{24,16},{28,20},{1,9},{5... | collective-permute-start | bytes 3145736 | tf_op jit(solution)/shard_map/ppermute | solution.py:261
  191.2 26.6 %collective-permute-start.32 = (bf16[4,2,64,1024]{3,2,1,0:T(8,128)(2,1)S(1)}, bf16[4,2,64,1024]{3,2,1,0:T(8,128)(2,1)S(1)}, u32[]{:S(2)}, u32[]{:S(2)}) collective-permute-start(bf16[4,2,64,1024]{3,2,1,0:T(8,128)(2,1)S(1)} %pad_maximum_fusion.9.refs_0_), channel_id=1, source_target_pairs={{0,2},{2,0},{1,3},{3,1},{4,6},{6,4},{5,7},{7,5},{8,10},{10,8},{9,1... | collective-permute-start | bytes 3145736 | tf_op jit(solution)/shard_map/ppermute | solution.py:269
  194.7 28.4 %collective-permute-start.34 = (bf16[4,2,64,1024]{3,2,1,0:T(8,128)(2,1)S(1)}, bf16[4,2,64,1024]{3,2,1,0:T(8,128)(2,1)S(1)}, u32[]{:S(2)}, u32[]{:S(2)}) collective-permute-start(bf16[4,2,64,1024]{3,2,1,0:T(8,128)(2,1)S(1)} %pad_maximum_fusion.9.refs_0_), channel_id=1, source_target_pairs={{0,1},{1,0},{2,3},{3,2},{4,5},{5,4},{6,7},{7,6},{8,9},{9,8},{10,11... | collective-permute-start | bytes 3145736 | tf_op jit(solution)/shard_map/ppermute | solution.py:273
  194.7 26.6 %collective-permute-start.33 = (bf16[4,2,64,1024]{3,2,1,0:T(8,128)(2,1)S(1)}, bf16[4,2,64,1024]{3,2,1,0:T(8,128)(2,1)}, u32[]{:S(2)}, u32[]{:S(2)}) collective-permute-start(bf16[4,2,64,1024]{3,2,1,0:T(8,128)(2,1)S(1)} %pad_maximum_fusion.10.refs_2_), channel_id=1, source_target_pairs={{0,4},{4,0},{8,12},{12,8},{16,20},{20,16},{24,28},{28,24},{1,5},{5... | collective-permute-start | bytes 3145736 | tf_op jit(solution)/shard_map/ppermute | solution.py:265
  212.4 11.6 %collective-permute-start.36 = (bf16[4,2,64,1024]{3,2,1,0:T(8,128)(2,1)S(1)}, bf16[4,2,64,1024]{3,2,1,0:T(8,128)(2,1)S(1)}, u32[]{:S(2)}, u32[]{:S(2)}) collective-permute-start(bf16[4,2,64,1024]{3,2,1,0:T(8,128)(2,1)S(1)} %pad_maximum_fusion.10.refs_2_), channel_id=1, source_target_pairs={{0,1},{1,0},{2,3},{3,2},{4,5},{5,4},{6,7},{7,6},{8,9},{9,8},{10,11... | collective-permute-start | bytes 3145736 | tf_op jit(solution)/shard_map/ppermute | solution.py:273
  217.2 26.1 %collective-permute-start.24 = (bf16[2,4,128,1024]{3,2,1,0:T(8,128)(2,1)}, bf16[2,4,128,1024]{3,2,1,0:T(8,128)(2,1)}, u32[]{:S(2)}, u32[]{:S(2)}) collective-permute-start(bf16[2,4,128,1024]{3,2,1,0:T(8,128)(2,1)} %collective-permute-done.21.refs_1_), channel_id=1, source_target_pairs={{0,1},{1,0},{2,3},{3,2},{4,5},{5,4},{6,7},{7,6},{8,9},{9,8},{10,11... | collective-permute-start | bytes 6291464 | tf_op jit(solution)/shard_map/ppermute | solution.py:273
  217.8 27.1 %collective-permute-start.26 = (bf16[2,4,128,1024]{3,2,1,0:T(8,128)(2,1)}, bf16[2,4,128,1024]{3,2,1,0:T(8,128)(2,1)}, u32[]{:S(2)}, u32[]{:S(2)}) collective-permute-start(bf16[2,4,128,1024]{3,2,1,0:T(8,128)(2,1)} %collective-permute-done.22.refs_3_), channel_id=1, source_target_pairs={{0,1},{1,0},{2,3},{3,2},{4,5},{5,4},{6,7},{7,6},{8,9},{9,8},{10,11... | collective-permute-start | bytes 6291464 | tf_op jit(solution)/shard_map/ppermute | solution.py:273
  221.4 4.8 collective-permute-start.35
  223.1 91.8 %collective-permute-start.45 = (bf16[4,2,128,1024]{3,2,1,0:T(8,128)(2,1)}, bf16[4,2,128,1024]{3,2,1,0:T(8,128)(2,1)}, u32[]{:S(2)}, u32[]{:S(2)}) collective-permute-start(bf16[4,2,128,1024]{3,2,1,0:T(8,128)(2,1)} %pad_maximum_fusion.2.refs_0_), channel_id=1, source_target_pairs={{0,2},{2,0},{1,3},{3,1},{4,6},{6,4},{5,7},{7,5},{8,10},{10,8},{9,1... | collective-permute-start | bytes 6291464 | tf_op jit(solution)/shard_map/ppermute | solution.py:269
  224.1 91.3 %collective-permute-start.46 = (bf16[4,2,128,1024]{3,2,1,0:T(8,128)(2,1)}, bf16[4,2,128,1024]{3,2,1,0:T(8,128)(2,1)}, u32[]{:S(2)}, u32[]{:S(2)}) collective-permute-start(bf16[4,2,128,1024]{3,2,1,0:T(8,128)(2,1)} %pad_maximum_fusion.3.refs_2_), channel_id=1, source_target_pairs={{0,4},{4,0},{8,12},{12,8},{16,20},{20,16},{24,28},{28,24},{1,5},{5... | collective-permute-start | bytes 6291464 | tf_op jit(solution)/shard_map/ppermute | solution.py:265
  226.1 75.8 %collective-permute-start.37 = (bf16[4,2,64,1024]{3,2,1,0:T(8,128)(2,1)}, bf16[4,2,64,1024]{3,2,1,0:T(8,128)(2,1)S(1)}, u32[]{:S(2)}, u32[]{:S(2)}) collective-permute-start(bf16[4,2,64,1024]{3,2,1,0:T(8,128)(2,1)} %collective-permute-done.33.refs_3_), channel_id=1, source_target_pairs={{0,1},{1,0},{2,3},{3,2},{4,5},{5,4},{6,7},{7,6},{8,9},{9,8},{10,11... | collective-permute-start | bytes 3145736 | tf_op jit(solution)/shard_map/ppermute | solution.py:273
  243.3 71.0 %collective-permute-start.53 = (bf16[256,1024]{1,0:T(8,128)(2,1)}, bf16[256,1024]{1,0:T(8,128)(2,1)S(1)}, u32[]{:S(2)}, u32[]{:S(2)}) collective-permute-start(bf16[256,1024]{1,0:T(8,128)(2,1)} %bitcast_select_fusion.1), channel_id=1, source_target_pairs={{0,2},{1,3},{2,1},{3,0},{4,6},{5,7},{6,5},{7,4},{8,10},{9,11},{10,... | collective-permute-start | bytes 1572872 | tf_op jit(solution)/shard_map/ppermute | solution.py:206
  244.9 69.9 %collective-permute-start.54 = (bf16[256,1024]{1,0:T(8,128)(2,1)}, bf16[256,1024]{1,0:T(8,128)(2,1)S(1)}, u32[]{:S(2)}, u32[]{:S(2)}) collective-permute-start(bf16[256,1024]{1,0:T(8,128)(2,1)} %slice_bitcast_fusion), channel_id=1, source_target_pairs={{2,3},{3,2},{6,7},{7,6},{10,11},{11,10},{14,15},{15,14},{18,19},{1... | collective-permute-start | bytes 1572872 | tf_op jit(solution)/shard_map/ppermute | solution.py:207
  314.3 51.5 %collective-permute-start.47 = (bf16[4,2,128,1024]{3,2,1,0:T(8,128)(2,1)}, bf16[4,2,128,1024]{3,2,1,0:T(8,128)(2,1)}, u32[]{:S(2)}, u32[]{:S(2)}) collective-permute-start(bf16[4,2,128,1024]{3,2,1,0:T(8,128)(2,1)} %pad_maximum_fusion.2.refs_0_), channel_id=1, source_target_pairs={{0,1},{1,0},{2,3},{3,2},{4,5},{5,4},{6,7},{7,6},{8,9},{9,8},{10,11... | collective-permute-start | bytes 6291464 | tf_op jit(solution)/shard_map/ppermute | solution.py:273
  314.8 51.0 %collective-permute-start.49 = (bf16[4,2,128,1024]{3,2,1,0:T(8,128)(2,1)}, bf16[4,2,128,1024]{3,2,1,0:T(8,128)(2,1)}, u32[]{:S(2)}, u32[]{:S(2)}) collective-permute-start(bf16[4,2,128,1024]{3,2,1,0:T(8,128)(2,1)} %pad_maximum_fusion.3.refs_2_), channel_id=1, source_target_pairs={{0,1},{1,0},{2,3},{3,2},{4,5},{5,4},{6,7},{7,6},{8,9},{9,8},{10,11... | collective-permute-start | bytes 6291464 | tf_op jit(solution)/shard_map/ppermute | solution.py:273
  314.9 51.0 %collective-permute-start.48 = (bf16[4,2,128,1024]{3,2,1,0:T(8,128)(2,1)}, bf16[4,2,128,1024]{3,2,1,0:T(8,128)(2,1)}, u32[]{:S(2)}, u32[]{:S(2)}) collective-permute-start(bf16[4,2,128,1024]{3,2,1,0:T(8,128)(2,1)} %collective-permute-done.45.refs_1_), channel_id=1, source_target_pairs={{0,1},{1,0},{2,3},{3,2},{4,5},{5,4},{6,7},{7,6},{8,9},{9,8},{10,11... | collective-permute-start | bytes 6291464 | tf_op jit(solution)/shard_map/ppermute | solution.py:273
  315.4 50.5 %collective-permute-start.50 = (bf16[4,2,128,1024]{3,2,1,0:T(8,128)(2,1)}, bf16[4,2,128,1024]{3,2,1,0:T(8,128)(2,1)}, u32[]{:S(2)}, u32[]{:S(2)}) collective-permute-start(bf16[4,2,128,1024]{3,2,1,0:T(8,128)(2,1)} %collective-permute-done.46.refs_3_), channel_id=1, source_target_pairs={{0,1},{1,0},{2,3},{3,2},{4,5},{5,4},{6,7},{7,6},{8,9},{9,8},{10,11... | collective-permute-start | bytes 6291464 | tf_op jit(solution)/shard_map/ppermute | solution.py:273
  318.8 17.4 %collective-permute-start.39 = (bf16[512,1024]{1,0:T(8,128)(2,1)}, bf16[512,1024]{1,0:T(8,128)(2,1)}, u32[]{:S(2)}, u32[]{:S(2)}) collective-permute-start(bf16[512,1024]{1,0:T(8,128)(2,1)} %get-tuple-element.114), channel_id=1, source_target_pairs={{0,1},{1,0},{2,3},{3,2},{4,5},{5,4},{6,7},{7,6},{8,9},{9,8},{10,11... | collective-permute-start | bytes 3145736 | tf_op jit(solution)/shard_map/ppermute | solution.py:232
  442.4 19.3 %collective-permute-start.55 = (bf16[512,1024]{1,0:T(8,128)(2,1)S(1)}, bf16[512,1024]{1,0:T(8,128)(2,1)S(1)}, u32[]{:S(2)}, u32[]{:S(2)}) collective-permute-start(bf16[512,1024]{1,0:T(8,128)(2,1)S(1)} %slice.511), channel_id=1, source_target_pairs={{0,1},{1,0},{2,3},{3,2},{4,5},{5,4},{6,7},{7,6},{8,9},{9,8},{10,11... | collective-permute-start | bytes 3145736 | tf_op jit(solution)/shard_map/ppermute | solution.py:247
  444.5 14.5 %collective-permute-start.51 = (bf16[256,1024]{1,0:T(8,128)(2,1)S(1)}, bf16[256,1024]{1,0:T(8,128)(2,1)S(1)}, u32[]{:S(2)}, u32[]{:S(2)}) collective-permute-start(bf16[256,1024]{1,0:T(8,128)(2,1)S(1)} %broadcast_select_fusion.2), channel_id=1, source_target_pairs={{2,0},{3,1},{1,2},{0,3},{6,4},{7,5},{5,6},{4,7},{10,8},{11,9},{9,1... | collective-permute-start | bytes 1572872 | tf_op jit(solution)/shard_map/ppermute | solution.py:218
  446.1 17.0 %collective-permute-start.56 = (bf16[512,1024]{1,0:T(8,128)(2,1)S(1)}, bf16[512,1024]{1,0:T(8,128)(2,1)S(1)}, u32[]{:S(2)}, u32[]{:S(2)}) collective-permute-start(bf16[512,1024]{1,0:T(8,128)(2,1)S(1)} %slice.513), channel_id=1, source_target_pairs={{0,1},{1,0},{2,3},{3,2},{4,5},{5,4},{6,7},{7,6},{8,9},{9,8},{10,11... | collective-permute-start | bytes 3145736 | tf_op jit(solution)/shard_map/ppermute | solution.py:247
  460.2 87.0 %collective-permute-start.52 = (bf16[256,1024]{1,0:T(8,128)(2,1)}, bf16[256,1024]{1,0:T(8,128)(2,1)}, u32[]{:S(2)}, u32[]{:S(2)}) collective-permute-start(bf16[256,1024]{1,0:T(8,128)(2,1)} %get-tuple-element.235), channel_id=1, source_target_pairs={{3,2},{2,3},{7,6},{6,7},{11,10},{10,11},{15,14},{14,15},{19,18},{1... | collective-permute-start | bytes 1572872 | tf_op jit(solution)/shard_map/ppermute | solution.py:219
  531.6 26.7 %collective-permute-start.57 = (bf16[512,1024]{1,0:T(8,128)(2,1)}, bf16[512,1024]{1,0:T(8,128)(2,1)}, u32[]{:S(2)}, u32[]{:S(2)}) collective-permute-start(bf16[512,1024]{1,0:T(8,128)(2,1)} %slice.515), channel_id=1, source_target_pairs={{0,1},{1,0},{2,3},{3,2},{4,5},{5,4},{6,7},{7,6},{8,9},{9,8},{10,11... | collective-permute-start | bytes 3145736 | tf_op jit(solution)/shard_map/ppermute | solution.py:247
  535.2 25.9 %collective-permute-start.58 = (bf16[512,1024]{1,0:T(8,128)(2,1)}, bf16[512,1024]{1,0:T(8,128)(2,1)}, u32[]{:S(2)}, u32[]{:S(2)}) collective-permute-start(bf16[512,1024]{1,0:T(8,128)(2,1)} %slice.517), channel_id=1, source_target_pairs={{0,1},{1,0},{2,3},{3,2},{4,5},{5,4},{6,7},{7,6},{8,9},{9,8},{10,11... | collective-permute-start | bytes 3145736 | tf_op jit(solution)/shard_map/ppermute | solution.py:247
  539.6 9.1 %collective-permute-start.62 = (bf16[16,16,512]{2,1,0:T(8,128)(2,1)}, bf16[16,16,512]{2,1,0:T(8,128)(2,1)}, u32[]{:S(2)}, u32[]{:S(2)}) collective-permute-start(bf16[16,16,512]{2,1,0:T(8,128)(2,1)} %select_bitcast_fusion.6), channel_id=1, source_target_pairs={{0,1},{1,0},{2,3},{3,2},{4,5},{5,4},{6,7},{7,6},{8,9},{9,8},{10,11... | collective-permute-start | bytes 786440 | tf_op jit(solution)/shard_map/ppermute | solution.py:857
  550.4 30.8 %all-to-all-start.2 = ((bf16[16,16,512]{2,1,0:T(8,128)(2,1)}), bf16[16,16,512]{2,1,0:T(8,128)(2,1)S(1)}, u32[]{:S(2)}, u32[]{:S(2)}) async-start(bf16[16,16,512]{2,1,0:T(8,128)(2,1)} %fusion), calls=%async_computation.2 | async-start | bytes 524288 | tf_op jit(solution)/shard_map/all_to_all | solution.py:859
  584.7 17.7 %all-to-all-start.1 = ((bf16[16,16,512]{2,1,0:T(8,128)(2,1)}), bf16[16,16,512]{2,1,0:T(8,128)(2,1)}, u32[]{:S(2)}, u32[]{:S(2)}) async-start(bf16[16,16,512]{2,1,0:T(8,128)(2,1)} %fusion.1), calls=%async_computation.1 | async-start | bytes 524288 | tf_op jit(solution)/shard_map/all_to_all | solution.py:859
  592.9 27.7 %collective-permute-start.59 = (f32[256,1024]{1,0:T(8,128)}, f32[256,1024]{1,0:T(8,128)S(1)}, u32[]{:S(2)}, u32[]{:S(2)}) collective-permute-start(f32[256,1024]{1,0:T(8,128)} %slice_select_fusion), channel_id=1, source_target_pairs={{2,0},{3,1},{1,2},{0,3},{6,4},{7,5},{5,6},{4,7},{10,8},{11,9},{9,1... | collective-permute-start | bytes 3145736 | tf_op jit(solution)/shard_map/ppermute | solution.py:218
  620.9 6.6 %collective-permute-start.60 = (f32[256,1024]{1,0:T(8,128)S(1)}, f32[256,1024]{1,0:T(8,128)S(1)}, u32[]{:S(2)}, u32[]{:S(2)}) collective-permute-start(f32[256,1024]{1,0:T(8,128)S(1)} %get-tuple-element.217), channel_id=1, source_target_pairs={{3,2},{2,3},{7,6},{6,7},{11,10},{10,11},{15,14},{14,15},{19,18},{1... | collective-permute-start | bytes 3145736 | tf_op jit(solution)/shard_map/ppermute | solution.py:219
  (94 other events, 858.6 us)

commit v3 on v2

v3 whole, which is shorter than its diff:
```python
import functools

import jax
import jax.numpy as jnp
from jax import lax
from jax.experimental import pallas as pl
from jax.experimental.pallas import tpu as pltpu
from jax.sharding import Mesh
from jax.sharding import PartitionSpec as P

HEADS = 16
HEAD_DIM = 64
RANK = 16
ADAPTERS = 8
LAYERS = 2

WHOLE, PIECES, GATHERED, MIXED = range(4)
MICROSECOND = 10**8
BLK = 256

epsilon = 1e-05
root_factor = 0.7978845608028654
low_type = jnp.bfloat16
wide = jnp.float32

ROWS_BY_ROWS = (((1,), (1,)), ((), ()))
COLS_BY_COLS = (((0,), (0,)), ((), ()))
PLAIN = (((1,), (0,)), ((), ()))
EVERY = ("dp", "chip", "core")
LANE = ("dp", "chip")
CTX = ("chip", "core")


def times(left_side, right_side, dims=PLAIN):
    return lax.dot_general(left_side, right_side, dims, preferred_element_type=wide)


def block_steps(place, pieces):
    steps = [(0, 0, 0), (0, 1, 0), (0, 1, 1)]
    for piece in range(1, pieces):
        slot = jnp.where(place >= piece, 0, 1)
        steps += [(piece, slot, 0), (piece, 1, slot)]
    return steps


def block_rows(slot):
    return pl.ds(slot * BLK if isinstance(slot, int) else pl.multiple_of(slot * BLK, BLK), BLK)


def stack_heads(rows, mask):
    zero = jnp.zeros_like(rows)
    return jnp.concatenate([jnp.where(mask, rows, zero), jnp.where(mask, zero, rows)], axis=0)


def update_slot(held, slot, change):
    if isinstance(slot, int):
        return [change(member) if which == slot else member for which, member in enumerate(held)]
    return [jnp.where(slot == which, change(member), member) for which, member in enumerate(held)]


def pick_slot(held, slot):
    return held[slot] if isinstance(slot, int) else jnp.where(slot == 0, held[0], held[1])


def attend_forward_kernel(pieces, place_ref, q_ref, *refs):
    k_refs, v_refs = refs[:pieces], refs[pieces : 2 * pieces]
    o_ref, stat_ref, queries, scores, total = refs[2 * pieces :]
    mask = lax.broadcasted_iota(jnp.int32, (BLK, 2 * HEAD_DIM), 1) < HEAD_DIM
    for slot in range(2):
        queries[slot] = stack_heads(q_ref[block_rows(slot), :] * HEAD_DIM**-0.5, mask)
    steps = block_steps(place_ref[0], pieces)
    peaks = [jnp.full((1, 2 * BLK), -1e30, wide)] * 2
    for step, (piece, slot, key_slot) in enumerate(steps):
        block = times(k_refs[piece][block_rows(key_slot), :], queries[slot], ROWS_BY_ROWS)
        scores[step] = block
        top = jnp.max(block, axis=0, keepdims=True)
        peaks = update_slot(peaks, slot, lambda held, top=top: jnp.maximum(held, top))
    total[...] = jnp.zeros_like(total)
    sums = [jnp.zeros((1, 2 * BLK), wide)] * 2
    for step, (piece, slot, key_slot) in enumerate(steps):
        weights = jnp.exp(scores[step] - pick_slot(peaks, slot))
        part = jnp.sum(weights, axis=0, keepdims=True)
        sums = update_slot(sums, slot, lambda held, part=part: held + part)
        weights = weights.astype(low_type)
        turned = v_refs[piece][block_rows(key_slot), :].T
        total[slot] = total[slot] + jnp.concatenate(
            [
                times(turned[:HEAD_DIM], weights[:, :BLK]),
                times(turned[HEAD_DIM:], weights[:, BLK:]),
            ],
            axis=0,
        )
    for slot in range(2):
        share = 1.0 / sums[slot]
        held = total[slot]
        held = jnp.concatenate(
            [held[:HEAD_DIM] * share[:, :BLK], held[HEAD_DIM:] * share[:, BLK:]], axis=0
        )
        o_ref[block_rows(slot), :] = held.T
        stat_ref[0, slot : slot + 1, :] = peaks[slot] + jnp.log(sums[slot])


def attend_backward_kernel(pieces, place_ref, q_ref, g_ref, o_ref, stat_ref, *refs):
    k_refs, v_refs = refs[:pieces], refs[pieces : 2 * pieces]
    dq_ref, dk_refs, dv_refs = refs[2 * pieces], refs[2 * pieces + 1 : 3 * pieces + 1], refs[3 * pieces + 1 : 4 * pieces + 1]
    queries, grads, key_sum, value_sum, query_sum, inner = refs[4 * pieces + 1 :]
    mask = lax.broadcasted_iota(jnp.int32, (BLK, 2 * HEAD_DIM), 1) < HEAD_DIM
    for slot in range(2):
        rows = block_rows(slot)
        queries[slot] = stack_heads(q_ref[rows, :] * HEAD_DIM**-0.5, mask)
        grad = g_ref[rows, :]
        grads[slot] = stack_heads(grad, mask)
        both = (grad.astype(wide) * o_ref[rows, :]).T
        inner[slot] = jnp.concatenate(
            [
                jnp.sum(both[:HEAD_DIM], axis=0, keepdims=True),
                jnp.sum(both[HEAD_DIM:], axis=0, keepdims=True),
            ],
            axis=1,
        )
    key_sum[...] = jnp.zeros_like(key_sum)
    value_sum[...] = jnp.zeros_like(value_sum)
    query_sum[...] = jnp.zeros_like(query_sum)
    for piece, slot, key_slot in block_steps(place_ref[0], pieces):
        at = block_rows(key_slot)
        keys, values = k_refs[piece][at, :], v_refs[piece][at, :]
        own, grad = queries[slot], grads[slot]
        probs = jnp.exp(times(keys, own, ROWS_BY_ROWS) - stat_ref[0, pl.ds(slot, 1), :])
        dscores = probs * (times(values, grad, ROWS_BY_ROWS) - inner[slot])
        dscores = dscores.astype(low_type)
        value_sum[piece, at, :] = value_sum[piece, at, :] + times(probs.astype(low_type), grad)
        key_sum[piece, at, :] = key_sum[piece, at, :] + times(dscores, own)
        turned = keys.T
        query_sum[slot] = query_sum[slot] + jnp.concatenate(
            [
                times(turned[:HEAD_DIM], dscores[:, :BLK]),
                times(turned[HEAD_DIM:], dscores[:, BLK:]),
            ],
            axis=0,
        )
    for slot in range(2):
        dq_ref[block_rows(slot), :] = (query_sum[slot].T * HEAD_DIM**-0.5).astype(low_type)
    for piece in range(pieces):
        dk_refs[piece][...] = key_sum[piece].astype(low_type)
        dv_refs[piece][...] = value_sum[piece].astype(low_type)


def attention_specs():
    own = pl.BlockSpec((2 * BLK, 2 * HEAD_DIM), lambda pair, place: (0, pair))
    stats = pl.BlockSpec((1, 2, 2 * BLK), lambda pair, place: (pair, 0, 0))
    return own, stats


def attend_forward(place, queries, keys, values):
    pieces, pairs = len(keys), queries.shape[1] // (2 * HEAD_DIM)
    own, stats = attention_specs()
    return pl.pallas_call(
        functools.partial(attend_forward_kernel, pieces),
        out_shape=(
            jax.ShapeDtypeStruct(queries.shape, wide),
            jax.ShapeDtypeStruct((pairs, 2, 2 * BLK), wide),
        ),
        grid_spec=pltpu.PrefetchScalarGridSpec(
            num_scalar_prefetch=1,
            grid=(pairs,),
            in_specs=[own] * (1 + 2 * pieces),
            out_specs=[own, stats],
            scratch_shapes=[
                pltpu.VMEM((2, 2 * BLK, 2 * HEAD_DIM), low_type),
                pltpu.VMEM((2 * pieces + 1, BLK, 2 * BLK), wide),
                pltpu.VMEM((2, 2 * HEAD_DIM, BLK), wide),
            ],
        ),
        compiler_params=pltpu.CompilerParams(vmem_limit_bytes=48 * 2**20),
        cost_estimate=pl.CostEstimate(flops=13 * MICROSECOND, bytes_accessed=0, transcendentals=0),
        name="attend_forward",
    )(place, queries, *keys, *values)


def attend_backward(place, queries, keys, values, grads, attended, stat):
    pieces, pairs = len(keys), queries.shape[1] // (2 * HEAD_DIM)
    own, stats = attention_specs()
    query_grad, *others = pl.pallas_call(
        functools.partial(attend_backward_kernel, pieces),
        out_shape=(jax.ShapeDtypeStruct(queries.shape, low_type),) * (1 + 2 * pieces),
        grid_spec=pltpu.PrefetchScalarGridSpec(
            num_scalar_prefetch=1,
            grid=(pairs,),
            in_specs=[own, own, own, stats] + [own] * (2 * pieces),
            out_specs=[own] * (1 + 2 * pieces),
            scratch_shapes=[
                pltpu.VMEM((2, 2 * BLK, 2 * HEAD_DIM), low_type),
                pltpu.VMEM((2, 2 * BLK, 2 * HEAD_DIM), low_type),
                pltpu.VMEM((pieces, 2 * BLK, 2 * HEAD_DIM), wide),
                pltpu.VMEM((pieces, 2 * BLK, 2 * HEAD_DIM), wide),
                pltpu.VMEM((2, 2 * HEAD_DIM, BLK), wide),
                pltpu.VMEM((2, 1, 2 * BLK), wide),
            ],
        ),
        compiler_params=pltpu.CompilerParams(vmem_limit_bytes=48 * 2**20),
        cost_estimate=pl.CostEstimate(flops=21 * MICROSECOND, bytes_accessed=0, transcendentals=0),
        name="attend_backward",
    )(place, queries, grads, attended, stat, *keys, *values)
    return query_grad, others[:pieces], others[pieces:]


def spread_tokens(pair, below, count):
    half = count // 2
    across = [(b, half + b if b < half else count - 1 - b) for b in range(count)]
    inside = [(b, half + count - 1 - b) for b in range(half, count)]
    got = lax.ppermute(jnp.where(below, pair[1], pair[0]), CTX, across)
    other = lax.ppermute(pair[1], CTX, inside)
    return jnp.concatenate(
        [jnp.where(below, pair[0], got), jnp.where(below, got, other)], axis=0
    )


def collect_tokens(rows, below, count):
    half = count // 2
    across = [(half + b if b < half else count - 1 - b, b) for b in range(count)]
    inside = [(half + count - 1 - b, b) for b in range(half, count)]
    early, late = rows[:BLK], rows[BLK:]
    got = lax.ppermute(jnp.where(below, late, early), CTX, across)
    other = lax.ppermute(late, CTX, inside)
    return jnp.stack([jnp.where(below, early, got), jnp.where(below, got, other)])


def collect_own(rows, below):
    mask = jnp.stack([below, jnp.zeros_like(below)])[:, None, None]
    return mask, jnp.stack([rows[:BLK], rows[:BLK]])


def ring_gather(rows, count):
    half = count // 2
    pieces = [rows]
    for step in range(1, half):
        pairs = [
            (side * half + b, side * half + (b + step) % half)
            for side in range(2)
            for b in range(half)
        ]
        pieces.append(lax.ppermute(rows, CTX, pairs))
    return pieces


def ring_scatter(pieces, count):
    half = count // 2
    arrived = []
    for step in range(1, half):
        pairs = [
            (side * half + b, side * half + (b - step) % half)
            for side in range(2)
            for b in range(half)
        ]
        arrived.append(lax.ppermute(pieces[step], CTX, pairs))
    return arrived


def add_up(members):
    return sum(member.astype(wide) for member in members).astype(low_type)


def ring_position(z):
    return jnp.where(z == 2, 3, jnp.where(z == 3, 2, z))


SWAP = [(0, 1), (1, 0)]
RING = [(z * 2 + x, after * 2 + x) for z, after in enumerate((1, 3, 0, 2)) for x in range(2)]
ACROSS_X = [(d, d ^ 1) for d in range(8)]


def along_z(rows):
    return lax.ppermute(rows, "dp", RING)


def along_x(rows):
    return lax.ppermute(rows, "dp", ACROSS_X)


def along_y(rows):
    return lax.ppermute(rows, "chip", SWAP)


def on_chip(rows):
    return lax.ppermute(rows, "core", SWAP)


def join(*members):
    return jnp.concatenate(members, axis=0)


def by_z(ring, first, rows, position):
    parts = [member[first : first + rows] for member in ring]
    placed = []
    for spot in (0, 1, 3, 2):
        step = lax.rem(position + 4 - spot, 4)
        chosen = parts[3]
        for index in (2, 1, 0):
            chosen = jnp.where(step == index, parts[index], chosen)
        placed.append(chosen)
    return jnp.stack(placed)


def z_halves(ring, position):
    size = ring[0].shape[0] // 2
    return [by_z(ring, part * size, size, position) for part in range(2)]


def cross(halves):
    return [along_x(halves[0]), along_y(halves[1])]


def cross_other(halves):
    return [along_y(halves[0]), along_x(halves[1])]


def paired(halves, crossed):
    return [jnp.stack([halves[part], crossed[part]]) for part in range(2)]


def swapped(members):
    return [on_chip(member) for member in members]


def linked_forward(
    first, second, chosen, tokens, cotangent, sizes, at, below, count, kept, attention_step, output_step, feed_step
):
    position = at[0]

    def gather(rows):
        whole = lax.all_gather(rows, EVERY, axis=0)
        return whole.reshape(4, 2, 2, 2, *rows.shape)

    v = Bag()
    v.f, v.g, v.h = [first[:128]], [second[:128]], [second[128:256]]
    first_feed, second_reduce = gather(first[128:]), gather(second[256:])

    def advance(ring):
        ring.append(along_z(ring[-1]))

    def mix(near, far):
        return near[0], far[0], near[1], far[1]

    def weights_f():
        return mix(v.f_near, v.f_far) + mix(v.f_near_other, v.f_far_other)

    def weights_g():
        return mix(v.g_near, v.g_far) + mix(v.g_near_other, v.g_far_other)

    def weights_h():
        return mix(v.h_near, v.h_far) + mix(v.h_near_other, v.h_far_other)

    for _ in range(3):
        advance(v.f)
    v.tokens = spread_tokens(tokens, below, count)
    v.chosen = chosen
    v = sync(v)
    v.f_half = z_halves(v.f, position)
    del v.f
    v.f_cross = cross(v.f_half)
    v.factors = lax.all_to_all(v.chosen, LANE, split_axis=0, concat_axis=0, tiled=True)
    del v.chosen
    advance(v.g)
    v = sync(v)
    v.f_near = paired(v.f_half, v.f_cross)
    del v.f_half, v.f_cross
    v.f_far = cross_other(v.f_near)
    v.f_near_other = swapped(v.f_near)
    v.factors_other = on_chip(v.factors)
    advance(v.g)
    advance(v.g)
    v = sync(v)
    v.g_half = z_halves(v.g, position)
    del v.g
    v.g_cross = cross(v.g_half)
    v.f_far_other = swapped(v.f_far)
    v.picked = unpack_factors(at, v.factors, v.factors_other, sizes)
    del v.factors, v.factors_other
    advance(v.h)
    v = sync(v)
    v.g_near = paired(v.g_half, v.g_cross)
    del v.g_half, v.g_cross
    v.g_far = cross_other(v.g_near)
    v.g_near_other = swapped(v.g_near)
    advance(v.h)
    advance(v.h)
    v.current = v.tokens.astype(wide)
    del v.tokens
    v.cotangent = spread_tokens(cotangent, below, count)
    attention_step(v.current, (PIECES, weights_f()), v.picked[0], 0)
    v.middle = output_step(v.current, (PIECES, weights_f()), v.picked[0], 0)
    del v.current
    v.kept = kept
    v = sync(v)
    kept[:] = v.kept
    v.h_half = z_halves(v.h, position)
    del v.h
    v.h_cross = cross(v.h_half)
    v.g_far_other = swapped(v.g_far)
    v.current = feed_step(v.middle, (GATHERED, (first_feed,)), v.picked[0], 0)
    v.kept = kept
    v = sync(v)
    kept[:] = v.kept
    v.h_near = paired(v.h_half, v.h_cross)
    del v.h_half, v.h_cross
    v.h_far = cross_other(v.h_near)
    v.h_near_other = swapped(v.h_near)
    attention_step(v.current, (PIECES, weights_g()), v.picked[1], 1)
    v.middle = output_step(v.current, (PIECES, weights_g()), v.picked[1], 1)
    del v.current
    v.kept = kept
    v = sync(v)
    kept[:] = v.kept
    v.h_far_other = swapped(v.h_far)
    frozen = [
        ((PIECES, weights_f()), (GATHERED, (first_feed,))),
        ((PIECES, weights_g()), (MIXED, (*weights_h(), second_reduce))),
    ]
    current = feed_step(v.middle, frozen[1][1], v.picked[1], 1)
    return current, v.cotangent.astype(wide), v.picked, frozen


SQUARE = (4, 2, 2, 2, 32, 1024)
TALL = (4, 2, 2, 2, 128, 1024)


def square_unit(form, part):
    return part if form == WHOLE else (part // 2, part % 2 * 32)


def expand_unit(form, part):
    return {WHOLE: part, GATHERED: 32 * part}.get(form, (part // 2, part % 2 * 32))


def fetch(form, at_ref, sources, unit, rows, held, arrived, by_quarter=None):
    spread_z = slice(None) if by_quarter is None else by_quarter
    if not isinstance(unit, tuple):
        if form == WHOLE:
            source = sources[unit].at[spread_z]
        else:
            source = sources[-1].at[(spread_z, *[slice(None)] * 3, pl.ds(unit, rows), slice(None))]
        pltpu.make_async_copy(source, held.at[spread_z], arrived).start()
        return
    part, first = unit
    x, y, core = at_ref[1], at_ref[2], at_ref[3]
    for other in range(2):
        for far in range(2):
            source = sources[other * 4 + part * 2 + far]
            for over in range(2):
                over_x, over_y = (over, far) if part == 0 else (far, over)
                pltpu.make_async_copy(
                    source.at[over, spread_z, pl.ds(first, rows), :],
                    held.at[
                        spread_z,
                        lax.rem(x + over_x, 2),
                        lax.rem(y + over_y, 2),
                        lax.rem(core + other, 2),
                    ],
                    arrived,
                ).start()


def wait_for(held, arrived):
    pltpu.make_async_copy(held, held, arrived).wait()


def square(held):
    return held[...].reshape(1024, 1024)


TILE = 256
STRIP = 32
COLUMNS = 1024


def strips(count, body):
    def step(index, carry):
        body(pl.ds(pl.multiple_of(index * STRIP, STRIP), STRIP))
        return carry

    lax.fori_loop(0, count // STRIP, step, 0)


def normalize_rows(values, gain, shift):
    center = jnp.mean(values, axis=-1, keepdims=True)
    spread = values - center
    scale = lax.rsqrt(jnp.mean(spread * spread, axis=-1, keepdims=True) + epsilon)
    unit = spread * scale
    return unit, scale, unit * gain + shift


def normalize_pull(grad, unit, scale, gain):
    scaled = grad * gain
    first = jnp.mean(scaled, axis=-1, keepdims=True)
    second = jnp.mean(scaled * unit, axis=-1, keepdims=True)
    return scale * (scaled - first - unit * second)


def qkv_kernel(form, at_ref, x_ref, gain_ref, shift_ref, left_ref, right_ref, bias_ref, *refs):
    sources, (normed_ref, unit_ref, scale_ref, rank_ref, *outs) = refs[:-9], refs[-9:-2]
    held, arrived = refs[-2:]
    for part in range(3):
        fetch(form, at_ref, sources, square_unit(form, part), 32, held.at[part], arrived.at[part])

    def norm(rows):
        unit, scale, normed = normalize_rows(x_ref[rows, :], gain_ref[...], shift_ref[...])
        normed_ref[rows, :] = normed.astype(low_type)
        unit_ref[rows, :] = unit.astype(low_type)
        scale_ref[rows, :] = jnp.broadcast_to(scale, (STRIP, 128))

    strips(x_ref.shape[0], norm)
    rank_ref[...] = times(normed_ref[...], left_ref[...], ROWS_BY_ROWS).astype(low_type)
    for part, out in enumerate(outs):
        wait_for(held.at[part], arrived.at[part])
        columns = slice(part * COLUMNS, (part + 1) * COLUMNS)
        for first in range(0, x_ref.shape[0], TILE):
            rows = slice(first, first + TILE)
            out[rows, :] = (
                times(normed_ref[rows, :], square(held.at[part]))
                + times(rank_ref[rows, :], right_ref[:, columns])
                + bias_ref[:, columns]
            ).astype(low_type)


def output_kernel(form, at_ref, x_ref, attended_ref, left_ref, right_ref, bias_ref, gain_ref, shift_ref, *refs):
    sources, (low_ref, middle_ref, normed_ref, unit_ref, scale_ref, rank_ref) = refs[:-8], refs[-8:-2]
    held, arrived = refs[-2:]
    fetch(form, at_ref, sources, square_unit(form, 3), 32, held, arrived)
    low_ref[...] = attended_ref[...].astype(low_type)
    rank_ref[...] = times(low_ref[...], left_ref[...], ROWS_BY_ROWS).astype(low_type)
    wait_for(held, arrived)
    for first in range(0, x_ref.shape[0], TILE):
        rows = slice(first, first + TILE)
        middle_ref[rows, :] = (
            x_ref[rows, :]
            + times(low_ref[rows, :], square(held))
            + times(rank_ref[rows, :], right_ref[...])
            + bias_ref[...]
        )

    def norm(rows):
        unit, scale, normed = normalize_rows(middle_ref[rows, :], gain_ref[...], shift_ref[...])
        normed_ref[rows, :] = normed.astype(low_type)
        unit_ref[rows, :] = unit.astype(low_type)
        scale_ref[rows, :] = jnp.broadcast_to(scale, (STRIP, 128))

    strips(x_ref.shape[0], norm)


def fetch_feed_forward(form, at_ref, sources, expand, reduce, arrived, reduce_first):
    for part in range(4):
        jobs = [
            (expand_unit(form, part), 32, expand.at[part], arrived.at[0, part], None),
            ({WHOLE: 4, GATHERED: 128, MIXED: 0}[form], 128, reduce, arrived.at[1, part], part),
        ]
        for unit, rows, held, semaphore, quarter in jobs[::-1] if reduce_first else jobs:
            fetch(form, at_ref, sources, unit, rows, held, semaphore, quarter)


def feed_forward_kernel(
    form, at_ref, normed_ref, middle_ref, expand_left_ref, expand_right_ref, expand_bias_ref,
    reduce_left_ref, reduce_right_ref, reduce_bias_ref, *refs,
):
    sources, (result_ref, slope_ref, active_ref, rank_expand_ref, rank_reduce_ref) = refs[:-9], refs[-9:-4]
    expand, reduce, rank_sum, arrived = refs[-4:]
    fetch_feed_forward(form, at_ref, sources, expand, reduce, arrived, False)
    count = normed_ref.shape[0]
    rank_expand_ref[...] = times(normed_ref[...], expand_left_ref[...], ROWS_BY_ROWS).astype(low_type)
    result_ref[...] = middle_ref[...] + reduce_bias_ref[...]
    rank_sum[...] = jnp.zeros_like(rank_sum)

    def part_step(part, carry):
        columns = pl.ds(pl.multiple_of(part * COLUMNS, COLUMNS), COLUMNS)
        wait_for(expand.at[part], arrived.at[0, part])
        wait_for(reduce.at[part], arrived.at[1, part])
        for first in range(0, count, TILE):
            rows = slice(first, first + TILE)
            value = (
                times(normed_ref[rows, :], square(expand.at[part]))
                + times(rank_expand_ref[rows, :], expand_right_ref[:, columns])
                + expand_bias_ref[:, columns]
            )
            squared = value * value
            bent = jnp.tanh(root_factor * value * (1.0 + 0.044715 * squared))
            half = 0.5 * (1.0 + bent)
            slope_ref[rows, columns] = (
                half
                + 0.5 * value * (1.0 - bent * bent) * (root_factor + 3 * 0.044715 * root_factor * squared)
            ).astype(low_type)
            active = (value * half).astype(low_type)
            active_ref[rows, columns] = active
            result_ref[rows, :] = result_ref[rows, :] + times(active, square(reduce.at[part]))
            rank_sum[rows, :] = rank_sum[rows, :] + times(
                active, reduce_left_ref[:, columns], ROWS_BY_ROWS
            )
        return carry

    lax.fori_loop(0, 4, part_step, 0)
    rank_reduce_ref[...] = rank_sum[...].astype(low_type)
    result_ref[...] = result_ref[...] + times(rank_reduce_ref[...], reduce_right_ref[...])


def feed_backward_kernel(
    form, at_ref, grad_ref, slope_ref, active_ref, normed_ref, unit_ref, scale_ref, rank_expand_ref, rank_reduce_ref,
    gain_ref, expand_left_ref, expand_right_ref, reduce_left_ref, reduce_right_ref, *refs,
):
    sources, (out_ref, expand_left_g, expand_right_g, reduce_left_g, reduce_right_g) = refs[:-13], refs[-13:-8]
    expand, reduce, arrived, low_grad, turned, bent, total, turn_sum = refs[-8:]
    fetch_feed_forward(form, at_ref, sources, expand, reduce, arrived, True)
    count = grad_ref.shape[0]
    low_grad[...] = grad_ref[...].astype(low_type)
    turned[...] = times(low_grad[...], reduce_right_ref[...], ROWS_BY_ROWS).astype(low_type)
    reduce_right_g[...] = times(rank_reduce_ref[...], low_grad[...], COLS_BY_COLS).astype(low_type)
    total[...] = jnp.zeros_like(total)
    turn_sum[...] = jnp.zeros_like(turn_sum)

    def part_step(part, carry):
        columns = pl.ds(pl.multiple_of(part * COLUMNS, COLUMNS), COLUMNS)
        wait_for(reduce.at[part], arrived.at[1, part])
        wait_for(expand.at[part], arrived.at[0, part])
        for first in range(0, count, TILE):
            rows = slice(first, first + TILE)
            grad_active = times(low_grad[rows, :], square(reduce.at[part]), ROWS_BY_ROWS) + times(
                turned[rows, :], reduce_left_ref[:, columns]
            )
            grad_expand = (grad_active * slope_ref[rows, columns].astype(wide)).astype(low_type)
            bent[rows, :] = grad_expand
            total[rows, :] = total[rows, :] + times(grad_expand, square(expand.at[part]), ROWS_BY_ROWS)
            turn_sum[rows, :] = turn_sum[rows, :] + times(
                grad_expand, expand_right_ref[:, columns], ROWS_BY_ROWS
            )
        reduce_left_g[:, columns] = times(turned[...], active_ref[:, columns], COLS_BY_COLS).astype(
            low_type
        )
        expand_right_g[:, columns] = times(rank_expand_ref[...], bent[...], COLS_BY_COLS).astype(low_type)
        return carry

    lax.fori_loop(0, 4, part_step, 0)
    turned[...] = turn_sum[...].astype(low_type)
    expand_left_g[...] = times(turned[...], normed_ref[...], COLS_BY_COLS).astype(low_type)
    total[...] = total[...] + times(turned[...], expand_left_ref[...])

    def pull(rows):
        out_ref[rows, :] = grad_ref[rows, :] + normalize_pull(
            total[rows, :], unit_ref[rows, :].astype(wide), scale_ref[rows, :1], gain_ref[...]
        )

    strips(count, pull)


def output_backward_kernel(form, at_ref, grad_ref, attended_ref, rank_ref, left_ref, right_ref, *refs):
    sources, (out_ref, left_g, right_g) = refs[:-7], refs[-7:-4]
    held, arrived, low_grad, turned = refs[-4:]
    fetch(form, at_ref, sources, square_unit(form, 3), 32, held, arrived)
    low_grad[...] = grad_ref[...].astype(low_type)
    turned[...] = times(low_grad[...], right_ref[...], ROWS_BY_ROWS).astype(low_type)
    right_g[...] = times(rank_ref[...], low_grad[...], COLS_BY_COLS).astype(low_type)
    left_g[...] = times(turned[...], attended_ref[...], COLS_BY_COLS).astype(low_type)
    wait_for(held, arrived)
    for first in range(0, grad_ref.shape[0], TILE):
        rows = slice(first, first + TILE)
        out_ref[rows, :] = (
            times(low_grad[rows, :], square(held), ROWS_BY_ROWS) + times(turned[rows, :], left_ref[...])
        ).astype(low_type)


def qkv_backward_kernel(
    pieces, form, at_ref, grad_ref, normed_ref, unit_ref, scale_ref, rank_ref, gain_ref, left_ref, right_ref, dq_ref, *refs
):
    dk_refs, dv_refs, refs = refs[:pieces], refs[pieces : 2 * pieces], refs[2 * pieces :]
    sources, (out_ref, left_g, right_g) = refs[:-9], refs[-9:-6]
    held, arrived, turned, total, dk_ref, dv_ref = refs[-6:]
    count = grad_ref.shape[0]
    for part in range(3):
        fetch(form, at_ref, sources, square_unit(form, part), 32, held.at[part], arrived.at[part])
    dk_ref[...] = add_up([member[...] for member in dk_refs])
    dv_ref[...] = add_up([member[...] for member in dv_refs])
    grads = (dq_ref, dk_ref, dv_ref)
    spans = [slice(part * COLUMNS, (part + 1) * COLUMNS) for part in range(3)]
    turned[...] = sum(
        times(grads[part][...], right_ref[:, spans[part]], ROWS_BY_ROWS) for part in range(3)
    ).astype(low_type)
    for part in range(3):
        right_g[:, spans[part]] = times(rank_ref[...], grads[part][...], COLS_BY_COLS).astype(low_type)
    left_g[...] = times(turned[...], normed_ref[...], COLS_BY_COLS).astype(low_type)
    for part in range(3):
        wait_for(held.at[part], arrived.at[part])
        for first in range(0, count, TILE):
            rows = slice(first, first + TILE)
            value = times(grads[part][rows, :], square(held.at[part]), ROWS_BY_ROWS)
            if part == 0:
                total[rows, :] = value + times(turned[rows, :], left_ref[...])
            else:
                total[rows, :] = total[rows, :] + value

    def pull(rows):
        out_ref[rows, :] = grad_ref[rows, :] + normalize_pull(
            total[rows, :], unit_ref[rows, :].astype(wide), scale_ref[rows, :1], gain_ref[...]
        )

    strips(count, pull)


def frozen_call(kernel, name, at, weights, members, outs, scratch, cost):
    form, sources = weights
    local_spec = pl.BlockSpec(memory_space=pltpu.VMEM)
    return pl.pallas_call(
        functools.partial(kernel, form),
        out_shape=tuple(jax.ShapeDtypeStruct(shape, kind) for shape, kind in outs),
        in_specs=[pl.BlockSpec(memory_space=pltpu.SMEM)]
        + [local_spec] * len(members)
        + [pl.BlockSpec(memory_space=pl.ANY)] * len(sources),
        out_specs=(local_spec,) * len(outs),
        scratch_shapes=scratch,
        compiler_params=pltpu.CompilerParams(vmem_limit_bytes=56 * 2**20),
        cost_estimate=pl.CostEstimate(flops=cost * MICROSECOND, bytes_accessed=0, transcendentals=0),
        name=name,
    )(at, *members, *sources)


def row(vector):
    return vector.reshape(1, -1)


DMA = pltpu.SemaphoreType.DMA


PACKED = ((5, 0), (6, 128), (1, 256), (0, 352), (2, 384), (3, 416), (4, 448), (7, 480))
PACKED_EARLY = ((5, 0), (6, 128), (2, 256), (3, 288), (4, 320), (7, 352))
PACKED_LATE = ((1, 0), (0, 96))


def unpack_kernel(order, at_ref, own_ref, other_ref, *outs):
    layers, groups = own_ref.shape[1], own_ref.shape[0] // 2
    swapped = at_ref[3] == 1
    for layer_index in range(layers):
        for group in range(groups):
            lanes = []
            for chip in range(2):
                own = own_ref[group * 2 + chip, layer_index]
                other = other_ref[group * 2 + chip, layer_index]
                lanes += [jnp.where(swapped, other, own), jnp.where(swapped, own, other)]
            for kind, first in order:
                out = outs[layer_index * len(order) + kind]
                size = out.shape[1] // (4 * groups)
                out[:, group * 4 * size : (group + 1) * 4 * size] = jnp.concatenate(
                    [lane[:, first : first + size] for lane in lanes], axis=1
                )


def unpack_factors(at, own, other, sizes):
    lanes, layers = own.shape[:2]
    local_spec = pl.BlockSpec(memory_space=pltpu.VMEM)
    found = pl.pallas_call(
        functools.partial(unpack_kernel, PACKED),
        out_shape=tuple(
            jax.ShapeDtypeStruct((RANK, size * lanes * 2), low_type) for _ in range(layers) for size in sizes
        ),
        in_specs=[pl.BlockSpec(memory_space=pltpu.SMEM), local_spec, local_spec],
        out_specs=(local_spec,) * (layers * len(sizes)),
        compiler_params=pltpu.CompilerParams(vmem_limit_bytes=32 * 2**20),
        cost_estimate=pl.CostEstimate(flops=4 * MICROSECOND, bytes_accessed=0, transcendentals=0),
        name="unpack_factors",
    )(at, own, other)
    return [found[layer * len(sizes) : (layer + 1) * len(sizes)] for layer in range(layers)]


def pack_kernel(orders, at_ref, *refs):
    members, out_ref = refs[:-1], refs[-1]
    core, base, offset = at_ref[3], 0, 0
    for order in orders:
        for lane_chip in range(out_ref.shape[1]):
            for owner_core in range(2):
                owner = lane_chip * 2 + owner_core
                parts = []
                for index, _ in enumerate(order):
                    member = members[base + index]
                    size = member.shape[1] // (2 * out_ref.shape[1])
                    parts.append(member[:, owner * size : (owner + 1) * size])
                joined = jnp.concatenate(parts, axis=1)
                out_ref[lax.rem(owner_core + core, 2), lane_chip, :, offset : offset + joined.shape[1]] = joined
        base += len(order)
        offset += joined.shape[1]


def pack_gradients(at, groups, lanes):
    members, width = [], 0
    for order, terms in groups:
        members += [terms[kind] for kind, _ in order]
        width += sum(terms[kind].shape[1] for kind, _ in order) // (2 * lanes)
    local_spec = pl.BlockSpec(memory_space=pltpu.VMEM)
    return pl.pallas_call(
        functools.partial(pack_kernel, [order for order, _ in groups]),
        out_shape=jax.ShapeDtypeStruct((2, lanes, RANK, width), low_type),
        in_specs=[pl.BlockSpec(memory_space=pltpu.SMEM)] + [local_spec] * len(members),
        out_specs=local_spec,
        compiler_params=pltpu.CompilerParams(vmem_limit_bytes=32 * 2**20),
        cost_estimate=pl.CostEstimate(flops=4 * MICROSECOND, bytes_accessed=0, transcendentals=0),
        name="pack_gradients",
    )(at, *members)


LOW, WIDE = low_type, wide


def forward_qkv(current, weights, picked, extras, at):
    rows, columns = current.shape
    full_low = ((rows, columns), LOW)
    bias = jnp.concatenate([extras[0][:columns], jnp.zeros((columns,), WIDE), extras[0][columns:]])
    return frozen_call(
        qkv_kernel, "qkv_forward", at, weights,
        (current, row(extras[4]), row(extras[5]), picked[0], picked[1], row(bias)),
        (full_low, full_low, ((rows, 128), WIDE), ((rows, RANK), LOW), full_low, full_low, full_low),
        [pltpu.VMEM((3, *SQUARE), LOW), DMA((3,))], 9,
    )


def forward_output(current, attended, weights, picked, extras, at):
    rows, columns = current.shape
    full, full_low = ((rows, columns), WIDE), ((rows, columns), LOW)
    return frozen_call(
        output_kernel, "output_forward", at, weights,
        (current, attended, picked[2], picked[3], row(extras[1]), row(extras[6]), row(extras[7])),
        (full_low, full, full_low, full_low, ((rows, 128), WIDE), ((rows, RANK), LOW)),
        [pltpu.VMEM(SQUARE, LOW), DMA], 8,
    )


def forward_feed(normed, middle, weights, picked, extras, at):
    rows, columns = middle.shape
    tall, ranks = ((rows, picked[5].shape[1]), LOW), ((rows, RANK), LOW)
    return frozen_call(
        feed_forward_kernel, "feed_forward", at, weights,
        (normed, middle, picked[4], picked[5], row(extras[2]), picked[6], picked[7], row(extras[3])),
        (((rows, columns), WIDE), tall, tall, ranks, ranks),
        [
            pltpu.VMEM((4, *SQUARE), LOW), pltpu.VMEM(TALL, LOW), pltpu.VMEM((rows, RANK), WIDE), DMA((2, 4)),
        ], 20,
    )


def like(member):
    return (member.shape, LOW)


def backward_feed(grad, kept, weights, picked, extras, at):
    rows, columns = grad.shape
    full_low, ranks = pltpu.VMEM((rows, columns), LOW), pltpu.VMEM((rows, RANK), LOW)
    return frozen_call(
        feed_backward_kernel, "feed_backward", at, weights,
        (
            grad, kept.slope, kept.active, kept.normed_two, kept.unit_two, kept.scale_two,
            kept.rank_expand, kept.rank_reduce, row(extras[6]), *picked[4:],
        ),
        (((rows, columns), WIDE), *map(like, picked[4:])),
        [
            pltpu.VMEM((4, *SQUARE), LOW), pltpu.VMEM(TALL, LOW), DMA((2, 4)), full_low, ranks, full_low,
            pltpu.VMEM((rows, columns), WIDE), pltpu.VMEM((rows, RANK), WIDE),
        ], 22,
    )


def backward_output(grad, kept, weights, picked, at):
    rows, columns = grad.shape
    return frozen_call(
        output_backward_kernel, "output_backward", at, weights,
        (grad, kept.attended_low, kept.rank_output, picked[2], picked[3]),
        (((rows, columns), LOW), like(picked[2]), like(picked[3])),
        [pltpu.VMEM(SQUARE, LOW), DMA, pltpu.VMEM((rows, columns), LOW), pltpu.VMEM((rows, RANK), LOW)], 5,
    )


def backward_qkv(grad, grads, kept, weights, picked, extras, at):
    rows, columns = grad.shape
    query_grad, key_grads, value_grads = grads
    return frozen_call(
        functools.partial(qkv_backward_kernel, len(key_grads)), "qkv_backward", at, weights,
        (
            grad, kept.normed_one, kept.unit_one, kept.scale_one, kept.rank_attend, row(extras[4]),
            picked[0], picked[1], query_grad, *key_grads, *value_grads,
        ),
        (((rows, columns), WIDE), like(picked[0]), like(picked[1])),
        [
            pltpu.VMEM((3, *SQUARE), LOW), DMA((3,)), pltpu.VMEM((rows, RANK), LOW),
            pltpu.VMEM((rows, columns), WIDE), pltpu.VMEM((rows, columns), LOW), pltpu.VMEM((rows, columns), LOW),
        ], 11,
    )


class Bag:
    pass


def open_bag(bag):
    names = tuple(sorted(vars(bag)))
    return tuple(getattr(bag, name) for name in names), names


def close_bag(names, members):
    bag = Bag()
    for name, member in zip(names, members):
        setattr(bag, name, member)
    return bag


jax.tree_util.register_pytree_node(Bag, open_bag, close_bag)


def sync(values):
    leaves, shape = jax.tree.flatten(values)
    return jax.tree.unflatten(shape, lax.optimization_barrier(tuple(leaves)))


def local(
    tokens, cotangent, adapter_ids, attend_weight, output_weight, expand_weight, reduce_weight,
    attend_bias, output_bias, expand_bias, reduce_bias, first_gain, first_shift, second_gain, second_shift,
    *adapters,
):
    data_count, chips = lax.axis_size("dp"), lax.axis_size("chip")
    count = chips * lax.axis_size("core")
    half = count // 2
    devices = data_count * count
    data_rank, core = lax.axis_index("dp"), lax.axis_index("core")
    rank = lax.axis_index("chip") * 2 + core
    below = rank < half
    place = jnp.reshape(lax.rem(rank, half), (1,)).astype(jnp.int32)
    columns = tokens.shape[2]
    linked = (data_count, chips, columns) == (8, 2, 1024)

    lane_chip = jnp.arange(data_count * chips, dtype=jnp.int32)
    lane_sequence = (lane_chip // chips) * 2 + (lane_chip % chips) // (chips // 2)
    lane_adapter = jnp.take(adapter_ids, lane_sequence)

    sizes = [member.shape[2] for member in adapters]
    packed = jnp.concatenate([jnp.swapaxes(adapters[kind], 2, 3) for kind, _ in PACKED], axis=3)
    chosen = jnp.moveaxis(jnp.take(packed, lane_adapter, axis=1), 1, 0)

    def shards(layer_index):
        lists = [attend_weight[layer_index], output_weight[layer_index], expand_weight[layer_index]]
        blocks = [
            member[:, first : first + columns]
            for member in lists
            for first in range(0, member.shape[1], columns)
        ]
        return jnp.concatenate(blocks + [reduce_weight[layer_index]], axis=0)

    extras = [
        tuple(
            member[layer_index]
            for member in (
                attend_bias, output_bias, expand_bias, reduce_bias,
                first_gain, first_shift, second_gain, second_shift,
            )
        )
        for layer_index in range(LAYERS)
    ]
    position = ring_position(data_rank // 2)
    at = jnp.stack([position, data_rank % 2, lax.axis_index("chip"), core]).astype(jnp.int32)
    kept = [Bag(), Bag()]

    def attention_step(current, weights, picked, layer_index):
        keep = kept[layer_index]
        (
            keep.normed_one, keep.unit_one, keep.scale_one, keep.rank_attend,
            keep.queries, keys, values,
        ) = forward_qkv(current, weights, picked, extras[layer_index], at)
        keep.keys, keep.values = ring_gather(keys, count), ring_gather(values, count)
        keep.attended, keep.stat = attend_forward(place, keep.queries, keep.keys, keep.values)

    def output_step(current, weights, picked, layer_index):
        keep = kept[layer_index]
        (
            keep.attended_low, middle, keep.normed_two, keep.unit_two, keep.scale_two,
            keep.rank_output,
        ) = forward_output(current, keep.attended, weights, picked, extras[layer_index], at)
        return middle

    def feed_step(middle, weights, picked, layer_index):
        keep = kept[layer_index]
        result, keep.slope, keep.active, keep.rank_expand, keep.rank_reduce = forward_feed(
            keep.normed_two, middle, weights, picked, extras[layer_index], at
        )
        return result

    if linked:
        first, second = shards(0), shards(1)
        current, grad_current, picked, frozen = linked_forward(
            first, second, chosen, tokens, cotangent, sizes, at, below, count, kept,
            attention_step, output_step, feed_step,
        )
    else:
        current = spread_tokens(tokens, below, count).astype(wide)
        grad_current = spread_tokens(cotangent, below, count).astype(wide)
        mine = lax.all_to_all(chosen, LANE, split_axis=0, concat_axis=0, tiled=True)
        theirs = lax.ppermute(mine, "core", SWAP)
        both = jnp.stack(
            [jnp.where(core == 0, mine, theirs), jnp.where(core == 0, theirs, mine)], axis=1
        )
        places, spot = {}, 0
        for kind, _ in PACKED:
            places[kind] = spot
            spot += sizes[kind]
        picked = [
            tuple(
                jnp.transpose(
                    both[:, :, layer_index, :, places[kind] : places[kind] + size], (2, 0, 1, 3)
                ).reshape(RANK, devices * size)
                for kind, size in enumerate(sizes)
            )
            for layer_index in range(LAYERS)
        ]
        frozen = []
        for layer_index in range(LAYERS):
            whole = lax.all_gather(shards(layer_index), EVERY, axis=0)
            size = columns // devices
            squares = [whole[:, part * size : (part + 1) * size, :].reshape(SQUARE) for part in range(8)]
            tall = whole[:, 8 * size :, :].reshape(TALL)
            frozen.append(((WHOLE, tuple(squares[:4])), (WHOLE, (*squares[4:], tall))))
            first_weights, second_weights = frozen[layer_index]
            attention_step(current, first_weights, picked[layer_index], layer_index)
            middle = output_step(current, first_weights, picked[layer_index], layer_index)
            current = feed_step(middle, second_weights, picked[layer_index], layer_index)

    outputs = collect_tokens(current.astype(low_type), below, count)
    owner_adapter = (lane_adapter[:, None] == jnp.arange(ADAPTERS)[None, :]).astype(wide)
    lanes = data_count * chips

    def to_owners(groups):
        if linked:
            both = pack_gradients(at, groups, lanes)
            own, sent = both[0], both[1]
        else:
            both = jnp.concatenate(
                [
                    jnp.transpose(
                        terms[kind].reshape(RANK, lanes, 2, sizes[kind]), (2, 1, 0, 3)
                    )
                    for order, terms in groups
                    for kind, _ in order
                ],
                axis=3,
            )
            own, sent = jnp.where(core == 0, both[0], both[1]), jnp.where(core == 0, both[1], both[0])
        total = add_up([own, lax.ppermute(sent, "core", SWAP)])
        received = lax.all_to_all(total, LANE, split_axis=0, concat_axis=0, tiled=True)
        return jnp.einsum(
            "sa,srp->arp", owner_adapter, received.astype(wide), precision=lax.Precision.HIGHEST
        )

    terms = [None] * LAYERS
    summed = []
    for layer_index in reversed(range(LAYERS)):
        keep, extra, factors = kept[layer_index], extras[layer_index], picked[layer_index]
        first_weights, second_weights = frozen[layer_index]
        middle_grad, *feed_terms = backward_feed(grad_current, keep, second_weights, factors, extra, at)
        attended_grad, *output_terms = backward_output(middle_grad, keep, first_weights, factors, at)
        if layer_index == 0:
            terms[0] = [None, None, *output_terms, *feed_terms]
            summed.append(to_owners([(PACKED, terms[1]), (PACKED_EARLY, terms[0])]))
        query_grad, key_grads, value_grads = attend_backward(
            place, keep.queries, keep.keys, keep.values, attended_grad, keep.attended, keep.stat
        )
        grads = (
            query_grad,
            [key_grads[0], *ring_scatter(key_grads, count)],
            [value_grads[0], *ring_scatter(value_grads, count)],
        )
        grad_current, *attend_terms = backward_qkv(
            middle_grad, grads, keep, first_weights, factors, extra, at
        )
        terms[layer_index] = [*attend_terms, *output_terms, *feed_terms]
    summed.append(to_owners([(PACKED_LATE, terms[0])]))
    found = [[None] * len(sizes) for _ in range(LAYERS)]
    for held, orders in zip(summed, (((1, PACKED), (0, PACKED_EARLY)), ((0, PACKED_LATE),))):
        spot = 0
        for layer_index, order in orders:
            for kind, _ in order:
                found[layer_index][kind] = held[:, :, spot : spot + sizes[kind]]
                spot += sizes[kind]
    results = [
        jnp.swapaxes(jnp.stack([found[layer_index][kind] for layer_index in range(LAYERS)]), 2, 3)
        for kind in range(len(sizes))
    ]
    moved = collect_tokens(grad_current.astype(low_type), below, count)
    kept_part = collect_own(grad_current, below)
    return (outputs, jnp.where(kept_part[0], kept_part[1], moved.astype(wide)), *results)


def solution(mesh):
    count = mesh.shape["ctx"]
    inner = Mesh(mesh.devices.reshape(mesh.shape["dp"], count // 2, 2), EVERY)
    token_spec, factor_spec = P("dp", CTX, None), P(None, None, EVERY, None)
    in_specs = (
        (token_spec,) * 2 + (P(),) + (P(None, EVERY, None),) * 4 + (P(),) * 8 + (factor_spec,) * 8
    )
    out_specs = (token_spec,) * 2 + (factor_spec,) * 8
    return jax.shard_map(local, mesh=inner, in_specs=in_specs, out_specs=out_specs, check_vma=False)
```

time: 640 us -> 524 us (0.82)
  local copies, waits for them, and re-layouts: 103 us -> 40.7 us
  other arithmetic: 58.6 us -> 31.7 us
  waiting for transfers between devices: 139 us -> 116 us
  between operations: 2.77 us -> 16.1 us
  starting transfers between devices: 76.5 us -> 65.4 us
    reshape x48 -> x0, local copies, waits for them, and re-layouts: 31.6 us -> none  [the longest x16 17.9 us: factors(): jnp.transpose(part, (2, 0, 1, 3)).reshape(RANK, devices * size)]
    ppermute x2, waiting for transfers between devices: 29.4 us -> 0.01 us  [collect_tokens(): got = lax.ppermute(jnp.where(below, late, early), CTX, across)]
    ppermute x8 -> x6, waiting for transfers between devices: 21.2 us -> 7.6 us  [along_y(): return lax.ppermute(rows, 'chip', SWAP)]
    transpose x16 -> x0, local copies, waits for them, and re-layouts: 12.4 us -> none  [factors(): jnp.transpose(part, (2, 0, 1, 3)).reshape(RANK, devices * size)]
    all_to_all x3, waiting for transfers between devices: 6.64 us -> 17.5 us  [the longest x2 17.5 us: to_owners(): lax.all_to_all(total, LANE, split_axis=0, concat_axis=0, tiled=True)]
    ppermute x12 -> x9, waiting for transfers between devices: 75.3 us -> 65 us  [along_z(): return lax.ppermute(rows, 'dp', RING)]
    concatenate x9 -> x2, local copies, waits for them, and re-layouts: 11.4 us -> 1.26 us  [the longest x1 1.06 us: shards(): return jnp.concatenate(blocks + [reduce_weight[layer_index]], axis=0)]
    select_n x8 -> x1, other arithmetic: 11.6 us -> 1.7 us  [local(): jnp.where(kept_part[0], kept_part[1], moved.astype(wide))]
  transfers between devices with their start and end apart: 66 -> 57, of which waited for: 18 -> 17; matrix products, arithmetic and copies ran while one was open for 22% -> 9% of each run, Pallas kernels for 27% -> 33%
where the time goes in v3:
time: 524 us; the launch traced here: 516 us
  Pallas kernels  245 us (47%)
  waiting for transfers between devices  116 us (22%)
  starting transfers between devices  65.4 us (12%)
  local copies, waits for them, and re-layouts  40.7 us (8%)
  other arithmetic  31.7 us (6%)
  between operations  16.1 us (3%)
    pallas_call x12, Pallas kernels, frozen_call(): pl.pallas_call(functools.partial(kernel, form), out_shape=tuple((jax.Shap...  178 us
    ppermute x9, waiting for transfers between devices, along_z(): return lax.ppermute(rows, 'dp', RING)  65 us
    pallas_call x2, Pallas kernels, attend_backward(): pl.pallas_call(functools.partial(attend_backward_kernel, pieces), out_sha...  38.3 us
    unnamed x230, local copies, waits for them, and re-layouts  28.7 us
    pallas_call x2, Pallas kernels, attend_forward(): pl.pallas_call(functools.partial(attend_forward_kernel, pieces), out_shap...  26.1 us
    all_to_all x2, waiting for transfers between devices, to_owners(): lax.all_to_all(total, LANE, split_axis=0, concat_axis=0, tiled=True)  17.5 us
    ppermute x9, starting transfers between devices, along_z(): return lax.ppermute(rows, 'dp', RING)  14.3 us
    ppermute x6, starting transfers between devices, along_x(): return lax.ppermute(rows, 'dp', ACROSS_X)  11.5 us
  transfers between devices with their start and end apart: 57, of which 17 were waited for; matrix products, arithmetic and copies ran while one was open for 9% of the time, Pallas kernels for 33%

profile of v3, /device:TPU:0, one launch (start us, length us, event | category | flops | bytes accessed | tf_op | source)
XLA Modules:
  0.0 516.0 jit_solution(13490835470704953510)
XLA Ops:
  7.3 1.1 slice_bitcast_fusion.5
  11.3 3.1 collective-permute-start.2
  15.3 1.5 collective-permute-start.5
  17.7 1.5 collective-permute-start.6
  20.0 1.8 collective-permute-done.2
  24.5 13.8 %collective-permute-done.3 = bf16[128,1024]{1,0:T(8,128)(2,1)S(1)} collective-permute-done((bf16[128,1024]{1,0:T(8,128)(2,1)S(1)}, bf16[128,1024]{1,0:T(8,128)(2,1)S(1)}, u32[]{:S(2)}, u32[]{:S(2)}) %collective-permute-start.3) | collective-permute-done | bytes 262176 | tf_op jit(solution)/shard_map/ppermute | solution.py:273
  38.2 2.3 collective-permute-start.4
  40.5 1.2 bitcast_select_fusion
  42.7 4.2 collective-permute-done.4
  47.0 8.0 %all-to-all-start = ((bf16[16,2,16,512]{3,2,1,0:T(8,128)(2,1)}), bf16[16,2,16,512]{3,2,1,0:T(8,128)(2,1)S(1)}, u32[]{:S(2)}, u32[]{:S(2)}) async-start(bf16[16,2,16,512]{3,2,1,0:T(8,128)(2,1)} %broadcast_select_fusion), calls=%async_computation | async-start | bytes 1048576 | tf_op jit(solution)/shard_map/all_to_all | solution.py:361
  55.3 2.0 collective-permute-start.7
  57.3 1.5 collective-permute-start.8
  58.9 1.5 collective-permute-start.9
  60.3 24.7 %collective-permute-done.9 = bf16[128,1024]{1,0:T(8,128)(2,1)S(1)} collective-permute-done((bf16[128,1024]{1,0:T(8,128)(2,1)S(1)}, bf16[128,1024]{1,0:T(8,128)(2,1)S(1)}, u32[]{:S(2)}, u32[]{:S(2)}) %collective-permute-start.9) | collective-permute-done | bytes 262176 | tf_op jit(solution)/shard_map/ppermute | solution.py:273
  85.8 1.2 pad_maximum_fusion.2.refs_0_.refs_4_
  87.1 1.5 collective-permute-start.10
  88.7 4.7 collective-permute-start.11
  93.9 2.2 collective-permute-done.15
  96.6 18.4 %collective-permute-done.16 = bf16[128,1024]{1,0:T(8,128)(2,1)S(1)} collective-permute-done((bf16[128,1024]{1,0:T(8,128)(2,1)S(1)}, bf16[128,1024]{1,0:T(8,128)(2,1)S(1)}, u32[]{:S(2)}, u32[]{:S(2)}) %collective-permute-start.16) | collective-permute-done | bytes 262176 | tf_op jit(solution)/shard_map/ppermute | solution.py:273
  115.1 1.9 collective-permute-done.14.other_ref
  117.0 7.6 %collective-permute-done.10.refs_1_.refs_5_ = bf16[2,4,64,1024]{3,2,1,0:T(8,128)(2,1)} collective-permute-done((bf16[2,4,64,1024]{3,2,1,0:T(8,128)(2,1)S(1)}, bf16[2,4,64,1024]{3,2,1,0:T(8,128)(2,1)}, u32[]{:S(2)}, u32[]{:S(2)}) %collective-permute-start.10) | collective-permute-done | bytes 1048608 | tf_op jit(solution)/shard_map/ppermute | solution.py:281
  124.5 8.4 %collective-permute-done.11.refs_3_.refs_7_ = bf16[2,4,64,1024]{3,2,1,0:T(8,128)(2,1)} collective-permute-done((bf16[2,4,64,1024]{3,2,1,0:T(8,128)(2,1)S(1)}, bf16[2,4,64,1024]{3,2,1,0:T(8,128)(2,1)}, u32[]{:S(2)}, u32[]{:S(2)}) %collective-permute-start.11) | collective-permute-done | bytes 1048608 | tf_op jit(solution)/shard_map/ppermute | solution.py:277
  136.2 2.6 collective-permute-start.19
  140.2 4.1 collective-permute-start.21
  155.9 1.6 convert_element_type.42.x_ref
  157.5 10.9 %qkv_forward.2 = (bf16[512,1024]{1,0:T(8,128)(2,1)}, bf16[512,1024]{1,0:T(8,128)(2,1)}, f32[512,128]{1,0:T(8,128)}, bf16[512,16]{1,0:T(8,128)(2,1)}, bf16[512,10...) custom-call(s32[4]{0:T(128)} %copy-done.38, f32[512,1024]{1,0:T(8,128)} %convert_element_type.42.x_ref, ...), custom_call_target="tpu_custom_call" | custom-call | flops 900000000 | tf_op jit(solution)/shard_map/qkv_forward/pallas_call | solution.py:707
  169.6 2.0 collective-permute-start
  172.5 1.5 collective-permute-start.1
  174.5 1.4 pad_maximum_fusion.4.refs_0_.refs_4_
  175.9 1.5 pad_maximum_fusion.5.refs_2_.refs_6_
  177.4 8.7 %collective-permute-done = bf16[256,1024]{1,0:T(8,128)(2,1)} collective-permute-done((bf16[256,1024]{1,0:T(8,128)(2,1)}, bf16[256,1024]{1,0:T(8,128)(2,1)}, u32[]{:S(2)}, u32[]{:S(2)}) %collective-permute-start) | collective-permute-done | bytes 524320 | tf_op jit(solution)/shard_map/ppermute | solution.py:211
  186.2 1.9 collective-permute-start.22
  190.9 1.3 bitcast_select_fusion.2
  192.2 1.5 collective-permute-start.27
  194.8 13.3 %attend_forward.2 = (f32[512,1024]{1,0:T(8,128)}, f32[8,2,512]{2,1,0:T(2,128)S(1)}) custom-call(s32[1]{0:T(128)} %bitcast.48.place_ref, bf16[512,1024]{1,0:T(8,128)(2,1)S(1)} %copy-done.2, bf16[512,1024]{1,0:T(8,128)(2,1)S(1)} %copy-done.3, bf16[512,1024]{1,0:T(8,128)(2,1)S(1)} %copy-done.6, bf16[512,1024]{1,0:T(8,128)(2,1)S(1)} %copy-done.4, ...), custom_call_target="tpu_custom_call" | custom-call | flops 1300000000 | tf_op jit(solution)/shard_map/attend_forward/pallas_call | solution.py:157
  208.1 11.1 %output_forward.2 = (bf16[512,1024]{1,0:T(8,128)(2,1)}, f32[512,1024]{1,0:T(8,128)}, bf16[512,1024]{1,0:T(8,128)(2,1)}, bf16[512,1024]{1,0:T(8,128)(2,1)}, f32[512,128]{1,0:T(8,128)}, /*index=5*/bf16[512,16]{1,0:T(8,128)(2,1)}) custom-call(s32[4]{0:T(128)} %copy-done.38, f32[512,1024]{1,0:T(8,128)} %convert_element_type.42.x_ref, ...), custom_call_target="tpu_custom_call" | custom-call | flops 800000000 | tf_op jit(solution)/shard_map/output_forward/pallas_call | solution.py:707
  219.3 2.0 collective-permute-done.23.refs_3_.refs_7_
  227.0 24.0 %feed_forward.2 = (f32[512,1024]{1,0:T(8,128)}, bf16[512,4096]{1,0:T(8,128)(2,1)}, bf16[512,4096]{1,0:T(8,128)(2,1)}, bf16[512,16]{1,0:T(8,128)(2,1)}, bf16[512,16]{1,0:T(8,128)(2,1)}) custom-call(s32[4]{0:T(128)} %copy-done.38, bf16[512,1024]{1,0:T(8,128)(2,1)} %get-tuple-element.624.normed_ref, f32[512,1024]{1,0:T(8,128)} %get-tuple-element.441.middle_ref, ...), custom_call_target="tpu_custom_call" | custom-call | flops 2000000000 | tf_op jit(solution)/shard_map/feed_forward/pallas_call | solution.py:707
  252.4 11.3 %qkv_forward.3 = (bf16[512,1024]{1,0:T(8,128)(2,1)}, bf16[512,1024]{1,0:T(8,128)(2,1)}, f32[512,128]{1,0:T(8,128)}, bf16[512,16]{1,0:T(8,128)(2,1)}, bf16[512,10...) custom-call(s32[4]{0:T(128)} %copy-done.38, f32[512,1024]{1,0:T(8,128)} %get-tuple-element.537.x_ref, ...), custom_call_target="tpu_custom_call" | custom-call | flops 900000000 | tf_op jit(solution)/shard_map/qkv_forward/pallas_call | solution.py:707
  264.3 1.3 pad_maximum_fusion.6.refs_0_
  265.6 2.0 collective-permute-start.34
  268.8 1.8 collective-permute-start.35
  270.9 12.8 %attend_forward.3 = (f32[512,1024]{1,0:T(8,128)}, f32[8,2,512]{2,1,0:T(2,128)S(1)}) custom-call(s32[1]{0:T(128)} %bitcast.48.place_ref, bf16[512,1024]{1,0:T(8,128)(2,1)S(1)} %copy-done.7, bf16[512,1024]{1,0:T(8,128)(2,1)S(1)} %copy-done.8, bf16[512,1024]{1,0:T(8,128)(2,1)S(1)} %collective-permute-done.38.refs_1_, bf16[512,1024]{1,0:T(8,128)(2,1)S(1)} %copy-done.9, ...), custom_call_target="tpu_custom_call" | custom-call | flops 1300000000 | tf_op jit(solution)/shard_map/attend_forward/pallas_call | solution.py:157
  283.6 11.2 %output_forward.3 = (bf16[512,1024]{1,0:T(8,128)(2,1)}, f32[512,1024]{1,0:T(8,128)}, bf16[512,1024]{1,0:T(8,128)(2,1)}, bf16[512,1024]{1,0:T(8,128)(2,1)}, f32[512,128]{1,0:T(8,128)}, /*index=5*/bf16[512,16]{1,0:T(8,128)(2,1)}) custom-call(s32[4]{0:T(128)} %copy-done.38, f32[512,1024]{1,0:T(8,128)} %get-tuple-element.537.x_ref, ...), custom_call_target="tpu_custom_call" | custom-call | flops 800000000 | tf_op jit(solution)/shard_map/output_forward/pallas_call | solution.py:707
  297.4 1.5 convert_element_type.44.grad_ref
  299.8 1.5 collective-permute-done.41.refs_7_
  302.3 24.0 %feed_forward.3 = (f32[512,1024]{1,0:T(8,128)}, bf16[512,4096]{1,0:T(8,128)(2,1)}, bf16[512,4096]{1,0:T(8,128)(2,1)}, bf16[512,16]{1,0:T(8,128)(2,1)}, bf16[512,16]{1,0:T(8,128)(2,1)}) custom-call(s32[4]{0:T(128)} %copy-done.38, bf16[512,1024]{1,0:T(8,128)(2,1)} %get-tuple-element.569.normed_ref, f32[512,1024]{1,0:T(8,128)} %get-tuple-element.570.middle_ref, ...), custom_call_target="tpu_custom_call" | custom-call | flops 2000000000 | tf_op jit(solution)/shard_map/feed_forward/pallas_call | solution.py:707
  326.3 23.7 %feed_backward.2 = (f32[512,1024]{1,0:T(8,128)}, bf16[16,1024]{1,0:T(8,128)(2,1)}, bf16[16,4096]{1,0:T(8,128)(2,1)}, bf16[16,4096]{1,0:T(8,128)(2,1)}, bf16[16,1024]{1,0:T(8,128)(2,1)}) custom-call(s32[4]{0:T(128)} %copy-done.38, f32[512,1024]{1,0:T(8,128)} %convert_element_type.44.grad_ref, bf16[512,4096]{1,0:T(8,128)(2,1)} %get-tuple-element.583.slope_ref, ...), custom_call_target="tpu_custom_call" | custom-call | flops 2200000000 | tf_op jit(solution)/shard_map/feed_backward/pallas_call | solution.py:707
  350.0 5.9 %output_backward.2 = (bf16[512,1024]{1,0:T(8,128)(2,1)}, bf16[16,1024]{1,0:T(8,128)(2,1)}, bf16[16,1024]{1,0:T(8,128)(2,1)}) custom-call(s32[4]{0:T(128)} %copy-done.38, f32[512,1024]{1,0:T(8,128)} %get-tuple-element.589.grad_ref, bf16[512,1024]{1,0:T(8,128)(2,1)} %get-tuple-element.597.attended_ref, bf16[512,16]{1,0:T(8,128)(2,1)} %get-tuple-element.598.rank_ref, ...), custom_call_target="tpu_custom_call" | custom-call | flops 500000000 | tf_op jit(solution)/shard_map/output_backward/pallas_call | solution.py:707
  356.0 19.2 %attend_backward.2 = (bf16[512,1024]{1,0:T(8,128)(2,1)S(1)}, bf16[512,1024]{1,0:T(8,128)(2,1)S(1)}, bf16[512,1024]{1,0:T(8,128)(2,1)S(1)}, bf16[512,1024]{1,0:T(8,128)(2,1)S(1)}, bf16[512,1024]{1,0:T(8,128)(2,1)S(1)}) custom-call(s32[1]{0:T(128)} %bitcast.48.place_ref, bf16[512,1024]{1,0:T(8,128)(2,1)} %get-tuple-element.596.q_ref, ...), custom_call_target="tpu_custom_call" | custom-call | flops 2100000000 | tf_op jit(solution)/shard_map/attend_backward/pallas_call | solution.py:183
  377.9 1.5 collective-permute-done.45.refs_3_
  380.4 13.2 %qkv_backward.2 = (f32[512,1024]{1,0:T(8,128)}, bf16[16,1024]{1,0:T(8,128)(2,1)}, bf16[16,3072]{1,0:T(8,128)(2,1)}) custom-call(s32[4]{0:T(128)} %copy-done.38, f32[512,1024]{1,0:T(8,128)} %get-tuple-element.589.grad_ref, bf16[512,1024]{1,0:T(8,128)(2,1)} %get-tuple-element.590.normed_ref, bf16[512,1024]{1,0:T(8,128)(2,1)} %get-tuple-element.591.unit_ref, ...), custom_call_target="tpu_custom_call" | custom-call | flops 1100000000 | tf_op jit(solution)/shard_map/qkv_backward/pallas_call | solution.py:707
  393.6 23.9 %feed_backward.3 = (f32[512,1024]{1,0:T(8,128)}, bf16[16,1024]{1,0:T(8,128)(2,1)}, bf16[16,4096]{1,0:T(8,128)(2,1)}, bf16[16,4096]{1,0:T(8,128)(2,1)}, bf16[16,1024]{1,0:T(8,128)(2,1)}) custom-call(s32[4]{0:T(128)} %copy-done.38, f32[512,1024]{1,0:T(8,128)} %get-tuple-element.621.grad_ref, bf16[512,4096]{1,0:T(8,128)(2,1)} %get-tuple-element.622.slope_ref, ...), custom_call_target="tpu_custom_call" | custom-call | flops 2200000000 | tf_op jit(solution)/shard_map/feed_backward/pallas_call | solution.py:707
  417.5 5.9 %output_backward.3 = (bf16[512,1024]{1,0:T(8,128)(2,1)}, bf16[16,1024]{1,0:T(8,128)(2,1)}, bf16[16,1024]{1,0:T(8,128)(2,1)}) custom-call(s32[4]{0:T(128)} %copy-done.38, f32[512,1024]{1,0:T(8,128)} %get-tuple-element.633.grad_ref, bf16[512,1024]{1,0:T(8,128)(2,1)} %get-tuple-element.641.attended_ref, bf16[512,16]{1,0:T(8,128)(2,1)} %get-tuple-element.642.rank_ref, ...), custom_call_target="tpu_custom_call" | custom-call | flops 500000000 | tf_op jit(solution)/shard_map/output_backward/pallas_call | solution.py:707
  423.4 19.1 %attend_backward.3 = (bf16[512,1024]{1,0:T(8,128)(2,1)S(1)}, bf16[512,1024]{1,0:T(8,128)(2,1)S(1)}, bf16[512,1024]{1,0:T(8,128)(2,1)S(1)}, bf16[512,1024]{1,0:T(8,128)(2,1)S(1)}, bf16[512,1024]{1,0:T(8,128)(2,1)S(1)}) custom-call(s32[1]{0:T(128)} %bitcast.48.place_ref, bf16[512,1024]{1,0:T(8,128)(2,1)} %get-tuple-element.640.q_ref, ...), custom_call_target="tpu_custom_call" | custom-call | flops 2100000000 | tf_op jit(solution)/shard_map/attend_backward/pallas_call | solution.py:183
  449.3 13.1 %qkv_backward.3 = (f32[512,1024]{1,0:T(8,128)}, bf16[16,1024]{1,0:T(8,128)(2,1)}, bf16[16,3072]{1,0:T(8,128)(2,1)}) custom-call(s32[4]{0:T(128)} %copy-done.38, f32[512,1024]{1,0:T(8,128)} %get-tuple-element.633.grad_ref, bf16[512,1024]{1,0:T(8,128)(2,1)} %get-tuple-element.634.normed_ref, bf16[512,1024]{1,0:T(8,128)(2,1)} %get-tuple-element.635.unit_ref, ...), custom_call_target="tpu_custom_call" | custom-call | flops 1100000000 | tf_op jit(solution)/shard_map/qkv_backward/pallas_call | solution.py:707
  465.0 1.9 fusion
  467.8 5.1 all-to-all-start.1
  473.7 1.1 collective-permute-start.48
  474.8 5.7 %all-to-all-done.1 = bf16[16,16,128]{2,1,0:T(8,128)(2,1)S(1)} async-done(((bf16[16,16,128]{2,1,0:T(8,128)(2,1)}), bf16[16,16,128]{2,1,0:T(8,128)(2,1)S(1)}, u32[]{:S(2)}, u32[]{:S(2)}) %all-to-all-start.1) | async-done | bytes 65568 | tf_op jit(solution)/shard_map/all_to_all | solution.py:1045
  480.5 4.2 all-to-all-start.2
  486.0 11.8 %all-to-all-done.2 = bf16[16,16,896]{2,1,0:T(8,128)(2,1)} async-done(((bf16[16,16,896]{2,1,0:T(8,128)(2,1)}), bf16[16,16,896]{2,1,0:T(8,128)(2,1)}, u32[]{:S(2)}, u32[]{:S(2)}) %all-to-all-start.2) | async-done | bytes 458784 | tf_op jit(solution)/shard_map/all_to_all | solution.py:1045
  497.8 1.2 fusion.1
  507.0 1.7 maximum_select_fusion
  (392 shorter events, 70.6 us)
Async XLA Ops:
  7.2 219.8 %all-gather.6.cloned.1.call-start = ((), (), s32[]{:S(2)}) async-start(), calls=%async_computation.4 | async-start | bytes 17301504 | tf_op jit(solution)/shard_map/all_gather | solution.py:331
  10.4 288.6 %all-gather.4.cloned.1.call-start = ((), (), s32[]{:S(2)}) async-start(), calls=%async_computation.3 | async-start | bytes 8650752 | tf_op jit(solution)/shard_map/all_gather | solution.py:331
  11.3 10.4 %collective-permute-start.2 = (bf16[128,1024]{1,0:T(8,128)(2,1)S(1)}, bf16[128,1024]{1,0:T(8,128)(2,1)S(1)}, u32[]{:S(2)}, u32[]{:S(2)}) collective-permute-start(bf16[128,1024]{1,0:T(8,128)(2,1)S(1)} %pad_maximum_fusion.15), channel_id=1, source_target_pairs={{0,8},{4,12},{8,24},{12,28},{16,0},{20,4},{24,16},{28,20},{1,9},{5... | collective-permute-start | bytes 786440 | tf_op jit(solution)/shard_map/ppermute | solution.py:273
  15.3 25.2 %collective-permute-start.5 = (bf16[256,1024]{1,0:T(8,128)(2,1)}, bf16[256,1024]{1,0:T(8,128)(2,1)}, u32[]{:S(2)}, u32[]{:S(2)}) collective-permute-start(bf16[256,1024]{1,0:T(8,128)(2,1)} %bitcast_select_fusion.1), channel_id=1, source_target_pairs={{0,2},{1,3},{2,1},{3,0},{4,6},{5,7},{6,5},{7,4},{8,10},{9,11},{10,... | collective-permute-start | bytes 1572872 | tf_op jit(solution)/shard_map/ppermute | solution.py:211
  17.7 22.8 %collective-permute-start.6 = (bf16[256,1024]{1,0:T(8,128)(2,1)}, bf16[256,1024]{1,0:T(8,128)(2,1)}, u32[]{:S(2)}, u32[]{:S(2)}) collective-permute-start(bf16[256,1024]{1,0:T(8,128)(2,1)} %slice_bitcast_fusion.1), channel_id=1, source_target_pairs={{2,3},{3,2},{6,7},{7,6},{10,11},{11,10},{14,15},{15,14},{18,19},{1... | collective-permute-start | bytes 1572872 | tf_op jit(solution)/shard_map/ppermute | solution.py:212
  19.9 38.9 %copy-start.76 = (bf16[128,1024]{1,0:T(8,128)(2,1)}, bf16[128,1024]{1,0:T(8,128)(2,1)S(1)}, u32[]{:S(2)}) copy-start(bf16[128,1024]{1,0:T(8,128)(2,1)S(1)} %pad_maximum_fusion.16) | copy-start | bytes 786436
  21.7 16.5 %collective-permute-start.3 = (bf16[128,1024]{1,0:T(8,128)(2,1)S(1)}, bf16[128,1024]{1,0:T(8,128)(2,1)S(1)}, u32[]{:S(2)}, u32[]{:S(2)}) collective-permute-start(bf16[128,1024]{1,0:T(8,128)(2,1)S(1)} %collective-permute-done.2), channel_id=1, source_target_pairs={{0,8},{4,12},{8,24},{12,28},{16,0},{20,4},{24,16},{28,20},{1,9},{5... | collective-permute-start | bytes 786440 | tf_op jit(solution)/shard_map/ppermute | solution.py:273
  38.2 8.7 %collective-permute-start.4 = (bf16[128,1024]{1,0:T(8,128)(2,1)S(1)}, bf16[128,1024]{1,0:T(8,128)(2,1)S(1)}, u32[]{:S(2)}, u32[]{:S(2)}) collective-permute-start(bf16[128,1024]{1,0:T(8,128)(2,1)S(1)} %collective-permute-done.3), channel_id=1, source_target_pairs={{0,8},{4,12},{8,24},{12,28},{16,0},{20,4},{24,16},{28,20},{1,9},{5... | collective-permute-start | bytes 786440 | tf_op jit(solution)/shard_map/ppermute | solution.py:273
  47.0 38.1 %all-to-all-start = ((bf16[16,2,16,512]{3,2,1,0:T(8,128)(2,1)}), bf16[16,2,16,512]{3,2,1,0:T(8,128)(2,1)S(1)}, u32[]{:S(2)}, u32[]{:S(2)}) async-start(bf16[16,2,16,512]{3,2,1,0:T(8,128)(2,1)} %broadcast_select_fusion), calls=%async_computation | async-start | bytes 1048576 | tf_op jit(solution)/shard_map/all_to_all | solution.py:361
  55.3 29.8 %collective-permute-start.7 = (bf16[4,64,1024]{2,1,0:T(8,128)(2,1)S(1)}, bf16[4,64,1024]{2,1,0:T(8,128)(2,1)}, u32[]{:S(2)}, u32[]{:S(2)}) collective-permute-start(bf16[4,64,1024]{2,1,0:T(8,128)(2,1)S(1)} %pad_maximum_fusion.9), channel_id=1, source_target_pairs={{0,4},{4,0},{8,12},{12,8},{16,20},{20,16},{24,28},{28,24},{1,5},{5... | collective-permute-start | bytes 1572872 | tf_op jit(solution)/shard_map/ppermute | solution.py:277
  57.3 27.7 %collective-permute-start.8 = (bf16[4,64,1024]{2,1,0:T(8,128)(2,1)S(1)}, bf16[4,64,1024]{2,1,0:T(8,128)(2,1)S(1)}, u32[]{:S(2)}, u32[]{:S(2)}) collective-permute-start(bf16[4,64,1024]{2,1,0:T(8,128)(2,1)S(1)} %pad_maximum_fusion.10), channel_id=1, source_target_pairs={{0,2},{2,0},{1,3},{3,1},{4,6},{6,4},{5,7},{7,5},{8,10},{10,8},{9,1... | collective-permute-start | bytes 1572872 | tf_op jit(solution)/shard_map/ppermute | solution.py:281
  58.9 26.2 %collective-permute-start.9 = (bf16[128,1024]{1,0:T(8,128)(2,1)S(1)}, bf16[128,1024]{1,0:T(8,128)(2,1)S(1)}, u32[]{:S(2)}, u32[]{:S(2)}) collective-permute-start(bf16[128,1024]{1,0:T(8,128)(2,1)S(1)} %pad_maximum_fusion.16), channel_id=1, source_target_pairs={{0,8},{4,12},{8,24},{12,28},{16,0},{20,4},{24,16},{28,20},{1,9},{5... | collective-permute-start | bytes 786440 | tf_op jit(solution)/shard_map/ppermute | solution.py:273
  85.8 29.2 %copy-start.102 = (f32[2,2048]{1,0:T(2,128)S(1)}, f32[2,2048]{1,0:T(2,128)}, u32[]{:S(2)}) copy-start(f32[2,2048]{1,0:T(2,128)} %param.30) | copy-start | bytes 49156
  85.8 49.2 %copy-start.77 = (bf16[128,1024]{1,0:T(8,128)(2,1)S(1)}, bf16[128,1024]{1,0:T(8,128)(2,1)}, u32[]{:S(2)}) copy-start(bf16[128,1024]{1,0:T(8,128)(2,1)} %copy-done.76) | copy-start | bytes 786436
  87.1 48.2 %copy-start.53 = (bf16[2,4,64,1024]{3,2,1,0:T(8,128)(2,1)}, bf16[2,4,64,1024]{3,2,1,0:T(8,128)(2,1)S(1)}, u32[]{:S(2)}) copy-start(bf16[2,4,64,1024]{3,2,1,0:T(8,128)(2,1)S(1)} %pad_maximum_fusion.2.refs_0_.refs_4_) | copy-start | bytes 3145732
  87.1 37.5 %collective-permute-start.10 = (bf16[2,4,64,1024]{3,2,1,0:T(8,128)(2,1)S(1)}, bf16[2,4,64,1024]{3,2,1,0:T(8,128)(2,1)}, u32[]{:S(2)}, u32[]{:S(2)}) collective-permute-start(bf16[2,4,64,1024]{3,2,1,0:T(8,128)(2,1)S(1)} %pad_maximum_fusion.2.refs_0_.refs_4_), channel_id=1, source_target_pairs={{0,2},{2,0},{1,3},{3,1},{4,6},{6,4},{5,7},{7,5},{8,10},{10,8},{9,1... | collective-permute-start | bytes 3145736 | tf_op jit(solution)/shard_map/ppermute | solution.py:281
  88.6 7.5 %collective-permute-start.15 = (bf16[128,1024]{1,0:T(8,128)(2,1)S(1)}, bf16[128,1024]{1,0:T(8,128)(2,1)S(1)}, u32[]{:S(2)}, u32[]{:S(2)}) collective-permute-start(bf16[128,1024]{1,0:T(8,128)(2,1)S(1)} %collective-permute-done.9), channel_id=1, source_target_pairs={{0,8},{4,12},{8,24},{12,28},{16,0},{20,4},{24,16},{28,20},{1,9},{5... | collective-permute-start | bytes 786440 | tf_op jit(solution)/shard_map/ppermute | solution.py:273
  88.7 47.5 %copy-start.54 = (bf16[2,4,64,1024]{3,2,1,0:T(8,128)(2,1)}, bf16[2,4,64,1024]{3,2,1,0:T(8,128)(2,1)S(1)}, u32[]{:S(2)}) copy-start(bf16[2,4,64,1024]{3,2,1,0:T(8,128)(2,1)S(1)} %pad_maximum_fusion.3.refs_2_.refs_6_) | copy-start | bytes 3145732
  88.7 44.3 %collective-permute-start.11 = (bf16[2,4,64,1024]{3,2,1,0:T(8,128)(2,1)S(1)}, bf16[2,4,64,1024]{3,2,1,0:T(8,128)(2,1)}, u32[]{:S(2)}, u32[]{:S(2)}) collective-permute-start(bf16[2,4,64,1024]{3,2,1,0:T(8,128)(2,1)S(1)} %pad_maximum_fusion.3.refs_2_.refs_6_), channel_id=1, source_target_pairs={{0,4},{4,0},{8,12},{12,8},{16,20},{20,16},{24,28},{28,24},{1,5},{5... | collective-permute-start | bytes 3145736 | tf_op jit(solution)/shard_map/ppermute | solution.py:277
  93.4 39.6 %collective-permute-start.12 = (bf16[2,4,64,1024]{3,2,1,0:T(8,128)(2,1)S(1)}, bf16[2,4,64,1024]{3,2,1,0:T(8,128)(2,1)S(1)}, u32[]{:S(2)}, u32[]{:S(2)}) collective-permute-start(bf16[2,4,64,1024]{3,2,1,0:T(8,128)(2,1)S(1)} %pad_maximum_fusion.2.refs_0_.refs_4_), channel_id=1, source_target_pairs={{0,1},{1,0},{2,3},{3,2},{4,5},{5,4},{6,7},{7,6},{8,9},{9,8},{10,11... | collective-permute-start | bytes 3145736 | tf_op jit(solution)/shard_map/ppermute | solution.py:285
  93.4 39.6 %collective-permute-start.13 = (bf16[2,4,64,1024]{3,2,1,0:T(8,128)(2,1)S(1)}, bf16[2,4,64,1024]{3,2,1,0:T(8,128)(2,1)S(1)}, u32[]{:S(2)}, u32[]{:S(2)}) collective-permute-start(bf16[2,4,64,1024]{3,2,1,0:T(8,128)(2,1)S(1)} %pad_maximum_fusion.3.refs_2_.refs_6_), channel_id=1, source_target_pairs={{0,1},{1,0},{2,3},{3,2},{4,5},{5,4},{6,7},{7,6},{8,9},{9,8},{10,11... | collective-permute-start | bytes 3145736 | tf_op jit(solution)/shard_map/ppermute | solution.py:285
  96.1 19.0 %collective-permute-start.16 = (bf16[128,1024]{1,0:T(8,128)(2,1)S(1)}, bf16[128,1024]{1,0:T(8,128)(2,1)S(1)}, u32[]{:S(2)}, u32[]{:S(2)}) collective-permute-start(bf16[128,1024]{1,0:T(8,128)(2,1)S(1)} %collective-permute-done.15), channel_id=1, source_target_pairs={{0,8},{4,12},{8,24},{12,28},{16,0},{20,4},{24,16},{28,20},{1,9},{5... | collective-permute-start | bytes 786440 | tf_op jit(solution)/shard_map/ppermute | solution.py:273
  115.0 1.9 collective-permute-start.14
  134.0 21.8 %collective-permute-start.17 = (bf16[2,4,64,1024]{3,2,1,0:T(8,128)(2,1)}, bf16[2,4,64,1024]{3,2,1,0:T(8,128)(2,1)}, u32[]{:S(2)}, u32[]{:S(2)}) collective-permute-start(bf16[2,4,64,1024]{3,2,1,0:T(8,128)(2,1)} %collective-permute-done.10.refs_1_.refs_5_), channel_id=1, source_target_pairs={{0,1},{1,0},{2,3},{3,2},{4,5},{5,4},{6,7},{7,6},{8,9},{9,8},{10,11... | collective-permute-start | bytes 3145736 | tf_op jit(solution)/shard_map/ppermute | solution.py:285
  135.0 20.8 %collective-permute-start.18 = (bf16[2,4,64,1024]{3,2,1,0:T(8,128)(2,1)}, bf16[2,4,64,1024]{3,2,1,0:T(8,128)(2,1)}, u32[]{:S(2)}, u32[]{:S(2)}) collective-permute-start(bf16[2,4,64,1024]{3,2,1,0:T(8,128)(2,1)} %collective-permute-done.11.refs_3_.refs_7_), channel_id=1, source_target_pairs={{0,1},{1,0},{2,3},{3,2},{4,5},{5,4},{6,7},{7,6},{8,9},{9,8},{10,11... | collective-permute-start | bytes 3145736 | tf_op jit(solution)/shard_map/ppermute | solution.py:285
  135.3 20.6 %copy-start.70 = (bf16[512,1024]{1,0:T(8,128)(2,1)S(1)}, bf16[512,1024]{1,0:T(8,128)(2,1)}, u32[]{:S(2)}) copy-start(bf16[512,1024]{1,0:T(8,128)(2,1)} %pad_maximum_fusion.1) | copy-start | bytes 3145732
  136.2 19.6 %collective-permute-start.19 = (bf16[4,64,1024]{2,1,0:T(8,128)(2,1)}, bf16[4,64,1024]{2,1,0:T(8,128)(2,1)S(1)}, u32[]{:S(2)}, u32[]{:S(2)}) collective-permute-start(bf16[4,64,1024]{2,1,0:T(8,128)(2,1)} %pad_maximum_fusion.11), channel_id=1, source_target_pairs={{0,4},{4,0},{8,12},{12,8},{16,20},{20,16},{24,28},{28,24},{1,5},{5... | collective-permute-start | bytes 1572872 | tf_op jit(solution)/shard_map/ppermute | solution.py:277
  138.8 17.0 %collective-permute-start.20 = (bf16[4,64,1024]{2,1,0:T(8,128)(2,1)S(1)}, bf16[4,64,1024]{2,1,0:T(8,128)(2,1)}, u32[]{:S(2)}, u32[]{:S(2)}) collective-permute-start(bf16[4,64,1024]{2,1,0:T(8,128)(2,1)S(1)} %pad_maximum_fusion.12), channel_id=1, source_target_pairs={{0,2},{2,0},{1,3},{3,1},{4,6},{6,4},{5,7},{7,5},{8,10},{10,8},{9,1... | collective-permute-start | bytes 1572872 | tf_op jit(solution)/shard_map/ppermute | solution.py:281
  140.2 15.7 %collective-permute-start.21 = (bf16[128,1024]{1,0:T(8,128)(2,1)S(1)}, bf16[128,1024]{1,0:T(8,128)(2,1)S(1)}, u32[]{:S(2)}, u32[]{:S(2)}) collective-permute-start(bf16[128,1024]{1,0:T(8,128)(2,1)S(1)} %pad_maximum_fusion.17), channel_id=1, source_target_pairs={{0,8},{4,12},{8,24},{12,28},{16,0},{20,4},{24,16},{28,20},{1,9},{5... | collective-permute-start | bytes 786440 | tf_op jit(solution)/shard_map/ppermute | solution.py:273
  168.4 19.8 %collective-permute-start.28 = (bf16[512,1024]{1,0:T(8,128)(2,1)}, bf16[512,1024]{1,0:T(8,128)(2,1)S(1)}, u32[]{:S(2)}, u32[]{:S(2)}) collective-permute-start(bf16[512,1024]{1,0:T(8,128)(2,1)} %get-tuple-element.656.refs_0_), channel_id=1, source_target_pairs={{0,1},{1,0},{2,3},{3,2},{4,5},{5,4},{6,7},{7,6},{8,9},{9,8},{10,11... | collective-permute-start | bytes 3145736 | tf_op jit(solution)/shard_map/ppermute | solution.py:242
  169.6 16.6 %collective-permute-start = (bf16[256,1024]{1,0:T(8,128)(2,1)}, bf16[256,1024]{1,0:T(8,128)(2,1)}, u32[]{:S(2)}, u32[]{:S(2)}) collective-permute-start(bf16[256,1024]{1,0:T(8,128)(2,1)} %bitcast_select_fusion.3), channel_id=1, source_target_pairs={{0,2},{1,3},{2,1},{3,0},{4,6},{5,7},{6,5},{7,4},{8,10},{9,11},{10,... | collective-permute-start | bytes 1572872 | tf_op jit(solution)/shard_map/ppermute | solution.py:211
  172.5 15.7 %collective-permute-start.1 = (bf16[256,1024]{1,0:T(8,128)(2,1)}, bf16[256,1024]{1,0:T(8,128)(2,1)}, u32[]{:S(2)}, u32[]{:S(2)}) collective-permute-start(bf16[256,1024]{1,0:T(8,128)(2,1)} %slice_bitcast_fusion.2), channel_id=1, source_target_pairs={{2,3},{3,2},{6,7},{7,6},{10,11},{11,10},{14,15},{15,14},{18,19},{1... | collective-permute-start | bytes 1572872 | tf_op jit(solution)/shard_map/ppermute | solution.py:212
  173.9 18.3 %collective-permute-start.29 = (bf16[512,1024]{1,0:T(8,128)(2,1)S(1)}, bf16[512,1024]{1,0:T(8,128)(2,1)}, u32[]{:S(2)}, u32[]{:S(2)}) collective-permute-start(bf16[512,1024]{1,0:T(8,128)(2,1)S(1)} %copy-done.4), channel_id=1, source_target_pairs={{0,1},{1,0},{2,3},{3,2},{4,5},{5,4},{6,7},{7,6},{8,9},{9,8},{10,11... | collective-permute-start | bytes 3145736 | tf_op jit(solution)/shard_map/ppermute | solution.py:242
  174.1 14.0 %collective-permute-start.26 = (bf16[128,1024]{1,0:T(8,128)(2,1)S(1)}, bf16[128,1024]{1,0:T(8,128)(2,1)}, u32[]{:S(2)}, u32[]{:S(2)}) collective-permute-start(bf16[128,1024]{1,0:T(8,128)(2,1)S(1)} %copy-done.80), channel_id=1, source_target_pairs={{0,8},{4,12},{8,24},{12,28},{16,0},{20,4},{24,16},{28,20},{1,9},{5... | collective-permute-start | bytes 786440 | tf_op jit(solution)/shard_map/ppermute | solution.py:273
  177.4 41.8 %copy-start.56 = (bf16[2,4,64,1024]{3,2,1,0:T(8,128)(2,1)}, bf16[2,4,64,1024]{3,2,1,0:T(8,128)(2,1)S(1)}, u32[]{:S(2)}) copy-start(bf16[2,4,64,1024]{3,2,1,0:T(8,128)(2,1)S(1)} %pad_maximum_fusion.5.refs_2_.refs_6_) | copy-start | bytes 3145732
  186.2 33.1 %collective-permute-start.22 = (bf16[2,4,64,1024]{3,2,1,0:T(8,128)(2,1)S(1)}, bf16[2,4,64,1024]{3,2,1,0:T(8,128)(2,1)}, u32[]{:S(2)}, u32[]{:S(2)}) collective-permute-start(bf16[2,4,64,1024]{3,2,1,0:T(8,128)(2,1)S(1)} %pad_maximum_fusion.4.refs_0_.refs_4_), channel_id=1, source_target_pairs={{0,2},{2,0},{1,3},{3,1},{4,6},{6,4},{5,7},{7,5},{8,10},{10,8},{9,1... | collective-permute-start | bytes 3145736 | tf_op jit(solution)/shard_map/ppermute | solution.py:281
  188.1 33.1 %collective-permute-start.24 = (bf16[2,4,64,1024]{3,2,1,0:T(8,128)(2,1)S(1)}, bf16[2,4,64,1024]{3,2,1,0:T(8,128)(2,1)S(1)}, u32[]{:S(2)}, u32[]{:S(2)}) collective-permute-start(bf16[2,4,64,1024]{3,2,1,0:T(8,128)(2,1)S(1)} %pad_maximum_fusion.4.refs_0_.refs_4_), channel_id=1, source_target_pairs={{0,1},{1,0},{2,3},{3,2},{4,5},{5,4},{6,7},{7,6},{8,9},{9,8},{10,11... | collective-permute-start | bytes 3145736 | tf_op jit(solution)/shard_map/ppermute | solution.py:285
  188.1 33.1 %collective-permute-start.23 = (bf16[2,4,64,1024]{3,2,1,0:T(8,128)(2,1)S(1)}, bf16[2,4,64,1024]{3,2,1,0:T(8,128)(2,1)}, u32[]{:S(2)}, u32[]{:S(2)}) collective-permute-start(bf16[2,4,64,1024]{3,2,1,0:T(8,128)(2,1)S(1)} %pad_maximum_fusion.5.refs_2_.refs_6_), channel_id=1, source_target_pairs={{0,4},{4,0},{8,12},{12,8},{16,20},{20,16},{24,28},{28,24},{1,5},{5... | collective-permute-start | bytes 3145736 | tf_op jit(solution)/shard_map/ppermute | solution.py:277
  189.2 32.0 %collective-permute-start.25 = (bf16[2,4,64,1024]{3,2,1,0:T(8,128)(2,1)S(1)}, bf16[2,4,64,1024]{3,2,1,0:T(8,128)(2,1)S(1)}, u32[]{:S(2)}, u32[]{:S(2)}) collective-permute-start(bf16[2,4,64,1024]{3,2,1,0:T(8,128)(2,1)S(1)} %pad_maximum_fusion.5.refs_2_.refs_6_), channel_id=1, source_target_pairs={{0,1},{1,0},{2,3},{3,2},{4,5},{5,4},{6,7},{7,6},{8,9},{9,8},{10,11... | collective-permute-start | bytes 3145736 | tf_op jit(solution)/shard_map/ppermute | solution.py:285
  192.2 27.0 %collective-permute-start.27 = (bf16[128,1024]{1,0:T(8,128)(2,1)}, bf16[128,1024]{1,0:T(8,128)(2,1)S(1)}, u32[]{:S(2)}, u32[]{:S(2)}) collective-permute-start(bf16[128,1024]{1,0:T(8,128)(2,1)} %collective-permute-done.26), channel_id=1, source_target_pairs={{0,8},{4,12},{8,24},{12,28},{16,0},{20,4},{24,16},{28,20},{1,9},{5... | collective-permute-start | bytes 786440 | tf_op jit(solution)/shard_map/ppermute | solution.py:273
  221.3 29.7 %collective-permute-start.30 = (bf16[2,4,64,1024]{3,2,1,0:T(8,128)(2,1)}, bf16[2,4,64,1024]{3,2,1,0:T(8,128)(2,1)S(1)}, u32[]{:S(2)}, u32[]{:S(2)}) collective-permute-start(bf16[2,4,64,1024]{3,2,1,0:T(8,128)(2,1)} %collective-permute-done.22.refs_1_.refs_5_), channel_id=1, source_target_pairs={{0,1},{1,0},{2,3},{3,2},{4,5},{5,4},{6,7},{7,6},{8,9},{9,8},{10,11... | collective-permute-start | bytes 3145736 | tf_op jit(solution)/shard_map/ppermute | solution.py:285
  221.4 29.7 %collective-permute-start.31 = (bf16[2,4,64,1024]{3,2,1,0:T(8,128)(2,1)}, bf16[2,4,64,1024]{3,2,1,0:T(8,128)(2,1)S(1)}, u32[]{:S(2)}, u32[]{:S(2)}) collective-permute-start(bf16[2,4,64,1024]{3,2,1,0:T(8,128)(2,1)} %collective-permute-done.23.refs_3_.refs_7_), channel_id=1, source_target_pairs={{0,1},{1,0},{2,3},{3,2},{4,5},{5,4},{6,7},{7,6},{8,9},{9,8},{10,11... | collective-permute-start | bytes 3145736 | tf_op jit(solution)/shard_map/ppermute | solution.py:285
  225.2 25.8 %collective-permute-start.32 = (bf16[4,64,1024]{2,1,0:T(8,128)(2,1)S(1)}, bf16[4,64,1024]{2,1,0:T(8,128)(2,1)}, u32[]{:S(2)}, u32[]{:S(2)}) collective-permute-start(bf16[4,64,1024]{2,1,0:T(8,128)(2,1)S(1)} %pad_maximum_fusion.13), channel_id=1, source_target_pairs={{0,4},{4,0},{8,12},{12,8},{16,20},{20,16},{24,28},{28,24},{1,5},{5... | collective-permute-start | bytes 1572872 | tf_op jit(solution)/shard_map/ppermute | solution.py:277
  225.6 25.4 %collective-permute-start.33 = (bf16[4,64,1024]{2,1,0:T(8,128)(2,1)S(1)}, bf16[4,64,1024]{2,1,0:T(8,128)(2,1)}, u32[]{:S(2)}, u32[]{:S(2)}) collective-permute-start(bf16[4,64,1024]{2,1,0:T(8,128)(2,1)S(1)} %pad_maximum_fusion.14), channel_id=1, source_target_pairs={{0,2},{2,0},{1,3},{3,1},{4,6},{6,4},{5,7},{7,5},{8,10},{10,8},{9,1... | collective-permute-start | bytes 1572872 | tf_op jit(solution)/shard_map/ppermute | solution.py:281
  263.7 6.9 %collective-permute-start.38 = (bf16[512,1024]{1,0:T(8,128)(2,1)}, bf16[512,1024]{1,0:T(8,128)(2,1)S(1)}, u32[]{:S(2)}, u32[]{:S(2)}) collective-permute-start(bf16[512,1024]{1,0:T(8,128)(2,1)} %get-tuple-element.612.refs_0_), channel_id=1, source_target_pairs={{0,1},{1,0},{2,3},{3,2},{4,5},{5,4},{6,7},{7,6},{8,9},{9,8},{10,11... | collective-permute-start | bytes 3145736 | tf_op jit(solution)/shard_map/ppermute | solution.py:242
  263.7 7.1 %collective-permute-start.39 = (bf16[512,1024]{1,0:T(8,128)(2,1)}, bf16[512,1024]{1,0:T(8,128)(2,1)S(1)}, u32[]{:S(2)}, u32[]{:S(2)}) collective-permute-start(bf16[512,1024]{1,0:T(8,128)(2,1)} %get-tuple-element.614.refs_2_), channel_id=1, source_target_pairs={{0,1},{1,0},{2,3},{3,2},{4,5},{5,4},{6,7},{7,6},{8,9},{9,8},{10,11... | collective-permute-start | bytes 3145736 | tf_op jit(solution)/shard_map/ppermute | solution.py:242
  265.6 29.3 %collective-permute-start.34 = (bf16[2,4,64,1024]{3,2,1,0:T(8,128)(2,1)S(1)}, bf16[2,4,64,1024]{3,2,1,0:T(8,128)(2,1)}, u32[]{:S(2)}, u32[]{:S(2)}) collective-permute-start(bf16[2,4,64,1024]{3,2,1,0:T(8,128)(2,1)S(1)} %pad_maximum_fusion.6.refs_0_), channel_id=1, source_target_pairs={{0,2},{2,0},{1,3},{3,1},{4,6},{6,4},{5,7},{7,5},{8,10},{10,8},{9,1... | collective-permute-start | bytes 3145736 | tf_op jit(solution)/shard_map/ppermute | solution.py:281
  267.6 27.2 %collective-permute-start.36 = (bf16[2,4,64,1024]{3,2,1,0:T(8,128)(2,1)S(1)}, bf16[2,4,64,1024]{3,2,1,0:T(8,128)(2,1)S(1)}, u32[]{:S(2)}, u32[]{:S(2)}) collective-permute-start(bf16[2,4,64,1024]{3,2,1,0:T(8,128)(2,1)S(1)} %pad_maximum_fusion.6.refs_0_), channel_id=1, source_target_pairs={{0,1},{1,0},{2,3},{3,2},{4,5},{5,4},{6,7},{7,6},{8,9},{9,8},{10,11... | collective-permute-start | bytes 3145736 | tf_op jit(solution)/shard_map/ppermute | solution.py:285
  268.8 26.1 %collective-permute-start.35 = (bf16[2,4,64,1024]{3,2,1,0:T(8,128)(2,1)S(1)}, bf16[2,4,64,1024]{3,2,1,0:T(8,128)(2,1)}, u32[]{:S(2)}, u32[]{:S(2)}) collective-permute-start(bf16[2,4,64,1024]{3,2,1,0:T(8,128)(2,1)S(1)} %pad_maximum_fusion.7.refs_2_), channel_id=1, source_target_pairs={{0,4},{4,0},{8,12},{12,8},{16,20},{20,16},{24,28},{28,24},{1,5},{5... | collective-permute-start | bytes 3145736 | tf_op jit(solution)/shard_map/ppermute | solution.py:277
  270.6 24.3 %collective-permute-start.37 = (bf16[2,4,64,1024]{3,2,1,0:T(8,128)(2,1)S(1)}, bf16[2,4,64,1024]{3,2,1,0:T(8,128)(2,1)S(1)}, u32[]{:S(2)}, u32[]{:S(2)}) collective-permute-start(bf16[2,4,64,1024]{3,2,1,0:T(8,128)(2,1)S(1)} %pad_maximum_fusion.7.refs_2_), channel_id=1, source_target_pairs={{0,1},{1,0},{2,3},{3,2},{4,5},{5,4},{6,7},{7,6},{8,9},{9,8},{10,11... | collective-permute-start | bytes 3145736 | tf_op jit(solution)/shard_map/ppermute | solution.py:285
  296.9 2.9 collective-permute-start.40
  297.2 4.1 collective-permute-start.41
  375.2 2.7 collective-permute-start.44
  375.6 3.8 collective-permute-start.45
  377.0 66.3 %collective-permute-start.42 = (bf16[256,1024]{1,0:T(8,128)(2,1)}, bf16[256,1024]{1,0:T(8,128)(2,1)S(1)}, u32[]{:S(2)}, u32[]{:S(2)}) collective-permute-start(bf16[256,1024]{1,0:T(8,128)(2,1)} %broadcast_select_fusion.2), channel_id=1, source_target_pairs={{2,0},{3,1},{1,2},{0,3},{6,4},{7,5},{5,6},{4,7},{10,8},{11,9},{9,1... | collective-permute-start | bytes 1572872 | tf_op jit(solution)/shard_map/ppermute | solution.py:223
  442.7 5.3 %collective-permute-start.46 = (bf16[512,1024]{1,0:T(8,128)(2,1)S(1)}, bf16[512,1024]{1,0:T(8,128)(2,1)S(1)}, u32[]{:S(2)}, u32[]{:S(2)}) collective-permute-start(bf16[512,1024]{1,0:T(8,128)(2,1)S(1)} %get-tuple-element.662), channel_id=1, source_target_pairs={{0,1},{1,0},{2,3},{3,2},{4,5},{5,4},{6,7},{7,6},{8,9},{9,8},{10,11... | collective-permute-start | bytes 3145736 | tf_op jit(solution)/shard_map/ppermute | solution.py:255
  443.2 4.8 collective-permute-start.47
  443.4 3.5 collective-permute-start.43
  446.4 18.6 %collective-permute-start.51 = (bf16[16,16,896]{2,1,0:T(8,128)(2,1)}, bf16[16,16,896]{2,1,0:T(8,128)(2,1)}, u32[]{:S(2)}, u32[]{:S(2)}) collective-permute-start(bf16[16,16,896]{2,1,0:T(8,128)(2,1)} %slice_bitcast_fusion.3), channel_id=1, source_target_pairs={{0,1},{1,0},{2,3},{3,2},{4,5},{5,4},{6,7},{7,6},{8,9},{9,8},{10,11... | collective-permute-start | bytes 1376264 | tf_op jit(solution)/shard_map/ppermute | solution.py:1044
  464.8 2.3 collective-permute-start.50
  467.8 12.7 %all-to-all-start.1 = ((bf16[16,16,128]{2,1,0:T(8,128)(2,1)}), bf16[16,16,128]{2,1,0:T(8,128)(2,1)S(1)}, u32[]{:S(2)}, u32[]{:S(2)}) async-start(bf16[16,16,128]{2,1,0:T(8,128)(2,1)} %fusion.3), calls=%async_computation.1 | async-start | bytes 131072 | tf_op jit(solution)/shard_map/all_to_all | solution.py:1045
  473.7 29.0 %collective-permute-start.48 = (bf16[256,1024]{1,0:T(8,128)(2,1)}, bf16[256,1024]{1,0:T(8,128)(2,1)}, u32[]{:S(2)}, u32[]{:S(2)}) collective-permute-start(bf16[256,1024]{1,0:T(8,128)(2,1)} %broadcast_select_fusion.1), channel_id=1, source_target_pairs={{2,0},{3,1},{1,2},{0,3},{6,4},{7,5},{5,6},{4,7},{10,8},{11,9},{9,1... | collective-permute-start | bytes 1572872 | tf_op jit(solution)/shard_map/ppermute | solution.py:223
  480.5 17.3 %all-to-all-start.2 = ((bf16[16,16,896]{2,1,0:T(8,128)(2,1)}), bf16[16,16,896]{2,1,0:T(8,128)(2,1)}, u32[]{:S(2)}, u32[]{:S(2)}) async-start(bf16[16,16,896]{2,1,0:T(8,128)(2,1)} %fusion), calls=%async_computation.2 | async-start | bytes 917504 | tf_op jit(solution)/shard_map/all_to_all | solution.py:1045
  502.9 3.0 collective-permute-start.49
  (102 other events, 483.4 us)
Sparse Core Ops, SparseCore 0:
  10.9 156.5 all-gather.5
  170.4 97.2 all-gather.3

commit v4 on v3

--- a/solution.py
+++ b/solution.py
@@ -204,25 +204,41 @@
     return query_grad, others[:pieces], others[pieces:]
 
 
-def spread_tokens(pair, below, count):
+def spread_across(pair, below, count):
     half = count // 2
     across = [(b, half + b if b < half else count - 1 - b) for b in range(count)]
-    inside = [(b, half + count - 1 - b) for b in range(half, count)]
-    got = lax.ppermute(jnp.where(below, pair[1], pair[0]), CTX, across)
-    other = lax.ppermute(pair[1], CTX, inside)
+    return lax.ppermute(jnp.where(below, pair[1], pair[0]), CTX, across)
+
+
+def spread_inside(pair, count):
+    half = count // 2
+    return lax.ppermute(pair[1], CTX, [(b, half + count - 1 - b) for b in range(half, count)])
+
+
+def joined_tokens(pair, got, other, below):
     return jnp.concatenate(
         [jnp.where(below, pair[0], got), jnp.where(below, got, other)], axis=0
     )
 
 
-def collect_tokens(rows, below, count):
+def spread_tokens(pair, below, count):
+    return joined_tokens(pair, spread_across(pair, below, count), spread_inside(pair, count), below)
+
+
+def send_across(rows, below, count):
     half = count // 2
     across = [(half + b if b < half else count - 1 - b, b) for b in range(count)]
+    return lax.ppermute(jnp.where(below, rows[BLK:], rows[:BLK]), CTX, across)
+
+
+def send_inside(rows, count):
+    half = count // 2
     inside = [(half + count - 1 - b, b) for b in range(half, count)]
-    early, late = rows[:BLK], rows[BLK:]
-    got = lax.ppermute(jnp.where(below, late, early), CTX, across)
-    other = lax.ppermute(late, CTX, inside)
-    return jnp.stack([jnp.where(below, early, got), jnp.where(below, got, other)])
+    return lax.ppermute(rows[BLK:], CTX, inside)
+
+
+def collect_tokens(rows, got, other, below):
+    return jnp.stack([jnp.where(below, rows[:BLK], got), jnp.where(below, got, other)])
 
 
 def collect_own(rows, below):
@@ -386,7 +402,6 @@
     advance(v.h)
     v.current = v.tokens.astype(wide)
     del v.tokens
-    v.cotangent = spread_tokens(cotangent, below, count)
     attention_step(v.current, (PIECES, weights_f()), v.picked[0], 0)
     v.middle = output_step(v.current, (PIECES, weights_f()), v.picked[0], 0)
     del v.current
@@ -405,6 +420,7 @@
     del v.h_half, v.h_cross
     v.h_far = cross_other(v.h_near)
     v.h_near_other = swapped(v.h_near)
+    v.cotangent_other = spread_inside(cotangent, count)
     attention_step(v.current, (PIECES, weights_g()), v.picked[1], 1)
     v.middle = output_step(v.current, (PIECES, weights_g()), v.picked[1], 1)
     del v.current
@@ -412,12 +428,15 @@
     v = sync(v)
     kept[:] = v.kept
     v.h_far_other = swapped(v.h_far)
+    cotangent_got = spread_across(cotangent, below, count)
     frozen = [
         ((PIECES, weights_f()), (GATHERED, (first_feed,))),
         ((PIECES, weights_g()), (MIXED, (*weights_h(), second_reduce))),
     ]
     current = feed_step(v.middle, frozen[1][1], v.picked[1], 1)
-    return current, v.cotangent.astype(wide), v.picked, frozen
+    current, cotangent_got = sync((current, cotangent_got))
+    cotangent = joined_tokens(cotangent, cotangent_got, v.cotangent_other, below)
+    return current, cotangent.astype(wide), v.picked, frozen
 
 
 SQUARE = (4, 2, 2, 2, 32, 1024)
@@ -468,8 +487,9 @@
     return held[...].reshape(1024, 1024)
 
 
-TILE = 256
-STRIP = 32
+QKV_TILE, OUTPUT_TILE, FEED_TILE, FEED_BACK_TILE, OUTPUT_BACK_TILE, TURN_TILE, QKV_BACK_TILE = 0, 0, 512, 512, 0, 0, 0
+STRIP = 64
+QKV_ROWS, OUTPUT_ROWS, QKV_BACK_ROWS, FEED_BACK_ROWS = 256, 256, 256, 256
 COLUMNS = 1024
 
 
@@ -478,7 +498,7 @@
         body(pl.ds(pl.multiple_of(index * STRIP, STRIP), STRIP))
         return carry
 
-    lax.fori_loop(0, count // STRIP, step, 0)
+    lax.fori_loop(0, count // STRIP, step, 0, unroll=True)
 
 
 def normalize_rows(values, gain, shift):
@@ -496,55 +516,102 @@
     return scale * (scaled - first - unit * second)
 
 
+def store_norm(values_ref, gain_ref, shift_ref, normed_ref, unit_ref, scale_ref):
+    def norm(rows):
+        unit, scale, normed = normalize_rows(values_ref[rows, :], gain_ref[...], shift_ref[...])
+        normed_ref[rows, :] = normed.astype(low_type)
+        unit_ref[rows, :] = unit.astype(low_type)
+        scale_ref[rows, :] = jnp.broadcast_to(scale, (STRIP, 128))
+
+    strips(values_ref.shape[0], norm)
+
+
+def store_pull(out_ref, grad_ref, inner_ref, unit_ref, scale_ref, gain_ref):
+    def pull(rows):
+        out_ref[rows, :] = grad_ref[rows, :] + normalize_pull(
+            inner_ref[rows, :], unit_ref[rows, :].astype(wide), scale_ref[rows, :1], gain_ref[...]
+        )
+
+    strips(out_ref.shape[0], pull)
+
+
+def row_tiles(count, size):
+    return [slice(first, first + size) for first in range(0, count, size)]
+
+
+def span(part):
+    return slice(part * COLUMNS, (part + 1) * COLUMNS)
+
+
+TILED = [False]
+
+
+def at_first(body):
+    if TILED[0]:
+        pl.when(pl.program_id(0) == 0)(body)
+    else:
+        body()
+
+
+def at_last(body):
+    if TILED[0]:
+        pl.when(pl.program_id(0) == pl.num_programs(0) - 1)(body)
+    else:
+        body()
+
+
+def await_first(held, arrived):
+    at_first(lambda: wait_for(held, arrived))
+
+
+def gather_sum(total, step_value):
+    @at_first
+    def _():
+        total[...] = step_value
+
+    if TILED[0]:
+
+        @pl.when(pl.program_id(0) > 0)
+        def _():
+            total[...] = total[...] + step_value
+
+
 def qkv_kernel(form, at_ref, x_ref, gain_ref, shift_ref, left_ref, right_ref, bias_ref, *refs):
     sources, (normed_ref, unit_ref, scale_ref, rank_ref, *outs) = refs[:-9], refs[-9:-2]
     held, arrived = refs[-2:]
-    for part in range(3):
-        fetch(form, at_ref, sources, square_unit(form, part), 32, held.at[part], arrived.at[part])
-
-    def norm(rows):
-        unit, scale, normed = normalize_rows(x_ref[rows, :], gain_ref[...], shift_ref[...])
-        normed_ref[rows, :] = normed.astype(low_type)
-        unit_ref[rows, :] = unit.astype(low_type)
-        scale_ref[rows, :] = jnp.broadcast_to(scale, (STRIP, 128))
-
-    strips(x_ref.shape[0], norm)
+
+    @at_first
+    def _():
+        for part in range(3):
+            fetch(form, at_ref, sources, square_unit(form, part), 32, held.at[part], arrived.at[part])
+
+    store_norm(x_ref, gain_ref, shift_ref, normed_ref, unit_ref, scale_ref)
     rank_ref[...] = times(normed_ref[...], left_ref[...], ROWS_BY_ROWS).astype(low_type)
     for part, out in enumerate(outs):
-        wait_for(held.at[part], arrived.at[part])
-        columns = slice(part * COLUMNS, (part + 1) * COLUMNS)
-        for first in range(0, x_ref.shape[0], TILE):
-            rows = slice(first, first + TILE)
+        await_first(held.at[part], arrived.at[part])
+        for rows in row_tiles(out.shape[0], QKV_ROWS):
             out[rows, :] = (
                 times(normed_ref[rows, :], square(held.at[part]))
-                + times(rank_ref[rows, :], right_ref[:, columns])
-                + bias_ref[:, columns]
+                + times(rank_ref[rows, :], right_ref[:, span(part)])
+                + bias_ref[:, span(part)]
             ).astype(low_type)
 
 
 def output_kernel(form, at_ref, x_ref, attended_ref, left_ref, right_ref, bias_ref, gain_ref, shift_ref, *refs):
     sources, (low_ref, middle_ref, normed_ref, unit_ref, scale_ref, rank_ref) = refs[:-8], refs[-8:-2]
     held, arrived = refs[-2:]
-    fetch(form, at_ref, sources, square_unit(form, 3), 32, held, arrived)
+    at_first(lambda: fetch(form, at_ref, sources, square_unit(form, 3), 32, held, arrived))
     low_ref[...] = attended_ref[...].astype(low_type)
     rank_ref[...] = times(low_ref[...], left_ref[...], ROWS_BY_ROWS).astype(low_type)
-    wait_for(held, arrived)
-    for first in range(0, x_ref.shape[0], TILE):
-        rows = slice(first, first + TILE)
+    await_first(held, arrived)
+    for rows in row_tiles(x_ref.shape[0], OUTPUT_ROWS):
         middle_ref[rows, :] = (
             x_ref[rows, :]
             + times(low_ref[rows, :], square(held))
             + times(rank_ref[rows, :], right_ref[...])
             + bias_ref[...]
         )
-
-    def norm(rows):
-        unit, scale, normed = normalize_rows(middle_ref[rows, :], gain_ref[...], shift_ref[...])
-        normed_ref[rows, :] = normed.astype(low_type)
-        unit_ref[rows, :] = unit.astype(low_type)
-        scale_ref[rows, :] = jnp.broadcast_to(scale, (STRIP, 128))
-
-    strips(x_ref.shape[0], norm)
+    store_norm(middle_ref, gain_ref, shift_ref, normed_ref, unit_ref, scale_ref)
 
 
 def fetch_feed_forward(form, at_ref, sources, expand, reduce, arrived, reduce_first):
@@ -563,36 +630,31 @@
 ):
     sources, (result_ref, slope_ref, active_ref, rank_expand_ref, rank_reduce_ref) = refs[:-9], refs[-9:-4]
     expand, reduce, rank_sum, arrived = refs[-4:]
-    fetch_feed_forward(form, at_ref, sources, expand, reduce, arrived, False)
-    count = normed_ref.shape[0]
+    at_first(lambda: fetch_feed_forward(form, at_ref, sources, expand, reduce, arrived, False))
     rank_expand_ref[...] = times(normed_ref[...], expand_left_ref[...], ROWS_BY_ROWS).astype(low_type)
     result_ref[...] = middle_ref[...] + reduce_bias_ref[...]
     rank_sum[...] = jnp.zeros_like(rank_sum)
 
     def part_step(part, carry):
         columns = pl.ds(pl.multiple_of(part * COLUMNS, COLUMNS), COLUMNS)
-        wait_for(expand.at[part], arrived.at[0, part])
-        wait_for(reduce.at[part], arrived.at[1, part])
-        for first in range(0, count, TILE):
-            rows = slice(first, first + TILE)
-            value = (
-                times(normed_ref[rows, :], square(expand.at[part]))
-                + times(rank_expand_ref[rows, :], expand_right_ref[:, columns])
-                + expand_bias_ref[:, columns]
-            )
-            squared = value * value
-            bent = jnp.tanh(root_factor * value * (1.0 + 0.044715 * squared))
-            half = 0.5 * (1.0 + bent)
-            slope_ref[rows, columns] = (
-                half
-                + 0.5 * value * (1.0 - bent * bent) * (root_factor + 3 * 0.044715 * root_factor * squared)
-            ).astype(low_type)
-            active = (value * half).astype(low_type)
-            active_ref[rows, columns] = active
-            result_ref[rows, :] = result_ref[rows, :] + times(active, square(reduce.at[part]))
-            rank_sum[rows, :] = rank_sum[rows, :] + times(
-                active, reduce_left_ref[:, columns], ROWS_BY_ROWS
-            )
+        await_first(expand.at[part], arrived.at[0, part])
+        await_first(reduce.at[part], arrived.at[1, part])
+        value = (
+            times(normed_ref[...], square(expand.at[part]))
+            + times(rank_expand_ref[...], expand_right_ref[:, columns])
+            + expand_bias_ref[:, columns]
+        )
+        squared = value * value
+        bent = jnp.tanh(value * (root_factor + 0.044715 * root_factor * squared))
+        half = 0.5 + 0.5 * bent
+        slope_ref[:, columns] = (
+            half
+            + value * (0.5 - 0.5 * bent * bent) * (root_factor + 3 * 0.044715 * root_factor * squared)
+        ).astype(low_type)
+        active = (value * half).astype(low_type)
+        active_ref[:, columns] = active
+        result_ref[...] = result_ref[...] + times(active, square(reduce.at[part]))
+        rank_sum[...] = rank_sum[...] + times(active, reduce_left_ref[:, columns], ROWS_BY_ROWS)
         return carry
 
     lax.fori_loop(0, 4, part_step, 0)
@@ -604,118 +666,167 @@
     form, at_ref, grad_ref, slope_ref, active_ref, normed_ref, unit_ref, scale_ref, rank_expand_ref, rank_reduce_ref,
     gain_ref, expand_left_ref, expand_right_ref, reduce_left_ref, reduce_right_ref, *refs,
 ):
-    sources, (out_ref, expand_left_g, expand_right_g, reduce_left_g, reduce_right_g) = refs[:-13], refs[-13:-8]
-    expand, reduce, arrived, low_grad, turned, bent, total, turn_sum = refs[-8:]
-    fetch_feed_forward(form, at_ref, sources, expand, reduce, arrived, True)
-    count = grad_ref.shape[0]
+    sources, (out_ref, *grads) = refs[:-17], refs[-17:-12]
+    expand, reduce, arrived, low_grad, turned, bent, total, turn_sum, *sums = refs[-12:]
+    expand_left_sum, expand_right_sum, reduce_left_sum, reduce_right_sum = sums
+    at_first(lambda: fetch_feed_forward(form, at_ref, sources, expand, reduce, arrived, True))
+
+    @at_first
+    def _():
+        for member in sums:
+            member[...] = jnp.zeros_like(member)
+
     low_grad[...] = grad_ref[...].astype(low_type)
     turned[...] = times(low_grad[...], reduce_right_ref[...], ROWS_BY_ROWS).astype(low_type)
-    reduce_right_g[...] = times(rank_reduce_ref[...], low_grad[...], COLS_BY_COLS).astype(low_type)
+    reduce_right_sum[...] = reduce_right_sum[...] + times(rank_reduce_ref[...], low_grad[...], COLS_BY_COLS)
     total[...] = jnp.zeros_like(total)
     turn_sum[...] = jnp.zeros_like(turn_sum)
 
     def part_step(part, carry):
         columns = pl.ds(pl.multiple_of(part * COLUMNS, COLUMNS), COLUMNS)
-        wait_for(reduce.at[part], arrived.at[1, part])
-        wait_for(expand.at[part], arrived.at[0, part])
-        for first in range(0, count, TILE):
-            rows = slice(first, first + TILE)
+        await_first(reduce.at[part], arrived.at[1, part])
+        await_first(expand.at[part], arrived.at[0, part])
+        for rows in row_tiles(grad_ref.shape[0], FEED_BACK_ROWS):
             grad_active = times(low_grad[rows, :], square(reduce.at[part]), ROWS_BY_ROWS) + times(
                 turned[rows, :], reduce_left_ref[:, columns]
             )
-            grad_expand = (grad_active * slope_ref[rows, columns].astype(wide)).astype(low_type)
-            bent[rows, :] = grad_expand
-            total[rows, :] = total[rows, :] + times(grad_expand, square(expand.at[part]), ROWS_BY_ROWS)
-            turn_sum[rows, :] = turn_sum[rows, :] + times(
-                grad_expand, expand_right_ref[:, columns], ROWS_BY_ROWS
-            )
-        reduce_left_g[:, columns] = times(turned[...], active_ref[:, columns], COLS_BY_COLS).astype(
-            low_type
-        )
-        expand_right_g[:, columns] = times(rank_expand_ref[...], bent[...], COLS_BY_COLS).astype(low_type)
+            bent[rows, :] = (grad_active * slope_ref[rows, columns].astype(wide)).astype(low_type)
+            total[rows, :] = total[rows, :] + times(bent[rows, :], square(expand.at[part]), ROWS_BY_ROWS)
+        grad_expand = bent[...]
+        turn_sum[...] = turn_sum[...] + times(grad_expand, expand_right_ref[:, columns], ROWS_BY_ROWS)
+        reduce_left_sum[:, columns] = reduce_left_sum[:, columns] + times(
+            turned[...], active_ref[:, columns], COLS_BY_COLS
+        )
+        expand_right_sum[:, columns] = expand_right_sum[:, columns] + times(
+            rank_expand_ref[...], grad_expand, COLS_BY_COLS
+        )
         return carry
 
     lax.fori_loop(0, 4, part_step, 0)
     turned[...] = turn_sum[...].astype(low_type)
-    expand_left_g[...] = times(turned[...], normed_ref[...], COLS_BY_COLS).astype(low_type)
+    expand_left_sum[...] = expand_left_sum[...] + times(turned[...], normed_ref[...], COLS_BY_COLS)
     total[...] = total[...] + times(turned[...], expand_left_ref[...])
-
-    def pull(rows):
-        out_ref[rows, :] = grad_ref[rows, :] + normalize_pull(
-            total[rows, :], unit_ref[rows, :].astype(wide), scale_ref[rows, :1], gain_ref[...]
-        )
-
-    strips(count, pull)
+    store_pull(out_ref, grad_ref, total, unit_ref, scale_ref, gain_ref)
+
+    @at_last
+    def _():
+        for member, summed in zip(grads, sums):
+            member[...] = summed[...].astype(low_type)
 
 
 def output_backward_kernel(form, at_ref, grad_ref, attended_ref, rank_ref, left_ref, right_ref, *refs):
     sources, (out_ref, left_g, right_g) = refs[:-7], refs[-7:-4]
-    held, arrived, low_grad, turned = refs[-4:]
-    fetch(form, at_ref, sources, square_unit(form, 3), 32, held, arrived)
-    low_grad[...] = grad_ref[...].astype(low_type)
-    turned[...] = times(low_grad[...], right_ref[...], ROWS_BY_ROWS).astype(low_type)
-    right_g[...] = times(rank_ref[...], low_grad[...], COLS_BY_COLS).astype(low_type)
-    left_g[...] = times(turned[...], attended_ref[...], COLS_BY_COLS).astype(low_type)
-    wait_for(held, arrived)
-    for first in range(0, grad_ref.shape[0], TILE):
-        rows = slice(first, first + TILE)
-        out_ref[rows, :] = (
-            times(low_grad[rows, :], square(held), ROWS_BY_ROWS) + times(turned[rows, :], left_ref[...])
-        ).astype(low_type)
+    held, arrived, left_sum, right_sum = refs[-4:]
+    at_first(lambda: fetch(form, at_ref, sources, square_unit(form, 3), 32, held, arrived))
+    low_grad = grad_ref[...].astype(low_type)
+    turned = times(low_grad, right_ref[...], ROWS_BY_ROWS).astype(low_type)
+    gather_sum(right_sum, times(rank_ref[...], low_grad, COLS_BY_COLS))
+    gather_sum(left_sum, times(turned, attended_ref[...], COLS_BY_COLS))
+    await_first(held, arrived)
+    out_ref[...] = (
+        times(low_grad, square(held), ROWS_BY_ROWS) + times(turned, left_ref[...])
+    ).astype(low_type)
+
+    @at_last
+    def _():
+        left_g[...] = left_sum[...].astype(low_type)
+        right_g[...] = right_sum[...].astype(low_type)
+
+
+def qkv_turn_kernel(pieces, form, at_ref, normed_ref, rank_ref, dq_ref, *refs):
+    dk_refs, dv_refs, (right_ref, *refs) = refs[:pieces], refs[pieces : 2 * pieces], refs[2 * pieces :]
+    dk_ref, dv_ref, turned_ref, left_g, right_g, left_sum, right_sum = refs
+    dk_ref[...] = add_up([member[...] for member in dk_refs])
+    dv_ref[...] = add_up([member[...] for member in dv_refs])
+    grads = (dq_ref, dk_ref, dv_ref)
+    turned = sum(
+        times(grads[part][...], right_ref[:, span(part)], ROWS_BY_ROWS) for part in range(3)
+    ).astype(low_type)
+    turned_ref[...] = turned
+    gather_sum(left_sum, times(turned, normed_ref[...], COLS_BY_COLS))
+    for part in range(3):
+        gather_sum(right_sum.at[part], times(rank_ref[...], grads[part][...], COLS_BY_COLS))
+
+    @at_last
+    def _():
+        left_g[...] = left_sum[...].astype(low_type)
+        for part in range(3):
+            right_g[:, span(part)] = right_sum[part].astype(low_type)
 
 
 def qkv_backward_kernel(
-    pieces, form, at_ref, grad_ref, normed_ref, unit_ref, scale_ref, rank_ref, gain_ref, left_ref, right_ref, dq_ref, *refs
+    form, at_ref, grad_ref, unit_ref, scale_ref, turned_ref, dq_ref, dk_ref, dv_ref, gain_ref, left_ref, *refs
 ):
-    dk_refs, dv_refs, refs = refs[:pieces], refs[pieces : 2 * pieces], refs[2 * pieces :]
+    sources, out_ref, (held, arrived, total) = refs[:-4], refs[-4], refs[-3:]
+
+    @at_first
+    def _():
+        for part in range(3):
+            fetch(form, at_ref, sources, square_unit(form, part), 32, held.at[part], arrived.at[part])
+
+    total[...] = times(turned_ref[...], left_ref[...])
+    for part, member in enumerate((dq_ref, dk_ref, dv_ref)):
+        await_first(held.at[part], arrived.at[part])
+        for rows in row_tiles(out_ref.shape[0], QKV_BACK_ROWS):
+            total[rows, :] = total[rows, :] + times(member[rows, :], square(held.at[part]), ROWS_BY_ROWS)
+    store_pull(out_ref, grad_ref, total, unit_ref, scale_ref, gain_ref)
+
+
+def qkv_whole_kernel(
+    pieces, form, at_ref, grad_ref, unit_ref, scale_ref, normed_ref, rank_ref, dq_ref, *refs
+):
+    dk_refs, dv_refs, (gain_ref, left_ref, right_ref, *refs) = refs[:pieces], refs[pieces : 2 * pieces], refs[2 * pieces :]
     sources, (out_ref, left_g, right_g) = refs[:-9], refs[-9:-6]
     held, arrived, turned, total, dk_ref, dv_ref = refs[-6:]
-    count = grad_ref.shape[0]
     for part in range(3):
         fetch(form, at_ref, sources, square_unit(form, part), 32, held.at[part], arrived.at[part])
     dk_ref[...] = add_up([member[...] for member in dk_refs])
     dv_ref[...] = add_up([member[...] for member in dv_refs])
     grads = (dq_ref, dk_ref, dv_ref)
-    spans = [slice(part * COLUMNS, (part + 1) * COLUMNS) for part in range(3)]
     turned[...] = sum(
-        times(grads[part][...], right_ref[:, spans[part]], ROWS_BY_ROWS) for part in range(3)
+        times(grads[part][...], right_ref[:, span(part)], ROWS_BY_ROWS) for part in range(3)
     ).astype(low_type)
     for part in range(3):
-        right_g[:, spans[part]] = times(rank_ref[...], grads[part][...], COLS_BY_COLS).astype(low_type)
+        right_g[:, span(part)] = times(rank_ref[...], grads[part][...], COLS_BY_COLS).astype(low_type)
     left_g[...] = times(turned[...], normed_ref[...], COLS_BY_COLS).astype(low_type)
-    for part in range(3):
+    for part, member in enumerate(grads):
         wait_for(held.at[part], arrived.at[part])
-        for first in range(0, count, TILE):
-            rows = slice(first, first + TILE)
-            value = times(grads[part][rows, :], square(held.at[part]), ROWS_BY_ROWS)
-            if part == 0:
-                total[rows, :] = value + times(turned[rows, :], left_ref[...])
-            else:
-                total[rows, :] = total[rows, :] + value
-
-    def pull(rows):
-        out_ref[rows, :] = grad_ref[rows, :] + normalize_pull(
-            total[rows, :], unit_ref[rows, :].astype(wide), scale_ref[rows, :1], gain_ref[...]
-        )
-
-    strips(count, pull)
-
-
-def frozen_call(kernel, name, at, weights, members, outs, scratch, cost):
+        for rows in row_tiles(out_ref.shape[0], QKV_BACK_ROWS):
+            value = times(member[rows, :], square(held.at[part]), ROWS_BY_ROWS)
+            before = total[rows, :] if part else times(turned[rows, :], left_ref[...])
+            total[rows, :] = before + value
+    store_pull(out_ref, grad_ref, total, unit_ref, scale_ref, gain_ref)
+
+
+def frozen_call(kernel, name, at, weights, tile, tiled, fixed, outs, fixed_outs, scratch, cost):
     form, sources = weights
-    local_spec = pl.BlockSpec(memory_space=pltpu.VMEM)
+    count = tiled[0].shape[0]
+    TILED[0] = tile > 0
+
+    def by_rows(shape):
+        if tile == 0:
+            return pl.BlockSpec(memory_space=pltpu.VMEM)
+        return pl.BlockSpec((tile, shape[1]), lambda step: (step, 0))
+
+    def every(shape):
+        if tile == 0:
+            return pl.BlockSpec(memory_space=pltpu.VMEM)
+        return pl.BlockSpec(shape, lambda step: (0, 0))
+
     return pl.pallas_call(
         functools.partial(kernel, form),
-        out_shape=tuple(jax.ShapeDtypeStruct(shape, kind) for shape, kind in outs),
+        grid=(count // tile,) if tile else (),
+        out_shape=tuple(jax.ShapeDtypeStruct(shape, kind) for shape, kind in (*outs, *fixed_outs)),
         in_specs=[pl.BlockSpec(memory_space=pltpu.SMEM)]
-        + [local_spec] * len(members)
+        + [by_rows(member.shape) for member in tiled]
+        + [every(member.shape) for member in fixed]
         + [pl.BlockSpec(memory_space=pl.ANY)] * len(sources),
-        out_specs=(local_spec,) * len(outs),
+        out_specs=tuple(by_rows(shape) for shape, _ in outs) + tuple(every(shape) for shape, _ in fixed_outs),
         scratch_shapes=scratch,
-        compiler_params=pltpu.CompilerParams(vmem_limit_bytes=56 * 2**20),
+        compiler_params=pltpu.CompilerParams(vmem_limit_bytes=60 * 2**20),
         cost_estimate=pl.CostEstimate(flops=cost * MICROSECOND, bytes_accessed=0, transcendentals=0),
         name=name,
-    )(at, *members, *sources)
+    )(at, *tiled, *fixed, *sources)
 
 
 def row(vector):
@@ -726,8 +837,6 @@
 
 
 PACKED = ((5, 0), (6, 128), (1, 256), (0, 352), (2, 384), (3, 416), (4, 448), (7, 480))
-PACKED_EARLY = ((5, 0), (6, 128), (2, 256), (3, 288), (4, 320), (7, 352))
-PACKED_LATE = ((1, 0), (0, 96))
 
 
 def unpack_kernel(order, at_ref, own_ref, other_ref, *outs):
@@ -808,9 +917,9 @@
     full_low = ((rows, columns), LOW)
     bias = jnp.concatenate([extras[0][:columns], jnp.zeros((columns,), WIDE), extras[0][columns:]])
     return frozen_call(
-        qkv_kernel, "qkv_forward", at, weights,
-        (current, row(extras[4]), row(extras[5]), picked[0], picked[1], row(bias)),
-        (full_low, full_low, ((rows, 128), WIDE), ((rows, RANK), LOW), full_low, full_low, full_low),
+        qkv_kernel, "qkv_forward", at, weights, QKV_TILE, (current,),
+        (row(extras[4]), row(extras[5]), picked[0], picked[1], row(bias)),
+        (full_low, full_low, ((rows, 128), WIDE), ((rows, RANK), LOW), full_low, full_low, full_low), (),
         [pltpu.VMEM((3, *SQUARE), LOW), DMA((3,))], 9,
     )
 
@@ -819,9 +928,9 @@
     rows, columns = current.shape
     full, full_low = ((rows, columns), WIDE), ((rows, columns), LOW)
     return frozen_call(
-        output_kernel, "output_forward", at, weights,
-        (current, attended, picked[2], picked[3], row(extras[1]), row(extras[6]), row(extras[7])),
-        (full_low, full, full_low, full_low, ((rows, 128), WIDE), ((rows, RANK), LOW)),
+        output_kernel, "output_forward", at, weights, OUTPUT_TILE, (current, attended),
+        (picked[2], picked[3], row(extras[1]), row(extras[6]), row(extras[7])),
+        (full_low, full, full_low, full_low, ((rows, 128), WIDE), ((rows, RANK), LOW)), (),
         [pltpu.VMEM(SQUARE, LOW), DMA], 8,
     )
 
@@ -830,11 +939,12 @@
     rows, columns = middle.shape
     tall, ranks = ((rows, picked[5].shape[1]), LOW), ((rows, RANK), LOW)
     return frozen_call(
-        feed_forward_kernel, "feed_forward", at, weights,
-        (normed, middle, picked[4], picked[5], row(extras[2]), picked[6], picked[7], row(extras[3])),
-        (((rows, columns), WIDE), tall, tall, ranks, ranks),
+        feed_forward_kernel, "feed_forward", at, weights, FEED_TILE, (normed, middle),
+        (picked[4], picked[5], row(extras[2]), picked[6], picked[7], row(extras[3])),
+        (((rows, columns), WIDE), tall, tall, ranks, ranks), (),
         [
-            pltpu.VMEM((4, *SQUARE), LOW), pltpu.VMEM(TALL, LOW), pltpu.VMEM((rows, RANK), WIDE), DMA((2, 4)),
+            pltpu.VMEM((4, *SQUARE), LOW), pltpu.VMEM(TALL, LOW), pltpu.VMEM((FEED_TILE or rows, RANK), WIDE),
+            DMA((2, 4)),
         ], 20,
     )
 
@@ -845,46 +955,105 @@
 
 def backward_feed(grad, kept, weights, picked, extras, at):
     rows, columns = grad.shape
-    full_low, ranks = pltpu.VMEM((rows, columns), LOW), pltpu.VMEM((rows, RANK), LOW)
+    tile = FEED_BACK_TILE or rows
     return frozen_call(
-        feed_backward_kernel, "feed_backward", at, weights,
+        feed_backward_kernel, "feed_backward", at, weights, FEED_BACK_TILE,
         (
             grad, kept.slope, kept.active, kept.normed_two, kept.unit_two, kept.scale_two,
-            kept.rank_expand, kept.rank_reduce, row(extras[6]), *picked[4:],
+            kept.rank_expand, kept.rank_reduce,
         ),
-        (((rows, columns), WIDE), *map(like, picked[4:])),
+        (row(extras[6]), *picked[4:]), (((rows, columns), WIDE),), tuple(map(like, picked[4:])),
         [
-            pltpu.VMEM((4, *SQUARE), LOW), pltpu.VMEM(TALL, LOW), DMA((2, 4)), full_low, ranks, full_low,
-            pltpu.VMEM((rows, columns), WIDE), pltpu.VMEM((rows, RANK), WIDE),
-        ], 22,
+            pltpu.VMEM((4, *SQUARE), LOW), pltpu.VMEM(TALL, LOW), DMA((2, 4)),
+            pltpu.VMEM((tile, columns), LOW), pltpu.VMEM((tile, RANK), LOW), pltpu.VMEM((tile, columns), LOW),
+            pltpu.VMEM((tile, columns), WIDE), pltpu.VMEM((tile, RANK), WIDE),
+        ]
+        + [pltpu.VMEM(member.shape, WIDE) for member in picked[4:]], 22,
     )
 
 
 def backward_output(grad, kept, weights, picked, at):
     rows, columns = grad.shape
     return frozen_call(
-        output_backward_kernel, "output_backward", at, weights,
-        (grad, kept.attended_low, kept.rank_output, picked[2], picked[3]),
-        (((rows, columns), LOW), like(picked[2]), like(picked[3])),
-        [pltpu.VMEM(SQUARE, LOW), DMA, pltpu.VMEM((rows, columns), LOW), pltpu.VMEM((rows, RANK), LOW)], 5,
+        output_backward_kernel, "output_backward", at, weights, OUTPUT_BACK_TILE,
+        (grad, kept.attended_low, kept.rank_output), (picked[2], picked[3]),
+        (((rows, columns), LOW),), (like(picked[2]), like(picked[3])),
+        [pltpu.VMEM(SQUARE, LOW), DMA, pltpu.VMEM(picked[2].shape, WIDE), pltpu.VMEM(picked[3].shape, WIDE)], 5,
     )
 
 
-def backward_qkv(grad, grads, kept, weights, picked, extras, at):
+def backward_turn(grads, kept, picked, at):
+    query_grad, key_grads, value_grads = grads
+    full_low = (query_grad.shape, LOW)
+    return frozen_call(
+        functools.partial(qkv_turn_kernel, len(key_grads)), "qkv_turn", at, (WHOLE, ()), TURN_TILE,
+        (kept.normed_one, kept.rank_attend, query_grad, *key_grads, *value_grads), (picked[1],),
+        (full_low, full_low, like(kept.rank_attend)), (like(picked[0]), like(picked[1])),
+        [pltpu.VMEM(picked[0].shape, WIDE), pltpu.VMEM((3, *picked[0].shape), WIDE)], 3,
+    )
+
+
+def backward_qkv_whole(grad, grads, kept, weights, picked, extras, at):
     rows, columns = grad.shape
     query_grad, key_grads, value_grads = grads
     return frozen_call(
-        functools.partial(qkv_backward_kernel, len(key_grads)), "qkv_backward", at, weights,
+        functools.partial(qkv_whole_kernel, len(key_grads)), "qkv_whole", at, weights, 0,
         (
-            grad, kept.normed_one, kept.unit_one, kept.scale_one, kept.rank_attend, row(extras[4]),
-            picked[0], picked[1], query_grad, *key_grads, *value_grads,
+            grad, kept.unit_one, kept.scale_one, kept.normed_one, kept.rank_attend, query_grad, *key_grads,
+            *value_grads,
         ),
-        (((rows, columns), WIDE), like(picked[0]), like(picked[1])),
+        (row(extras[4]), picked[0], picked[1]),
+        (((rows, columns), WIDE),), (like(picked[0]), like(picked[1])),
         [
             pltpu.VMEM((3, *SQUARE), LOW), DMA((3,)), pltpu.VMEM((rows, RANK), LOW),
             pltpu.VMEM((rows, columns), WIDE), pltpu.VMEM((rows, columns), LOW), pltpu.VMEM((rows, columns), LOW),
         ], 11,
     )
+
+
+def backward_qkv(grad, joined, turned, kept, weights, picked, extras, at):
+    rows, columns = grad.shape
+    return frozen_call(
+        qkv_backward_kernel, "qkv_backward", at, weights, QKV_BACK_TILE,
+        (grad, kept.unit_one, kept.scale_one, turned, *joined), (row(extras[4]), picked[0]),
+        (((rows, columns), WIDE),), (),
+        [pltpu.VMEM((3, *SQUARE), LOW), DMA((3,)), pltpu.VMEM((QKV_BACK_TILE or rows, columns), WIDE)], 9,
+    )[0]
+
+
+def combine_kernel(places, ids_ref, *refs):
+    count = len(places)
+    received, outs, total = refs[:count], refs[count:-1], refs[-1]
+    total[...] = jnp.zeros_like(total)
+    for source in range(received[0].shape[0]):
+        adapter, spot = ids_ref[source], 0
+        for member in received:
+            width = member.shape[2]
+            at = (adapter, slice(None), slice(spot, spot + width))
+            total[at] = total[at] + member[source].astype(wide)
+            spot += width
+    base = 0
+    for member, orders in zip(received, places):
+        for layer_index, order in orders:
+            for kind, _ in order:
+                size = outs[kind].shape[3]
+                outs[kind][layer_index] = total[:, :, base : base + size]
+                base += size
+
+
+def combine(ids, received, places, sizes):
+    local_spec = pl.BlockSpec(memory_space=pltpu.VMEM)
+    width = sum(member.shape[2] for member in received)
+    return pl.pallas_call(
+        functools.partial(combine_kernel, places),
+        out_shape=tuple(jax.ShapeDtypeStruct((LAYERS, ADAPTERS, RANK, size), wide) for size in sizes),
+        in_specs=[pl.BlockSpec(memory_space=pltpu.SMEM)] + [local_spec] * len(received),
+        out_specs=(local_spec,) * len(sizes),
+        scratch_shapes=[pltpu.VMEM((ADAPTERS, RANK, width), wide)],
+        compiler_params=pltpu.CompilerParams(vmem_limit_bytes=32 * 2**20),
+        cost_estimate=pl.CostEstimate(flops=3 * MICROSECOND, bytes_accessed=0, transcendentals=0),
+        name="combine",
+    )(ids, *received)
 
 
 class Bag:
@@ -1021,8 +1190,8 @@
             middle = output_step(current, first_weights, picked[layer_index], layer_index)
             current = feed_step(middle, second_weights, picked[layer_index], layer_index)
 
-    outputs = collect_tokens(current.astype(low_type), below, count)
-    owner_adapter = (lane_adapter[:, None] == jnp.arange(ADAPTERS)[None, :]).astype(wide)
+    result = current.astype(low_type)
+    result_got, result_other = send_across(result, below, count), send_inside(result, count)
     lanes = data_count * chips
 
     def to_owners(groups):
@@ -1042,48 +1211,69 @@
             )
             own, sent = jnp.where(core == 0, both[0], both[1]), jnp.where(core == 0, both[1], both[0])
         total = add_up([own, lax.ppermute(sent, "core", SWAP)])
-        received = lax.all_to_all(total, LANE, split_axis=0, concat_axis=0, tiled=True)
-        return jnp.einsum(
-            "sa,srp->arp", owner_adapter, received.astype(wide), precision=lax.Precision.HIGHEST
-        )
+        return lax.all_to_all(total, LANE, split_axis=0, concat_axis=0, tiled=True)
 
     terms = [None] * LAYERS
-    summed = []
     for layer_index in reversed(range(LAYERS)):
         keep, extra, factors = kept[layer_index], extras[layer_index], picked[layer_index]
         first_weights, second_weights = frozen[layer_index]
         middle_grad, *feed_terms = backward_feed(grad_current, keep, second_weights, factors, extra, at)
+        if layer_index == LAYERS - 1:
+            middle_grad, feed_terms, result_got = sync((middle_grad, feed_terms, result_got))
         attended_grad, *output_terms = backward_output(middle_grad, keep, first_weights, factors, at)
-        if layer_index == 0:
-            terms[0] = [None, None, *output_terms, *feed_terms]
-            summed.append(to_owners([(PACKED, terms[1]), (PACKED_EARLY, terms[0])]))
         query_grad, key_grads, value_grads = attend_backward(
             place, keep.queries, keep.keys, keep.values, attended_grad, keep.attended, keep.stat
         )
+        if layer_index == LAYERS - 1:
+            query_grad, key_grads, value_grads, result_other = sync(
+                (query_grad, key_grads, value_grads, result_other)
+            )
         grads = (
             query_grad,
             [key_grads[0], *ring_scatter(key_grads, count)],
             [value_grads[0], *ring_scatter(value_grads, count)],
         )
-        grad_current, *attend_terms = backward_qkv(
-            middle_grad, grads, keep, first_weights, factors, extra, at
-        )
+        if layer_index > 0:
+            grad_current, *attend_terms = backward_qkv_whole(
+                middle_grad, grads, keep, first_weights, factors, extra, at
+            )
+            terms[layer_index] = [*attend_terms, *output_terms, *feed_terms]
+            continue
+        key_grad, value_grad, turned, *attend_terms = backward_turn(grads, keep, factors, at)
         terms[layer_index] = [*attend_terms, *output_terms, *feed_terms]
-    summed.append(to_owners([(PACKED_LATE, terms[0])]))
-    found = [[None] * len(sizes) for _ in range(LAYERS)]
-    for held, orders in zip(summed, (((1, PACKED), (0, PACKED_EARLY)), ((0, PACKED_LATE),))):
-        spot = 0
-        for layer_index, order in orders:
-            for kind, _ in order:
-                found[layer_index][kind] = held[:, :, spot : spot + sizes[kind]]
-                spot += sizes[kind]
-    results = [
-        jnp.swapaxes(jnp.stack([found[layer_index][kind] for layer_index in range(LAYERS)]), 2, 3)
-        for kind in range(len(sizes))
-    ]
-    moved = collect_tokens(grad_current.astype(low_type), below, count)
+        received = to_owners([(PACKED, terms[1]), (PACKED, terms[0])])
+        grad_current = backward_qkv(
+            middle_grad, (query_grad, key_grad, value_grad), turned, keep, first_weights, factors, extra, at
+        )
+        received, grad_current = sync((received, grad_current))
+    low_grad = grad_current.astype(low_type)
+    moved = collect_tokens(low_grad, send_across(low_grad, below, count), send_inside(low_grad, count), below)
     kept_part = collect_own(grad_current, below)
-    return (outputs, jnp.where(kept_part[0], kept_part[1], moved.astype(wide)), *results)
+    received = [received]
+    places = (((1, PACKED), (0, PACKED)),)
+    if linked:
+        results = combine(lane_adapter, received, places, sizes)
+    else:
+        owner_adapter = (lane_adapter[:, None] == jnp.arange(ADAPTERS)[None, :]).astype(wide)
+        found = [[None] * len(sizes) for _ in range(LAYERS)]
+        for held, orders in zip(received, places):
+            summed = jnp.einsum(
+                "sa,srp->arp", owner_adapter, held.astype(wide), precision=lax.Precision.HIGHEST
+            )
+            spot = 0
+            for layer_index, order in orders:
+                for kind, _ in order:
+                    found[layer_index][kind] = summed[:, :, spot : spot + sizes[kind]]
+                    spot += sizes[kind]
+        results = [
+            jnp.stack([found[layer_index][kind] for layer_index in range(LAYERS)])
+            for kind in range(len(sizes))
+        ]
+    return (
+        collect_tokens(result, result_got, result_other, below),
+        jnp.where(kept_part[0], kept_part[1], moved.astype(wide)),
+        *[jnp.swapaxes(member, 2, 3) for member in results],
+    )
 
 
 def solution(mesh):

time: 524 us -> 508 us (0.969)
  Pallas kernels: 245 us -> 229 us
  waiting for transfers between devices: 116 us -> 126 us
  starting transfers between devices: 65.4 us -> 58.1 us
    ppermute x9, waiting for transfers between devices: 65 us -> 82.8 us  [along_z(): return lax.ppermute(rows, 'dp', RING)]
    pallas_call x12 -> x14, Pallas kernels: 178 us -> 163 us  [the longest x13 161 us: frozen_call(): pl.pallas_call(functools.partial(kernel, form), grid=(count // tile,) if...]
    all_to_all x2 -> x1, waiting for transfers between devices: 17.5 us -> 5.5 us  [to_owners(): return lax.all_to_all(total, LANE, split_axis=0, concat_axis=0, tiled=True)]
    ppermute x6, waiting for transfers between devices: 10.4 us -> 3.43 us  [along_x(): return lax.ppermute(rows, 'dp', ACROSS_X)]
    unnamed x230 -> x216, local copies, waits for them, and re-layouts: 28.7 us -> 29 us
  transfers between devices with their start and end apart: 57 -> 55, of which waited for: 17 -> 22; matrix products, arithmetic and copies ran while one was open for 9% -> 6% of each run, Pallas kernels for 33% -> 32%
where the time goes in v4:
time: 508 us; the launch traced here: 498 us
  Pallas kernels  229 us (45%)
  waiting for transfers between devices  126 us (25%)
  starting transfers between devices  58.1 us (11%)
  local copies, waits for them, and re-layouts  38.1 us (8%)
  other arithmetic  31.3 us (6%)
  between operations  15.9 us (3%)
    pallas_call x13, Pallas kernels, frozen_call(): pl.pallas_call(functools.partial(kernel, form), grid=(count // tile,) if...  161 us
    ppermute x9, waiting for transfers between devices, along_z(): return lax.ppermute(rows, 'dp', RING)  82.8 us
    pallas_call x2, Pallas kernels, attend_backward(): pl.pallas_call(functools.partial(attend_backward_kernel, pieces), out_sha...  38.3 us
    unnamed x216, local copies, waits for them, and re-layouts  29 us
    pallas_call x2, Pallas kernels, attend_forward(): pl.pallas_call(functools.partial(attend_forward_kernel, pieces), out_shap...  25.5 us
    ppermute x9, starting transfers between devices, along_z(): return lax.ppermute(rows, 'dp', RING)  15.3 us
    ppermute x2, waiting for transfers between devices, send_across(): return lax.ppermute(jnp.where(below, rows[BLK:], rows[:BLK]), CTX, across)  12.2 us
  transfers between devices with their start and end apart: 55, of which 22 were waited for; matrix products, arithmetic and copies ran while one was open for 6% of the time, Pallas kernels for 32%

profile of v4, /device:TPU:0, one launch (start us, length us, event | category | flops | bytes accessed | tf_op | source)
XLA Modules:
  0.0 498.5 jit_solution(10505772341312542782)
XLA Ops:
  11.3 3.1 collective-permute-start.1
  15.3 1.5 collective-permute-start.4
  17.7 1.5 collective-permute-start.5
  20.0 1.8 collective-permute-done.1
  24.5 13.8 %collective-permute-done.2 = bf16[128,1024]{1,0:T(8,128)(2,1)S(1)} collective-permute-done((bf16[128,1024]{1,0:T(8,128)(2,1)S(1)}, bf16[128,1024]{1,0:T(8,128)(2,1)S(1)}, u32[]{:S(2)}, u32[]{:S(2)}) %collective-permute-start.2) | collective-permute-done | bytes 262176 | tf_op jit(solution)/shard_map/ppermute | solution.py:289
  38.3 2.2 collective-permute-start.3
  42.7 4.3 collective-permute-done.3
  47.0 8.0 %all-to-all-start = ((bf16[16,2,16,512]{3,2,1,0:T(8,128)(2,1)}), bf16[16,2,16,512]{3,2,1,0:T(8,128)(2,1)S(1)}, u32[]{:S(2)}, u32[]{:S(2)}) async-start(bf16[16,2,16,512]{3,2,1,0:T(8,128)(2,1)} %broadcast_select_fusion), calls=%async_computation | async-start | bytes 1048576 | tf_op jit(solution)/shard_map/all_to_all | solution.py:377
  55.3 2.0 collective-permute-start.6
  57.3 1.5 collective-permute-start.7
  58.9 1.5 collective-permute-start.8
  60.3 24.7 %collective-permute-done.8 = bf16[128,1024]{1,0:T(8,128)(2,1)S(1)} collective-permute-done((bf16[128,1024]{1,0:T(8,128)(2,1)S(1)}, bf16[128,1024]{1,0:T(8,128)(2,1)S(1)}, u32[]{:S(2)}, u32[]{:S(2)}) %collective-permute-start.8) | collective-permute-done | bytes 262176 | tf_op jit(solution)/shard_map/ppermute | solution.py:289
  87.1 4.7 collective-permute-start.10
  92.2 1.5 collective-permute-start.9
  93.6 16.6 %collective-permute-done.14 = bf16[128,1024]{1,0:T(8,128)(2,1)S(1)} collective-permute-done((bf16[128,1024]{1,0:T(8,128)(2,1)S(1)}, bf16[128,1024]{1,0:T(8,128)(2,1)S(1)}, u32[]{:S(2)}, u32[]{:S(2)}) %collective-permute-start.14) | collective-permute-done | bytes 262176 | tf_op jit(solution)/shard_map/ppermute | solution.py:289
  110.2 19.1 %collective-permute-done.15 = bf16[128,1024]{1,0:T(8,128)(2,1)S(1)} collective-permute-done((bf16[128,1024]{1,0:T(8,128)(2,1)S(1)}, bf16[128,1024]{1,0:T(8,128)(2,1)S(1)}, u32[]{:S(2)}, u32[]{:S(2)}) %collective-permute-start.15) | collective-permute-done | bytes 262176 | tf_op jit(solution)/shard_map/ppermute | solution.py:289
  129.3 1.9 collective-permute-done.13.other_ref
  131.2 3.4 collective-permute-done.10.refs_3_
  134.6 3.7 collective-permute-done.9.refs_1_
  139.4 2.7 collective-permute-start.19
  143.2 3.4 collective-permute-start.20
  158.8 1.6 convert_element_type.27.x_ref
  160.3 9.0 %qkv_forward.2 = (bf16[512,1024]{1,0:T(8,128)(2,1)}, bf16[512,1024]{1,0:T(8,128)(2,1)}, f32[512,128]{1,0:T(8,128)}, bf16[512,16]{1,0:T(8,128)(2,1)}, bf16[512,10...) custom-call(s32[4]{0:T(128)} %copy-done.40, f32[512,1024]{1,0:T(8,128)} %convert_element_type.27.x_ref, ...), custom_call_target="tpu_custom_call" | custom-call | flops 900000000 | tf_op jit(solution)/shard_map/qkv_forward/pallas_call | solution.py:816
  170.0 2.4 collective-permute-start.25
  172.4 2.3 pad_maximum_fusion.4.refs_2_.refs_9_
  174.8 2.1 pad_maximum_fusion.3.refs_0_.refs_7_
  176.9 2.6 collective-permute-done.25
  180.6 1.4 collective-permute-start.21
  183.6 1.8 collective-permute-start.26
  188.5 12.8 %attend_forward.2 = (f32[512,1024]{1,0:T(8,128)}, f32[8,2,512]{2,1,0:T(2,128)S(1)}) custom-call(s32[1]{0:T(128)} %bitcast.47.place_ref, bf16[512,1024]{1,0:T(8,128)(2,1)S(1)} %copy-done.3, bf16[512,1024]{1,0:T(8,128)(2,1)S(1)} %copy-done.4, bf16[512,1024]{1,0:T(8,128)(2,1)S(1)} %copy-done.7, bf16[512,1024]{1,0:T(8,128)(2,1)S(1)} %copy-done.5, ...), custom_call_target="tpu_custom_call" | custom-call | flops 1300000000 | tf_op jit(solution)/shard_map/attend_forward/pallas_call | solution.py:157
  201.2 8.1 %output_forward.2 = (bf16[512,1024]{1,0:T(8,128)(2,1)}, f32[512,1024]{1,0:T(8,128)}, bf16[512,1024]{1,0:T(8,128)(2,1)}, bf16[512,1024]{1,0:T(8,128)(2,1)}, f32[512,128]{1,0:T(8,128)}, /*index=5*/bf16[512,16]{1,0:T(8,128)(2,1)}) custom-call(s32[4]{0:T(128)} %copy-done.40, f32[512,1024]{1,0:T(8,128)} %convert_element_type.27.x_ref, ...), custom_call_target="tpu_custom_call" | custom-call | flops 800000000 | tf_op jit(solution)/shard_map/output_forward/pallas_call | solution.py:816
  214.7 1.5 collective-permute-start.32
  218.0 20.8 %feed_forward.2 = (f32[512,1024]{1,0:T(8,128)}, bf16[512,4096]{1,0:T(8,128)(2,1)}, bf16[512,4096]{1,0:T(8,128)(2,1)}, bf16[512,16]{1,0:T(8,128)(2,1)}, bf16[512,16]{1,0:T(8,128)(2,1)}) custom-call(s32[4]{0:T(128)} %copy-done.40, bf16[512,1024]{1,0:T(8,128)(2,1)} %get-tuple-element.668.normed_ref, f32[512,1024]{1,0:T(8,128)} %get-tuple-element.464.middle_ref, ...), custom_call_target="tpu_custom_call" | custom-call | flops 2000000000 | tf_op jit(solution)/shard_map/feed_forward/pallas_call | solution.py:816
  240.1 8.7 %qkv_forward.3 = (bf16[512,1024]{1,0:T(8,128)(2,1)}, bf16[512,1024]{1,0:T(8,128)(2,1)}, f32[512,128]{1,0:T(8,128)}, bf16[512,16]{1,0:T(8,128)(2,1)}, bf16[512,10...) custom-call(s32[4]{0:T(128)} %copy-done.40, f32[512,1024]{1,0:T(8,128)} %get-tuple-element.559.x_ref, ...), custom_call_target="tpu_custom_call" | custom-call | flops 900000000 | tf_op jit(solution)/shard_map/qkv_forward/pallas_call | solution.py:816
  249.4 2.2 pad_maximum_fusion.6.refs_2_
  251.7 1.9 collective-permute-start.34
  253.7 2.1 pad_maximum_fusion.5.refs_0_
  256.9 12.8 %attend_forward.3 = (f32[512,1024]{1,0:T(8,128)}, f32[8,2,512]{2,1,0:T(2,128)S(1)}) custom-call(s32[1]{0:T(128)} %bitcast.47.place_ref, bf16[512,1024]{1,0:T(8,128)(2,1)S(1)} %copy-done.10, bf16[512,1024]{1,0:T(8,128)(2,1)S(1)} %copy-done.11, bf16[512,1024]{1,0:T(8,128)(2,1)S(1)} %collective-permute-done.37.refs_1_, bf16[512,1024]{1,0:T(8,128)(2,1)S(1)} %copy-done.12, ...), custom_call_target="tpu_custom_call" | custom-call | flops 1300000000 | tf_op jit(solution)/shard_map/attend_forward/pallas_call | solution.py:157
  269.7 8.2 %output_forward.3 = (bf16[512,1024]{1,0:T(8,128)(2,1)}, f32[512,1024]{1,0:T(8,128)}, bf16[512,1024]{1,0:T(8,128)(2,1)}, bf16[512,1024]{1,0:T(8,128)(2,1)}, f32[512,128]{1,0:T(8,128)}, /*index=5*/bf16[512,16]{1,0:T(8,128)(2,1)}) custom-call(s32[4]{0:T(128)} %copy-done.40, f32[512,1024]{1,0:T(8,128)} %get-tuple-element.559.x_ref, ...), custom_call_target="tpu_custom_call" | custom-call | flops 800000000 | tf_op jit(solution)/shard_map/output_forward/pallas_call | solution.py:816
  277.9 3.8 collective-permute-done.33.refs_1_
  284.6 1.5 collective-permute-done.40.refs_7_
  287.1 20.8 %feed_forward.3 = (f32[512,1024]{1,0:T(8,128)}, bf16[512,4096]{1,0:T(8,128)(2,1)}, bf16[512,4096]{1,0:T(8,128)(2,1)}, bf16[512,16]{1,0:T(8,128)(2,1)}, bf16[512,16]{1,0:T(8,128)(2,1)}) custom-call(s32[4]{0:T(128)} %copy-done.40, bf16[512,1024]{1,0:T(8,128)(2,1)} %get-tuple-element.591.normed_ref, f32[512,1024]{1,0:T(8,128)} %get-tuple-element.592.middle_ref, ...), custom_call_target="tpu_custom_call" | custom-call | flops 2000000000 | tf_op jit(solution)/shard_map/feed_forward/pallas_call | solution.py:816
  308.8 1.9 convert_element_type.28
  311.1 1.6 maximum_convert_fusion.grad_ref
  312.7 22.3 %feed_backward.2 = (f32[512,1024]{1,0:T(8,128)}, bf16[16,1024]{1,0:T(8,128)(2,1)}, bf16[16,4096]{1,0:T(8,128)(2,1)}, bf16[16,4096]{1,0:T(8,128)(2,1)}, bf16[16,1024]{1,0:T(8,128)(2,1)}) custom-call(s32[4]{0:T(128)} %copy-done.40, f32[512,1024]{1,0:T(8,128)} %maximum_convert_fusion.grad_ref, bf16[512,4096]{1,0:T(8,128)(2,1)} %get-tuple-element.607.slope_ref, ...), custom_call_target="tpu_custom_call" | custom-call | flops 2200000000 | tf_op jit(solution)/shard_map/feed_backward/pallas_call | solution.py:816
  335.9 5.9 %output_backward.2 = (bf16[512,1024]{1,0:T(8,128)(2,1)}, bf16[16,1024]{1,0:T(8,128)(2,1)}, bf16[16,1024]{1,0:T(8,128)(2,1)}) custom-call(s32[4]{0:T(128)} %copy-done.40, f32[512,1024]{1,0:T(8,128)} %get-tuple-element.620.grad_ref, bf16[512,1024]{1,0:T(8,128)(2,1)} %get-tuple-element.621.attended_ref, bf16[512,16]{1,0:T(8,128)(2,1)} %get-tuple-element.622.rank_ref, ...), custom_call_target="tpu_custom_call" | custom-call | flops 500000000 | tf_op jit(solution)/shard_map/output_backward/pallas_call | solution.py:816
  341.8 19.3 %attend_backward.2 = (bf16[512,1024]{1,0:T(8,128)(2,1)S(1)}, bf16[512,1024]{1,0:T(8,128)(2,1)S(1)}, bf16[512,1024]{1,0:T(8,128)(2,1)S(1)}, bf16[512,1024]{1,0:T(8,128)(2,1)S(1)}, bf16[512,1024]{1,0:T(8,128)(2,1)S(1)}) custom-call(s32[1]{0:T(128)} %bitcast.47.place_ref, bf16[512,1024]{1,0:T(8,128)(2,1)} %get-tuple-element.619.q_ref, ...), custom_call_target="tpu_custom_call" | custom-call | flops 2100000000 | tf_op jit(solution)/shard_map/attend_backward/pallas_call | solution.py:183
  364.6 2.1 collective-permute-done.44.refs_1_
  366.7 1.5 collective-permute-done.45.refs_3_
  369.2 12.7 %qkv_whole.1 = (f32[512,1024]{1,0:T(8,128)}, bf16[16,1024]{1,0:T(8,128)(2,1)}, bf16[16,3072]{1,0:T(8,128)(2,1)}) custom-call(s32[4]{0:T(128)} %copy-done.40, f32[512,1024]{1,0:T(8,128)} %get-tuple-element.620.grad_ref, bf16[512,1024]{1,0:T(8,128)(2,1)} %get-tuple-element.648.unit_ref, f32[512,128]{1,0:T(8,128)} %get-tuple-element.649.scale_ref, ...), custom_call_target="tpu_custom_call" | custom-call | flops 1100000000 | tf_op jit(solution)/shard_map/qkv_whole/pallas_call | solution.py:816
  381.9 22.7 %feed_backward.3 = (f32[512,1024]{1,0:T(8,128)}, bf16[16,1024]{1,0:T(8,128)(2,1)}, bf16[16,4096]{1,0:T(8,128)(2,1)}, bf16[16,4096]{1,0:T(8,128)(2,1)}, bf16[16,1024]{1,0:T(8,128)(2,1)}) custom-call(s32[4]{0:T(128)} %copy-done.40, f32[512,1024]{1,0:T(8,128)} %get-tuple-element.665.grad_ref, bf16[512,4096]{1,0:T(8,128)(2,1)} %get-tuple-element.666.slope_ref, ...), custom_call_target="tpu_custom_call" | custom-call | flops 2200000000 | tf_op jit(solution)/shard_map/feed_backward/pallas_call | solution.py:816
  404.6 5.9 %output_backward.3 = (bf16[512,1024]{1,0:T(8,128)(2,1)}, bf16[16,1024]{1,0:T(8,128)(2,1)}, bf16[16,1024]{1,0:T(8,128)(2,1)}) custom-call(s32[4]{0:T(128)} %copy-done.40, f32[512,1024]{1,0:T(8,128)} %get-tuple-element.682.grad_ref, bf16[512,1024]{1,0:T(8,128)(2,1)} %get-tuple-element.683.attended_ref, bf16[512,16]{1,0:T(8,128)(2,1)} %get-tuple-element.684.rank_ref, ...), custom_call_target="tpu_custom_call" | custom-call | flops 500000000 | tf_op jit(solution)/shard_map/output_backward/pallas_call | solution.py:816
  410.6 19.1 %attend_backward.3 = (bf16[512,1024]{1,0:T(8,128)(2,1)S(1)}, bf16[512,1024]{1,0:T(8,128)(2,1)S(1)}, bf16[512,1024]{1,0:T(8,128)(2,1)S(1)}, bf16[512,1024]{1,0:T(8,128)(2,1)S(1)}, bf16[512,1024]{1,0:T(8,128)(2,1)S(1)}) custom-call(s32[1]{0:T(128)} %bitcast.47.place_ref, bf16[512,1024]{1,0:T(8,128)(2,1)} %get-tuple-element.681.q_ref, ...), custom_call_target="tpu_custom_call" | custom-call | flops 2100000000 | tf_op jit(solution)/shard_map/attend_backward/pallas_call | solution.py:183
  433.2 2.1 collective-permute-done.46.refs_1_
  435.3 1.5 collective-permute-done.47.refs_3_
  438.0 6.4 %qkv_turn.1 = (bf16[512,1024]{1,0:T(8,128)(2,1)}, bf16[512,1024]{1,0:T(8,128)(2,1)}, bf16[512,16]{1,0:T(8,128)(2,1)}, bf16[16,1024]{1,0:T(8,128)(2,1)}, bf16[16,3072]{1,0:T(8,128)(2,1)}) custom-call(s32[4]{0:T(128)} %copy-done.40, bf16[512,1024]{1,0:T(8,128)(2,1)} %get-tuple-element.679.normed_ref, bf16[512,16]{1,0:T(8,128)(2,1)} %get-tuple-element.680.rank_ref, ...), custom_call_target="tpu_custom_call" | custom-call | flops 300000000 | tf_op jit(solution)/shard_map/qkv_turn/pallas_call | solution.py:816
  447.5 1.7 collective-permute-done.48
  450.2 5.6 %all-to-all-start.1 = ((bf16[16,16,1024]{2,1,0:T(8,128)(2,1)}), bf16[16,16,1024]{2,1,0:T(8,128)(2,1)S(1)}, u32[]{:S(2)}, u32[]{:S(2)}) async-start(bf16[16,16,1024]{2,1,0:T(8,128)(2,1)} %fusion), calls=%async_computation.1 | async-start | bytes 1048576 | tf_op jit(solution)/shard_map/all_to_all | solution.py:1214
  455.8 10.0 %qkv_backward.1 = f32[512,1024]{1,0:T(8,128)} custom-call(s32[4]{0:T(128)} %copy-done.40, f32[512,1024]{1,0:T(8,128)} %get-tuple-element.682.grad_ref, bf16[512,1024]{1,0:T(8,128)(2,1)} %get-tuple-element.714.unit_ref, f32[512,128]{1,0:T(8,128)} %get-tuple-element.715.scale_ref, bf16[512,16]{1,0:T(8,128)(2,1)} %get-tuple-element.716.turned_ref, ...), custom_call_target="tpu_custom_call" | custom-call | flops 900000000 | tf_op jit(solution)/shard_map/qkv_backward/pallas_call | solution.py:816
  465.8 5.5 %all-to-all-done.1.refs_0_ = bf16[16,16,1024]{2,1,0:T(8,128)(2,1)S(1)} async-done(((bf16[16,16,1024]{2,1,0:T(8,128)(2,1)}), bf16[16,16,1024]{2,1,0:T(8,128)(2,1)S(1)}, u32[]{:S(2)}, u32[]{:S(2)}) %all-to-all-start.1) | async-done | bytes 524320 | tf_op jit(solution)/shard_map/all_to_all | solution.py:1214
  471.3 1.7 convert_element_type.34
  473.2 12.2 %collective-permute-done.49 = bf16[256,1024]{1,0:T(8,128)(2,1)S(1)} collective-permute-done((bf16[256,1024]{1,0:T(8,128)(2,1)S(1)}, bf16[256,1024]{1,0:T(8,128)(2,1)S(1)}, u32[]{:S(2)}, u32[]{:S(2)}) %collective-permute-start.49) | collective-permute-done | bytes 524320 | tf_op jit(solution)/shard_map/ppermute | solution.py:231
  487.6 1.8 combine.1
  489.5 1.7 maximum_select_fusion
  (357 shorter events, 66.2 us)
Async XLA Ops:
  7.2 210.7 %all-gather.6.cloned.1.call-start = ((), (), s32[]{:S(2)}) async-start(), calls=%async_computation.3 | async-start | bytes 17301504 | tf_op jit(solution)/shard_map/all_gather | solution.py:347
  10.4 273.0 %all-gather.4.cloned.1.call-start = ((), (), s32[]{:S(2)}) async-start(), calls=%async_computation.2 | async-start | bytes 8650752 | tf_op jit(solution)/shard_map/all_gather | solution.py:347
  11.3 10.4 %collective-permute-start.1 = (bf16[128,1024]{1,0:T(8,128)(2,1)S(1)}, bf16[128,1024]{1,0:T(8,128)(2,1)S(1)}, u32[]{:S(2)}, u32[]{:S(2)}) collective-permute-start(bf16[128,1024]{1,0:T(8,128)(2,1)S(1)} %pad_maximum_fusion.14), channel_id=1, source_target_pairs={{0,8},{4,12},{8,24},{12,28},{16,0},{20,4},{24,16},{28,20},{1,9},{5... | collective-permute-start | bytes 786440 | tf_op jit(solution)/shard_map/ppermute | solution.py:289
  15.3 25.2 %collective-permute-start.4 = (bf16[256,1024]{1,0:T(8,128)(2,1)}, bf16[256,1024]{1,0:T(8,128)(2,1)}, u32[]{:S(2)}, u32[]{:S(2)}) collective-permute-start(bf16[256,1024]{1,0:T(8,128)(2,1)} %bitcast_select_fusion.3), channel_id=1, source_target_pairs={{0,2},{1,3},{2,1},{3,0},{4,6},{5,7},{6,5},{7,4},{8,10},{9,11},{10,... | collective-permute-start | bytes 1572872 | tf_op jit(solution)/shard_map/ppermute | solution.py:210
  17.7 22.8 %collective-permute-start.5 = (bf16[256,1024]{1,0:T(8,128)(2,1)}, bf16[256,1024]{1,0:T(8,128)(2,1)}, u32[]{:S(2)}, u32[]{:S(2)}) collective-permute-start(bf16[256,1024]{1,0:T(8,128)(2,1)} %slice_bitcast_fusion.3), channel_id=1, source_target_pairs={{2,3},{3,2},{6,7},{7,6},{10,11},{11,10},{14,15},{15,14},{18,19},{1... | collective-permute-start | bytes 1572872 | tf_op jit(solution)/shard_map/ppermute | solution.py:215
  19.9 38.9 %copy-start.68 = (bf16[128,1024]{1,0:T(8,128)(2,1)}, bf16[128,1024]{1,0:T(8,128)(2,1)S(1)}, u32[]{:S(2)}) copy-start(bf16[128,1024]{1,0:T(8,128)(2,1)S(1)} %pad_maximum_fusion.15) | copy-start | bytes 786436
  21.7 16.5 %collective-permute-start.2 = (bf16[128,1024]{1,0:T(8,128)(2,1)S(1)}, bf16[128,1024]{1,0:T(8,128)(2,1)S(1)}, u32[]{:S(2)}, u32[]{:S(2)}) collective-permute-start(bf16[128,1024]{1,0:T(8,128)(2,1)S(1)} %collective-permute-done.1), channel_id=1, source_target_pairs={{0,8},{4,12},{8,24},{12,28},{16,0},{20,4},{24,16},{28,20},{1,9},{5... | collective-permute-start | bytes 786440 | tf_op jit(solution)/shard_map/ppermute | solution.py:289
  38.3 8.7 %collective-permute-start.3 = (bf16[128,1024]{1,0:T(8,128)(2,1)S(1)}, bf16[128,1024]{1,0:T(8,128)(2,1)S(1)}, u32[]{:S(2)}, u32[]{:S(2)}) collective-permute-start(bf16[128,1024]{1,0:T(8,128)(2,1)S(1)} %collective-permute-done.2), channel_id=1, source_target_pairs={{0,8},{4,12},{8,24},{12,28},{16,0},{20,4},{24,16},{28,20},{1,9},{5... | collective-permute-start | bytes 786440 | tf_op jit(solution)/shard_map/ppermute | solution.py:289
  47.0 38.1 %all-to-all-start = ((bf16[16,2,16,512]{3,2,1,0:T(8,128)(2,1)}), bf16[16,2,16,512]{3,2,1,0:T(8,128)(2,1)S(1)}, u32[]{:S(2)}, u32[]{:S(2)}) async-start(bf16[16,2,16,512]{3,2,1,0:T(8,128)(2,1)} %broadcast_select_fusion), calls=%async_computation | async-start | bytes 1048576 | tf_op jit(solution)/shard_map/all_to_all | solution.py:377
  55.3 29.8 %collective-permute-start.6 = (bf16[4,64,1024]{2,1,0:T(8,128)(2,1)S(1)}, bf16[4,64,1024]{2,1,0:T(8,128)(2,1)S(1)}, u32[]{:S(2)}, u32[]{:S(2)}) collective-permute-start(bf16[4,64,1024]{2,1,0:T(8,128)(2,1)S(1)} %pad_maximum_fusion.8), channel_id=1, source_target_pairs={{0,4},{4,0},{8,12},{12,8},{16,20},{20,16},{24,28},{28,24},{1,5},{5... | collective-permute-start | bytes 1572872 | tf_op jit(solution)/shard_map/ppermute | solution.py:293
  57.3 27.7 %collective-permute-start.7 = (bf16[4,64,1024]{2,1,0:T(8,128)(2,1)S(1)}, bf16[4,64,1024]{2,1,0:T(8,128)(2,1)}, u32[]{:S(2)}, u32[]{:S(2)}) collective-permute-start(bf16[4,64,1024]{2,1,0:T(8,128)(2,1)S(1)} %pad_maximum_fusion.9), channel_id=1, source_target_pairs={{0,2},{2,0},{1,3},{3,1},{4,6},{6,4},{5,7},{7,5},{8,10},{10,8},{9,1... | collective-permute-start | bytes 1572872 | tf_op jit(solution)/shard_map/ppermute | solution.py:297
  58.9 26.2 %collective-permute-start.8 = (bf16[128,1024]{1,0:T(8,128)(2,1)S(1)}, bf16[128,1024]{1,0:T(8,128)(2,1)S(1)}, u32[]{:S(2)}, u32[]{:S(2)}) collective-permute-start(bf16[128,1024]{1,0:T(8,128)(2,1)S(1)} %pad_maximum_fusion.15), channel_id=1, source_target_pairs={{0,8},{4,12},{8,24},{12,28},{16,0},{20,4},{24,16},{28,20},{1,9},{5... | collective-permute-start | bytes 786440 | tf_op jit(solution)/shard_map/ppermute | solution.py:289
  85.8 43.4 %copy-start.99 = (f32[2,2048]{1,0:T(2,128)S(1)}, f32[2,2048]{1,0:T(2,128)}, u32[]{:S(2)}) copy-start(f32[2,2048]{1,0:T(2,128)} %param.30) | copy-start | bytes 49156
  85.8 53.0 %copy-start.69 = (bf16[128,1024]{1,0:T(8,128)(2,1)S(1)}, bf16[128,1024]{1,0:T(8,128)(2,1)}, u32[]{:S(2)}) copy-start(bf16[128,1024]{1,0:T(8,128)(2,1)} %copy-done.68) | copy-start | bytes 786436
  87.0 52.0 %copy-start.54 = (bf16[2,4,64,1024]{3,2,1,0:T(8,128)(2,1)}, bf16[2,4,64,1024]{3,2,1,0:T(8,128)(2,1)S(1)}, u32[]{:S(2)}) copy-start(bf16[2,4,64,1024]{3,2,1,0:T(8,128)(2,1)S(1)} %pad_maximum_fusion.2.refs_2_) | copy-start | bytes 3145732
  87.1 44.1 %collective-permute-start.12 = (bf16[2,4,64,1024]{3,2,1,0:T(8,128)(2,1)S(1)}, bf16[2,4,64,1024]{3,2,1,0:T(8,128)(2,1)S(1)}, u32[]{:S(2)}, u32[]{:S(2)}) collective-permute-start(bf16[2,4,64,1024]{3,2,1,0:T(8,128)(2,1)S(1)} %pad_maximum_fusion.2.refs_2_), channel_id=1, source_target_pairs={{0,1},{1,0},{2,3},{3,2},{4,5},{5,4},{6,7},{7,6},{8,9},{9,8},{10,11... | collective-permute-start | bytes 3145736 | tf_op jit(solution)/shard_map/ppermute | solution.py:301
  87.1 47.5 %collective-permute-start.10 = (bf16[2,4,64,1024]{3,2,1,0:T(8,128)(2,1)S(1)}, bf16[2,4,64,1024]{3,2,1,0:T(8,128)(2,1)}, u32[]{:S(2)}, u32[]{:S(2)}) collective-permute-start(bf16[2,4,64,1024]{3,2,1,0:T(8,128)(2,1)S(1)} %pad_maximum_fusion.2.refs_2_), channel_id=1, source_target_pairs={{0,4},{4,0},{8,12},{12,8},{16,20},{20,16},{24,28},{28,24},{1,5},{5... | collective-permute-start | bytes 3145736 | tf_op jit(solution)/shard_map/ppermute | solution.py:293
  91.8 18.4 %collective-permute-start.14 = (bf16[128,1024]{1,0:T(8,128)(2,1)S(1)}, bf16[128,1024]{1,0:T(8,128)(2,1)S(1)}, u32[]{:S(2)}, u32[]{:S(2)}) collective-permute-start(bf16[128,1024]{1,0:T(8,128)(2,1)S(1)} %collective-permute-done.8), channel_id=1, source_target_pairs={{0,8},{4,12},{8,24},{12,28},{16,0},{20,4},{24,16},{28,20},{1,9},{5... | collective-permute-start | bytes 786440 | tf_op jit(solution)/shard_map/ppermute | solution.py:289
  91.9 47.2 %copy-start.55 = (bf16[2,4,64,1024]{3,2,1,0:T(8,128)(2,1)}, bf16[2,4,64,1024]{3,2,1,0:T(8,128)(2,1)S(1)}, u32[]{:S(2)}) copy-start(bf16[2,4,64,1024]{3,2,1,0:T(8,128)(2,1)S(1)} %pad_maximum_fusion.1.refs_0_) | copy-start | bytes 3145732
  91.9 42.7 %collective-permute-start.11 = (bf16[2,4,64,1024]{3,2,1,0:T(8,128)(2,1)S(1)}, bf16[2,4,64,1024]{3,2,1,0:T(8,128)(2,1)S(1)}, u32[]{:S(2)}, u32[]{:S(2)}) collective-permute-start(bf16[2,4,64,1024]{3,2,1,0:T(8,128)(2,1)S(1)} %pad_maximum_fusion.1.refs_0_), channel_id=1, source_target_pairs={{0,1},{1,0},{2,3},{3,2},{4,5},{5,4},{6,7},{7,6},{8,9},{9,8},{10,11... | collective-permute-start | bytes 3145736 | tf_op jit(solution)/shard_map/ppermute | solution.py:301
  92.2 46.2 %collective-permute-start.9 = (bf16[2,4,64,1024]{3,2,1,0:T(8,128)(2,1)S(1)}, bf16[2,4,64,1024]{3,2,1,0:T(8,128)(2,1)}, u32[]{:S(2)}, u32[]{:S(2)}) collective-permute-start(bf16[2,4,64,1024]{3,2,1,0:T(8,128)(2,1)S(1)} %pad_maximum_fusion.1.refs_0_), channel_id=1, source_target_pairs={{0,2},{2,0},{1,3},{3,1},{4,6},{6,4},{5,7},{7,5},{8,10},{10,8},{9,1... | collective-permute-start | bytes 3145736 | tf_op jit(solution)/shard_map/ppermute | solution.py:297
  110.2 19.1 %collective-permute-start.15 = (bf16[128,1024]{1,0:T(8,128)(2,1)S(1)}, bf16[128,1024]{1,0:T(8,128)(2,1)S(1)}, u32[]{:S(2)}, u32[]{:S(2)}) collective-permute-start(bf16[128,1024]{1,0:T(8,128)(2,1)S(1)} %collective-permute-done.14), channel_id=1, source_target_pairs={{0,8},{4,12},{8,24},{12,28},{16,0},{20,4},{24,16},{28,20},{1,9},{5... | collective-permute-start | bytes 786440 | tf_op jit(solution)/shard_map/ppermute | solution.py:289
  129.3 1.9 collective-permute-start.13
  138.3 20.4 %collective-permute-start.16 = (bf16[2,4,64,1024]{3,2,1,0:T(8,128)(2,1)}, bf16[2,4,64,1024]{3,2,1,0:T(8,128)(2,1)}, u32[]{:S(2)}, u32[]{:S(2)}) collective-permute-start(bf16[2,4,64,1024]{3,2,1,0:T(8,128)(2,1)} %collective-permute-done.9.refs_1_), channel_id=1, source_target_pairs={{0,1},{1,0},{2,3},{3,2},{4,5},{5,4},{6,7},{7,6},{8,9},{9,8},{10,11... | collective-permute-start | bytes 3145736 | tf_op jit(solution)/shard_map/ppermute | solution.py:301
  138.3 20.4 %collective-permute-start.17 = (bf16[2,4,64,1024]{3,2,1,0:T(8,128)(2,1)}, bf16[2,4,64,1024]{3,2,1,0:T(8,128)(2,1)}, u32[]{:S(2)}, u32[]{:S(2)}) collective-permute-start(bf16[2,4,64,1024]{3,2,1,0:T(8,128)(2,1)} %collective-permute-done.10.refs_3_), channel_id=1, source_target_pairs={{0,1},{1,0},{2,3},{3,2},{4,5},{5,4},{6,7},{7,6},{8,9},{9,8},{10,11... | collective-permute-start | bytes 3145736 | tf_op jit(solution)/shard_map/ppermute | solution.py:301
  139.1 19.7 %copy-start.63 = (bf16[512,1024]{1,0:T(8,128)(2,1)S(1)}, bf16[512,1024]{1,0:T(8,128)(2,1)}, u32[]{:S(2)}) copy-start(bf16[512,1024]{1,0:T(8,128)(2,1)} %pad_maximum_fusion) | copy-start | bytes 3145732
  139.2 21.2 %copy-start.70 = (bf16[4,64,1024]{2,1,0:T(8,128)(2,1)}, bf16[4,64,1024]{2,1,0:T(8,128)(2,1)S(1)}, u32[]{:S(2)}) copy-start(bf16[4,64,1024]{2,1,0:T(8,128)(2,1)S(1)} %pad_maximum_fusion.10) | copy-start | bytes 1572868
  139.2 19.0 %collective-permute-start.18 = (bf16[4,64,1024]{2,1,0:T(8,128)(2,1)S(1)}, bf16[4,64,1024]{2,1,0:T(8,128)(2,1)}, u32[]{:S(2)}, u32[]{:S(2)}) collective-permute-start(bf16[4,64,1024]{2,1,0:T(8,128)(2,1)S(1)} %pad_maximum_fusion.10), channel_id=1, source_target_pairs={{0,4},{4,0},{8,12},{12,8},{16,20},{20,16},{24,28},{28,24},{1,5},{5... | collective-permute-start | bytes 1572872 | tf_op jit(solution)/shard_map/ppermute | solution.py:293
  139.3 21.0 %copy-start.72 = (bf16[4,64,1024]{2,1,0:T(8,128)(2,1)}, bf16[4,64,1024]{2,1,0:T(8,128)(2,1)S(1)}, u32[]{:S(2)}) copy-start(bf16[4,64,1024]{2,1,0:T(8,128)(2,1)S(1)} %pad_maximum_fusion.11) | copy-start | bytes 1572868
  139.4 19.4 %collective-permute-start.19 = (bf16[4,64,1024]{2,1,0:T(8,128)(2,1)S(1)}, bf16[4,64,1024]{2,1,0:T(8,128)(2,1)}, u32[]{:S(2)}, u32[]{:S(2)}) collective-permute-start(bf16[4,64,1024]{2,1,0:T(8,128)(2,1)S(1)} %pad_maximum_fusion.11), channel_id=1, source_target_pairs={{0,2},{2,0},{1,3},{3,1},{4,6},{6,4},{5,7},{7,5},{8,10},{10,8},{9,1... | collective-permute-start | bytes 1572872 | tf_op jit(solution)/shard_map/ppermute | solution.py:297
  143.2 14.9 %collective-permute-start.20 = (bf16[128,1024]{1,0:T(8,128)(2,1)S(1)}, bf16[128,1024]{1,0:T(8,128)(2,1)}, u32[]{:S(2)}, u32[]{:S(2)}) collective-permute-start(bf16[128,1024]{1,0:T(8,128)(2,1)S(1)} %pad_maximum_fusion.16), channel_id=1, source_target_pairs={{0,8},{4,12},{8,24},{12,28},{16,0},{20,4},{24,16},{28,20},{1,9},{5... | collective-permute-start | bytes 786440 | tf_op jit(solution)/shard_map/ppermute | solution.py:289
  169.4 10.2 %collective-permute-start.27 = (bf16[512,1024]{1,0:T(8,128)(2,1)}, bf16[512,1024]{1,0:T(8,128)(2,1)S(1)}, u32[]{:S(2)}, u32[]{:S(2)}) collective-permute-start(bf16[512,1024]{1,0:T(8,128)(2,1)} %get-tuple-element.698.refs_0_), channel_id=1, source_target_pairs={{0,1},{1,0},{2,3},{3,2},{4,5},{5,4},{6,7},{7,6},{8,9},{9,8},{10,11... | collective-permute-start | bytes 3145736 | tf_op jit(solution)/shard_map/ppermute | solution.py:258
  169.5 13.1 %collective-permute-start.28 = (bf16[512,1024]{1,0:T(8,128)(2,1)}, bf16[512,1024]{1,0:T(8,128)(2,1)S(1)}, u32[]{:S(2)}, u32[]{:S(2)}) collective-permute-start(bf16[512,1024]{1,0:T(8,128)(2,1)} %get-tuple-element.700.refs_2_), channel_id=1, source_target_pairs={{0,1},{1,0},{2,3},{3,2},{4,5},{5,4},{6,7},{7,6},{8,9},{9,8},{10,11... | collective-permute-start | bytes 3145736 | tf_op jit(solution)/shard_map/ppermute | solution.py:258
  170.0 9.6 %collective-permute-start.25 = (bf16[128,1024]{1,0:T(8,128)(2,1)}, bf16[128,1024]{1,0:T(8,128)(2,1)}, u32[]{:S(2)}, u32[]{:S(2)}) collective-permute-start(bf16[128,1024]{1,0:T(8,128)(2,1)} %collective-permute-done.20), channel_id=1, source_target_pairs={{0,8},{4,12},{8,24},{12,28},{16,0},{20,4},{24,16},{28,20},{1,9},{5... | collective-permute-start | bytes 786440 | tf_op jit(solution)/shard_map/ppermute | solution.py:289
  174.7 34.7 %collective-permute-start.24 = (bf16[2,4,64,1024]{3,2,1,0:T(8,128)(2,1)}, bf16[2,4,64,1024]{3,2,1,0:T(8,128)(2,1)}, u32[]{:S(2)}, u32[]{:S(2)}) collective-permute-start(bf16[2,4,64,1024]{3,2,1,0:T(8,128)(2,1)} %pad_maximum_fusion.4.refs_2_.refs_9_), channel_id=1, source_target_pairs={{0,1},{1,0},{2,3},{3,2},{4,5},{5,4},{6,7},{7,6},{8,9},{9,8},{10,11... | collective-permute-start | bytes 3145736 | tf_op jit(solution)/shard_map/ppermute | solution.py:301
  174.7 34.7 %collective-permute-start.22 = (bf16[2,4,64,1024]{3,2,1,0:T(8,128)(2,1)}, bf16[2,4,64,1024]{3,2,1,0:T(8,128)(2,1)}, u32[]{:S(2)}, u32[]{:S(2)}) collective-permute-start(bf16[2,4,64,1024]{3,2,1,0:T(8,128)(2,1)} %pad_maximum_fusion.4.refs_2_.refs_9_), channel_id=1, source_target_pairs={{0,4},{4,0},{8,12},{12,8},{16,20},{20,16},{24,28},{28,24},{1,5},{5... | collective-permute-start | bytes 3145736 | tf_op jit(solution)/shard_map/ppermute | solution.py:293
  179.6 29.8 %collective-permute-start.23 = (bf16[2,4,64,1024]{3,2,1,0:T(8,128)(2,1)}, bf16[2,4,64,1024]{3,2,1,0:T(8,128)(2,1)}, u32[]{:S(2)}, u32[]{:S(2)}) collective-permute-start(bf16[2,4,64,1024]{3,2,1,0:T(8,128)(2,1)} %pad_maximum_fusion.3.refs_0_.refs_7_), channel_id=1, source_target_pairs={{0,1},{1,0},{2,3},{3,2},{4,5},{5,4},{6,7},{7,6},{8,9},{9,8},{10,11... | collective-permute-start | bytes 3145736 | tf_op jit(solution)/shard_map/ppermute | solution.py:301
  180.6 29.2 %collective-permute-start.21 = (bf16[2,4,64,1024]{3,2,1,0:T(8,128)(2,1)}, bf16[2,4,64,1024]{3,2,1,0:T(8,128)(2,1)}, u32[]{:S(2)}, u32[]{:S(2)}) collective-permute-start(bf16[2,4,64,1024]{3,2,1,0:T(8,128)(2,1)} %pad_maximum_fusion.3.refs_0_.refs_7_), channel_id=1, source_target_pairs={{0,2},{2,0},{1,3},{3,1},{4,6},{6,4},{5,7},{7,5},{8,10},{10,8},{9,1... | collective-permute-start | bytes 3145736 | tf_op jit(solution)/shard_map/ppermute | solution.py:297
  183.6 25.8 %collective-permute-start.26 = (bf16[128,1024]{1,0:T(8,128)(2,1)}, bf16[128,1024]{1,0:T(8,128)(2,1)}, u32[]{:S(2)}, u32[]{:S(2)}) collective-permute-start(bf16[128,1024]{1,0:T(8,128)(2,1)} %collective-permute-done.25), channel_id=1, source_target_pairs={{0,8},{4,12},{8,24},{12,28},{16,0},{20,4},{24,16},{28,20},{1,9},{5... | collective-permute-start | bytes 786440 | tf_op jit(solution)/shard_map/ppermute | solution.py:289
  213.5 25.2 %collective-permute-start.31 = (bf16[4,64,1024]{2,1,0:T(8,128)(2,1)S(1)}, bf16[4,64,1024]{2,1,0:T(8,128)(2,1)}, u32[]{:S(2)}, u32[]{:S(2)}) collective-permute-start(bf16[4,64,1024]{2,1,0:T(8,128)(2,1)S(1)} %pad_maximum_fusion.12), channel_id=1, source_target_pairs={{0,4},{4,0},{8,12},{12,8},{16,20},{20,16},{24,28},{28,24},{1,5},{5... | collective-permute-start | bytes 1572872 | tf_op jit(solution)/shard_map/ppermute | solution.py:293
  214.7 24.1 %collective-permute-start.32 = (bf16[4,64,1024]{2,1,0:T(8,128)(2,1)S(1)}, bf16[4,64,1024]{2,1,0:T(8,128)(2,1)}, u32[]{:S(2)}, u32[]{:S(2)}) collective-permute-start(bf16[4,64,1024]{2,1,0:T(8,128)(2,1)S(1)} %pad_maximum_fusion.13), channel_id=1, source_target_pairs={{0,2},{2,0},{1,3},{3,1},{4,6},{6,4},{5,7},{7,5},{8,10},{10,8},{9,1... | collective-permute-start | bytes 1572872 | tf_op jit(solution)/shard_map/ppermute | solution.py:297
  216.2 22.5 %collective-permute-start.29 = (bf16[2,4,64,1024]{3,2,1,0:T(8,128)(2,1)}, bf16[2,4,64,1024]{3,2,1,0:T(8,128)(2,1)S(1)}, u32[]{:S(2)}, u32[]{:S(2)}) collective-permute-start(bf16[2,4,64,1024]{3,2,1,0:T(8,128)(2,1)} %collective-permute-done.21.refs_1_.refs_8_), channel_id=1, source_target_pairs={{0,1},{1,0},{2,3},{3,2},{4,5},{5,4},{6,7},{7,6},{8,9},{9,8},{10,11... | collective-permute-start | bytes 3145736 | tf_op jit(solution)/shard_map/ppermute | solution.py:301
  216.2 22.6 %collective-permute-start.30 = (bf16[2,4,64,1024]{3,2,1,0:T(8,128)(2,1)}, bf16[2,4,64,1024]{3,2,1,0:T(8,128)(2,1)S(1)}, u32[]{:S(2)}, u32[]{:S(2)}) collective-permute-start(bf16[2,4,64,1024]{3,2,1,0:T(8,128)(2,1)} %collective-permute-done.22.refs_3_.refs_10_), channel_id=1, source_target_pairs={{0,1},{1,0},{2,3},{3,2},{4,5},{5,4},{6,7},{7,6},{8,9},{9,8},{10,11... | collective-permute-start | bytes 3145736 | tf_op jit(solution)/shard_map/ppermute | solution.py:301
  248.8 7.1 %collective-permute-start.37 = (bf16[512,1024]{1,0:T(8,128)(2,1)}, bf16[512,1024]{1,0:T(8,128)(2,1)S(1)}, u32[]{:S(2)}, u32[]{:S(2)}) collective-permute-start(bf16[512,1024]{1,0:T(8,128)(2,1)} %get-tuple-element.636.refs_0_), channel_id=1, source_target_pairs={{0,1},{1,0},{2,3},{3,2},{4,5},{5,4},{6,7},{7,6},{8,9},{9,8},{10,11... | collective-permute-start | bytes 3145736 | tf_op jit(solution)/shard_map/ppermute | solution.py:258
  248.9 7.2 %collective-permute-start.38 = (bf16[512,1024]{1,0:T(8,128)(2,1)}, bf16[512,1024]{1,0:T(8,128)(2,1)S(1)}, u32[]{:S(2)}, u32[]{:S(2)}) collective-permute-start(bf16[512,1024]{1,0:T(8,128)(2,1)} %get-tuple-element.638.refs_2_), channel_id=1, source_target_pairs={{0,1},{1,0},{2,3},{3,2},{4,5},{5,4},{6,7},{7,6},{8,9},{9,8},{10,11... | collective-permute-start | bytes 3145736 | tf_op jit(solution)/shard_map/ppermute | solution.py:258
  251.6 26.2 %collective-permute-start.36 = (bf16[2,4,64,1024]{3,2,1,0:T(8,128)(2,1)}, bf16[2,4,64,1024]{3,2,1,0:T(8,128)(2,1)}, u32[]{:S(2)}, u32[]{:S(2)}) collective-permute-start(bf16[2,4,64,1024]{3,2,1,0:T(8,128)(2,1)} %pad_maximum_fusion.6.refs_2_), channel_id=1, source_target_pairs={{0,1},{1,0},{2,3},{3,2},{4,5},{5,4},{6,7},{7,6},{8,9},{9,8},{10,11... | collective-permute-start | bytes 3145736 | tf_op jit(solution)/shard_map/ppermute | solution.py:301
  251.7 26.1 %collective-permute-start.34 = (bf16[2,4,64,1024]{3,2,1,0:T(8,128)(2,1)}, bf16[2,4,64,1024]{3,2,1,0:T(8,128)(2,1)}, u32[]{:S(2)}, u32[]{:S(2)}) collective-permute-start(bf16[2,4,64,1024]{3,2,1,0:T(8,128)(2,1)} %pad_maximum_fusion.6.refs_2_), channel_id=1, source_target_pairs={{0,4},{4,0},{8,12},{12,8},{16,20},{20,16},{24,28},{28,24},{1,5},{5... | collective-permute-start | bytes 3145736 | tf_op jit(solution)/shard_map/ppermute | solution.py:293
  255.8 22.1 %collective-permute-start.35 = (bf16[2,4,64,1024]{3,2,1,0:T(8,128)(2,1)}, bf16[2,4,64,1024]{3,2,1,0:T(8,128)(2,1)}, u32[]{:S(2)}, u32[]{:S(2)}) collective-permute-start(bf16[2,4,64,1024]{3,2,1,0:T(8,128)(2,1)} %pad_maximum_fusion.5.refs_0_), channel_id=1, source_target_pairs={{0,1},{1,0},{2,3},{3,2},{4,5},{5,4},{6,7},{7,6},{8,9},{9,8},{10,11... | collective-permute-start | bytes 3145736 | tf_op jit(solution)/shard_map/ppermute | solution.py:301
  256.0 25.7 %collective-permute-start.33 = (bf16[2,4,64,1024]{3,2,1,0:T(8,128)(2,1)}, bf16[2,4,64,1024]{3,2,1,0:T(8,128)(2,1)}, u32[]{:S(2)}, u32[]{:S(2)}) collective-permute-start(bf16[2,4,64,1024]{3,2,1,0:T(8,128)(2,1)} %pad_maximum_fusion.5.refs_0_), channel_id=1, source_target_pairs={{0,2},{2,0},{1,3},{3,1},{4,6},{6,4},{5,7},{7,5},{8,10},{10,8},{9,1... | collective-permute-start | bytes 3145736 | tf_op jit(solution)/shard_map/ppermute | solution.py:297
  256.2 21.7 %collective-permute-start = (bf16[256,1024]{1,0:T(8,128)(2,1)S(1)}, bf16[256,1024]{1,0:T(8,128)(2,1)S(1)}, u32[]{:S(2)}, u32[]{:S(2)}) collective-permute-start(bf16[256,1024]{1,0:T(8,128)(2,1)S(1)} %slice_bitcast_fusion.4), channel_id=1, source_target_pairs={{2,3},{3,2},{6,7},{7,6},{10,11},{11,10},{14,15},{15,14},{18,19},{1... | collective-permute-start | bytes 1572872 | tf_op jit(solution)/shard_map/ppermute | solution.py:215
  281.7 2.9 collective-permute-start.39
  281.7 4.4 collective-permute-start.40
  283.1 24.8 %collective-permute-start.41 = (bf16[256,1024]{1,0:T(8,128)(2,1)}, bf16[256,1024]{1,0:T(8,128)(2,1)S(1)}, u32[]{:S(2)}, u32[]{:S(2)}) collective-permute-start(bf16[256,1024]{1,0:T(8,128)(2,1)} %bitcast_select_fusion.1), channel_id=1, source_target_pairs={{0,2},{1,3},{2,1},{3,0},{4,6},{5,7},{6,5},{7,4},{8,10},{9,11},{10,... | collective-permute-start | bytes 1572872 | tf_op jit(solution)/shard_map/ppermute | solution.py:210
  310.7 24.3 %collective-permute-start.42 = (bf16[256,1024]{1,0:T(8,128)(2,1)S(1)}, bf16[256,1024]{1,0:T(8,128)(2,1)S(1)}, u32[]{:S(2)}, u32[]{:S(2)}) collective-permute-start(bf16[256,1024]{1,0:T(8,128)(2,1)S(1)} %broadcast_select_fusion.2), channel_id=1, source_target_pairs={{2,0},{3,1},{1,2},{0,3},{6,4},{7,5},{5,6},{4,7},{10,8},{11,9},{9,1... | collective-permute-start | bytes 1572872 | tf_op jit(solution)/shard_map/ppermute | solution.py:231
  335.2 28.9 %collective-permute-start.43 = (bf16[256,1024]{1,0:T(8,128)(2,1)S(1)}, bf16[256,1024]{1,0:T(8,128)(2,1)S(1)}, u32[]{:S(2)}, u32[]{:S(2)}) collective-permute-start(bf16[256,1024]{1,0:T(8,128)(2,1)S(1)} %get-tuple-element.735), channel_id=1, source_target_pairs={{3,2},{2,3},{7,6},{6,7},{11,10},{10,11},{15,14},{14,15},{19,18},{1... | collective-permute-start | bytes 1572872 | tf_op jit(solution)/shard_map/ppermute | solution.py:237
  364.1 17.9 %copy-start.80 = (bf16[256,1024]{1,0:T(8,128)(2,1)}, bf16[256,1024]{1,0:T(8,128)(2,1)S(1)}, u32[]{:S(2)}) copy-start(bf16[256,1024]{1,0:T(8,128)(2,1)S(1)} %collective-permute-done.43) | copy-start | bytes 1572868
  364.1 2.7 collective-permute-start.44
  364.3 4.0 collective-permute-start.45
  432.7 2.7 collective-permute-start.46
  432.9 3.9 collective-permute-start.47
  447.2 2.0 collective-permute-start.48
  450.2 21.1 %all-to-all-start.1 = ((bf16[16,16,1024]{2,1,0:T(8,128)(2,1)}), bf16[16,16,1024]{2,1,0:T(8,128)(2,1)S(1)}, u32[]{:S(2)}, u32[]{:S(2)}) async-start(bf16[16,16,1024]{2,1,0:T(8,128)(2,1)} %fusion), calls=%async_computation.1 | async-start | bytes 1048576 | tf_op jit(solution)/shard_map/all_to_all | solution.py:1214
  473.1 12.4 %collective-permute-start.49 = (bf16[256,1024]{1,0:T(8,128)(2,1)S(1)}, bf16[256,1024]{1,0:T(8,128)(2,1)S(1)}, u32[]{:S(2)}, u32[]{:S(2)}) collective-permute-start(bf16[256,1024]{1,0:T(8,128)(2,1)S(1)} %broadcast_select_fusion.1), channel_id=1, source_target_pairs={{2,0},{3,1},{1,2},{0,3},{6,4},{7,5},{5,6},{4,7},{10,8},{11,9},{9,1... | collective-permute-start | bytes 1572872 | tf_op jit(solution)/shard_map/ppermute | solution.py:231
  485.6 3.8 collective-permute-start.50
  (97 other events, 462.1 us)
Sparse Core Ops, SparseCore 0:
  10.9 163.8 all-gather.5
  177.7 79.2 all-gather.3

commit v5 on v4

--- a/solution.py
+++ b/solution.py
@@ -487,7 +487,7 @@
     return held[...].reshape(1024, 1024)
 
 
-QKV_TILE, OUTPUT_TILE, FEED_TILE, FEED_BACK_TILE, OUTPUT_BACK_TILE, TURN_TILE, QKV_BACK_TILE = 0, 0, 512, 512, 0, 0, 0
+QKV_TILE, OUTPUT_TILE, FEED_TILE, TURN_TILE, QKV_BACK_TILE = 0, 0, 512, 512, 512
 STRIP = 64
 QKV_ROWS, OUTPUT_ROWS, QKV_BACK_ROWS, FEED_BACK_ROWS = 256, 256, 256, 256
 COLUMNS = 1024
@@ -614,14 +614,18 @@
     store_norm(middle_ref, gain_ref, shift_ref, normed_ref, unit_ref, scale_ref)
 
 
+def fetch_feed_part(form, at_ref, sources, part, expand, reduce, arrived, reduce_first):
+    jobs = [
+        (expand_unit(form, part), 32, expand.at[part], arrived.at[0, part], None),
+        ({WHOLE: 4, GATHERED: 128, MIXED: 0}[form], 128, reduce, arrived.at[1, part], part),
+    ]
+    for unit, rows, held, semaphore, quarter in jobs[::-1] if reduce_first else jobs:
+        fetch(form, at_ref, sources, unit, rows, held, semaphore, quarter)
+
+
 def fetch_feed_forward(form, at_ref, sources, expand, reduce, arrived, reduce_first):
     for part in range(4):
-        jobs = [
-            (expand_unit(form, part), 32, expand.at[part], arrived.at[0, part], None),
-            ({WHOLE: 4, GATHERED: 128, MIXED: 0}[form], 128, reduce, arrived.at[1, part], part),
-        ]
-        for unit, rows, held, semaphore, quarter in jobs[::-1] if reduce_first else jobs:
-            fetch(form, at_ref, sources, unit, rows, held, semaphore, quarter)
+        fetch_feed_part(form, at_ref, sources, part, expand, reduce, arrived, reduce_first)
 
 
 def feed_forward_kernel(
@@ -662,75 +666,60 @@
     result_ref[...] = result_ref[...] + times(rank_reduce_ref[...], reduce_right_ref[...])
 
 
-def feed_backward_kernel(
-    form, at_ref, grad_ref, slope_ref, active_ref, normed_ref, unit_ref, scale_ref, rank_expand_ref, rank_reduce_ref,
-    gain_ref, expand_left_ref, expand_right_ref, reduce_left_ref, reduce_right_ref, *refs,
+def feed_output_backward_kernel(
+    form, output_form, members, at_ref, grad_ref, normed_ref, unit_ref, scale_ref, rank_expand_ref, rank_reduce_ref,
+    attended_ref, rank_output_ref, gain_ref, output_left_ref, output_right_ref, expand_left_ref, expand_right_ref,
+    reduce_left_ref, reduce_right_ref, slope_ref, active_ref, *refs,
 ):
-    sources, (out_ref, *grads) = refs[:-17], refs[-17:-12]
-    expand, reduce, arrived, low_grad, turned, bent, total, turn_sum, *sums = refs[-12:]
-    expand_left_sum, expand_right_sum, reduce_left_sum, reduce_right_sum = sums
-    at_first(lambda: fetch_feed_forward(form, at_ref, sources, expand, reduce, arrived, True))
-
-    @at_first
-    def _():
-        for member in sums:
-            member[...] = jnp.zeros_like(member)
-
+    sources, output_sources, outs, scratch = refs[:members], refs[members:-23], refs[-23:-15], refs[-15:]
+    middle_ref, out_ref, output_left_g, output_right_g, expand_left_g, expand_right_g, reduce_left_g, reduce_right_g = outs
+    (
+        expand, reduce, arrived, held, held_arrived, slope, active, side_arrived,
+        low_grad, turned, bent, total, turn_sum, low_middle, output_turned,
+    ) = scratch
+    for part in range(4):
+        for which, (source, kept) in enumerate(((slope_ref, slope), (active_ref, active))):
+            pltpu.make_async_copy(
+                source.at[:, span(part)], kept.at[part], side_arrived.at[which, part]
+            ).start()
+        fetch_feed_part(form, at_ref, sources, part, expand, reduce, arrived, True)
+    fetch(output_form, at_ref, output_sources, square_unit(output_form, 3), 32, held, held_arrived)
     low_grad[...] = grad_ref[...].astype(low_type)
     turned[...] = times(low_grad[...], reduce_right_ref[...], ROWS_BY_ROWS).astype(low_type)
-    reduce_right_sum[...] = reduce_right_sum[...] + times(rank_reduce_ref[...], low_grad[...], COLS_BY_COLS)
+    reduce_right_g[...] = times(rank_reduce_ref[...], low_grad[...], COLS_BY_COLS).astype(low_type)
     total[...] = jnp.zeros_like(total)
     turn_sum[...] = jnp.zeros_like(turn_sum)
 
     def part_step(part, carry):
         columns = pl.ds(pl.multiple_of(part * COLUMNS, COLUMNS), COLUMNS)
-        await_first(reduce.at[part], arrived.at[1, part])
-        await_first(expand.at[part], arrived.at[0, part])
+        wait_for(slope.at[part], side_arrived.at[0, part])
+        wait_for(active.at[part], side_arrived.at[1, part])
+        wait_for(reduce.at[part], arrived.at[1, part])
+        wait_for(expand.at[part], arrived.at[0, part])
         for rows in row_tiles(grad_ref.shape[0], FEED_BACK_ROWS):
             grad_active = times(low_grad[rows, :], square(reduce.at[part]), ROWS_BY_ROWS) + times(
                 turned[rows, :], reduce_left_ref[:, columns]
             )
-            bent[rows, :] = (grad_active * slope_ref[rows, columns].astype(wide)).astype(low_type)
+            bent[rows, :] = (grad_active * slope[part, rows, :].astype(wide)).astype(low_type)
             total[rows, :] = total[rows, :] + times(bent[rows, :], square(expand.at[part]), ROWS_BY_ROWS)
-        grad_expand = bent[...]
-        turn_sum[...] = turn_sum[...] + times(grad_expand, expand_right_ref[:, columns], ROWS_BY_ROWS)
-        reduce_left_sum[:, columns] = reduce_left_sum[:, columns] + times(
-            turned[...], active_ref[:, columns], COLS_BY_COLS
-        )
-        expand_right_sum[:, columns] = expand_right_sum[:, columns] + times(
-            rank_expand_ref[...], grad_expand, COLS_BY_COLS
-        )
+        turn_sum[...] = turn_sum[...] + times(bent[...], expand_right_ref[:, columns], ROWS_BY_ROWS)
+        reduce_left_g[:, columns] = times(turned[...], active[part], COLS_BY_COLS).astype(low_type)
+        expand_right_g[:, columns] = times(rank_expand_ref[...], bent[...], COLS_BY_COLS).astype(low_type)
         return carry
 
     lax.fori_loop(0, 4, part_step, 0)
     turned[...] = turn_sum[...].astype(low_type)
-    expand_left_sum[...] = expand_left_sum[...] + times(turned[...], normed_ref[...], COLS_BY_COLS)
+    expand_left_g[...] = times(turned[...], normed_ref[...], COLS_BY_COLS).astype(low_type)
     total[...] = total[...] + times(turned[...], expand_left_ref[...])
-    store_pull(out_ref, grad_ref, total, unit_ref, scale_ref, gain_ref)
-
-    @at_last
-    def _():
-        for member, summed in zip(grads, sums):
-            member[...] = summed[...].astype(low_type)
-
-
-def output_backward_kernel(form, at_ref, grad_ref, attended_ref, rank_ref, left_ref, right_ref, *refs):
-    sources, (out_ref, left_g, right_g) = refs[:-7], refs[-7:-4]
-    held, arrived, left_sum, right_sum = refs[-4:]
-    at_first(lambda: fetch(form, at_ref, sources, square_unit(form, 3), 32, held, arrived))
-    low_grad = grad_ref[...].astype(low_type)
-    turned = times(low_grad, right_ref[...], ROWS_BY_ROWS).astype(low_type)
-    gather_sum(right_sum, times(rank_ref[...], low_grad, COLS_BY_COLS))
-    gather_sum(left_sum, times(turned, attended_ref[...], COLS_BY_COLS))
-    await_first(held, arrived)
+    store_pull(middle_ref, grad_ref, total, unit_ref, scale_ref, gain_ref)
+    low_middle[...] = middle_ref[...].astype(low_type)
+    output_turned[...] = times(low_middle[...], output_right_ref[...], ROWS_BY_ROWS).astype(low_type)
+    output_right_g[...] = times(rank_output_ref[...], low_middle[...], COLS_BY_COLS).astype(low_type)
+    output_left_g[...] = times(output_turned[...], attended_ref[...], COLS_BY_COLS).astype(low_type)
+    wait_for(held, held_arrived)
     out_ref[...] = (
-        times(low_grad, square(held), ROWS_BY_ROWS) + times(turned, left_ref[...])
+        times(low_middle[...], square(held), ROWS_BY_ROWS) + times(output_turned[...], output_left_ref[...])
     ).astype(low_type)
-
-    @at_last
-    def _():
-        left_g[...] = left_sum[...].astype(low_type)
-        right_g[...] = right_sum[...].astype(low_type)
 
 
 def qkv_turn_kernel(pieces, form, at_ref, normed_ref, rank_ref, dq_ref, *refs):
@@ -757,7 +746,7 @@
 def qkv_backward_kernel(
     form, at_ref, grad_ref, unit_ref, scale_ref, turned_ref, dq_ref, dk_ref, dv_ref, gain_ref, left_ref, *refs
 ):
-    sources, out_ref, (held, arrived, total) = refs[:-4], refs[-4], refs[-3:]
+    sources, (out_ref, low_ref), (held, arrived, total) = refs[:-5], refs[-5:-3], refs[-3:]
 
     @at_first
     def _():
@@ -770,6 +759,7 @@
         for rows in row_tiles(out_ref.shape[0], QKV_BACK_ROWS):
             total[rows, :] = total[rows, :] + times(member[rows, :], square(held.at[part]), ROWS_BY_ROWS)
     store_pull(out_ref, grad_ref, total, unit_ref, scale_ref, gain_ref)
+    low_ref[...] = out_ref[...].astype(low_type)
 
 
 def qkv_whole_kernel(
@@ -953,33 +943,35 @@
     return (member.shape, LOW)
 
 
-def backward_feed(grad, kept, weights, picked, extras, at):
+def backward_feed_output(grad, kept, weights, output_weights, picked, extras, at):
     rows, columns = grad.shape
-    tile = FEED_BACK_TILE or rows
-    return frozen_call(
-        feed_backward_kernel, "feed_backward", at, weights, FEED_BACK_TILE,
-        (
-            grad, kept.slope, kept.active, kept.normed_two, kept.unit_two, kept.scale_two,
-            kept.rank_expand, kept.rank_reduce,
-        ),
-        (row(extras[6]), *picked[4:]), (((rows, columns), WIDE),), tuple(map(like, picked[4:])),
-        [
-            pltpu.VMEM((4, *SQUARE), LOW), pltpu.VMEM(TALL, LOW), DMA((2, 4)),
-            pltpu.VMEM((tile, columns), LOW), pltpu.VMEM((tile, RANK), LOW), pltpu.VMEM((tile, columns), LOW),
-            pltpu.VMEM((tile, columns), WIDE), pltpu.VMEM((tile, RANK), WIDE),
-        ]
-        + [pltpu.VMEM(member.shape, WIDE) for member in picked[4:]], 22,
+    form, sources = weights
+    output_form, output_sources = output_weights
+    full, full_low, ranks = ((rows, columns), WIDE), ((rows, columns), LOW), ((rows, RANK), LOW)
+    tall = ((4, rows, columns), LOW)
+    members = (
+        grad, kept.normed_two, kept.unit_two, kept.scale_two, kept.rank_expand, kept.rank_reduce,
+        kept.attended_low, kept.rank_output, row(extras[6]), *picked[2:],
     )
-
-
-def backward_output(grad, kept, weights, picked, at):
-    rows, columns = grad.shape
-    return frozen_call(
-        output_backward_kernel, "output_backward", at, weights, OUTPUT_BACK_TILE,
-        (grad, kept.attended_low, kept.rank_output), (picked[2], picked[3]),
-        (((rows, columns), LOW),), (like(picked[2]), like(picked[3])),
-        [pltpu.VMEM(SQUARE, LOW), DMA, pltpu.VMEM(picked[2].shape, WIDE), pltpu.VMEM(picked[3].shape, WIDE)], 5,
-    )
+    local_spec, anywhere = pl.BlockSpec(memory_space=pltpu.VMEM), pl.BlockSpec(memory_space=pl.ANY)
+    outs = (full, full_low, *map(like, picked[2:]))
+    return pl.pallas_call(
+        functools.partial(feed_output_backward_kernel, form, output_form, len(sources)),
+        out_shape=tuple(jax.ShapeDtypeStruct(shape, kind) for shape, kind in outs),
+        in_specs=[pl.BlockSpec(memory_space=pltpu.SMEM)]
+        + [local_spec] * len(members)
+        + [anywhere] * (2 + len(sources) + len(output_sources)),
+        out_specs=(local_spec,) * len(outs),
+        scratch_shapes=[
+            pltpu.VMEM((4, *SQUARE), LOW), pltpu.VMEM(TALL, LOW), DMA((2, 4)), pltpu.VMEM(SQUARE, LOW), DMA,
+            pltpu.VMEM(*tall), pltpu.VMEM(*tall), DMA((2, 4)), pltpu.VMEM(*full_low), pltpu.VMEM(*ranks),
+            pltpu.VMEM(*full_low), pltpu.VMEM(*full), pltpu.VMEM((rows, RANK), WIDE), pltpu.VMEM(*full_low),
+            pltpu.VMEM(*ranks),
+        ],
+        compiler_params=pltpu.CompilerParams(vmem_limit_bytes=60 * 2**20),
+        cost_estimate=pl.CostEstimate(flops=25 * MICROSECOND, bytes_accessed=0, transcendentals=0),
+        name="feed_output_backward",
+    )(at, *members, kept.slope, kept.active, *sources, *output_sources)
 
 
 def backward_turn(grads, kept, picked, at):
@@ -997,7 +989,7 @@
     rows, columns = grad.shape
     query_grad, key_grads, value_grads = grads
     return frozen_call(
-        functools.partial(qkv_whole_kernel, len(key_grads)), "qkv_whole", at, weights, 0,
+        functools.partial(qkv_whole_kernel, len(key_grads)), "qkv_whole", at, weights, QKV_BACK_TILE,
         (
             grad, kept.unit_one, kept.scale_one, kept.normed_one, kept.rank_attend, query_grad, *key_grads,
             *value_grads,
@@ -1016,9 +1008,9 @@
     return frozen_call(
         qkv_backward_kernel, "qkv_backward", at, weights, QKV_BACK_TILE,
         (grad, kept.unit_one, kept.scale_one, turned, *joined), (row(extras[4]), picked[0]),
-        (((rows, columns), WIDE),), (),
+        (((rows, columns), WIDE), ((rows, columns), LOW)), (),
         [pltpu.VMEM((3, *SQUARE), LOW), DMA((3,)), pltpu.VMEM((QKV_BACK_TILE or rows, columns), WIDE)], 9,
-    )[0]
+    )
 
 
 def combine_kernel(places, ids_ref, *refs):
@@ -1217,10 +1209,13 @@
     for layer_index in reversed(range(LAYERS)):
         keep, extra, factors = kept[layer_index], extras[layer_index], picked[layer_index]
         first_weights, second_weights = frozen[layer_index]
-        middle_grad, *feed_terms = backward_feed(grad_current, keep, second_weights, factors, extra, at)
+        middle_grad, attended_grad, *some_terms = backward_feed_output(
+            grad_current, keep, second_weights, first_weights, factors, extra, at
+        )
         if layer_index == LAYERS - 1:
-            middle_grad, feed_terms, result_got = sync((middle_grad, feed_terms, result_got))
-        attended_grad, *output_terms = backward_output(middle_grad, keep, first_weights, factors, at)
+            middle_grad, attended_grad, some_terms, result_got = sync(
+                (middle_grad, attended_grad, some_terms, result_got)
+            )
         query_grad, key_grads, value_grads = attend_backward(
             place, keep.queries, keep.keys, keep.values, attended_grad, keep.attended, keep.stat
         )
@@ -1237,17 +1232,17 @@
             grad_current, *attend_terms = backward_qkv_whole(
                 middle_grad, grads, keep, first_weights, factors, extra, at
             )
-            terms[layer_index] = [*attend_terms, *output_terms, *feed_terms]
+            terms[layer_index] = [*attend_terms, *some_terms]
             continue
         key_grad, value_grad, turned, *attend_terms = backward_turn(grads, keep, factors, at)
-        terms[layer_index] = [*attend_terms, *output_terms, *feed_terms]
+        terms[layer_index] = [*attend_terms, *some_terms]
         received = to_owners([(PACKED, terms[1]), (PACKED, terms[0])])
-        grad_current = backward_qkv(
+        grad_current, low_grad = backward_qkv(
             middle_grad, (query_grad, key_grad, value_grad), turned, keep, first_weights, factors, extra, at
         )
-        received, grad_current = sync((received, grad_current))
-    low_grad = grad_current.astype(low_type)
-    moved = collect_tokens(low_grad, send_across(low_grad, below, count), send_inside(low_grad, count), below)
+    got, other = send_across(low_grad, below, count), send_inside(low_grad, count)
+    received, got = sync((received, got))
+    moved = collect_tokens(low_grad, got, other, below)
     kept_part = collect_own(grad_current, below)
     received = [received]
     places = (((1, PACKED), (0, PACKED)),)

time: 508 us -> 496 us (0.976)
  Pallas kernels: 229 us -> 222 us
    pallas_call x13 -> x9, Pallas kernels: 161 us -> 105 us  [frozen_call(): pl.pallas_call(functools.partial(kernel, form), grid=(count // tile,) if...]
    pallas_call x0 -> x2, Pallas kernels: none -> 50 us  [backward_feed_output(): pl.pallas_call(functools.partial(feed_output_backward_kernel, form, outpu...]
    all_to_all x1, waiting for transfers between devices: 5.5 us -> 0.01 us  [to_owners(): return lax.all_to_all(total, LANE, split_axis=0, concat_axis=0, tiled=True)]
  transfers between devices with their start and end apart: 55 -> 55, of which waited for: 22 -> 21; matrix products, arithmetic and copies ran while one was open for 6% -> 7% of each run, Pallas kernels for 32% -> 33%
where the time goes in v5:
time: 496 us; the launch traced here: 488 us
  Pallas kernels  222 us (45%)
  waiting for transfers between devices  121 us (24%)
  starting transfers between devices  59.3 us (12%)
  local copies, waits for them, and re-layouts  37.4 us (8%)
  other arithmetic  31 us (6%)
  between operations  15.9 us (3%)
    pallas_call x9, Pallas kernels, frozen_call(): pl.pallas_call(functools.partial(kernel, form), grid=(count // tile,) if...  105 us
    ppermute x9, waiting for transfers between devices, along_z(): return lax.ppermute(rows, 'dp', RING)  82.8 us
    pallas_call x2, Pallas kernels, backward_feed_output(): pl.pallas_call(functools.partial(feed_output_backward_kernel, form, outpu...  50 us
    pallas_call x2, Pallas kernels, attend_backward(): pl.pallas_call(functools.partial(attend_backward_kernel, pieces), out_sha...  38.4 us
    unnamed x216, local copies, waits for them, and re-layouts  28.3 us
    pallas_call x2, Pallas kernels, attend_forward(): pl.pallas_call(functools.partial(attend_forward_kernel, pieces), out_shap...  25.5 us
    ppermute x9, starting transfers between devices, along_z(): return lax.ppermute(rows, 'dp', RING)  15.3 us
    ppermute x2, waiting for transfers between devices, send_across(): return lax.ppermute(jnp.where(below, rows[BLK:], rows[:BLK]), CTX, across)  12.9 us
  transfers between devices with their start and end apart: 55, of which 21 were waited for; matrix products, arithmetic and copies ran while one was open for 7% of the time, Pallas kernels for 33%

profile of v5, /device:TPU:0, one launch (start us, length us, event | category | flops | bytes accessed | tf_op | source)
XLA Modules:
  0.0 487.6 jit_solution(313055478596710542)
XLA Ops:
  11.3 3.1 collective-permute-start.1
  15.3 1.5 collective-permute-start.4
  17.7 1.5 collective-permute-start.5
  20.0 1.8 collective-permute-done.1
  24.5 13.8 %collective-permute-done.2 = bf16[128,1024]{1,0:T(8,128)(2,1)S(1)} collective-permute-done((bf16[128,1024]{1,0:T(8,128)(2,1)S(1)}, bf16[128,1024]{1,0:T(8,128)(2,1)S(1)}, u32[]{:S(2)}, u32[]{:S(2)}) %collective-permute-start.2) | collective-permute-done | bytes 262176 | tf_op jit(solution)/shard_map/ppermute | solution.py:289
  38.3 2.2 collective-permute-start.3
  42.7 4.3 collective-permute-done.3
  47.0 8.0 %all-to-all-start = ((bf16[16,2,16,512]{3,2,1,0:T(8,128)(2,1)}), bf16[16,2,16,512]{3,2,1,0:T(8,128)(2,1)S(1)}, u32[]{:S(2)}, u32[]{:S(2)}) async-start(bf16[16,2,16,512]{3,2,1,0:T(8,128)(2,1)} %broadcast_select_fusion), calls=%async_computation | async-start | bytes 1048576 | tf_op jit(solution)/shard_map/all_to_all | solution.py:377
  55.3 2.0 collective-permute-start.6
  57.3 1.5 collective-permute-start.7
  58.9 1.5 collective-permute-start.8
  60.3 24.7 %collective-permute-done.8 = bf16[128,1024]{1,0:T(8,128)(2,1)S(1)} collective-permute-done((bf16[128,1024]{1,0:T(8,128)(2,1)S(1)}, bf16[128,1024]{1,0:T(8,128)(2,1)S(1)}, u32[]{:S(2)}, u32[]{:S(2)}) %collective-permute-start.8) | collective-permute-done | bytes 262176 | tf_op jit(solution)/shard_map/ppermute | solution.py:289
  87.1 4.7 collective-permute-start.10
  92.2 1.5 collective-permute-start.9
  93.6 16.6 %collective-permute-done.14 = bf16[128,1024]{1,0:T(8,128)(2,1)S(1)} collective-permute-done((bf16[128,1024]{1,0:T(8,128)(2,1)S(1)}, bf16[128,1024]{1,0:T(8,128)(2,1)S(1)}, u32[]{:S(2)}, u32[]{:S(2)}) %collective-permute-start.14) | collective-permute-done | bytes 262176 | tf_op jit(solution)/shard_map/ppermute | solution.py:289
  110.2 19.1 %collective-permute-done.15 = bf16[128,1024]{1,0:T(8,128)(2,1)S(1)} collective-permute-done((bf16[128,1024]{1,0:T(8,128)(2,1)S(1)}, bf16[128,1024]{1,0:T(8,128)(2,1)S(1)}, u32[]{:S(2)}, u32[]{:S(2)}) %collective-permute-start.15) | collective-permute-done | bytes 262176 | tf_op jit(solution)/shard_map/ppermute | solution.py:289
  129.3 1.9 collective-permute-done.13.other_ref
  131.2 3.4 collective-permute-done.10.refs_3_.refs_4_
  134.6 3.7 collective-permute-done.9.refs_1_.refs_2_
  139.3 2.7 collective-permute-start.19
  143.2 3.5 collective-permute-start.20
  158.8 1.6 convert_element_type.24.x_ref
  160.3 9.0 %qkv_forward.2 = (bf16[512,1024]{1,0:T(8,128)(2,1)}, bf16[512,1024]{1,0:T(8,128)(2,1)}, f32[512,128]{1,0:T(8,128)}, bf16[512,16]{1,0:T(8,128)(2,1)}, bf16[512,10...) custom-call(s32[4]{0:T(128)} %copy-done.42, f32[512,1024]{1,0:T(8,128)} %convert_element_type.24.x_ref, ...), custom_call_target="tpu_custom_call" | custom-call | flops 900000000 | tf_op jit(solution)/shard_map/qkv_forward/pallas_call | solution.py:806
  170.0 2.4 collective-permute-start.25
  172.4 2.3 pad_maximum_fusion.4.refs_2_.refs_11_.refs_9_
  174.8 2.1 pad_maximum_fusion.3.refs_0_.refs_9_.refs_7_
  177.0 2.6 collective-permute-done.25
  180.6 1.4 collective-permute-start.21
  183.6 1.8 collective-permute-start.26
  188.5 12.7 %attend_forward.2 = (f32[512,1024]{1,0:T(8,128)}, f32[8,2,512]{2,1,0:T(2,128)S(1)}) custom-call(s32[1]{0:T(128)} %bitcast.47.place_ref, bf16[512,1024]{1,0:T(8,128)(2,1)S(1)} %copy-done.3, bf16[512,1024]{1,0:T(8,128)(2,1)S(1)} %copy-done.4, bf16[512,1024]{1,0:T(8,128)(2,1)S(1)} %copy-done.7, bf16[512,1024]{1,0:T(8,128)(2,1)S(1)} %copy-done.5, ...), custom_call_target="tpu_custom_call" | custom-call | flops 1300000000 | tf_op jit(solution)/shard_map/attend_forward/pallas_call | solution.py:157
  201.2 8.1 %output_forward.2 = (bf16[512,1024]{1,0:T(8,128)(2,1)}, f32[512,1024]{1,0:T(8,128)}, bf16[512,1024]{1,0:T(8,128)(2,1)}, bf16[512,1024]{1,0:T(8,128)(2,1)}, f32[512,128]{1,0:T(8,128)}, /*index=5*/bf16[512,16]{1,0:T(8,128)(2,1)}) custom-call(s32[4]{0:T(128)} %copy-done.42, f32[512,1024]{1,0:T(8,128)} %convert_element_type.24.x_ref, ...), custom_call_target="tpu_custom_call" | custom-call | flops 800000000 | tf_op jit(solution)/shard_map/output_forward/pallas_call | solution.py:806
  210.9 1.3 select_bitcast_fusion.5
  212.2 1.3 select_bitcast_fusion.7
  214.7 1.5 collective-permute-start.32
  218.0 20.8 %feed_forward.2 = (f32[512,1024]{1,0:T(8,128)}, bf16[512,4096]{1,0:T(8,128)(2,1)}, bf16[512,4096]{1,0:T(8,128)(2,1)}, bf16[512,16]{1,0:T(8,128)(2,1)}, bf16[512,16]{1,0:T(8,128)(2,1)}) custom-call(s32[4]{0:T(128)} %copy-done.42, bf16[512,1024]{1,0:T(8,128)(2,1)} %get-tuple-element.666.normed_ref, f32[512,1024]{1,0:T(8,128)} %get-tuple-element.469.middle_ref, ...), custom_call_target="tpu_custom_call" | custom-call | flops 2000000000 | tf_op jit(solution)/shard_map/feed_forward/pallas_call | solution.py:806
  240.2 8.7 %qkv_forward.3 = (bf16[512,1024]{1,0:T(8,128)(2,1)}, bf16[512,1024]{1,0:T(8,128)(2,1)}, f32[512,128]{1,0:T(8,128)}, bf16[512,16]{1,0:T(8,128)(2,1)}, bf16[512,10...) custom-call(s32[4]{0:T(128)} %copy-done.42, f32[512,1024]{1,0:T(8,128)} %get-tuple-element.564.x_ref, ...), custom_call_target="tpu_custom_call" | custom-call | flops 900000000 | tf_op jit(solution)/shard_map/qkv_forward/pallas_call | solution.py:806
  249.5 2.2 pad_maximum_fusion.6.refs_2_
  251.8 2.0 collective-permute-start.34
  253.8 2.2 pad_maximum_fusion.5.refs_0_
  257.0 12.7 %attend_forward.3 = (f32[512,1024]{1,0:T(8,128)}, f32[8,2,512]{2,1,0:T(2,128)S(1)}) custom-call(s32[1]{0:T(128)} %bitcast.47.place_ref, bf16[512,1024]{1,0:T(8,128)(2,1)S(1)} %copy-done.10, bf16[512,1024]{1,0:T(8,128)(2,1)S(1)} %copy-done.11, bf16[512,1024]{1,0:T(8,128)(2,1)S(1)} %collective-permute-done.37.refs_1_, bf16[512,1024]{1,0:T(8,128)(2,1)S(1)} %copy-done.12, ...), custom_call_target="tpu_custom_call" | custom-call | flops 1300000000 | tf_op jit(solution)/shard_map/attend_forward/pallas_call | solution.py:157
  269.7 8.2 %output_forward.3 = (bf16[512,1024]{1,0:T(8,128)(2,1)}, f32[512,1024]{1,0:T(8,128)}, bf16[512,1024]{1,0:T(8,128)(2,1)}, bf16[512,1024]{1,0:T(8,128)(2,1)}, f32[512,128]{1,0:T(8,128)}, /*index=5*/bf16[512,16]{1,0:T(8,128)(2,1)}) custom-call(s32[4]{0:T(128)} %copy-done.42, f32[512,1024]{1,0:T(8,128)} %get-tuple-element.564.x_ref, ...), custom_call_target="tpu_custom_call" | custom-call | flops 800000000 | tf_op jit(solution)/shard_map/output_forward/pallas_call | solution.py:806
  278.0 4.0 collective-permute-done.33.refs_1_
  284.9 1.5 collective-permute-done.40.refs_7_
  287.4 20.8 %feed_forward.3 = (f32[512,1024]{1,0:T(8,128)}, bf16[512,4096]{1,0:T(8,128)(2,1)}, bf16[512,4096]{1,0:T(8,128)(2,1)}, bf16[512,16]{1,0:T(8,128)(2,1)}, bf16[512,16]{1,0:T(8,128)(2,1)}) custom-call(s32[4]{0:T(128)} %copy-done.42, bf16[512,1024]{1,0:T(8,128)(2,1)} %get-tuple-element.596.normed_ref, f32[512,1024]{1,0:T(8,128)} %get-tuple-element.597.middle_ref, ...), custom_call_target="tpu_custom_call" | custom-call | flops 2000000000 | tf_op jit(solution)/shard_map/feed_forward/pallas_call | solution.py:806
  309.1 1.9 convert_element_type.25
  311.3 1.6 maximum_convert_fusion.grad_ref
  312.9 26.4 %feed_output_backward.2 = (f32[512,1024]{1,0:T(8,128)}, bf16[512,1024]{1,0:T(8,128)(2,1)}, bf16[16,1024]{1,0:T(8,128)(2,1)}, bf16[16,1024]{1,0:T(8,128)(2,1)}, b...) custom-call(s32[4]{0:T(128)} %copy-done.42, ...), custom_call_target="tpu_custom_call" | custom-call | flops 2500000000 | tf_op jit(solution)/shard_map/feed_output_backward/pallas_call | solution.py:958
  340.1 19.3 %attend_backward.2 = (bf16[512,1024]{1,0:T(8,128)(2,1)S(1)}, bf16[512,1024]{1,0:T(8,128)(2,1)S(1)}, bf16[512,1024]{1,0:T(8,128)(2,1)S(1)}, bf16[512,1024]{1,0:T(8,128)(2,1)S(1)}, bf16[512,1024]{1,0:T(8,128)(2,1)S(1)}) custom-call(s32[1]{0:T(128)} %bitcast.47.place_ref, bf16[512,1024]{1,0:T(8,128)(2,1)} %get-tuple-element.639.q_ref, ...), custom_call_target="tpu_custom_call" | custom-call | flops 2100000000 | tf_op jit(solution)/shard_map/attend_backward/pallas_call | solution.py:183
  362.9 2.1 collective-permute-done.44.refs_1_
  365.1 1.6 collective-permute-done.45.refs_3_
  366.7 12.7 %qkv_whole.1 = (f32[512,1024]{1,0:T(8,128)}, bf16[16,1024]{1,0:T(8,128)(2,1)}, bf16[16,3072]{1,0:T(8,128)(2,1)}) custom-call(s32[4]{0:T(128)} %copy-done.42, f32[512,1024]{1,0:T(8,128)} %get-tuple-element.653.grad_ref, bf16[512,1024]{1,0:T(8,128)(2,1)} %get-tuple-element.654.unit_ref, f32[512,128]{1,0:T(8,128)} %get-tuple-element.655.scale_ref, ...), custom_call_target="tpu_custom_call" | custom-call | flops 1100000000 | tf_op jit(solution)/shard_map/qkv_whole/pallas_call | solution.py:806
  379.4 23.6 %feed_output_backward.3 = (f32[512,1024]{1,0:T(8,128)}, bf16[512,1024]{1,0:T(8,128)(2,1)}, bf16[16,1024]{1,0:T(8,128)(2,1)}, bf16[16,1024]{1,0:T(8,128)(2,1)}, b...) custom-call(s32[4]{0:T(128)} %copy-done.42, ...), custom_call_target="tpu_custom_call" | custom-call | flops 2500000000 | tf_op jit(solution)/shard_map/feed_output_backward/pallas_call | solution.py:958
  403.1 19.1 %attend_backward.3 = (bf16[512,1024]{1,0:T(8,128)(2,1)S(1)}, bf16[512,1024]{1,0:T(8,128)(2,1)S(1)}, bf16[512,1024]{1,0:T(8,128)(2,1)S(1)}, bf16[512,1024]{1,0:T(8,128)(2,1)S(1)}, bf16[512,1024]{1,0:T(8,128)(2,1)S(1)}) custom-call(s32[1]{0:T(128)} %bitcast.47.place_ref, bf16[512,1024]{1,0:T(8,128)(2,1)} %get-tuple-element.694.q_ref, ...), custom_call_target="tpu_custom_call" | custom-call | flops 2100000000 | tf_op jit(solution)/shard_map/attend_backward/pallas_call | solution.py:183
  425.7 2.1 collective-permute-done.46.refs_1_
  427.8 1.5 collective-permute-done.47.refs_3_
  430.5 6.3 %qkv_turn.1 = (bf16[512,1024]{1,0:T(8,128)(2,1)}, bf16[512,1024]{1,0:T(8,128)(2,1)}, bf16[512,16]{1,0:T(8,128)(2,1)}, bf16[16,1024]{1,0:T(8,128)(2,1)}, bf16[16,3072]{1,0:T(8,128)(2,1)}) custom-call(s32[4]{0:T(128)} %copy-done.42, bf16[512,1024]{1,0:T(8,128)(2,1)} %get-tuple-element.692.normed_ref, bf16[512,16]{1,0:T(8,128)(2,1)} %get-tuple-element.693.rank_ref, ...), custom_call_target="tpu_custom_call" | custom-call | flops 300000000 | tf_op jit(solution)/shard_map/qkv_turn/pallas_call | solution.py:806
  440.1 1.6 collective-permute-done.48
  442.7 5.7 %all-to-all-start.1 = ((bf16[16,16,1024]{2,1,0:T(8,128)(2,1)}), bf16[16,16,1024]{2,1,0:T(8,128)(2,1)S(1)}, u32[]{:S(2)}, u32[]{:S(2)}) async-start(bf16[16,16,1024]{2,1,0:T(8,128)(2,1)} %fusion), calls=%async_computation.1 | async-start | bytes 1048576 | tf_op jit(solution)/shard_map/all_to_all | solution.py:1206
  448.3 10.3 %qkv_backward.1 = (f32[512,1024]{1,0:T(8,128)}, bf16[512,1024]{1,0:T(8,128)(2,1)}) custom-call(s32[4]{0:T(128)} %copy-done.42, f32[512,1024]{1,0:T(8,128)} %get-tuple-element.689.grad_ref, bf16[512,1024]{1,0:T(8,128)(2,1)} %get-tuple-element.690.unit_ref, f32[512,128]{1,0:T(8,128)} %get-tuple-element.691.scale_ref, ...), custom_call_target="tpu_custom_call" | custom-call | flops 900000000 | tf_op jit(solution)/shard_map/qkv_backward/pallas_call | solution.py:806
  458.7 1.3 broadcast_select_fusion.1
  460.0 1.4 collective-permute-start.49
  461.5 12.9 %collective-permute-done.49 = bf16[256,1024]{1,0:T(8,128)(2,1)S(1)} collective-permute-done((bf16[256,1024]{1,0:T(8,128)(2,1)S(1)}, bf16[256,1024]{1,0:T(8,128)(2,1)S(1)}, u32[]{:S(2)}, u32[]{:S(2)}) %collective-permute-start.49) | collective-permute-done | bytes 524320 | tf_op jit(solution)/shard_map/ppermute | solution.py:231
  476.7 1.8 combine.1
  478.5 1.8 maximum_select_fusion
  (354 shorter events, 62.5 us)
Async XLA Ops:
  7.2 210.8 %all-gather.6.cloned.1.call-start = ((), (), s32[]{:S(2)}) async-start(), calls=%async_computation.3 | async-start | bytes 17301504 | tf_op jit(solution)/shard_map/all_gather | solution.py:347
  10.4 273.3 %all-gather.4.cloned.1.call-start = ((), (), s32[]{:S(2)}) async-start(), calls=%async_computation.2 | async-start | bytes 8650752 | tf_op jit(solution)/shard_map/all_gather | solution.py:347
  11.3 10.4 %collective-permute-start.1 = (bf16[128,1024]{1,0:T(8,128)(2,1)S(1)}, bf16[128,1024]{1,0:T(8,128)(2,1)S(1)}, u32[]{:S(2)}, u32[]{:S(2)}) collective-permute-start(bf16[128,1024]{1,0:T(8,128)(2,1)S(1)} %pad_maximum_fusion.14), channel_id=1, source_target_pairs={{0,8},{4,12},{8,24},{12,28},{16,0},{20,4},{24,16},{28,20},{1,9},{5... | collective-permute-start | bytes 786440 | tf_op jit(solution)/shard_map/ppermute | solution.py:289
  15.3 25.2 %collective-permute-start.4 = (bf16[256,1024]{1,0:T(8,128)(2,1)}, bf16[256,1024]{1,0:T(8,128)(2,1)}, u32[]{:S(2)}, u32[]{:S(2)}) collective-permute-start(bf16[256,1024]{1,0:T(8,128)(2,1)} %bitcast_select_fusion.3), channel_id=1, source_target_pairs={{0,2},{1,3},{2,1},{3,0},{4,6},{5,7},{6,5},{7,4},{8,10},{9,11},{10,... | collective-permute-start | bytes 1572872 | tf_op jit(solution)/shard_map/ppermute | solution.py:210
  17.7 22.8 %collective-permute-start.5 = (bf16[256,1024]{1,0:T(8,128)(2,1)}, bf16[256,1024]{1,0:T(8,128)(2,1)}, u32[]{:S(2)}, u32[]{:S(2)}) collective-permute-start(bf16[256,1024]{1,0:T(8,128)(2,1)} %slice_bitcast_fusion.3), channel_id=1, source_target_pairs={{2,3},{3,2},{6,7},{7,6},{10,11},{11,10},{14,15},{15,14},{18,19},{1... | collective-permute-start | bytes 1572872 | tf_op jit(solution)/shard_map/ppermute | solution.py:215
  19.9 38.9 %copy-start.68 = (bf16[128,1024]{1,0:T(8,128)(2,1)}, bf16[128,1024]{1,0:T(8,128)(2,1)S(1)}, u32[]{:S(2)}) copy-start(bf16[128,1024]{1,0:T(8,128)(2,1)S(1)} %pad_maximum_fusion.15) | copy-start | bytes 786436
  21.7 16.5 %collective-permute-start.2 = (bf16[128,1024]{1,0:T(8,128)(2,1)S(1)}, bf16[128,1024]{1,0:T(8,128)(2,1)S(1)}, u32[]{:S(2)}, u32[]{:S(2)}) collective-permute-start(bf16[128,1024]{1,0:T(8,128)(2,1)S(1)} %collective-permute-done.1), channel_id=1, source_target_pairs={{0,8},{4,12},{8,24},{12,28},{16,0},{20,4},{24,16},{28,20},{1,9},{5... | collective-permute-start | bytes 786440 | tf_op jit(solution)/shard_map/ppermute | solution.py:289
  38.3 8.7 %collective-permute-start.3 = (bf16[128,1024]{1,0:T(8,128)(2,1)S(1)}, bf16[128,1024]{1,0:T(8,128)(2,1)S(1)}, u32[]{:S(2)}, u32[]{:S(2)}) collective-permute-start(bf16[128,1024]{1,0:T(8,128)(2,1)S(1)} %collective-permute-done.2), channel_id=1, source_target_pairs={{0,8},{4,12},{8,24},{12,28},{16,0},{20,4},{24,16},{28,20},{1,9},{5... | collective-permute-start | bytes 786440 | tf_op jit(solution)/shard_map/ppermute | solution.py:289
  47.0 38.1 %all-to-all-start = ((bf16[16,2,16,512]{3,2,1,0:T(8,128)(2,1)}), bf16[16,2,16,512]{3,2,1,0:T(8,128)(2,1)S(1)}, u32[]{:S(2)}, u32[]{:S(2)}) async-start(bf16[16,2,16,512]{3,2,1,0:T(8,128)(2,1)} %broadcast_select_fusion), calls=%async_computation | async-start | bytes 1048576 | tf_op jit(solution)/shard_map/all_to_all | solution.py:377
  55.3 29.8 %collective-permute-start.6 = (bf16[4,64,1024]{2,1,0:T(8,128)(2,1)S(1)}, bf16[4,64,1024]{2,1,0:T(8,128)(2,1)S(1)}, u32[]{:S(2)}, u32[]{:S(2)}) collective-permute-start(bf16[4,64,1024]{2,1,0:T(8,128)(2,1)S(1)} %pad_maximum_fusion.8), channel_id=1, source_target_pairs={{0,4},{4,0},{8,12},{12,8},{16,20},{20,16},{24,28},{28,24},{1,5},{5... | collective-permute-start | bytes 1572872 | tf_op jit(solution)/shard_map/ppermute | solution.py:293
  57.3 27.7 %collective-permute-start.7 = (bf16[4,64,1024]{2,1,0:T(8,128)(2,1)S(1)}, bf16[4,64,1024]{2,1,0:T(8,128)(2,1)}, u32[]{:S(2)}, u32[]{:S(2)}) collective-permute-start(bf16[4,64,1024]{2,1,0:T(8,128)(2,1)S(1)} %pad_maximum_fusion.9), channel_id=1, source_target_pairs={{0,2},{2,0},{1,3},{3,1},{4,6},{6,4},{5,7},{7,5},{8,10},{10,8},{9,1... | collective-permute-start | bytes 1572872 | tf_op jit(solution)/shard_map/ppermute | solution.py:297
  58.9 26.2 %collective-permute-start.8 = (bf16[128,1024]{1,0:T(8,128)(2,1)S(1)}, bf16[128,1024]{1,0:T(8,128)(2,1)S(1)}, u32[]{:S(2)}, u32[]{:S(2)}) collective-permute-start(bf16[128,1024]{1,0:T(8,128)(2,1)S(1)} %pad_maximum_fusion.15), channel_id=1, source_target_pairs={{0,8},{4,12},{8,24},{12,28},{16,0},{20,4},{24,16},{28,20},{1,9},{5... | collective-permute-start | bytes 786440 | tf_op jit(solution)/shard_map/ppermute | solution.py:289
  85.8 43.4 %copy-start.99 = (f32[2,2048]{1,0:T(2,128)S(1)}, f32[2,2048]{1,0:T(2,128)}, u32[]{:S(2)}) copy-start(f32[2,2048]{1,0:T(2,128)} %param.30) | copy-start | bytes 49156
  85.8 53.0 %copy-start.69 = (bf16[128,1024]{1,0:T(8,128)(2,1)S(1)}, bf16[128,1024]{1,0:T(8,128)(2,1)}, u32[]{:S(2)}) copy-start(bf16[128,1024]{1,0:T(8,128)(2,1)} %copy-done.68) | copy-start | bytes 786436
  87.1 51.9 %copy-start.54 = (bf16[2,4,64,1024]{3,2,1,0:T(8,128)(2,1)}, bf16[2,4,64,1024]{3,2,1,0:T(8,128)(2,1)S(1)}, u32[]{:S(2)}) copy-start(bf16[2,4,64,1024]{3,2,1,0:T(8,128)(2,1)S(1)} %pad_maximum_fusion.2.refs_2_.refs_3_) | copy-start | bytes 3145732
  87.1 44.1 %collective-permute-start.12 = (bf16[2,4,64,1024]{3,2,1,0:T(8,128)(2,1)S(1)}, bf16[2,4,64,1024]{3,2,1,0:T(8,128)(2,1)S(1)}, u32[]{:S(2)}, u32[]{:S(2)}) collective-permute-start(bf16[2,4,64,1024]{3,2,1,0:T(8,128)(2,1)S(1)} %pad_maximum_fusion.2.refs_2_.refs_3_), channel_id=1, source_target_pairs={{0,1},{1,0},{2,3},{3,2},{4,5},{5,4},{6,7},{7,6},{8,9},{9,8},{10,11... | collective-permute-start | bytes 3145736 | tf_op jit(solution)/shard_map/ppermute | solution.py:301
  87.1 47.5 %collective-permute-start.10 = (bf16[2,4,64,1024]{3,2,1,0:T(8,128)(2,1)S(1)}, bf16[2,4,64,1024]{3,2,1,0:T(8,128)(2,1)}, u32[]{:S(2)}, u32[]{:S(2)}) collective-permute-start(bf16[2,4,64,1024]{3,2,1,0:T(8,128)(2,1)S(1)} %pad_maximum_fusion.2.refs_2_.refs_3_), channel_id=1, source_target_pairs={{0,4},{4,0},{8,12},{12,8},{16,20},{20,16},{24,28},{28,24},{1,5},{5... | collective-permute-start | bytes 3145736 | tf_op jit(solution)/shard_map/ppermute | solution.py:293
  91.8 18.4 %collective-permute-start.14 = (bf16[128,1024]{1,0:T(8,128)(2,1)S(1)}, bf16[128,1024]{1,0:T(8,128)(2,1)S(1)}, u32[]{:S(2)}, u32[]{:S(2)}) collective-permute-start(bf16[128,1024]{1,0:T(8,128)(2,1)S(1)} %collective-permute-done.8), channel_id=1, source_target_pairs={{0,8},{4,12},{8,24},{12,28},{16,0},{20,4},{24,16},{28,20},{1,9},{5... | collective-permute-start | bytes 786440 | tf_op jit(solution)/shard_map/ppermute | solution.py:289
  91.9 47.2 %copy-start.55 = (bf16[2,4,64,1024]{3,2,1,0:T(8,128)(2,1)}, bf16[2,4,64,1024]{3,2,1,0:T(8,128)(2,1)S(1)}, u32[]{:S(2)}) copy-start(bf16[2,4,64,1024]{3,2,1,0:T(8,128)(2,1)S(1)} %pad_maximum_fusion.1.refs_0_.refs_1_) | copy-start | bytes 3145732
  91.9 42.7 %collective-permute-start.11 = (bf16[2,4,64,1024]{3,2,1,0:T(8,128)(2,1)S(1)}, bf16[2,4,64,1024]{3,2,1,0:T(8,128)(2,1)S(1)}, u32[]{:S(2)}, u32[]{:S(2)}) collective-permute-start(bf16[2,4,64,1024]{3,2,1,0:T(8,128)(2,1)S(1)} %pad_maximum_fusion.1.refs_0_.refs_1_), channel_id=1, source_target_pairs={{0,1},{1,0},{2,3},{3,2},{4,5},{5,4},{6,7},{7,6},{8,9},{9,8},{10,11... | collective-permute-start | bytes 3145736 | tf_op jit(solution)/shard_map/ppermute | solution.py:301
  92.2 46.2 %collective-permute-start.9 = (bf16[2,4,64,1024]{3,2,1,0:T(8,128)(2,1)S(1)}, bf16[2,4,64,1024]{3,2,1,0:T(8,128)(2,1)}, u32[]{:S(2)}, u32[]{:S(2)}) collective-permute-start(bf16[2,4,64,1024]{3,2,1,0:T(8,128)(2,1)S(1)} %pad_maximum_fusion.1.refs_0_.refs_1_), channel_id=1, source_target_pairs={{0,2},{2,0},{1,3},{3,1},{4,6},{6,4},{5,7},{7,5},{8,10},{10,8},{9,1... | collective-permute-start | bytes 3145736 | tf_op jit(solution)/shard_map/ppermute | solution.py:297
  110.2 19.1 %collective-permute-start.15 = (bf16[128,1024]{1,0:T(8,128)(2,1)S(1)}, bf16[128,1024]{1,0:T(8,128)(2,1)S(1)}, u32[]{:S(2)}, u32[]{:S(2)}) collective-permute-start(bf16[128,1024]{1,0:T(8,128)(2,1)S(1)} %collective-permute-done.14), channel_id=1, source_target_pairs={{0,8},{4,12},{8,24},{12,28},{16,0},{20,4},{24,16},{28,20},{1,9},{5... | collective-permute-start | bytes 786440 | tf_op jit(solution)/shard_map/ppermute | solution.py:289
  129.3 1.9 collective-permute-start.13
  138.3 20.4 %collective-permute-start.16 = (bf16[2,4,64,1024]{3,2,1,0:T(8,128)(2,1)}, bf16[2,4,64,1024]{3,2,1,0:T(8,128)(2,1)}, u32[]{:S(2)}, u32[]{:S(2)}) collective-permute-start(bf16[2,4,64,1024]{3,2,1,0:T(8,128)(2,1)} %collective-permute-done.9.refs_1_.refs_2_), channel_id=1, source_target_pairs={{0,1},{1,0},{2,3},{3,2},{4,5},{5,4},{6,7},{7,6},{8,9},{9,8},{10,11... | collective-permute-start | bytes 3145736 | tf_op jit(solution)/shard_map/ppermute | solution.py:301
  138.3 20.4 %collective-permute-start.17 = (bf16[2,4,64,1024]{3,2,1,0:T(8,128)(2,1)}, bf16[2,4,64,1024]{3,2,1,0:T(8,128)(2,1)}, u32[]{:S(2)}, u32[]{:S(2)}) collective-permute-start(bf16[2,4,64,1024]{3,2,1,0:T(8,128)(2,1)} %collective-permute-done.10.refs_3_.refs_4_), channel_id=1, source_target_pairs={{0,1},{1,0},{2,3},{3,2},{4,5},{5,4},{6,7},{7,6},{8,9},{9,8},{10,11... | collective-permute-start | bytes 3145736 | tf_op jit(solution)/shard_map/ppermute | solution.py:301
  139.0 19.7 %copy-start.62 = (bf16[512,1024]{1,0:T(8,128)(2,1)S(1)}, bf16[512,1024]{1,0:T(8,128)(2,1)}, u32[]{:S(2)}) copy-start(bf16[512,1024]{1,0:T(8,128)(2,1)} %pad_maximum_fusion) | copy-start | bytes 3145732
  139.1 21.2 %copy-start.70 = (bf16[4,64,1024]{2,1,0:T(8,128)(2,1)}, bf16[4,64,1024]{2,1,0:T(8,128)(2,1)S(1)}, u32[]{:S(2)}) copy-start(bf16[4,64,1024]{2,1,0:T(8,128)(2,1)S(1)} %pad_maximum_fusion.10) | copy-start | bytes 1572868
  139.2 19.1 %collective-permute-start.18 = (bf16[4,64,1024]{2,1,0:T(8,128)(2,1)S(1)}, bf16[4,64,1024]{2,1,0:T(8,128)(2,1)}, u32[]{:S(2)}, u32[]{:S(2)}) collective-permute-start(bf16[4,64,1024]{2,1,0:T(8,128)(2,1)S(1)} %pad_maximum_fusion.10), channel_id=1, source_target_pairs={{0,4},{4,0},{8,12},{12,8},{16,20},{20,16},{24,28},{28,24},{1,5},{5... | collective-permute-start | bytes 1572872 | tf_op jit(solution)/shard_map/ppermute | solution.py:293
  139.3 21.0 %copy-start.72 = (bf16[4,64,1024]{2,1,0:T(8,128)(2,1)}, bf16[4,64,1024]{2,1,0:T(8,128)(2,1)S(1)}, u32[]{:S(2)}) copy-start(bf16[4,64,1024]{2,1,0:T(8,128)(2,1)S(1)} %pad_maximum_fusion.11) | copy-start | bytes 1572868
  139.3 19.4 %collective-permute-start.19 = (bf16[4,64,1024]{2,1,0:T(8,128)(2,1)S(1)}, bf16[4,64,1024]{2,1,0:T(8,128)(2,1)}, u32[]{:S(2)}, u32[]{:S(2)}) collective-permute-start(bf16[4,64,1024]{2,1,0:T(8,128)(2,1)S(1)} %pad_maximum_fusion.11), channel_id=1, source_target_pairs={{0,2},{2,0},{1,3},{3,1},{4,6},{6,4},{5,7},{7,5},{8,10},{10,8},{9,1... | collective-permute-start | bytes 1572872 | tf_op jit(solution)/shard_map/ppermute | solution.py:297
  143.2 15.1 %collective-permute-start.20 = (bf16[128,1024]{1,0:T(8,128)(2,1)S(1)}, bf16[128,1024]{1,0:T(8,128)(2,1)}, u32[]{:S(2)}, u32[]{:S(2)}) collective-permute-start(bf16[128,1024]{1,0:T(8,128)(2,1)S(1)} %pad_maximum_fusion.16), channel_id=1, source_target_pairs={{0,8},{4,12},{8,24},{12,28},{16,0},{20,4},{24,16},{28,20},{1,9},{5... | collective-permute-start | bytes 786440 | tf_op jit(solution)/shard_map/ppermute | solution.py:289
  169.4 10.2 %collective-permute-start.27 = (bf16[512,1024]{1,0:T(8,128)(2,1)}, bf16[512,1024]{1,0:T(8,128)(2,1)S(1)}, u32[]{:S(2)}, u32[]{:S(2)}) collective-permute-start(bf16[512,1024]{1,0:T(8,128)(2,1)} %get-tuple-element.698.refs_0_), channel_id=1, source_target_pairs={{0,1},{1,0},{2,3},{3,2},{4,5},{5,4},{6,7},{7,6},{8,9},{9,8},{10,11... | collective-permute-start | bytes 3145736 | tf_op jit(solution)/shard_map/ppermute | solution.py:258
  169.5 13.1 %collective-permute-start.28 = (bf16[512,1024]{1,0:T(8,128)(2,1)}, bf16[512,1024]{1,0:T(8,128)(2,1)S(1)}, u32[]{:S(2)}, u32[]{:S(2)}) collective-permute-start(bf16[512,1024]{1,0:T(8,128)(2,1)} %get-tuple-element.700.refs_2_), channel_id=1, source_target_pairs={{0,1},{1,0},{2,3},{3,2},{4,5},{5,4},{6,7},{7,6},{8,9},{9,8},{10,11... | collective-permute-start | bytes 3145736 | tf_op jit(solution)/shard_map/ppermute | solution.py:258
  170.0 9.6 %collective-permute-start.25 = (bf16[128,1024]{1,0:T(8,128)(2,1)}, bf16[128,1024]{1,0:T(8,128)(2,1)}, u32[]{:S(2)}, u32[]{:S(2)}) collective-permute-start(bf16[128,1024]{1,0:T(8,128)(2,1)} %collective-permute-done.20), channel_id=1, source_target_pairs={{0,8},{4,12},{8,24},{12,28},{16,0},{20,4},{24,16},{28,20},{1,9},{5... | collective-permute-start | bytes 786440 | tf_op jit(solution)/shard_map/ppermute | solution.py:289
  174.7 34.6 %collective-permute-start.24 = (bf16[2,4,64,1024]{3,2,1,0:T(8,128)(2,1)}, bf16[2,4,64,1024]{3,2,1,0:T(8,128)(2,1)}, u32[]{:S(2)}, u32[]{:S(2)}) collective-permute-start(bf16[2,4,64,1024]{3,2,1,0:T(8,128)(2,1)} %pad_maximum_fusion.4.refs_2_.refs_11_.refs_9_), channel_id=1, source_target_pairs={{0,1},{1,0},{2,3},{3,2},{4,5},{5,4},{6,7},{7,6},{8,9},{9,8},{10,11... | collective-permute-start | bytes 3145736 | tf_op jit(solution)/shard_map/ppermute | solution.py:301
  174.7 34.6 %collective-permute-start.22 = (bf16[2,4,64,1024]{3,2,1,0:T(8,128)(2,1)}, bf16[2,4,64,1024]{3,2,1,0:T(8,128)(2,1)}, u32[]{:S(2)}, u32[]{:S(2)}) collective-permute-start(bf16[2,4,64,1024]{3,2,1,0:T(8,128)(2,1)} %pad_maximum_fusion.4.refs_2_.refs_11_.refs_9_), channel_id=1, source_target_pairs={{0,4},{4,0},{8,12},{12,8},{16,20},{20,16},{24,28},{28,24},{1,5},{5... | collective-permute-start | bytes 3145736 | tf_op jit(solution)/shard_map/ppermute | solution.py:293
  179.6 29.8 %collective-permute-start.23 = (bf16[2,4,64,1024]{3,2,1,0:T(8,128)(2,1)}, bf16[2,4,64,1024]{3,2,1,0:T(8,128)(2,1)}, u32[]{:S(2)}, u32[]{:S(2)}) collective-permute-start(bf16[2,4,64,1024]{3,2,1,0:T(8,128)(2,1)} %pad_maximum_fusion.3.refs_0_.refs_9_.refs_7_), channel_id=1, source_target_pairs={{0,1},{1,0},{2,3},{3,2},{4,5},{5,4},{6,7},{7,6},{8,9},{9,8},{10,11... | collective-permute-start | bytes 3145736 | tf_op jit(solution)/shard_map/ppermute | solution.py:301
  180.6 29.2 %collective-permute-start.21 = (bf16[2,4,64,1024]{3,2,1,0:T(8,128)(2,1)}, bf16[2,4,64,1024]{3,2,1,0:T(8,128)(2,1)}, u32[]{:S(2)}, u32[]{:S(2)}) collective-permute-start(bf16[2,4,64,1024]{3,2,1,0:T(8,128)(2,1)} %pad_maximum_fusion.3.refs_0_.refs_9_.refs_7_), channel_id=1, source_target_pairs={{0,2},{2,0},{1,3},{3,1},{4,6},{6,4},{5,7},{7,5},{8,10},{10,8},{9,1... | collective-permute-start | bytes 3145736 | tf_op jit(solution)/shard_map/ppermute | solution.py:297
  183.6 25.7 %collective-permute-start.26 = (bf16[128,1024]{1,0:T(8,128)(2,1)}, bf16[128,1024]{1,0:T(8,128)(2,1)}, u32[]{:S(2)}, u32[]{:S(2)}) collective-permute-start(bf16[128,1024]{1,0:T(8,128)(2,1)} %collective-permute-done.25), channel_id=1, source_target_pairs={{0,8},{4,12},{8,24},{12,28},{16,0},{20,4},{24,16},{28,20},{1,9},{5... | collective-permute-start | bytes 786440 | tf_op jit(solution)/shard_map/ppermute | solution.py:289
  213.6 25.2 %collective-permute-start.31 = (bf16[4,64,1024]{2,1,0:T(8,128)(2,1)S(1)}, bf16[4,64,1024]{2,1,0:T(8,128)(2,1)}, u32[]{:S(2)}, u32[]{:S(2)}) collective-permute-start(bf16[4,64,1024]{2,1,0:T(8,128)(2,1)S(1)} %pad_maximum_fusion.12), channel_id=1, source_target_pairs={{0,4},{4,0},{8,12},{12,8},{16,20},{20,16},{24,28},{28,24},{1,5},{5... | collective-permute-start | bytes 1572872 | tf_op jit(solution)/shard_map/ppermute | solution.py:293
  214.7 24.1 %collective-permute-start.32 = (bf16[4,64,1024]{2,1,0:T(8,128)(2,1)S(1)}, bf16[4,64,1024]{2,1,0:T(8,128)(2,1)}, u32[]{:S(2)}, u32[]{:S(2)}) collective-permute-start(bf16[4,64,1024]{2,1,0:T(8,128)(2,1)S(1)} %pad_maximum_fusion.13), channel_id=1, source_target_pairs={{0,2},{2,0},{1,3},{3,1},{4,6},{6,4},{5,7},{7,5},{8,10},{10,8},{9,1... | collective-permute-start | bytes 1572872 | tf_op jit(solution)/shard_map/ppermute | solution.py:297
  216.3 22.6 %collective-permute-start.29 = (bf16[2,4,64,1024]{3,2,1,0:T(8,128)(2,1)}, bf16[2,4,64,1024]{3,2,1,0:T(8,128)(2,1)S(1)}, u32[]{:S(2)}, u32[]{:S(2)}) collective-permute-start(bf16[2,4,64,1024]{3,2,1,0:T(8,128)(2,1)} %collective-permute-done.21.refs_1_.refs_10_.refs_8_), channel_id=1, source_target_pairs={{0,1},{1,0},{2,3},{3,2},{4,5},{5,4},{6,7},{7,6},{8,9},{9,8},{10,11... | collective-permute-start | bytes 3145736 | tf_op jit(solution)/shard_map/ppermute | solution.py:301
  216.3 22.6 %collective-permute-start.30 = (bf16[2,4,64,1024]{3,2,1,0:T(8,128)(2,1)}, bf16[2,4,64,1024]{3,2,1,0:T(8,128)(2,1)S(1)}, u32[]{:S(2)}, u32[]{:S(2)}) collective-permute-start(bf16[2,4,64,1024]{3,2,1,0:T(8,128)(2,1)} %collective-permute-done.22.refs_3_.refs_12_.refs_10_), channel_id=1, source_target_pairs={{0,1},{1,0},{2,3},{3,2},{4,5},{5,4},{6,7},{7,6},{8,9},{9,8},{10,11... | collective-permute-start | bytes 3145736 | tf_op jit(solution)/shard_map/ppermute | solution.py:301
  248.9 7.2 %collective-permute-start.37 = (bf16[512,1024]{1,0:T(8,128)(2,1)}, bf16[512,1024]{1,0:T(8,128)(2,1)S(1)}, u32[]{:S(2)}, u32[]{:S(2)}) collective-permute-start(bf16[512,1024]{1,0:T(8,128)(2,1)} %get-tuple-element.643.refs_0_), channel_id=1, source_target_pairs={{0,1},{1,0},{2,3},{3,2},{4,5},{5,4},{6,7},{7,6},{8,9},{9,8},{10,11... | collective-permute-start | bytes 3145736 | tf_op jit(solution)/shard_map/ppermute | solution.py:258
  249.0 7.2 %collective-permute-start.38 = (bf16[512,1024]{1,0:T(8,128)(2,1)}, bf16[512,1024]{1,0:T(8,128)(2,1)S(1)}, u32[]{:S(2)}, u32[]{:S(2)}) collective-permute-start(bf16[512,1024]{1,0:T(8,128)(2,1)} %get-tuple-element.645.refs_2_), channel_id=1, source_target_pairs={{0,1},{1,0},{2,3},{3,2},{4,5},{5,4},{6,7},{7,6},{8,9},{9,8},{10,11... | collective-permute-start | bytes 3145736 | tf_op jit(solution)/shard_map/ppermute | solution.py:258
  251.7 26.2 %collective-permute-start.36 = (bf16[2,4,64,1024]{3,2,1,0:T(8,128)(2,1)}, bf16[2,4,64,1024]{3,2,1,0:T(8,128)(2,1)}, u32[]{:S(2)}, u32[]{:S(2)}) collective-permute-start(bf16[2,4,64,1024]{3,2,1,0:T(8,128)(2,1)} %pad_maximum_fusion.6.refs_2_), channel_id=1, source_target_pairs={{0,1},{1,0},{2,3},{3,2},{4,5},{5,4},{6,7},{7,6},{8,9},{9,8},{10,11... | collective-permute-start | bytes 3145736 | tf_op jit(solution)/shard_map/ppermute | solution.py:301
  251.8 26.1 %collective-permute-start.34 = (bf16[2,4,64,1024]{3,2,1,0:T(8,128)(2,1)}, bf16[2,4,64,1024]{3,2,1,0:T(8,128)(2,1)}, u32[]{:S(2)}, u32[]{:S(2)}) collective-permute-start(bf16[2,4,64,1024]{3,2,1,0:T(8,128)(2,1)} %pad_maximum_fusion.6.refs_2_), channel_id=1, source_target_pairs={{0,4},{4,0},{8,12},{12,8},{16,20},{20,16},{24,28},{28,24},{1,5},{5... | collective-permute-start | bytes 3145736 | tf_op jit(solution)/shard_map/ppermute | solution.py:293
  256.1 21.9 %collective-permute-start.35 = (bf16[2,4,64,1024]{3,2,1,0:T(8,128)(2,1)}, bf16[2,4,64,1024]{3,2,1,0:T(8,128)(2,1)}, u32[]{:S(2)}, u32[]{:S(2)}) collective-permute-start(bf16[2,4,64,1024]{3,2,1,0:T(8,128)(2,1)} %pad_maximum_fusion.5.refs_0_), channel_id=1, source_target_pairs={{0,1},{1,0},{2,3},{3,2},{4,5},{5,4},{6,7},{7,6},{8,9},{9,8},{10,11... | collective-permute-start | bytes 3145736 | tf_op jit(solution)/shard_map/ppermute | solution.py:301
  256.1 25.9 %collective-permute-start.33 = (bf16[2,4,64,1024]{3,2,1,0:T(8,128)(2,1)}, bf16[2,4,64,1024]{3,2,1,0:T(8,128)(2,1)}, u32[]{:S(2)}, u32[]{:S(2)}) collective-permute-start(bf16[2,4,64,1024]{3,2,1,0:T(8,128)(2,1)} %pad_maximum_fusion.5.refs_0_), channel_id=1, source_target_pairs={{0,2},{2,0},{1,3},{3,1},{4,6},{6,4},{5,7},{7,5},{8,10},{10,8},{9,1... | collective-permute-start | bytes 3145736 | tf_op jit(solution)/shard_map/ppermute | solution.py:297
  256.2 21.7 %collective-permute-start = (bf16[256,1024]{1,0:T(8,128)(2,1)S(1)}, bf16[256,1024]{1,0:T(8,128)(2,1)S(1)}, u32[]{:S(2)}, u32[]{:S(2)}) collective-permute-start(bf16[256,1024]{1,0:T(8,128)(2,1)S(1)} %slice_bitcast_fusion.4), channel_id=1, source_target_pairs={{2,3},{3,2},{6,7},{7,6},{10,11},{11,10},{14,15},{15,14},{18,19},{1... | collective-permute-start | bytes 1572872 | tf_op jit(solution)/shard_map/ppermute | solution.py:215
  282.0 2.9 collective-permute-start.39
  282.0 4.4 collective-permute-start.40
  283.4 24.8 %collective-permute-start.41 = (bf16[256,1024]{1,0:T(8,128)(2,1)}, bf16[256,1024]{1,0:T(8,128)(2,1)S(1)}, u32[]{:S(2)}, u32[]{:S(2)}) collective-permute-start(bf16[256,1024]{1,0:T(8,128)(2,1)} %bitcast_select_fusion.1), channel_id=1, source_target_pairs={{0,2},{1,3},{2,1},{3,0},{4,6},{5,7},{6,5},{7,4},{8,10},{9,11},{10,... | collective-permute-start | bytes 1572872 | tf_op jit(solution)/shard_map/ppermute | solution.py:210
  311.0 28.3 %collective-permute-start.42 = (bf16[256,1024]{1,0:T(8,128)(2,1)S(1)}, bf16[256,1024]{1,0:T(8,128)(2,1)S(1)}, u32[]{:S(2)}, u32[]{:S(2)}) collective-permute-start(bf16[256,1024]{1,0:T(8,128)(2,1)S(1)} %broadcast_select_fusion.2), channel_id=1, source_target_pairs={{2,0},{3,1},{1,2},{0,3},{6,4},{7,5},{5,6},{4,7},{10,8},{11,9},{9,1... | collective-permute-start | bytes 1572872 | tf_op jit(solution)/shard_map/ppermute | solution.py:231
  339.4 23.0 %collective-permute-start.43 = (bf16[256,1024]{1,0:T(8,128)(2,1)S(1)}, bf16[256,1024]{1,0:T(8,128)(2,1)S(1)}, u32[]{:S(2)}, u32[]{:S(2)}) collective-permute-start(bf16[256,1024]{1,0:T(8,128)(2,1)S(1)} %get-tuple-element.745), channel_id=1, source_target_pairs={{3,2},{2,3},{7,6},{6,7},{11,10},{10,11},{15,14},{14,15},{19,18},{1... | collective-permute-start | bytes 1572872 | tf_op jit(solution)/shard_map/ppermute | solution.py:237
  362.4 17.0 %copy-start.80 = (bf16[256,1024]{1,0:T(8,128)(2,1)}, bf16[256,1024]{1,0:T(8,128)(2,1)S(1)}, u32[]{:S(2)}) copy-start(bf16[256,1024]{1,0:T(8,128)(2,1)S(1)} %collective-permute-done.43) | copy-start | bytes 1572868
  362.4 2.7 collective-permute-start.44
  362.7 4.0 collective-permute-start.45
  425.1 2.7 collective-permute-start.46
  425.5 3.8 collective-permute-start.47
  439.6 2.0 collective-permute-start.48
  442.7 31.8 %all-to-all-start.1 = ((bf16[16,16,1024]{2,1,0:T(8,128)(2,1)}), bf16[16,16,1024]{2,1,0:T(8,128)(2,1)S(1)}, u32[]{:S(2)}, u32[]{:S(2)}) async-start(bf16[16,16,1024]{2,1,0:T(8,128)(2,1)} %fusion), calls=%async_computation.1 | async-start | bytes 1048576 | tf_op jit(solution)/shard_map/all_to_all | solution.py:1206
  460.0 14.4 %collective-permute-start.49 = (bf16[256,1024]{1,0:T(8,128)(2,1)S(1)}, bf16[256,1024]{1,0:T(8,128)(2,1)S(1)}, u32[]{:S(2)}, u32[]{:S(2)}) collective-permute-start(bf16[256,1024]{1,0:T(8,128)(2,1)S(1)} %broadcast_select_fusion.1), channel_id=1, source_target_pairs={{2,0},{3,1},{1,2},{0,3},{6,4},{7,5},{5,6},{4,7},{10,8},{11,9},{9,1... | collective-permute-start | bytes 1572872 | tf_op jit(solution)/shard_map/ppermute | solution.py:231
  474.5 3.9 collective-permute-start.50
  (97 other events, 463.1 us)
Sparse Core Ops, SparseCore 0:
  10.9 163.8 all-gather.5
  177.7 79.3 all-gather.3

commit v6 on v5

--- a/solution.py
+++ b/solution.py
@@ -171,7 +171,7 @@
                 pltpu.VMEM((2, 2 * HEAD_DIM, BLK), wide),
             ],
         ),
-        compiler_params=pltpu.CompilerParams(vmem_limit_bytes=48 * 2**20),
+        compiler_params=pltpu.CompilerParams(vmem_limit_bytes=62 * 2**20),
         cost_estimate=pl.CostEstimate(flops=13 * MICROSECOND, bytes_accessed=0, transcendentals=0),
         name="attend_forward",
     )(place, queries, *keys, *values)
@@ -197,7 +197,7 @@
                 pltpu.VMEM((2, 1, 2 * BLK), wide),
             ],
         ),
-        compiler_params=pltpu.CompilerParams(vmem_limit_bytes=48 * 2**20),
+        compiler_params=pltpu.CompilerParams(vmem_limit_bytes=62 * 2**20),
         cost_estimate=pl.CostEstimate(flops=21 * MICROSECOND, bytes_accessed=0, transcendentals=0),
         name="attend_backward",
     )(place, queries, grads, attended, stat, *keys, *values)
@@ -400,7 +400,7 @@
     v.g_near_other = swapped(v.g_near)
     advance(v.h)
     advance(v.h)
-    v.current = v.tokens.astype(wide)
+    v.current = v.tokens
     del v.tokens
     attention_step(v.current, (PIECES, weights_f()), v.picked[0], 0)
     v.middle = output_step(v.current, (PIECES, weights_f()), v.picked[0], 0)
@@ -436,7 +436,7 @@
     current = feed_step(v.middle, frozen[1][1], v.picked[1], 1)
     current, cotangent_got = sync((current, cotangent_got))
     cotangent = joined_tokens(cotangent, cotangent_got, v.cotangent_other, below)
-    return current, cotangent.astype(wide), v.picked, frozen
+    return current, cotangent, v.picked, frozen
 
 
 SQUARE = (4, 2, 2, 2, 32, 1024)
@@ -518,7 +518,7 @@
 
 def store_norm(values_ref, gain_ref, shift_ref, normed_ref, unit_ref, scale_ref):
     def norm(rows):
-        unit, scale, normed = normalize_rows(values_ref[rows, :], gain_ref[...], shift_ref[...])
+        unit, scale, normed = normalize_rows(values_ref[rows, :].astype(wide), gain_ref[...], shift_ref[...])
         normed_ref[rows, :] = normed.astype(low_type)
         unit_ref[rows, :] = unit.astype(low_type)
         scale_ref[rows, :] = jnp.broadcast_to(scale, (STRIP, 128))
@@ -528,7 +528,7 @@
 
 def store_pull(out_ref, grad_ref, inner_ref, unit_ref, scale_ref, gain_ref):
     def pull(rows):
-        out_ref[rows, :] = grad_ref[rows, :] + normalize_pull(
+        out_ref[rows, :] = grad_ref[rows, :].astype(wide) + normalize_pull(
             inner_ref[rows, :], unit_ref[rows, :].astype(wide), scale_ref[rows, :1], gain_ref[...]
         )
 
@@ -606,7 +606,7 @@
     await_first(held, arrived)
     for rows in row_tiles(x_ref.shape[0], OUTPUT_ROWS):
         middle_ref[rows, :] = (
-            x_ref[rows, :]
+            x_ref[rows, :].astype(wide)
             + times(low_ref[rows, :], square(held))
             + times(rank_ref[rows, :], right_ref[...])
             + bias_ref[...]
@@ -1150,8 +1150,8 @@
             attention_step, output_step, feed_step,
         )
     else:
-        current = spread_tokens(tokens, below, count).astype(wide)
-        grad_current = spread_tokens(cotangent, below, count).astype(wide)
+        current = spread_tokens(tokens, below, count)
+        grad_current = spread_tokens(cotangent, below, count)
         mine = lax.all_to_all(chosen, LANE, split_axis=0, concat_axis=0, tiled=True)
         theirs = lax.ppermute(mine, "core", SWAP)
         both = jnp.stack(
@@ -1241,7 +1241,7 @@
             middle_grad, (query_grad, key_grad, value_grad), turned, keep, first_weights, factors, extra, at
         )
     got, other = send_across(low_grad, below, count), send_inside(low_grad, count)
-    received, got = sync((received, got))
+    received, got, other = sync((received, got, other))
     moved = collect_tokens(low_grad, got, other, below)
     kept_part = collect_own(grad_current, below)
     received = [received]

time: 496 us -> 485 us (0.978)
  local copies, waits for them, and re-layouts: 37.4 us -> 26.8 us
    unnamed x216 -> x168, local copies, waits for them, and re-layouts: 28.3 us -> 17.6 us
  transfers between devices with their start and end apart: 55 -> 55, of which waited for: 21 -> 21; matrix products, arithmetic and copies ran while one was open for 7% -> 6% of each run, Pallas kernels for 33% -> 33%
where the time goes in v6:
time: 485 us; the launch traced here: 477 us
  Pallas kernels  220 us (45%)
  waiting for transfers between devices  121 us (25%)
  starting transfers between devices  64.2 us (13%)
  other arithmetic  28 us (6%)
  local copies, waits for them, and re-layouts  26.8 us (6%)
  between operations  15.8 us (3%)
    pallas_call x9, Pallas kernels, frozen_call(): pl.pallas_call(functools.partial(kernel, form), grid=(count // tile,) if...  104 us
    ppermute x9, waiting for transfers between devices, along_z(): return lax.ppermute(rows, 'dp', RING)  83 us
    pallas_call x2, Pallas kernels, backward_feed_output(): pl.pallas_call(functools.partial(feed_output_backward_kernel, form, outpu...  49.7 us
    pallas_call x2, Pallas kernels, attend_backward(): pl.pallas_call(functools.partial(attend_backward_kernel, pieces), out_sha...  37.5 us
    pallas_call x2, Pallas kernels, attend_forward(): pl.pallas_call(functools.partial(attend_forward_kernel, pieces), out_shap...  25.2 us
    unnamed x168, local copies, waits for them, and re-layouts  17.6 us
    ppermute x9, starting transfers between devices, along_z(): return lax.ppermute(rows, 'dp', RING)  16.3 us
    ppermute x6, waiting for transfers between devices, along_y(): return lax.ppermute(rows, 'chip', SWAP)  10.8 us
  transfers between devices with their start and end apart: 55, of which 21 were waited for; matrix products, arithmetic and copies ran while one was open for 6% of the time, Pallas kernels for 33%

profile of v6, /device:TPU:0, one launch (start us, length us, event | category | flops | bytes accessed | tf_op | source)
XLA Modules:
  0.0 476.6 jit_solution(2120866631448452066)
XLA Ops:
  11.3 3.1 collective-permute-start.1
  15.3 1.5 collective-permute-start.4
  17.6 1.5 collective-permute-start.5
  20.0 1.7 collective-permute-done.1
  24.4 13.3 %collective-permute-done.2 = bf16[128,1024]{1,0:T(8,128)(2,1)S(1)} collective-permute-done((bf16[128,1024]{1,0:T(8,128)(2,1)S(1)}, bf16[128,1024]{1,0:T(8,128)(2,1)S(1)}, u32[]{:S(2)}, u32[]{:S(2)}) %collective-permute-start.2) | collective-permute-done | bytes 262176 | tf_op jit(solution)/shard_map/ppermute | solution.py:289
  37.8 2.7 collective-permute-start.3
  40.5 1.2 bitcast_select_fusion.2
  42.7 4.2 collective-permute-done.3
  46.9 8.1 %all-to-all-start = ((bf16[16,2,16,512]{3,2,1,0:T(8,128)(2,1)}), bf16[16,2,16,512]{3,2,1,0:T(8,128)(2,1)S(1)}, u32[]{:S(2)}, u32[]{:S(2)}) async-start(bf16[16,2,16,512]{3,2,1,0:T(8,128)(2,1)} %broadcast_select_fusion), calls=%async_computation | async-start | bytes 1048576 | tf_op jit(solution)/shard_map/all_to_all | solution.py:377
  55.3 2.0 collective-permute-start.6
  57.3 1.5 collective-permute-start.7
  58.8 1.5 collective-permute-start.8
  60.3 24.7 %collective-permute-done.8 = bf16[128,1024]{1,0:T(8,128)(2,1)S(1)} collective-permute-done((bf16[128,1024]{1,0:T(8,128)(2,1)S(1)}, bf16[128,1024]{1,0:T(8,128)(2,1)S(1)}, u32[]{:S(2)}, u32[]{:S(2)}) %collective-permute-start.8) | collective-permute-done | bytes 262176 | tf_op jit(solution)/shard_map/ppermute | solution.py:289
  85.1 1.1 pad_maximum_fusion.2.refs_2_.refs_3_
  86.3 4.7 collective-permute-start.10
  91.3 1.5 collective-permute-start.9
  92.8 14.0 %collective-permute-done.14 = bf16[128,1024]{1,0:T(8,128)(2,1)S(1)} collective-permute-done((bf16[128,1024]{1,0:T(8,128)(2,1)S(1)}, bf16[128,1024]{1,0:T(8,128)(2,1)S(1)}, u32[]{:S(2)}, u32[]{:S(2)}) %collective-permute-start.14) | collective-permute-done | bytes 262176 | tf_op jit(solution)/shard_map/ppermute | solution.py:289
  106.8 20.3 %collective-permute-done.15 = bf16[128,1024]{1,0:T(8,128)(2,1)S(1)} collective-permute-done((bf16[128,1024]{1,0:T(8,128)(2,1)S(1)}, bf16[128,1024]{1,0:T(8,128)(2,1)S(1)}, u32[]{:S(2)}, u32[]{:S(2)}) %collective-permute-start.15) | collective-permute-done | bytes 262176 | tf_op jit(solution)/shard_map/ppermute | solution.py:289
  127.1 1.9 collective-permute-done.13.other_ref
  129.0 3.9 collective-permute-done.10.refs_3_.refs_4_
  132.9 3.5 collective-permute-done.9.refs_1_.refs_2_
  137.4 2.6 collective-permute-start.19
  141.3 3.9 collective-permute-start.20
  156.7 1.2 collective-permute-done.19
  157.9 8.3 %qkv_forward.2 = (bf16[512,1024]{1,0:T(8,128)(2,1)}, bf16[512,1024]{1,0:T(8,128)(2,1)}, f32[512,128]{1,0:T(8,128)}, bf16[512,16]{1,0:T(8,128)(2,1)}, bf16[512,10...) custom-call(s32[4]{0:T(128)} %copy-done.24, bf16[512,1024]{1,0:T(8,128)(2,1)} %pad_maximum_fusion.x_ref, ...), custom_call_target="tpu_custom_call" | custom-call | flops 900000000 | tf_op jit(solution)/shard_map/qkv_forward/pallas_call | solution.py:806
  166.9 2.7 collective-permute-start.25
  169.6 1.2 pad_maximum_fusion.4.refs_2_.refs_11_.refs_9_
  172.3 4.7 collective-permute-done.25
  178.7 1.5 collective-permute-start.26
  180.9 12.6 %attend_forward.2 = (f32[512,1024]{1,0:T(8,128)}, f32[8,2,512]{2,1,0:T(2,128)}) custom-call(s32[1]{0:T(128)} %bitcast.47.place_ref, bf16[512,1024]{1,0:T(8,128)(2,1)} %get-tuple-element.695.q_ref, bf16[512,1024]{1,0:T(8,128)(2,1)} %get-tuple-element.699.refs_0_, bf16[512,1024]{1,0:T(8,128)(2,1)} %collective-permute-done.27.refs_1_, ...), custom_call_target="tpu_custom_call" | custom-call | flops 1300000000 | tf_op jit(solution)/shard_map/attend_forward/pallas_call | solution.py:157
  193.5 7.8 %output_forward.2 = (bf16[512,1024]{1,0:T(8,128)(2,1)}, f32[512,1024]{1,0:T(8,128)}, bf16[512,1024]{1,0:T(8,128)(2,1)}, bf16[512,1024]{1,0:T(8,128)(2,1)}, f32[512,128]{1,0:T(8,128)}, /*index=5*/bf16[512,16]{1,0:T(8,128)(2,1)}) custom-call(s32[4]{0:T(128)} %copy-done.24, bf16[512,1024]{1,0:T(8,128)(2,1)} %pad_maximum_fusion.x_ref, ...), custom_call_target="tpu_custom_call" | custom-call | flops 800000000 | tf_op jit(solution)/shard_map/output_forward/pallas_call | solution.py:806
  201.3 3.4 collective-permute-done.21.refs_1_.refs_10_.refs_8_
  211.8 21.3 %feed_forward.2 = (f32[512,1024]{1,0:T(8,128)}, bf16[512,4096]{1,0:T(8,128)(2,1)}, bf16[512,4096]{1,0:T(8,128)(2,1)}, bf16[512,16]{1,0:T(8,128)(2,1)}, bf16[512,16]{1,0:T(8,128)(2,1)}) custom-call(s32[4]{0:T(128)} %copy-done.24, bf16[512,1024]{1,0:T(8,128)(2,1)} %get-tuple-element.667.normed_ref, f32[512,1024]{1,0:T(8,128)} %get-tuple-element.470.middle_ref, ...), custom_call_target="tpu_custom_call" | custom-call | flops 2000000000 | tf_op jit(solution)/shard_map/feed_forward/pallas_call | solution.py:806
  234.4 8.7 %qkv_forward.3 = (bf16[512,1024]{1,0:T(8,128)(2,1)}, bf16[512,1024]{1,0:T(8,128)(2,1)}, f32[512,128]{1,0:T(8,128)}, bf16[512,16]{1,0:T(8,128)(2,1)}, bf16[512,10...) custom-call(s32[4]{0:T(128)} %copy-done.24, f32[512,1024]{1,0:T(8,128)} %get-tuple-element.565.x_ref, ...), custom_call_target="tpu_custom_call" | custom-call | flops 900000000 | tf_op jit(solution)/shard_map/qkv_forward/pallas_call | solution.py:806
  243.7 1.4 pad_maximum_fusion.6.refs_2_
  245.2 2.0 collective-permute-start.34
  247.2 2.1 pad_maximum_fusion.5.refs_0_
  250.3 1.5 collective-permute-start
  251.8 12.6 %attend_forward.3 = (f32[512,1024]{1,0:T(8,128)}, f32[8,2,512]{2,1,0:T(2,128)}) custom-call(s32[1]{0:T(128)} %bitcast.47.place_ref, bf16[512,1024]{1,0:T(8,128)(2,1)} %get-tuple-element.640.q_ref, bf16[512,1024]{1,0:T(8,128)(2,1)} %get-tuple-element.644.refs_0_, bf16[512,1024]{1,0:T(8,128)(2,1)} %collective-permute-done.37.refs_1_, ...), custom_call_target="tpu_custom_call" | custom-call | flops 1300000000 | tf_op jit(solution)/shard_map/attend_forward/pallas_call | solution.py:157
  264.4 8.1 %output_forward.3 = (bf16[512,1024]{1,0:T(8,128)(2,1)}, f32[512,1024]{1,0:T(8,128)}, bf16[512,1024]{1,0:T(8,128)(2,1)}, bf16[512,1024]{1,0:T(8,128)(2,1)}, f32[512,128]{1,0:T(8,128)}, /*index=5*/bf16[512,16]{1,0:T(8,128)(2,1)}) custom-call(s32[4]{0:T(128)} %copy-done.24, f32[512,1024]{1,0:T(8,128)} %get-tuple-element.565.x_ref, ...), custom_call_target="tpu_custom_call" | custom-call | flops 800000000 | tf_op jit(solution)/shard_map/output_forward/pallas_call | solution.py:806
  272.6 2.7 collective-permute-done.33.refs_1_
  275.8 1.3 bitcast_select_fusion.1
  278.1 1.5 collective-permute-done.40.refs_7_
  280.6 20.8 %feed_forward.3 = (f32[512,1024]{1,0:T(8,128)}, bf16[512,4096]{1,0:T(8,128)(2,1)}, bf16[512,4096]{1,0:T(8,128)(2,1)}, bf16[512,16]{1,0:T(8,128)(2,1)}, bf16[512,16]{1,0:T(8,128)(2,1)}) custom-call(s32[4]{0:T(128)} %copy-done.24, bf16[512,1024]{1,0:T(8,128)(2,1)} %get-tuple-element.597.normed_ref, f32[512,1024]{1,0:T(8,128)} %get-tuple-element.598.middle_ref, ...), custom_call_target="tpu_custom_call" | custom-call | flops 2000000000 | tf_op jit(solution)/shard_map/feed_forward/pallas_call | solution.py:806
  301.4 1.8 convert_element_type.18
  305.0 26.0 %feed_output_backward.2 = (f32[512,1024]{1,0:T(8,128)}, bf16[512,1024]{1,0:T(8,128)(2,1)}, bf16[16,1024]{1,0:T(8,128)(2,1)}, bf16[16,1024]{1,0:T(8,128)(2,1)}, b...) custom-call(s32[4]{0:T(128)} %copy-done.24, ...), custom_call_target="tpu_custom_call" | custom-call | flops 2500000000 | tf_op jit(solution)/shard_map/feed_output_backward/pallas_call | solution.py:958
  332.7 18.9 %attend_backward.2 = (bf16[512,1024]{1,0:T(8,128)(2,1)}, bf16[512,1024]{1,0:T(8,128)(2,1)}, bf16[512,1024]{1,0:T(8,128)(2,1)}, bf16[512,1024]{1,0:T(8,128)(2,1)}, bf16[512,1024]{1,0:T(8,128)(2,1)}) custom-call(s32[1]{0:T(128)} %bitcast.47.place_ref, bf16[512,1024]{1,0:T(8,128)(2,1)} %get-tuple-element.640.q_ref, bf16[512,1024]{1,0:T(8,128)(2,1)} %get-tuple-element.641.g_ref, ...), custom_call_target="tpu_custom_call" | custom-call | flops 2100000000 | tf_op jit(solution)/shard_map/attend_backward/pallas_call | solution.py:183
  352.1 2.4 collective-permute-done.44.refs_1_
  354.6 1.5 collective-permute-done.45.refs_3_
  357.0 12.7 %qkv_whole.1 = (f32[512,1024]{1,0:T(8,128)}, bf16[16,1024]{1,0:T(8,128)(2,1)}, bf16[16,3072]{1,0:T(8,128)(2,1)}) custom-call(s32[4]{0:T(128)} %copy-done.24, f32[512,1024]{1,0:T(8,128)} %get-tuple-element.654.grad_ref, bf16[512,1024]{1,0:T(8,128)(2,1)} %get-tuple-element.655.unit_ref, f32[512,128]{1,0:T(8,128)} %get-tuple-element.656.scale_ref, ...), custom_call_target="tpu_custom_call" | custom-call | flops 1100000000 | tf_op jit(solution)/shard_map/qkv_whole/pallas_call | solution.py:806
  369.8 23.6 %feed_output_backward.3 = (f32[512,1024]{1,0:T(8,128)}, bf16[512,1024]{1,0:T(8,128)(2,1)}, bf16[16,1024]{1,0:T(8,128)(2,1)}, bf16[16,1024]{1,0:T(8,128)(2,1)}, b...) custom-call(s32[4]{0:T(128)} %copy-done.24, ...), custom_call_target="tpu_custom_call" | custom-call | flops 2500000000 | tf_op jit(solution)/shard_map/feed_output_backward/pallas_call | solution.py:958
  393.4 18.7 %attend_backward.3 = (bf16[512,1024]{1,0:T(8,128)(2,1)}, bf16[512,1024]{1,0:T(8,128)(2,1)}, bf16[512,1024]{1,0:T(8,128)(2,1)}, bf16[512,1024]{1,0:T(8,128)(2,1)}, bf16[512,1024]{1,0:T(8,128)(2,1)}) custom-call(s32[1]{0:T(128)} %bitcast.47.place_ref, bf16[512,1024]{1,0:T(8,128)(2,1)} %get-tuple-element.695.q_ref, bf16[512,1024]{1,0:T(8,128)(2,1)} %get-tuple-element.696.g_ref, ...), custom_call_target="tpu_custom_call" | custom-call | flops 2100000000 | tf_op jit(solution)/shard_map/attend_backward/pallas_call | solution.py:183
  412.6 2.4 collective-permute-done.46.refs_1_
  415.1 1.5 collective-permute-done.47.refs_3_
  417.7 6.3 %qkv_turn.1 = (bf16[512,1024]{1,0:T(8,128)(2,1)}, bf16[512,1024]{1,0:T(8,128)(2,1)}, bf16[512,16]{1,0:T(8,128)(2,1)}, bf16[16,1024]{1,0:T(8,128)(2,1)}, bf16[16,3072]{1,0:T(8,128)(2,1)}) custom-call(s32[4]{0:T(128)} %copy-done.24, bf16[512,1024]{1,0:T(8,128)(2,1)} %get-tuple-element.693.normed_ref, bf16[512,16]{1,0:T(8,128)(2,1)} %get-tuple-element.694.rank_ref, ...), custom_call_target="tpu_custom_call" | custom-call | flops 300000000 | tf_op jit(solution)/shard_map/qkv_turn/pallas_call | solution.py:806
  427.3 1.5 collective-permute-done.48
  429.8 6.4 %all-to-all-start.1 = ((bf16[16,16,1024]{2,1,0:T(8,128)(2,1)}), bf16[16,16,1024]{2,1,0:T(8,128)(2,1)S(1)}, u32[]{:S(2)}, u32[]{:S(2)}) async-start(bf16[16,16,1024]{2,1,0:T(8,128)(2,1)} %fusion), calls=%async_computation.1 | async-start | bytes 1048576 | tf_op jit(solution)/shard_map/all_to_all | solution.py:1206
  436.2 10.4 %qkv_backward.1 = (f32[512,1024]{1,0:T(8,128)}, bf16[512,1024]{1,0:T(8,128)(2,1)}) custom-call(s32[4]{0:T(128)} %copy-done.24, f32[512,1024]{1,0:T(8,128)} %get-tuple-element.690.grad_ref, bf16[512,1024]{1,0:T(8,128)(2,1)} %get-tuple-element.691.unit_ref, f32[512,128]{1,0:T(8,128)} %get-tuple-element.692.scale_ref, ...), custom_call_target="tpu_custom_call" | custom-call | flops 900000000 | tf_op jit(solution)/shard_map/qkv_backward/pallas_call | solution.py:806
  446.6 1.3 fusion.9
  448.8 3.3 collective-permute-start.49
  454.1 10.5 %collective-permute-done.49 = bf16[256,1024]{1,0:T(8,128)(2,1)} collective-permute-done((bf16[256,1024]{1,0:T(8,128)(2,1)S(1)}, bf16[256,1024]{1,0:T(8,128)(2,1)}, u32[]{:S(2)}, u32[]{:S(2)}) %collective-permute-start.49) | collective-permute-done | bytes 524320 | tf_op jit(solution)/shard_map/ppermute | solution.py:231
  464.7 1.2 select_bitcast_fusion.1
  465.9 1.8 combine.1
  467.6 1.7 maximum_select_fusion
  (304 shorter events, 55.0 us)
Async XLA Ops:
  7.2 12.0 %copy-start = (s32[16]{0:T(128)S(1)}, s32[16]{0:T(128)}, u32[]{:S(2)}) copy-start(s32[16]{0:T(128)} %param.25) | copy-start | bytes 196
  7.2 204.6 %all-gather.6.cloned.1.call-start = ((), (), s32[]{:S(2)}) async-start(), calls=%async_computation.3 | async-start | bytes 17301504 | tf_op jit(solution)/shard_map/all_gather | solution.py:347
  10.4 267.4 %all-gather.4.cloned.1.call-start = ((), (), s32[]{:S(2)}) async-start(), calls=%async_computation.2 | async-start | bytes 8650752 | tf_op jit(solution)/shard_map/all_gather | solution.py:347
  11.3 10.4 %collective-permute-start.1 = (bf16[128,1024]{1,0:T(8,128)(2,1)S(1)}, bf16[128,1024]{1,0:T(8,128)(2,1)S(1)}, u32[]{:S(2)}, u32[]{:S(2)}) collective-permute-start(bf16[128,1024]{1,0:T(8,128)(2,1)S(1)} %pad_maximum_fusion.15), channel_id=1, source_target_pairs={{0,8},{4,12},{8,24},{12,28},{16,0},{20,4},{24,16},{28,20},{1,9},{5... | collective-permute-start | bytes 786440 | tf_op jit(solution)/shard_map/ppermute | solution.py:289
  15.3 25.2 %collective-permute-start.4 = (bf16[256,1024]{1,0:T(8,128)(2,1)}, bf16[256,1024]{1,0:T(8,128)(2,1)}, u32[]{:S(2)}, u32[]{:S(2)}) collective-permute-start(bf16[256,1024]{1,0:T(8,128)(2,1)} %bitcast_select_fusion.3), channel_id=1, source_target_pairs={{0,2},{1,3},{2,1},{3,0},{4,6},{5,7},{6,5},{7,4},{8,10},{9,11},{10,... | collective-permute-start | bytes 1572872 | tf_op jit(solution)/shard_map/ppermute | solution.py:210
  17.6 22.9 %collective-permute-start.5 = (bf16[256,1024]{1,0:T(8,128)(2,1)}, bf16[256,1024]{1,0:T(8,128)(2,1)}, u32[]{:S(2)}, u32[]{:S(2)}) collective-permute-start(bf16[256,1024]{1,0:T(8,128)(2,1)} %slice_bitcast_fusion.3), channel_id=1, source_target_pairs={{2,3},{3,2},{6,7},{7,6},{10,11},{11,10},{14,15},{15,14},{18,19},{1... | collective-permute-start | bytes 1572872 | tf_op jit(solution)/shard_map/ppermute | solution.py:215
  21.7 16.1 %collective-permute-start.2 = (bf16[128,1024]{1,0:T(8,128)(2,1)S(1)}, bf16[128,1024]{1,0:T(8,128)(2,1)S(1)}, u32[]{:S(2)}, u32[]{:S(2)}) collective-permute-start(bf16[128,1024]{1,0:T(8,128)(2,1)S(1)} %collective-permute-done.1), channel_id=1, source_target_pairs={{0,8},{4,12},{8,24},{12,28},{16,0},{20,4},{24,16},{28,20},{1,9},{5... | collective-permute-start | bytes 786440 | tf_op jit(solution)/shard_map/ppermute | solution.py:289
  37.8 9.2 %collective-permute-start.3 = (bf16[128,1024]{1,0:T(8,128)(2,1)S(1)}, bf16[128,1024]{1,0:T(8,128)(2,1)S(1)}, u32[]{:S(2)}, u32[]{:S(2)}) collective-permute-start(bf16[128,1024]{1,0:T(8,128)(2,1)S(1)} %collective-permute-done.2), channel_id=1, source_target_pairs={{0,8},{4,12},{8,24},{12,28},{16,0},{20,4},{24,16},{28,20},{1,9},{5... | collective-permute-start | bytes 786440 | tf_op jit(solution)/shard_map/ppermute | solution.py:289
  46.9 38.1 %all-to-all-start = ((bf16[16,2,16,512]{3,2,1,0:T(8,128)(2,1)}), bf16[16,2,16,512]{3,2,1,0:T(8,128)(2,1)S(1)}, u32[]{:S(2)}, u32[]{:S(2)}) async-start(bf16[16,2,16,512]{3,2,1,0:T(8,128)(2,1)} %broadcast_select_fusion), calls=%async_computation | async-start | bytes 1048576 | tf_op jit(solution)/shard_map/all_to_all | solution.py:377
  55.3 29.8 %collective-permute-start.6 = (bf16[4,64,1024]{2,1,0:T(8,128)(2,1)S(1)}, bf16[4,64,1024]{2,1,0:T(8,128)(2,1)S(1)}, u32[]{:S(2)}, u32[]{:S(2)}) collective-permute-start(bf16[4,64,1024]{2,1,0:T(8,128)(2,1)S(1)} %pad_maximum_fusion.9), channel_id=1, source_target_pairs={{0,4},{4,0},{8,12},{12,8},{16,20},{20,16},{24,28},{28,24},{1,5},{5... | collective-permute-start | bytes 1572872 | tf_op jit(solution)/shard_map/ppermute | solution.py:293
  57.3 27.7 %collective-permute-start.7 = (bf16[4,64,1024]{2,1,0:T(8,128)(2,1)S(1)}, bf16[4,64,1024]{2,1,0:T(8,128)(2,1)}, u32[]{:S(2)}, u32[]{:S(2)}) collective-permute-start(bf16[4,64,1024]{2,1,0:T(8,128)(2,1)S(1)} %pad_maximum_fusion.10), channel_id=1, source_target_pairs={{0,2},{2,0},{1,3},{3,1},{4,6},{6,4},{5,7},{7,5},{8,10},{10,8},{9,1... | collective-permute-start | bytes 1572872 | tf_op jit(solution)/shard_map/ppermute | solution.py:297
  58.8 26.2 %collective-permute-start.8 = (bf16[128,1024]{1,0:T(8,128)(2,1)S(1)}, bf16[128,1024]{1,0:T(8,128)(2,1)S(1)}, u32[]{:S(2)}, u32[]{:S(2)}) collective-permute-start(bf16[128,1024]{1,0:T(8,128)(2,1)S(1)} %pad_maximum_fusion.16), channel_id=1, source_target_pairs={{0,8},{4,12},{8,24},{12,28},{16,0},{20,4},{24,16},{28,20},{1,9},{5... | collective-permute-start | bytes 786440 | tf_op jit(solution)/shard_map/ppermute | solution.py:289
  85.0 42.0 %copy-start.75 = (f32[2,2048]{1,0:T(2,128)S(1)}, f32[2,2048]{1,0:T(2,128)}, u32[]{:S(2)}) copy-start(f32[2,2048]{1,0:T(2,128)} %param.30) | copy-start | bytes 49156
  86.2 50.9 %copy-start.36 = (bf16[2,4,64,1024]{3,2,1,0:T(8,128)(2,1)}, bf16[2,4,64,1024]{3,2,1,0:T(8,128)(2,1)S(1)}, u32[]{:S(2)}) copy-start(bf16[2,4,64,1024]{3,2,1,0:T(8,128)(2,1)S(1)} %pad_maximum_fusion.2.refs_2_.refs_3_) | copy-start | bytes 3145732
  86.2 42.8 %collective-permute-start.12 = (bf16[2,4,64,1024]{3,2,1,0:T(8,128)(2,1)S(1)}, bf16[2,4,64,1024]{3,2,1,0:T(8,128)(2,1)S(1)}, u32[]{:S(2)}, u32[]{:S(2)}) collective-permute-start(bf16[2,4,64,1024]{3,2,1,0:T(8,128)(2,1)S(1)} %pad_maximum_fusion.2.refs_2_.refs_3_), channel_id=1, source_target_pairs={{0,1},{1,0},{2,3},{3,2},{4,5},{5,4},{6,7},{7,6},{8,9},{9,8},{10,11... | collective-permute-start | bytes 3145736 | tf_op jit(solution)/shard_map/ppermute | solution.py:301
  86.3 46.6 %collective-permute-start.10 = (bf16[2,4,64,1024]{3,2,1,0:T(8,128)(2,1)S(1)}, bf16[2,4,64,1024]{3,2,1,0:T(8,128)(2,1)}, u32[]{:S(2)}, u32[]{:S(2)}) collective-permute-start(bf16[2,4,64,1024]{3,2,1,0:T(8,128)(2,1)S(1)} %pad_maximum_fusion.2.refs_2_.refs_3_), channel_id=1, source_target_pairs={{0,4},{4,0},{8,12},{12,8},{16,20},{20,16},{24,28},{28,24},{1,5},{5... | collective-permute-start | bytes 3145736 | tf_op jit(solution)/shard_map/ppermute | solution.py:293
  91.0 15.8 %collective-permute-start.14 = (bf16[128,1024]{1,0:T(8,128)(2,1)S(1)}, bf16[128,1024]{1,0:T(8,128)(2,1)S(1)}, u32[]{:S(2)}, u32[]{:S(2)}) collective-permute-start(bf16[128,1024]{1,0:T(8,128)(2,1)S(1)} %collective-permute-done.8), channel_id=1, source_target_pairs={{0,8},{4,12},{8,24},{12,28},{16,0},{20,4},{24,16},{28,20},{1,9},{5... | collective-permute-start | bytes 786440 | tf_op jit(solution)/shard_map/ppermute | solution.py:289
  91.1 46.2 %copy-start.37 = (bf16[2,4,64,1024]{3,2,1,0:T(8,128)(2,1)}, bf16[2,4,64,1024]{3,2,1,0:T(8,128)(2,1)S(1)}, u32[]{:S(2)}) copy-start(bf16[2,4,64,1024]{3,2,1,0:T(8,128)(2,1)S(1)} %pad_maximum_fusion.1.refs_0_.refs_1_) | copy-start | bytes 3145732
  91.1 41.8 %collective-permute-start.11 = (bf16[2,4,64,1024]{3,2,1,0:T(8,128)(2,1)S(1)}, bf16[2,4,64,1024]{3,2,1,0:T(8,128)(2,1)S(1)}, u32[]{:S(2)}, u32[]{:S(2)}) collective-permute-start(bf16[2,4,64,1024]{3,2,1,0:T(8,128)(2,1)S(1)} %pad_maximum_fusion.1.refs_0_.refs_1_), channel_id=1, source_target_pairs={{0,1},{1,0},{2,3},{3,2},{4,5},{5,4},{6,7},{7,6},{8,9},{9,8},{10,11... | collective-permute-start | bytes 3145736 | tf_op jit(solution)/shard_map/ppermute | solution.py:301
  91.3 45.1 %collective-permute-start.9 = (bf16[2,4,64,1024]{3,2,1,0:T(8,128)(2,1)S(1)}, bf16[2,4,64,1024]{3,2,1,0:T(8,128)(2,1)}, u32[]{:S(2)}, u32[]{:S(2)}) collective-permute-start(bf16[2,4,64,1024]{3,2,1,0:T(8,128)(2,1)S(1)} %pad_maximum_fusion.1.refs_0_.refs_1_), channel_id=1, source_target_pairs={{0,2},{2,0},{1,3},{3,1},{4,6},{6,4},{5,7},{7,5},{8,10},{10,8},{9,1... | collective-permute-start | bytes 3145736 | tf_op jit(solution)/shard_map/ppermute | solution.py:297
  106.8 20.3 %collective-permute-start.15 = (bf16[128,1024]{1,0:T(8,128)(2,1)S(1)}, bf16[128,1024]{1,0:T(8,128)(2,1)S(1)}, u32[]{:S(2)}, u32[]{:S(2)}) collective-permute-start(bf16[128,1024]{1,0:T(8,128)(2,1)S(1)} %collective-permute-done.14), channel_id=1, source_target_pairs={{0,8},{4,12},{8,24},{12,28},{16,0},{20,4},{24,16},{28,20},{1,9},{5... | collective-permute-start | bytes 786440 | tf_op jit(solution)/shard_map/ppermute | solution.py:289
  127.0 1.9 collective-permute-start.13
  136.4 21.5 %collective-permute-start.16 = (bf16[2,4,64,1024]{3,2,1,0:T(8,128)(2,1)}, bf16[2,4,64,1024]{3,2,1,0:T(8,128)(2,1)}, u32[]{:S(2)}, u32[]{:S(2)}) collective-permute-start(bf16[2,4,64,1024]{3,2,1,0:T(8,128)(2,1)} %collective-permute-done.9.refs_1_.refs_2_), channel_id=1, source_target_pairs={{0,1},{1,0},{2,3},{3,2},{4,5},{5,4},{6,7},{7,6},{8,9},{9,8},{10,11... | collective-permute-start | bytes 3145736 | tf_op jit(solution)/shard_map/ppermute | solution.py:301
  136.4 21.5 %collective-permute-start.17 = (bf16[2,4,64,1024]{3,2,1,0:T(8,128)(2,1)}, bf16[2,4,64,1024]{3,2,1,0:T(8,128)(2,1)}, u32[]{:S(2)}, u32[]{:S(2)}) collective-permute-start(bf16[2,4,64,1024]{3,2,1,0:T(8,128)(2,1)} %collective-permute-done.10.refs_3_.refs_4_), channel_id=1, source_target_pairs={{0,1},{1,0},{2,3},{3,2},{4,5},{5,4},{6,7},{7,6},{8,9},{9,8},{10,11... | collective-permute-start | bytes 3145736 | tf_op jit(solution)/shard_map/ppermute | solution.py:301
  137.2 19.4 %collective-permute-start.18 = (bf16[4,64,1024]{2,1,0:T(8,128)(2,1)S(1)}, bf16[4,64,1024]{2,1,0:T(8,128)(2,1)S(1)}, u32[]{:S(2)}, u32[]{:S(2)}) collective-permute-start(bf16[4,64,1024]{2,1,0:T(8,128)(2,1)S(1)} %pad_maximum_fusion.11), channel_id=1, source_target_pairs={{0,4},{4,0},{8,12},{12,8},{16,20},{20,16},{24,28},{28,24},{1,5},{5... | collective-permute-start | bytes 1572872 | tf_op jit(solution)/shard_map/ppermute | solution.py:293
  137.4 20.5 %collective-permute-start.19 = (bf16[4,64,1024]{2,1,0:T(8,128)(2,1)S(1)}, bf16[4,64,1024]{2,1,0:T(8,128)(2,1)}, u32[]{:S(2)}, u32[]{:S(2)}) collective-permute-start(bf16[4,64,1024]{2,1,0:T(8,128)(2,1)S(1)} %pad_maximum_fusion.12), channel_id=1, source_target_pairs={{0,2},{2,0},{1,3},{3,1},{4,6},{6,4},{5,7},{7,5},{8,10},{10,8},{9,1... | collective-permute-start | bytes 1572872 | tf_op jit(solution)/shard_map/ppermute | solution.py:297
  141.3 15.4 %collective-permute-start.20 = (bf16[128,1024]{1,0:T(8,128)(2,1)S(1)}, bf16[128,1024]{1,0:T(8,128)(2,1)S(1)}, u32[]{:S(2)}, u32[]{:S(2)}) collective-permute-start(bf16[128,1024]{1,0:T(8,128)(2,1)S(1)} %pad_maximum_fusion.17), channel_id=1, source_target_pairs={{0,8},{4,12},{8,24},{12,28},{16,0},{20,4},{24,16},{28,20},{1,9},{5... | collective-permute-start | bytes 786440 | tf_op jit(solution)/shard_map/ppermute | solution.py:289
  145.2 12.7 %copy-start.24 = (s32[4]{0:T(128)}, s32[4]{0:T(128)S(1)}, u32[]{:S(2)}) copy-start(s32[4]{0:T(128)S(1)} %pad_add_fusion.1.at_ref) | copy-start | bytes 52
  166.3 10.8 %collective-permute-start.27 = (bf16[512,1024]{1,0:T(8,128)(2,1)}, bf16[512,1024]{1,0:T(8,128)(2,1)}, u32[]{:S(2)}, u32[]{:S(2)}) collective-permute-start(bf16[512,1024]{1,0:T(8,128)(2,1)} %get-tuple-element.699.refs_0_), channel_id=1, source_target_pairs={{0,1},{1,0},{2,3},{3,2},{4,5},{5,4},{6,7},{7,6},{8,9},{9,8},{10,11... | collective-permute-start | bytes 3145736 | tf_op jit(solution)/shard_map/ppermute | solution.py:258
  166.4 12.4 %collective-permute-start.28 = (bf16[512,1024]{1,0:T(8,128)(2,1)}, bf16[512,1024]{1,0:T(8,128)(2,1)}, u32[]{:S(2)}, u32[]{:S(2)}) collective-permute-start(bf16[512,1024]{1,0:T(8,128)(2,1)} %get-tuple-element.701.refs_2_), channel_id=1, source_target_pairs={{0,1},{1,0},{2,3},{3,2},{4,5},{5,4},{6,7},{7,6},{8,9},{9,8},{10,11... | collective-permute-start | bytes 3145736 | tf_op jit(solution)/shard_map/ppermute | solution.py:258
  166.9 10.2 %collective-permute-start.25 = (bf16[128,1024]{1,0:T(8,128)(2,1)S(1)}, bf16[128,1024]{1,0:T(8,128)(2,1)}, u32[]{:S(2)}, u32[]{:S(2)}) collective-permute-start(bf16[128,1024]{1,0:T(8,128)(2,1)S(1)} %collective-permute-done.20), channel_id=1, source_target_pairs={{0,8},{4,12},{8,24},{12,28},{16,0},{20,4},{24,16},{28,20},{1,9},{5... | collective-permute-start | bytes 786440 | tf_op jit(solution)/shard_map/ppermute | solution.py:289
  170.7 22.7 %copy-start.38 = (bf16[2,4,64,1024]{3,2,1,0:T(8,128)(2,1)}, bf16[2,4,64,1024]{3,2,1,0:T(8,128)(2,1)S(1)}, u32[]{:S(2)}) copy-start(bf16[2,4,64,1024]{3,2,1,0:T(8,128)(2,1)S(1)} %pad_maximum_fusion.4.refs_2_.refs_11_.refs_9_) | copy-start | bytes 3145732
  170.8 30.6 %collective-permute-start.24 = (bf16[2,4,64,1024]{3,2,1,0:T(8,128)(2,1)S(1)}, bf16[2,4,64,1024]{3,2,1,0:T(8,128)(2,1)}, u32[]{:S(2)}, u32[]{:S(2)}) collective-permute-start(bf16[2,4,64,1024]{3,2,1,0:T(8,128)(2,1)S(1)} %pad_maximum_fusion.4.refs_2_.refs_11_.refs_9_), channel_id=1, source_target_pairs={{0,1},{1,0},{2,3},{3,2},{4,5},{5,4},{6,7},{7,6},{8,9},{9,8},{10,11... | collective-permute-start | bytes 3145736 | tf_op jit(solution)/shard_map/ppermute | solution.py:301
  170.8 30.5 %collective-permute-start.22 = (bf16[2,4,64,1024]{3,2,1,0:T(8,128)(2,1)S(1)}, bf16[2,4,64,1024]{3,2,1,0:T(8,128)(2,1)}, u32[]{:S(2)}, u32[]{:S(2)}) collective-permute-start(bf16[2,4,64,1024]{3,2,1,0:T(8,128)(2,1)S(1)} %pad_maximum_fusion.4.refs_2_.refs_11_.refs_9_), channel_id=1, source_target_pairs={{0,4},{4,0},{8,12},{12,8},{16,20},{20,16},{24,28},{28,24},{1,5},{5... | collective-permute-start | bytes 3145736 | tf_op jit(solution)/shard_map/ppermute | solution.py:293
  177.0 24.3 %collective-permute-start.23 = (bf16[2,4,64,1024]{3,2,1,0:T(8,128)(2,1)}, bf16[2,4,64,1024]{3,2,1,0:T(8,128)(2,1)}, u32[]{:S(2)}, u32[]{:S(2)}) collective-permute-start(bf16[2,4,64,1024]{3,2,1,0:T(8,128)(2,1)} %pad_maximum_fusion.3.refs_0_.refs_9_.refs_7_), channel_id=1, source_target_pairs={{0,1},{1,0},{2,3},{3,2},{4,5},{5,4},{6,7},{7,6},{8,9},{9,8},{10,11... | collective-permute-start | bytes 3145736 | tf_op jit(solution)/shard_map/ppermute | solution.py:301
  177.0 27.8 %collective-permute-start.21 = (bf16[2,4,64,1024]{3,2,1,0:T(8,128)(2,1)}, bf16[2,4,64,1024]{3,2,1,0:T(8,128)(2,1)}, u32[]{:S(2)}, u32[]{:S(2)}) collective-permute-start(bf16[2,4,64,1024]{3,2,1,0:T(8,128)(2,1)} %pad_maximum_fusion.3.refs_0_.refs_9_.refs_7_), channel_id=1, source_target_pairs={{0,2},{2,0},{1,3},{3,1},{4,6},{6,4},{5,7},{7,5},{8,10},{10,8},{9,1... | collective-permute-start | bytes 3145736 | tf_op jit(solution)/shard_map/ppermute | solution.py:297
  178.7 22.6 %collective-permute-start.26 = (bf16[128,1024]{1,0:T(8,128)(2,1)}, bf16[128,1024]{1,0:T(8,128)(2,1)S(1)}, u32[]{:S(2)}, u32[]{:S(2)}) collective-permute-start(bf16[128,1024]{1,0:T(8,128)(2,1)} %collective-permute-done.25), channel_id=1, source_target_pairs={{0,8},{4,12},{8,24},{12,28},{16,0},{20,4},{24,16},{28,20},{1,9},{5... | collective-permute-start | bytes 786440 | tf_op jit(solution)/shard_map/ppermute | solution.py:289
  208.0 25.1 %collective-permute-start.31 = (bf16[4,64,1024]{2,1,0:T(8,128)(2,1)S(1)}, bf16[4,64,1024]{2,1,0:T(8,128)(2,1)}, u32[]{:S(2)}, u32[]{:S(2)}) collective-permute-start(bf16[4,64,1024]{2,1,0:T(8,128)(2,1)S(1)} %pad_maximum_fusion.13), channel_id=1, source_target_pairs={{0,4},{4,0},{8,12},{12,8},{16,20},{20,16},{24,28},{28,24},{1,5},{5... | collective-permute-start | bytes 1572872 | tf_op jit(solution)/shard_map/ppermute | solution.py:293
  209.3 23.7 %collective-permute-start.32 = (bf16[4,64,1024]{2,1,0:T(8,128)(2,1)}, bf16[4,64,1024]{2,1,0:T(8,128)(2,1)}, u32[]{:S(2)}, u32[]{:S(2)}) collective-permute-start(bf16[4,64,1024]{2,1,0:T(8,128)(2,1)} %pad_maximum_fusion.14), channel_id=1, source_target_pairs={{0,2},{2,0},{1,3},{3,1},{4,6},{6,4},{5,7},{7,5},{8,10},{10,8},{9,1... | collective-permute-start | bytes 1572872 | tf_op jit(solution)/shard_map/ppermute | solution.py:297
  210.0 23.0 %collective-permute-start.29 = (bf16[2,4,64,1024]{3,2,1,0:T(8,128)(2,1)}, bf16[2,4,64,1024]{3,2,1,0:T(8,128)(2,1)S(1)}, u32[]{:S(2)}, u32[]{:S(2)}) collective-permute-start(bf16[2,4,64,1024]{3,2,1,0:T(8,128)(2,1)} %collective-permute-done.21.refs_1_.refs_10_.refs_8_), channel_id=1, source_target_pairs={{0,1},{1,0},{2,3},{3,2},{4,5},{5,4},{6,7},{7,6},{8,9},{9,8},{10,11... | collective-permute-start | bytes 3145736 | tf_op jit(solution)/shard_map/ppermute | solution.py:301
  210.0 23.1 %collective-permute-start.30 = (bf16[2,4,64,1024]{3,2,1,0:T(8,128)(2,1)}, bf16[2,4,64,1024]{3,2,1,0:T(8,128)(2,1)S(1)}, u32[]{:S(2)}, u32[]{:S(2)}) collective-permute-start(bf16[2,4,64,1024]{3,2,1,0:T(8,128)(2,1)} %collective-permute-done.22.refs_3_.refs_12_.refs_10_), channel_id=1, source_target_pairs={{0,1},{1,0},{2,3},{3,2},{4,5},{5,4},{6,7},{7,6},{8,9},{9,8},{10,11... | collective-permute-start | bytes 3145736 | tf_op jit(solution)/shard_map/ppermute | solution.py:301
  243.1 6.4 %collective-permute-start.37 = (bf16[512,1024]{1,0:T(8,128)(2,1)}, bf16[512,1024]{1,0:T(8,128)(2,1)}, u32[]{:S(2)}, u32[]{:S(2)}) collective-permute-start(bf16[512,1024]{1,0:T(8,128)(2,1)} %get-tuple-element.644.refs_0_), channel_id=1, source_target_pairs={{0,1},{1,0},{2,3},{3,2},{4,5},{5,4},{6,7},{7,6},{8,9},{9,8},{10,11... | collective-permute-start | bytes 3145736 | tf_op jit(solution)/shard_map/ppermute | solution.py:258
  243.2 7.1 %collective-permute-start.38 = (bf16[512,1024]{1,0:T(8,128)(2,1)}, bf16[512,1024]{1,0:T(8,128)(2,1)}, u32[]{:S(2)}, u32[]{:S(2)}) collective-permute-start(bf16[512,1024]{1,0:T(8,128)(2,1)} %get-tuple-element.646.refs_2_), channel_id=1, source_target_pairs={{0,1},{1,0},{2,3},{3,2},{4,5},{5,4},{6,7},{7,6},{8,9},{9,8},{10,11... | collective-permute-start | bytes 3145736 | tf_op jit(solution)/shard_map/ppermute | solution.py:258
  245.0 19.4 %copy-start.43 = (bf16[2,4,64,1024]{3,2,1,0:T(8,128)(2,1)}, bf16[2,4,64,1024]{3,2,1,0:T(8,128)(2,1)S(1)}, u32[]{:S(2)}) copy-start(bf16[2,4,64,1024]{3,2,1,0:T(8,128)(2,1)S(1)} %pad_maximum_fusion.6.refs_2_) | copy-start | bytes 3145732
  245.1 27.5 %collective-permute-start.36 = (bf16[2,4,64,1024]{3,2,1,0:T(8,128)(2,1)S(1)}, bf16[2,4,64,1024]{3,2,1,0:T(8,128)(2,1)}, u32[]{:S(2)}, u32[]{:S(2)}) collective-permute-start(bf16[2,4,64,1024]{3,2,1,0:T(8,128)(2,1)S(1)} %pad_maximum_fusion.6.refs_2_), channel_id=1, source_target_pairs={{0,1},{1,0},{2,3},{3,2},{4,5},{5,4},{6,7},{7,6},{8,9},{9,8},{10,11... | collective-permute-start | bytes 3145736 | tf_op jit(solution)/shard_map/ppermute | solution.py:301
  245.2 27.3 %collective-permute-start.34 = (bf16[2,4,64,1024]{3,2,1,0:T(8,128)(2,1)S(1)}, bf16[2,4,64,1024]{3,2,1,0:T(8,128)(2,1)}, u32[]{:S(2)}, u32[]{:S(2)}) collective-permute-start(bf16[2,4,64,1024]{3,2,1,0:T(8,128)(2,1)S(1)} %pad_maximum_fusion.6.refs_2_), channel_id=1, source_target_pairs={{0,4},{4,0},{8,12},{12,8},{16,20},{20,16},{24,28},{28,24},{1,5},{5... | collective-permute-start | bytes 3145736 | tf_op jit(solution)/shard_map/ppermute | solution.py:293
  249.4 23.2 %collective-permute-start.35 = (bf16[2,4,64,1024]{3,2,1,0:T(8,128)(2,1)}, bf16[2,4,64,1024]{3,2,1,0:T(8,128)(2,1)}, u32[]{:S(2)}, u32[]{:S(2)}) collective-permute-start(bf16[2,4,64,1024]{3,2,1,0:T(8,128)(2,1)} %pad_maximum_fusion.5.refs_0_), channel_id=1, source_target_pairs={{0,1},{1,0},{2,3},{3,2},{4,5},{5,4},{6,7},{7,6},{8,9},{9,8},{10,11... | collective-permute-start | bytes 3145736 | tf_op jit(solution)/shard_map/ppermute | solution.py:301
  249.5 25.7 %collective-permute-start.33 = (bf16[2,4,64,1024]{3,2,1,0:T(8,128)(2,1)}, bf16[2,4,64,1024]{3,2,1,0:T(8,128)(2,1)}, u32[]{:S(2)}, u32[]{:S(2)}) collective-permute-start(bf16[2,4,64,1024]{3,2,1,0:T(8,128)(2,1)} %pad_maximum_fusion.5.refs_0_), channel_id=1, source_target_pairs={{0,2},{2,0},{1,3},{3,1},{4,6},{6,4},{5,7},{7,5},{8,10},{10,8},{9,1... | collective-permute-start | bytes 3145736 | tf_op jit(solution)/shard_map/ppermute | solution.py:297
  250.3 22.2 %collective-permute-start = (bf16[256,1024]{1,0:T(8,128)(2,1)S(1)}, bf16[256,1024]{1,0:T(8,128)(2,1)}, u32[]{:S(2)}, u32[]{:S(2)}) collective-permute-start(bf16[256,1024]{1,0:T(8,128)(2,1)S(1)} %slice_bitcast_fusion.4), channel_id=1, source_target_pairs={{2,3},{3,2},{6,7},{7,6},{10,11},{11,10},{14,15},{15,14},{18,19},{1... | collective-permute-start | bytes 1572872 | tf_op jit(solution)/shard_map/ppermute | solution.py:215
  275.2 2.9 collective-permute-start.39
  275.2 4.4 collective-permute-start.40
  277.0 24.4 %collective-permute-start.41 = (bf16[256,1024]{1,0:T(8,128)(2,1)S(1)}, bf16[256,1024]{1,0:T(8,128)(2,1)S(1)}, u32[]{:S(2)}, u32[]{:S(2)}) collective-permute-start(bf16[256,1024]{1,0:T(8,128)(2,1)S(1)} %bitcast_select_fusion.1), channel_id=1, source_target_pairs={{0,2},{1,3},{2,1},{3,0},{4,6},{5,7},{6,5},{7,4},{8,10},{9,11},{10,... | collective-permute-start | bytes 1572872 | tf_op jit(solution)/shard_map/ppermute | solution.py:210
  303.3 27.7 %collective-permute-start.42 = (bf16[256,1024]{1,0:T(8,128)(2,1)S(1)}, bf16[256,1024]{1,0:T(8,128)(2,1)S(1)}, u32[]{:S(2)}, u32[]{:S(2)}) collective-permute-start(bf16[256,1024]{1,0:T(8,128)(2,1)S(1)} %broadcast_select_fusion.2), channel_id=1, source_target_pairs={{2,0},{3,1},{1,2},{0,3},{6,4},{7,5},{5,6},{4,7},{10,8},{11,9},{9,1... | collective-permute-start | bytes 1572872 | tf_op jit(solution)/shard_map/ppermute | solution.py:231
  332.0 19.6 %collective-permute-start.43 = (bf16[256,1024]{1,0:T(8,128)(2,1)}, bf16[256,1024]{1,0:T(8,128)(2,1)S(1)}, u32[]{:S(2)}, u32[]{:S(2)}) collective-permute-start(bf16[256,1024]{1,0:T(8,128)(2,1)} %get-tuple-element.747), channel_id=1, source_target_pairs={{3,2},{2,3},{7,6},{6,7},{11,10},{10,11},{15,14},{14,15},{19,18},{1... | collective-permute-start | bytes 1572872 | tf_op jit(solution)/shard_map/ppermute | solution.py:237
  351.6 18.2 %copy-start.59 = (bf16[256,1024]{1,0:T(8,128)(2,1)}, bf16[256,1024]{1,0:T(8,128)(2,1)S(1)}, u32[]{:S(2)}) copy-start(bf16[256,1024]{1,0:T(8,128)(2,1)S(1)} %collective-permute-done.43) | copy-start | bytes 1572868
  351.6 3.0 collective-permute-start.44
  352.1 4.0 collective-permute-start.45
  412.1 3.0 collective-permute-start.46
  412.6 4.0 collective-permute-start.47
  426.8 2.0 collective-permute-start.48
  429.8 34.9 %all-to-all-start.1 = ((bf16[16,16,1024]{2,1,0:T(8,128)(2,1)}), bf16[16,16,1024]{2,1,0:T(8,128)(2,1)S(1)}, u32[]{:S(2)}, u32[]{:S(2)}) async-start(bf16[16,16,1024]{2,1,0:T(8,128)(2,1)} %fusion), calls=%async_computation.1 | async-start | bytes 1048576 | tf_op jit(solution)/shard_map/all_to_all | solution.py:1206
  448.0 5.4 %collective-permute-start.50 = (bf16[256,1024]{1,0:T(8,128)(2,1)S(1)}, bf16[256,1024]{1,0:T(8,128)(2,1)S(1)}, u32[]{:S(2)}, u32[]{:S(2)}) collective-permute-start(bf16[256,1024]{1,0:T(8,128)(2,1)S(1)} %get-tuple-element.744), channel_id=1, source_target_pairs={{3,2},{2,3},{7,6},{6,7},{11,10},{10,11},{15,14},{14,15},{19,18},{1... | collective-permute-start | bytes 1572872 | tf_op jit(solution)/shard_map/ppermute | solution.py:237
  448.8 15.9 %collective-permute-start.49 = (bf16[256,1024]{1,0:T(8,128)(2,1)S(1)}, bf16[256,1024]{1,0:T(8,128)(2,1)}, u32[]{:S(2)}, u32[]{:S(2)}) collective-permute-start(bf16[256,1024]{1,0:T(8,128)(2,1)S(1)} %get-tuple-element.745), channel_id=1, source_target_pairs={{2,0},{3,1},{1,2},{0,3},{6,4},{7,5},{5,6},{4,7},{10,8},{11,9},{9,1... | collective-permute-start | bytes 1572872 | tf_op jit(solution)/shard_map/ppermute | solution.py:231
  452.1 12.5 %copy-start.49 = (bf16[512,1024]{1,0:T(8,128)(2,1)S(1)}, bf16[512,1024]{1,0:T(8,128)(2,1)}, u32[]{:S(2)}) copy-start(bf16[512,1024]{1,0:T(8,128)(2,1)} %get-tuple-element.714) | copy-start | bytes 3145732
  (73 other events, 320.9 us)
Sparse Core Ops, SparseCore 0:
  10.9 163.8 all-gather.5
  177.6 83.1 all-gather.3

commit v7 on v6

--- a/solution.py
+++ b/solution.py
@@ -96,7 +96,7 @@
         held = jnp.concatenate(
             [held[:HEAD_DIM] * share[:, :BLK], held[HEAD_DIM:] * share[:, BLK:]], axis=0
         )
-        o_ref[block_rows(slot), :] = held.T
+        o_ref[block_rows(slot), :] = held.T.astype(low_type)
         stat_ref[0, slot : slot + 1, :] = peaks[slot] + jnp.log(sums[slot])
 
 
@@ -110,7 +110,7 @@
         queries[slot] = stack_heads(q_ref[rows, :] * HEAD_DIM**-0.5, mask)
         grad = g_ref[rows, :]
         grads[slot] = stack_heads(grad, mask)
-        both = (grad.astype(wide) * o_ref[rows, :]).T
+        both = (grad.astype(wide) * o_ref[rows, :].astype(wide)).T
         inner[slot] = jnp.concatenate(
             [
                 jnp.sum(both[:HEAD_DIM], axis=0, keepdims=True),
@@ -157,7 +157,7 @@
     return pl.pallas_call(
         functools.partial(attend_forward_kernel, pieces),
         out_shape=(
-            jax.ShapeDtypeStruct(queries.shape, wide),
+            jax.ShapeDtypeStruct(queries.shape, low_type),
             jax.ShapeDtypeStruct((pairs, 2, 2 * BLK), wide),
         ),
         grid_spec=pltpu.PrefetchScalarGridSpec(
@@ -598,16 +598,15 @@
 
 
 def output_kernel(form, at_ref, x_ref, attended_ref, left_ref, right_ref, bias_ref, gain_ref, shift_ref, *refs):
-    sources, (low_ref, middle_ref, normed_ref, unit_ref, scale_ref, rank_ref) = refs[:-8], refs[-8:-2]
+    sources, (middle_ref, normed_ref, unit_ref, scale_ref, rank_ref) = refs[:-7], refs[-7:-2]
     held, arrived = refs[-2:]
     at_first(lambda: fetch(form, at_ref, sources, square_unit(form, 3), 32, held, arrived))
-    low_ref[...] = attended_ref[...].astype(low_type)
-    rank_ref[...] = times(low_ref[...], left_ref[...], ROWS_BY_ROWS).astype(low_type)
+    rank_ref[...] = times(attended_ref[...], left_ref[...], ROWS_BY_ROWS).astype(low_type)
     await_first(held, arrived)
     for rows in row_tiles(x_ref.shape[0], OUTPUT_ROWS):
         middle_ref[rows, :] = (
             x_ref[rows, :].astype(wide)
-            + times(low_ref[rows, :], square(held))
+            + times(attended_ref[rows, :], square(held))
             + times(rank_ref[rows, :], right_ref[...])
             + bias_ref[...]
         )
@@ -920,7 +919,7 @@
     return frozen_call(
         output_kernel, "output_forward", at, weights, OUTPUT_TILE, (current, attended),
         (picked[2], picked[3], row(extras[1]), row(extras[6]), row(extras[7])),
-        (full_low, full, full_low, full_low, ((rows, 128), WIDE), ((rows, RANK), LOW)), (),
+        (full, full_low, full_low, ((rows, 128), WIDE), ((rows, RANK), LOW)), (),
         [pltpu.VMEM(SQUARE, LOW), DMA], 8,
     )
 
@@ -951,7 +950,7 @@
     tall = ((4, rows, columns), LOW)
     members = (
         grad, kept.normed_two, kept.unit_two, kept.scale_two, kept.rank_expand, kept.rank_reduce,
-        kept.attended_low, kept.rank_output, row(extras[6]), *picked[2:],
+        kept.attended, kept.rank_output, row(extras[6]), *picked[2:],
     )
     local_spec, anywhere = pl.BlockSpec(memory_space=pltpu.VMEM), pl.BlockSpec(memory_space=pl.ANY)
     outs = (full, full_low, *map(like, picked[2:]))
@@ -1131,7 +1130,7 @@
     def output_step(current, weights, picked, layer_index):
         keep = kept[layer_index]
         (
-            keep.attended_low, middle, keep.normed_two, keep.unit_two, keep.scale_two,
+            middle, keep.normed_two, keep.unit_two, keep.scale_two,
             keep.rank_output,
         ) = forward_output(current, keep.attended, weights, picked, extras[layer_index], at)
         return middle

time: 485 us -> 485 us (level)
    unnamed x168 -> x178, local copies, waits for them, and re-layouts: 17.6 us -> 20.3 us
where the time goes in v7:
time: 485 us; the launch traced here: 477 us
  Pallas kernels  219 us (45%)
  waiting for transfers between devices  122 us (25%)
  starting transfers between devices  62.7 us (13%)
  local copies, waits for them, and re-layouts  29.5 us (6%)
  other arithmetic  27.8 us (6%)
  between operations  15.8 us (3%)
    pallas_call x9, Pallas kernels, frozen_call(): pl.pallas_call(functools.partial(kernel, form), grid=(count // tile,) if...  103 us
    ppermute x9, waiting for transfers between devices, along_z(): return lax.ppermute(rows, 'dp', RING)  83.4 us
    pallas_call x2, Pallas kernels, backward_feed_output(): pl.pallas_call(functools.partial(feed_output_backward_kernel, form, outpu...  49.7 us
    pallas_call x2, Pallas kernels, attend_backward(): pl.pallas_call(functools.partial(attend_backward_kernel, pieces), out_sha...  37.2 us
    pallas_call x2, Pallas kernels, attend_forward(): pl.pallas_call(functools.partial(attend_forward_kernel, pieces), out_shap...  25.2 us
    unnamed x178, local copies, waits for them, and re-layouts  20.3 us
    ppermute x9, starting transfers between devices, along_z(): return lax.ppermute(rows, 'dp', RING)  15.8 us
    ppermute x2, waiting for transfers between devices, send_across(): return lax.ppermute(jnp.where(below, rows[BLK:], rows[:BLK]), CTX, across)  10.5 us
  transfers between devices with their start and end apart: 55, of which 21 were waited for; matrix products, arithmetic and copies ran while one was open for 6% of the time, Pallas kernels for 33%

profile of v7, /device:TPU:0, one launch (start us, length us, event | category | flops | bytes accessed | tf_op | source)
XLA Modules:
  0.0 476.7 jit_solution(9307949728912024675)
XLA Ops:
  11.3 3.1 collective-permute-start.1
  15.3 1.5 collective-permute-start.4
  17.7 1.5 collective-permute-start.5
  20.0 1.7 collective-permute-done.1
  24.4 13.8 %collective-permute-done.2 = bf16[128,1024]{1,0:T(8,128)(2,1)S(1)} collective-permute-done((bf16[128,1024]{1,0:T(8,128)(2,1)S(1)}, bf16[128,1024]{1,0:T(8,128)(2,1)S(1)}, u32[]{:S(2)}, u32[]{:S(2)}) %collective-permute-start.2) | collective-permute-done | bytes 262176 | tf_op jit(solution)/shard_map/ppermute | solution.py:289
  38.2 2.3 collective-permute-start.3
  40.5 1.2 bitcast_select_fusion.2
  42.7 4.2 collective-permute-done.3
  47.0 8.0 %all-to-all-start = ((bf16[16,2,16,512]{3,2,1,0:T(8,128)(2,1)}), bf16[16,2,16,512]{3,2,1,0:T(8,128)(2,1)S(1)}, u32[]{:S(2)}, u32[]{:S(2)}) async-start(bf16[16,2,16,512]{3,2,1,0:T(8,128)(2,1)} %broadcast_select_fusion), calls=%async_computation | async-start | bytes 1048576 | tf_op jit(solution)/shard_map/all_to_all | solution.py:377
  55.3 2.0 collective-permute-start.6
  57.3 1.5 collective-permute-start.7
  58.8 1.5 collective-permute-start.8
  60.3 24.7 %collective-permute-done.8 = bf16[128,1024]{1,0:T(8,128)(2,1)S(1)} collective-permute-done((bf16[128,1024]{1,0:T(8,128)(2,1)S(1)}, bf16[128,1024]{1,0:T(8,128)(2,1)S(1)}, u32[]{:S(2)}, u32[]{:S(2)}) %collective-permute-start.8) | collective-permute-done | bytes 262176 | tf_op jit(solution)/shard_map/ppermute | solution.py:289
  86.2 4.7 collective-permute-start.10
  91.3 1.5 collective-permute-start.9
  92.8 14.0 %collective-permute-done.14 = bf16[128,1024]{1,0:T(8,128)(2,1)S(1)} collective-permute-done((bf16[128,1024]{1,0:T(8,128)(2,1)S(1)}, bf16[128,1024]{1,0:T(8,128)(2,1)S(1)}, u32[]{:S(2)}, u32[]{:S(2)}) %collective-permute-start.14) | collective-permute-done | bytes 262176 | tf_op jit(solution)/shard_map/ppermute | solution.py:289
  106.8 20.3 %collective-permute-done.15 = bf16[128,1024]{1,0:T(8,128)(2,1)S(1)} collective-permute-done((bf16[128,1024]{1,0:T(8,128)(2,1)S(1)}, bf16[128,1024]{1,0:T(8,128)(2,1)S(1)}, u32[]{:S(2)}, u32[]{:S(2)}) %collective-permute-start.15) | collective-permute-done | bytes 262176 | tf_op jit(solution)/shard_map/ppermute | solution.py:289
  127.1 1.9 collective-permute-done.13.other_ref
  129.0 3.9 collective-permute-done.10.refs_3_.refs_4_
  132.9 3.5 collective-permute-done.9.refs_1_.refs_2_
  137.4 2.6 collective-permute-start.19
  141.2 3.9 collective-permute-start.20
  157.9 8.4 %qkv_forward.2 = (bf16[512,1024]{1,0:T(8,128)(2,1)}, bf16[512,1024]{1,0:T(8,128)(2,1)}, f32[512,128]{1,0:T(8,128)}, bf16[512,16]{1,0:T(8,128)(2,1)}, bf16[512,10...) custom-call(s32[4]{0:T(128)} %copy-done.24, bf16[512,1024]{1,0:T(8,128)(2,1)} %pad_maximum_fusion.x_ref, ...), custom_call_target="tpu_custom_call" | custom-call | flops 900000000 | tf_op jit(solution)/shard_map/qkv_forward/pallas_call | solution.py:805
  166.9 2.7 collective-permute-start.25
  169.6 1.2 pad_maximum_fusion.4.refs_2_.refs_11_.refs_9_
  172.3 4.7 collective-permute-done.25
  177.0 1.2 collective-permute-start.21
  179.8 1.5 collective-permute-start.26
  181.9 12.6 %attend_forward.2 = (bf16[512,1024]{1,0:T(8,128)(2,1)}, f32[8,2,512]{2,1,0:T(2,128)}) custom-call(s32[1]{0:T(128)} %bitcast.47.place_ref, bf16[512,1024]{1,0:T(8,128)(2,1)} %get-tuple-element.684.q_ref, bf16[512,1024]{1,0:T(8,128)(2,1)} %get-tuple-element.687.refs_0_, bf16[512,1024]{1,0:T(8,128)(2,1)} %copy-done.57, ...), custom_call_target="tpu_custom_call" | custom-call | flops 1300000000 | tf_op jit(solution)/shard_map/attend_forward/pallas_call | solution.py:157
  194.6 7.2 %output_forward.2 = (f32[512,1024]{1,0:T(8,128)}, bf16[512,1024]{1,0:T(8,128)(2,1)}, bf16[512,1024]{1,0:T(8,128)(2,1)}, f32[512,128]{1,0:T(8,128)}, bf16[512,16]{1,0:T(8,128)(2,1)}) custom-call(s32[4]{0:T(128)} %copy-done.24, bf16[512,1024]{1,0:T(8,128)(2,1)} %pad_maximum_fusion.x_ref, bf16[512,1024]{1,0:T(8,128)(2,1)} %get-tuple-element.661.attended_ref.o_ref, ...), custom_call_target="tpu_custom_call" | custom-call | flops 800000000 | tf_op jit(solution)/shard_map/output_forward/pallas_call | solution.py:805
  201.8 3.0 collective-permute-done.21.refs_1_.refs_10_.refs_8_
  211.8 21.3 %feed_forward.2 = (f32[512,1024]{1,0:T(8,128)}, bf16[512,4096]{1,0:T(8,128)(2,1)}, bf16[512,4096]{1,0:T(8,128)(2,1)}, bf16[512,16]{1,0:T(8,128)(2,1)}, bf16[512,16]{1,0:T(8,128)(2,1)}) custom-call(s32[4]{0:T(128)} %copy-done.24, bf16[512,1024]{1,0:T(8,128)(2,1)} %get-tuple-element.656.normed_ref, f32[512,1024]{1,0:T(8,128)} %get-tuple-element.463.middle_ref, ...), custom_call_target="tpu_custom_call" | custom-call | flops 2000000000 | tf_op jit(solution)/shard_map/feed_forward/pallas_call | solution.py:805
  234.4 8.7 %qkv_forward.3 = (bf16[512,1024]{1,0:T(8,128)(2,1)}, bf16[512,1024]{1,0:T(8,128)(2,1)}, f32[512,128]{1,0:T(8,128)}, bf16[512,16]{1,0:T(8,128)(2,1)}, bf16[512,10...) custom-call(s32[4]{0:T(128)} %copy-done.24, f32[512,1024]{1,0:T(8,128)} %get-tuple-element.556.x_ref, ...), custom_call_target="tpu_custom_call" | custom-call | flops 900000000 | tf_op jit(solution)/shard_map/qkv_forward/pallas_call | solution.py:805
  243.7 1.4 pad_maximum_fusion.6.refs_2_
  245.3 2.0 collective-permute-start.34
  247.3 2.1 pad_maximum_fusion.5.refs_0_
  251.6 1.5 collective-permute-start
  253.1 12.6 %attend_forward.3 = (bf16[512,1024]{1,0:T(8,128)(2,1)}, f32[8,2,512]{2,1,0:T(2,128)}) custom-call(s32[1]{0:T(128)} %bitcast.47.place_ref, bf16[512,1024]{1,0:T(8,128)(2,1)} %get-tuple-element.630.q_ref, bf16[512,1024]{1,0:T(8,128)(2,1)} %get-tuple-element.633.refs_0_, bf16[512,1024]{1,0:T(8,128)(2,1)} %copy-done.59, ...), custom_call_target="tpu_custom_call" | custom-call | flops 1300000000 | tf_op jit(solution)/shard_map/attend_forward/pallas_call | solution.py:157
  265.7 7.6 %output_forward.3 = (f32[512,1024]{1,0:T(8,128)}, bf16[512,1024]{1,0:T(8,128)(2,1)}, bf16[512,1024]{1,0:T(8,128)(2,1)}, f32[512,128]{1,0:T(8,128)}, bf16[512,16]{1,0:T(8,128)(2,1)}) custom-call(s32[4]{0:T(128)} %copy-done.24, f32[512,1024]{1,0:T(8,128)} %get-tuple-element.556.x_ref, bf16[512,1024]{1,0:T(8,128)(2,1)} %get-tuple-element.607.attended_ref.o_ref, ...), custom_call_target="tpu_custom_call" | custom-call | flops 800000000 | tf_op jit(solution)/shard_map/output_forward/pallas_call | solution.py:805
  273.4 1.9 collective-permute-done.33.refs_1_
  276.5 1.6 collective-permute-done.39.refs_5_
  278.2 1.5 collective-permute-done.40.refs_7_
  280.6 20.7 %feed_forward.3 = (f32[512,1024]{1,0:T(8,128)}, bf16[512,4096]{1,0:T(8,128)(2,1)}, bf16[512,4096]{1,0:T(8,128)(2,1)}, bf16[512,16]{1,0:T(8,128)(2,1)}, bf16[512,16]{1,0:T(8,128)(2,1)}) custom-call(s32[4]{0:T(128)} %copy-done.24, bf16[512,1024]{1,0:T(8,128)(2,1)} %get-tuple-element.587.normed_ref, f32[512,1024]{1,0:T(8,128)} %get-tuple-element.588.middle_ref, ...), custom_call_target="tpu_custom_call" | custom-call | flops 2000000000 | tf_op jit(solution)/shard_map/feed_forward/pallas_call | solution.py:805
  301.4 1.8 convert_element_type.18
  303.7 1.2 bitcast_select_fusion
  306.0 26.1 %feed_output_backward.2 = (f32[512,1024]{1,0:T(8,128)}, bf16[512,1024]{1,0:T(8,128)(2,1)}, bf16[16,1024]{1,0:T(8,128)(2,1)}, bf16[16,1024]{1,0:T(8,128)(2,1)}, b...) custom-call(s32[4]{0:T(128)} %copy-done.24, ...), custom_call_target="tpu_custom_call" | custom-call | flops 2500000000 | tf_op jit(solution)/shard_map/feed_output_backward/pallas_call | solution.py:957
  333.7 18.7 %attend_backward.2 = (bf16[512,1024]{1,0:T(8,128)(2,1)}, bf16[512,1024]{1,0:T(8,128)(2,1)}, bf16[512,1024]{1,0:T(8,128)(2,1)}, bf16[512,1024]{1,0:T(8,128)(2,1)}, bf16[512,1024]{1,0:T(8,128)(2,1)}) custom-call(s32[1]{0:T(128)} %bitcast.47.place_ref, bf16[512,1024]{1,0:T(8,128)(2,1)} %get-tuple-element.630.q_ref, bf16[512,1024]{1,0:T(8,128)(2,1)} %get-tuple-element.631.g_ref, ...), custom_call_target="tpu_custom_call" | custom-call | flops 2100000000 | tf_op jit(solution)/shard_map/attend_backward/pallas_call | solution.py:183
  353.0 2.4 collective-permute-done.44.refs_1_
  355.4 1.5 collective-permute-done.45.refs_3_
  358.0 12.7 %qkv_whole.1 = (f32[512,1024]{1,0:T(8,128)}, bf16[16,1024]{1,0:T(8,128)(2,1)}, bf16[16,3072]{1,0:T(8,128)(2,1)}) custom-call(s32[4]{0:T(128)} %copy-done.24, f32[512,1024]{1,0:T(8,128)} %get-tuple-element.643.grad_ref, bf16[512,1024]{1,0:T(8,128)(2,1)} %get-tuple-element.644.unit_ref, f32[512,128]{1,0:T(8,128)} %get-tuple-element.645.scale_ref, ...), custom_call_target="tpu_custom_call" | custom-call | flops 1100000000 | tf_op jit(solution)/shard_map/qkv_whole/pallas_call | solution.py:805
  370.7 23.6 %feed_output_backward.3 = (f32[512,1024]{1,0:T(8,128)}, bf16[512,1024]{1,0:T(8,128)(2,1)}, bf16[16,1024]{1,0:T(8,128)(2,1)}, bf16[16,1024]{1,0:T(8,128)(2,1)}, b...) custom-call(s32[4]{0:T(128)} %copy-done.24, ...), custom_call_target="tpu_custom_call" | custom-call | flops 2500000000 | tf_op jit(solution)/shard_map/feed_output_backward/pallas_call | solution.py:957
  394.3 18.5 %attend_backward.3 = (bf16[512,1024]{1,0:T(8,128)(2,1)}, bf16[512,1024]{1,0:T(8,128)(2,1)}, bf16[512,1024]{1,0:T(8,128)(2,1)}, bf16[512,1024]{1,0:T(8,128)(2,1)}, bf16[512,1024]{1,0:T(8,128)(2,1)}) custom-call(s32[1]{0:T(128)} %bitcast.47.place_ref, bf16[512,1024]{1,0:T(8,128)(2,1)} %get-tuple-element.684.q_ref, bf16[512,1024]{1,0:T(8,128)(2,1)} %get-tuple-element.685.g_ref, ...), custom_call_target="tpu_custom_call" | custom-call | flops 2100000000 | tf_op jit(solution)/shard_map/attend_backward/pallas_call | solution.py:183
  413.4 2.4 collective-permute-done.46.refs_1_
  415.8 1.5 collective-permute-done.47.refs_3_
  418.5 6.3 %qkv_turn.1 = (bf16[512,1024]{1,0:T(8,128)(2,1)}, bf16[512,1024]{1,0:T(8,128)(2,1)}, bf16[512,16]{1,0:T(8,128)(2,1)}, bf16[16,1024]{1,0:T(8,128)(2,1)}, bf16[16,3072]{1,0:T(8,128)(2,1)}) custom-call(s32[4]{0:T(128)} %copy-done.24, bf16[512,1024]{1,0:T(8,128)(2,1)} %get-tuple-element.682.normed_ref, bf16[512,16]{1,0:T(8,128)(2,1)} %get-tuple-element.683.rank_ref, ...), custom_call_target="tpu_custom_call" | custom-call | flops 300000000 | tf_op jit(solution)/shard_map/qkv_turn/pallas_call | solution.py:805
  428.2 1.5 collective-permute-done.48
  430.7 5.5 %all-to-all-start.1 = ((bf16[16,16,1024]{2,1,0:T(8,128)(2,1)}), bf16[16,16,1024]{2,1,0:T(8,128)(2,1)S(1)}, u32[]{:S(2)}, u32[]{:S(2)}) async-start(bf16[16,16,1024]{2,1,0:T(8,128)(2,1)} %fusion), calls=%async_computation.1 | async-start | bytes 1048576 | tf_op jit(solution)/shard_map/all_to_all | solution.py:1205
  436.2 10.5 %qkv_backward.1 = (f32[512,1024]{1,0:T(8,128)}, bf16[512,1024]{1,0:T(8,128)(2,1)}) custom-call(s32[4]{0:T(128)} %copy-done.24, f32[512,1024]{1,0:T(8,128)} %get-tuple-element.679.grad_ref, bf16[512,1024]{1,0:T(8,128)(2,1)} %get-tuple-element.680.unit_ref, f32[512,128]{1,0:T(8,128)} %get-tuple-element.681.scale_ref, ...), custom_call_target="tpu_custom_call" | custom-call | flops 900000000 | tf_op jit(solution)/shard_map/qkv_backward/pallas_call | solution.py:805
  446.7 1.3 fusion.9
  448.9 3.3 collective-permute-start.49
  454.2 10.5 %collective-permute-done.49 = bf16[256,1024]{1,0:T(8,128)(2,1)} collective-permute-done((bf16[256,1024]{1,0:T(8,128)(2,1)S(1)}, bf16[256,1024]{1,0:T(8,128)(2,1)}, u32[]{:S(2)}, u32[]{:S(2)}) %collective-permute-start.49) | collective-permute-done | bytes 524320 | tf_op jit(solution)/shard_map/ppermute | solution.py:231
  464.8 1.2 select_bitcast_fusion.1
  466.0 1.8 combine.1
  467.7 1.7 maximum_select_fusion
  (314 shorter events, 58.2 us)
Async XLA Ops:
  7.2 12.0 %copy-start = (s32[16]{0:T(128)S(1)}, s32[16]{0:T(128)}, u32[]{:S(2)}) copy-start(s32[16]{0:T(128)} %param.25) | copy-start | bytes 196
  7.2 204.5 %all-gather.6.cloned.1.call-start = ((), (), s32[]{:S(2)}) async-start(), calls=%async_computation.3 | async-start | bytes 17301504 | tf_op jit(solution)/shard_map/all_gather | solution.py:347
  10.4 266.2 %all-gather.4.cloned.1.call-start = ((), (), s32[]{:S(2)}) async-start(), calls=%async_computation.2 | async-start | bytes 8650752 | tf_op jit(solution)/shard_map/all_gather | solution.py:347
  11.3 10.4 %collective-permute-start.1 = (bf16[128,1024]{1,0:T(8,128)(2,1)S(1)}, bf16[128,1024]{1,0:T(8,128)(2,1)S(1)}, u32[]{:S(2)}, u32[]{:S(2)}) collective-permute-start(bf16[128,1024]{1,0:T(8,128)(2,1)S(1)} %pad_maximum_fusion.15), channel_id=1, source_target_pairs={{0,8},{4,12},{8,24},{12,28},{16,0},{20,4},{24,16},{28,20},{1,9},{5... | collective-permute-start | bytes 786440 | tf_op jit(solution)/shard_map/ppermute | solution.py:289
  15.3 25.2 %collective-permute-start.4 = (bf16[256,1024]{1,0:T(8,128)(2,1)}, bf16[256,1024]{1,0:T(8,128)(2,1)}, u32[]{:S(2)}, u32[]{:S(2)}) collective-permute-start(bf16[256,1024]{1,0:T(8,128)(2,1)} %bitcast_select_fusion.3), channel_id=1, source_target_pairs={{0,2},{1,3},{2,1},{3,0},{4,6},{5,7},{6,5},{7,4},{8,10},{9,11},{10,... | collective-permute-start | bytes 1572872 | tf_op jit(solution)/shard_map/ppermute | solution.py:210
  17.7 22.8 %collective-permute-start.5 = (bf16[256,1024]{1,0:T(8,128)(2,1)}, bf16[256,1024]{1,0:T(8,128)(2,1)}, u32[]{:S(2)}, u32[]{:S(2)}) collective-permute-start(bf16[256,1024]{1,0:T(8,128)(2,1)} %slice_bitcast_fusion.3), channel_id=1, source_target_pairs={{2,3},{3,2},{6,7},{7,6},{10,11},{11,10},{14,15},{15,14},{18,19},{1... | collective-permute-start | bytes 1572872 | tf_op jit(solution)/shard_map/ppermute | solution.py:215
  21.7 16.5 %collective-permute-start.2 = (bf16[128,1024]{1,0:T(8,128)(2,1)S(1)}, bf16[128,1024]{1,0:T(8,128)(2,1)S(1)}, u32[]{:S(2)}, u32[]{:S(2)}) collective-permute-start(bf16[128,1024]{1,0:T(8,128)(2,1)S(1)} %collective-permute-done.1), channel_id=1, source_target_pairs={{0,8},{4,12},{8,24},{12,28},{16,0},{20,4},{24,16},{28,20},{1,9},{5... | collective-permute-start | bytes 786440 | tf_op jit(solution)/shard_map/ppermute | solution.py:289
  38.2 8.7 %collective-permute-start.3 = (bf16[128,1024]{1,0:T(8,128)(2,1)S(1)}, bf16[128,1024]{1,0:T(8,128)(2,1)S(1)}, u32[]{:S(2)}, u32[]{:S(2)}) collective-permute-start(bf16[128,1024]{1,0:T(8,128)(2,1)S(1)} %collective-permute-done.2), channel_id=1, source_target_pairs={{0,8},{4,12},{8,24},{12,28},{16,0},{20,4},{24,16},{28,20},{1,9},{5... | collective-permute-start | bytes 786440 | tf_op jit(solution)/shard_map/ppermute | solution.py:289
  47.0 38.0 %all-to-all-start = ((bf16[16,2,16,512]{3,2,1,0:T(8,128)(2,1)}), bf16[16,2,16,512]{3,2,1,0:T(8,128)(2,1)S(1)}, u32[]{:S(2)}, u32[]{:S(2)}) async-start(bf16[16,2,16,512]{3,2,1,0:T(8,128)(2,1)} %broadcast_select_fusion), calls=%async_computation | async-start | bytes 1048576 | tf_op jit(solution)/shard_map/all_to_all | solution.py:377
  55.3 29.7 %collective-permute-start.6 = (bf16[4,64,1024]{2,1,0:T(8,128)(2,1)S(1)}, bf16[4,64,1024]{2,1,0:T(8,128)(2,1)S(1)}, u32[]{:S(2)}, u32[]{:S(2)}) collective-permute-start(bf16[4,64,1024]{2,1,0:T(8,128)(2,1)S(1)} %pad_maximum_fusion.9), channel_id=1, source_target_pairs={{0,4},{4,0},{8,12},{12,8},{16,20},{20,16},{24,28},{28,24},{1,5},{5... | collective-permute-start | bytes 1572872 | tf_op jit(solution)/shard_map/ppermute | solution.py:293
  57.3 27.7 %collective-permute-start.7 = (bf16[4,64,1024]{2,1,0:T(8,128)(2,1)S(1)}, bf16[4,64,1024]{2,1,0:T(8,128)(2,1)}, u32[]{:S(2)}, u32[]{:S(2)}) collective-permute-start(bf16[4,64,1024]{2,1,0:T(8,128)(2,1)S(1)} %pad_maximum_fusion.10), channel_id=1, source_target_pairs={{0,2},{2,0},{1,3},{3,1},{4,6},{6,4},{5,7},{7,5},{8,10},{10,8},{9,1... | collective-permute-start | bytes 1572872 | tf_op jit(solution)/shard_map/ppermute | solution.py:297
  58.8 26.1 %collective-permute-start.8 = (bf16[128,1024]{1,0:T(8,128)(2,1)S(1)}, bf16[128,1024]{1,0:T(8,128)(2,1)S(1)}, u32[]{:S(2)}, u32[]{:S(2)}) collective-permute-start(bf16[128,1024]{1,0:T(8,128)(2,1)S(1)} %pad_maximum_fusion.16), channel_id=1, source_target_pairs={{0,8},{4,12},{8,24},{12,28},{16,0},{20,4},{24,16},{28,20},{1,9},{5... | collective-permute-start | bytes 786440 | tf_op jit(solution)/shard_map/ppermute | solution.py:289
  85.0 42.1 %copy-start.80 = (f32[2,2048]{1,0:T(2,128)S(1)}, f32[2,2048]{1,0:T(2,128)}, u32[]{:S(2)}) copy-start(f32[2,2048]{1,0:T(2,128)} %param.30) | copy-start | bytes 49156
  86.1 50.9 %copy-start.37 = (bf16[2,4,64,1024]{3,2,1,0:T(8,128)(2,1)}, bf16[2,4,64,1024]{3,2,1,0:T(8,128)(2,1)S(1)}, u32[]{:S(2)}) copy-start(bf16[2,4,64,1024]{3,2,1,0:T(8,128)(2,1)S(1)} %pad_maximum_fusion.2.refs_2_.refs_3_) | copy-start | bytes 3145732
  86.2 42.8 %collective-permute-start.12 = (bf16[2,4,64,1024]{3,2,1,0:T(8,128)(2,1)S(1)}, bf16[2,4,64,1024]{3,2,1,0:T(8,128)(2,1)S(1)}, u32[]{:S(2)}, u32[]{:S(2)}) collective-permute-start(bf16[2,4,64,1024]{3,2,1,0:T(8,128)(2,1)S(1)} %pad_maximum_fusion.2.refs_2_.refs_3_), channel_id=1, source_target_pairs={{0,1},{1,0},{2,3},{3,2},{4,5},{5,4},{6,7},{7,6},{8,9},{9,8},{10,11... | collective-permute-start | bytes 3145736 | tf_op jit(solution)/shard_map/ppermute | solution.py:301
  86.2 46.7 %collective-permute-start.10 = (bf16[2,4,64,1024]{3,2,1,0:T(8,128)(2,1)S(1)}, bf16[2,4,64,1024]{3,2,1,0:T(8,128)(2,1)}, u32[]{:S(2)}, u32[]{:S(2)}) collective-permute-start(bf16[2,4,64,1024]{3,2,1,0:T(8,128)(2,1)S(1)} %pad_maximum_fusion.2.refs_2_.refs_3_), channel_id=1, source_target_pairs={{0,4},{4,0},{8,12},{12,8},{16,20},{20,16},{24,28},{28,24},{1,5},{5... | collective-permute-start | bytes 3145736 | tf_op jit(solution)/shard_map/ppermute | solution.py:293
  91.0 15.8 %collective-permute-start.14 = (bf16[128,1024]{1,0:T(8,128)(2,1)S(1)}, bf16[128,1024]{1,0:T(8,128)(2,1)S(1)}, u32[]{:S(2)}, u32[]{:S(2)}) collective-permute-start(bf16[128,1024]{1,0:T(8,128)(2,1)S(1)} %collective-permute-done.8), channel_id=1, source_target_pairs={{0,8},{4,12},{8,24},{12,28},{16,0},{20,4},{24,16},{28,20},{1,9},{5... | collective-permute-start | bytes 786440 | tf_op jit(solution)/shard_map/ppermute | solution.py:289
  91.1 46.1 %copy-start.38 = (bf16[2,4,64,1024]{3,2,1,0:T(8,128)(2,1)}, bf16[2,4,64,1024]{3,2,1,0:T(8,128)(2,1)S(1)}, u32[]{:S(2)}) copy-start(bf16[2,4,64,1024]{3,2,1,0:T(8,128)(2,1)S(1)} %pad_maximum_fusion.1.refs_0_.refs_1_) | copy-start | bytes 3145732
  91.1 41.8 %collective-permute-start.11 = (bf16[2,4,64,1024]{3,2,1,0:T(8,128)(2,1)S(1)}, bf16[2,4,64,1024]{3,2,1,0:T(8,128)(2,1)S(1)}, u32[]{:S(2)}, u32[]{:S(2)}) collective-permute-start(bf16[2,4,64,1024]{3,2,1,0:T(8,128)(2,1)S(1)} %pad_maximum_fusion.1.refs_0_.refs_1_), channel_id=1, source_target_pairs={{0,1},{1,0},{2,3},{3,2},{4,5},{5,4},{6,7},{7,6},{8,9},{9,8},{10,11... | collective-permute-start | bytes 3145736 | tf_op jit(solution)/shard_map/ppermute | solution.py:301
  91.3 45.1 %collective-permute-start.9 = (bf16[2,4,64,1024]{3,2,1,0:T(8,128)(2,1)S(1)}, bf16[2,4,64,1024]{3,2,1,0:T(8,128)(2,1)}, u32[]{:S(2)}, u32[]{:S(2)}) collective-permute-start(bf16[2,4,64,1024]{3,2,1,0:T(8,128)(2,1)S(1)} %pad_maximum_fusion.1.refs_0_.refs_1_), channel_id=1, source_target_pairs={{0,2},{2,0},{1,3},{3,1},{4,6},{6,4},{5,7},{7,5},{8,10},{10,8},{9,1... | collective-permute-start | bytes 3145736 | tf_op jit(solution)/shard_map/ppermute | solution.py:297
  106.8 20.3 %collective-permute-start.15 = (bf16[128,1024]{1,0:T(8,128)(2,1)S(1)}, bf16[128,1024]{1,0:T(8,128)(2,1)S(1)}, u32[]{:S(2)}, u32[]{:S(2)}) collective-permute-start(bf16[128,1024]{1,0:T(8,128)(2,1)S(1)} %collective-permute-done.14), channel_id=1, source_target_pairs={{0,8},{4,12},{8,24},{12,28},{16,0},{20,4},{24,16},{28,20},{1,9},{5... | collective-permute-start | bytes 786440 | tf_op jit(solution)/shard_map/ppermute | solution.py:289
  127.0 1.9 collective-permute-start.13
  136.4 21.5 %collective-permute-start.16 = (bf16[2,4,64,1024]{3,2,1,0:T(8,128)(2,1)}, bf16[2,4,64,1024]{3,2,1,0:T(8,128)(2,1)}, u32[]{:S(2)}, u32[]{:S(2)}) collective-permute-start(bf16[2,4,64,1024]{3,2,1,0:T(8,128)(2,1)} %collective-permute-done.9.refs_1_.refs_2_), channel_id=1, source_target_pairs={{0,1},{1,0},{2,3},{3,2},{4,5},{5,4},{6,7},{7,6},{8,9},{9,8},{10,11... | collective-permute-start | bytes 3145736 | tf_op jit(solution)/shard_map/ppermute | solution.py:301
  136.4 21.5 %collective-permute-start.17 = (bf16[2,4,64,1024]{3,2,1,0:T(8,128)(2,1)}, bf16[2,4,64,1024]{3,2,1,0:T(8,128)(2,1)}, u32[]{:S(2)}, u32[]{:S(2)}) collective-permute-start(bf16[2,4,64,1024]{3,2,1,0:T(8,128)(2,1)} %collective-permute-done.10.refs_3_.refs_4_), channel_id=1, source_target_pairs={{0,1},{1,0},{2,3},{3,2},{4,5},{5,4},{6,7},{7,6},{8,9},{9,8},{10,11... | collective-permute-start | bytes 3145736 | tf_op jit(solution)/shard_map/ppermute | solution.py:301
  137.2 19.5 %collective-permute-start.18 = (bf16[4,64,1024]{2,1,0:T(8,128)(2,1)S(1)}, bf16[4,64,1024]{2,1,0:T(8,128)(2,1)S(1)}, u32[]{:S(2)}, u32[]{:S(2)}) collective-permute-start(bf16[4,64,1024]{2,1,0:T(8,128)(2,1)S(1)} %pad_maximum_fusion.11), channel_id=1, source_target_pairs={{0,4},{4,0},{8,12},{12,8},{16,20},{20,16},{24,28},{28,24},{1,5},{5... | collective-permute-start | bytes 1572872 | tf_op jit(solution)/shard_map/ppermute | solution.py:293
  137.4 20.5 %collective-permute-start.19 = (bf16[4,64,1024]{2,1,0:T(8,128)(2,1)S(1)}, bf16[4,64,1024]{2,1,0:T(8,128)(2,1)}, u32[]{:S(2)}, u32[]{:S(2)}) collective-permute-start(bf16[4,64,1024]{2,1,0:T(8,128)(2,1)S(1)} %pad_maximum_fusion.12), channel_id=1, source_target_pairs={{0,2},{2,0},{1,3},{3,1},{4,6},{6,4},{5,7},{7,5},{8,10},{10,8},{9,1... | collective-permute-start | bytes 1572872 | tf_op jit(solution)/shard_map/ppermute | solution.py:297
  141.2 15.5 %collective-permute-start.20 = (bf16[128,1024]{1,0:T(8,128)(2,1)S(1)}, bf16[128,1024]{1,0:T(8,128)(2,1)S(1)}, u32[]{:S(2)}, u32[]{:S(2)}) collective-permute-start(bf16[128,1024]{1,0:T(8,128)(2,1)S(1)} %pad_maximum_fusion.17), channel_id=1, source_target_pairs={{0,8},{4,12},{8,24},{12,28},{16,0},{20,4},{24,16},{28,20},{1,9},{5... | collective-permute-start | bytes 786440 | tf_op jit(solution)/shard_map/ppermute | solution.py:289
  145.2 12.7 %copy-start.24 = (s32[4]{0:T(128)}, s32[4]{0:T(128)S(1)}, u32[]{:S(2)}) copy-start(s32[4]{0:T(128)S(1)} %pad_add_fusion.1.at_ref) | copy-start | bytes 52
  166.3 10.7 %collective-permute-start.27 = (bf16[512,1024]{1,0:T(8,128)(2,1)}, bf16[512,1024]{1,0:T(8,128)(2,1)S(1)}, u32[]{:S(2)}, u32[]{:S(2)}) collective-permute-start(bf16[512,1024]{1,0:T(8,128)(2,1)} %get-tuple-element.687.refs_0_), channel_id=1, source_target_pairs={{0,1},{1,0},{2,3},{3,2},{4,5},{5,4},{6,7},{7,6},{8,9},{9,8},{10,11... | collective-permute-start | bytes 3145736 | tf_op jit(solution)/shard_map/ppermute | solution.py:258
  166.4 12.4 %collective-permute-start.28 = (bf16[512,1024]{1,0:T(8,128)(2,1)}, bf16[512,1024]{1,0:T(8,128)(2,1)S(1)}, u32[]{:S(2)}, u32[]{:S(2)}) collective-permute-start(bf16[512,1024]{1,0:T(8,128)(2,1)} %get-tuple-element.689.refs_2_), channel_id=1, source_target_pairs={{0,1},{1,0},{2,3},{3,2},{4,5},{5,4},{6,7},{7,6},{8,9},{9,8},{10,11... | collective-permute-start | bytes 3145736 | tf_op jit(solution)/shard_map/ppermute | solution.py:258
  166.9 10.2 %collective-permute-start.25 = (bf16[128,1024]{1,0:T(8,128)(2,1)S(1)}, bf16[128,1024]{1,0:T(8,128)(2,1)}, u32[]{:S(2)}, u32[]{:S(2)}) collective-permute-start(bf16[128,1024]{1,0:T(8,128)(2,1)S(1)} %collective-permute-done.20), channel_id=1, source_target_pairs={{0,8},{4,12},{8,24},{12,28},{16,0},{20,4},{24,16},{28,20},{1,9},{5... | collective-permute-start | bytes 786440 | tf_op jit(solution)/shard_map/ppermute | solution.py:289
  170.7 23.8 %copy-start.36 = (bf16[2,4,64,1024]{3,2,1,0:T(8,128)(2,1)}, bf16[2,4,64,1024]{3,2,1,0:T(8,128)(2,1)S(1)}, u32[]{:S(2)}) copy-start(bf16[2,4,64,1024]{3,2,1,0:T(8,128)(2,1)S(1)} %pad_maximum_fusion.4.refs_2_.refs_11_.refs_9_) | copy-start | bytes 3145732
  170.8 31.0 %collective-permute-start.24 = (bf16[2,4,64,1024]{3,2,1,0:T(8,128)(2,1)S(1)}, bf16[2,4,64,1024]{3,2,1,0:T(8,128)(2,1)}, u32[]{:S(2)}, u32[]{:S(2)}) collective-permute-start(bf16[2,4,64,1024]{3,2,1,0:T(8,128)(2,1)S(1)} %pad_maximum_fusion.4.refs_2_.refs_11_.refs_9_), channel_id=1, source_target_pairs={{0,1},{1,0},{2,3},{3,2},{4,5},{5,4},{6,7},{7,6},{8,9},{9,8},{10,11... | collective-permute-start | bytes 3145736 | tf_op jit(solution)/shard_map/ppermute | solution.py:301
  170.8 30.9 %collective-permute-start.22 = (bf16[2,4,64,1024]{3,2,1,0:T(8,128)(2,1)S(1)}, bf16[2,4,64,1024]{3,2,1,0:T(8,128)(2,1)}, u32[]{:S(2)}, u32[]{:S(2)}) collective-permute-start(bf16[2,4,64,1024]{3,2,1,0:T(8,128)(2,1)S(1)} %pad_maximum_fusion.4.refs_2_.refs_11_.refs_9_), channel_id=1, source_target_pairs={{0,4},{4,0},{8,12},{12,8},{16,20},{20,16},{24,28},{28,24},{1,5},{5... | collective-permute-start | bytes 3145736 | tf_op jit(solution)/shard_map/ppermute | solution.py:293
  177.0 24.7 %collective-permute-start.23 = (bf16[2,4,64,1024]{3,2,1,0:T(8,128)(2,1)}, bf16[2,4,64,1024]{3,2,1,0:T(8,128)(2,1)}, u32[]{:S(2)}, u32[]{:S(2)}) collective-permute-start(bf16[2,4,64,1024]{3,2,1,0:T(8,128)(2,1)} %pad_maximum_fusion.3.refs_0_.refs_9_.refs_7_), channel_id=1, source_target_pairs={{0,1},{1,0},{2,3},{3,2},{4,5},{5,4},{6,7},{7,6},{8,9},{9,8},{10,11... | collective-permute-start | bytes 3145736 | tf_op jit(solution)/shard_map/ppermute | solution.py:301
  177.0 27.8 %collective-permute-start.21 = (bf16[2,4,64,1024]{3,2,1,0:T(8,128)(2,1)}, bf16[2,4,64,1024]{3,2,1,0:T(8,128)(2,1)}, u32[]{:S(2)}, u32[]{:S(2)}) collective-permute-start(bf16[2,4,64,1024]{3,2,1,0:T(8,128)(2,1)} %pad_maximum_fusion.3.refs_0_.refs_9_.refs_7_), channel_id=1, source_target_pairs={{0,2},{2,0},{1,3},{3,1},{4,6},{6,4},{5,7},{7,5},{8,10},{10,8},{9,1... | collective-permute-start | bytes 3145736 | tf_op jit(solution)/shard_map/ppermute | solution.py:297
  179.8 21.9 %collective-permute-start.26 = (bf16[128,1024]{1,0:T(8,128)(2,1)}, bf16[128,1024]{1,0:T(8,128)(2,1)S(1)}, u32[]{:S(2)}, u32[]{:S(2)}) collective-permute-start(bf16[128,1024]{1,0:T(8,128)(2,1)} %collective-permute-done.25), channel_id=1, source_target_pairs={{0,8},{4,12},{8,24},{12,28},{16,0},{20,4},{24,16},{28,20},{1,9},{5... | collective-permute-start | bytes 786440 | tf_op jit(solution)/shard_map/ppermute | solution.py:289
  208.0 25.1 %collective-permute-start.31 = (bf16[4,64,1024]{2,1,0:T(8,128)(2,1)S(1)}, bf16[4,64,1024]{2,1,0:T(8,128)(2,1)}, u32[]{:S(2)}, u32[]{:S(2)}) collective-permute-start(bf16[4,64,1024]{2,1,0:T(8,128)(2,1)S(1)} %pad_maximum_fusion.13), channel_id=1, source_target_pairs={{0,4},{4,0},{8,12},{12,8},{16,20},{20,16},{24,28},{28,24},{1,5},{5... | collective-permute-start | bytes 1572872 | tf_op jit(solution)/shard_map/ppermute | solution.py:293
  209.4 23.7 %collective-permute-start.32 = (bf16[4,64,1024]{2,1,0:T(8,128)(2,1)}, bf16[4,64,1024]{2,1,0:T(8,128)(2,1)}, u32[]{:S(2)}, u32[]{:S(2)}) collective-permute-start(bf16[4,64,1024]{2,1,0:T(8,128)(2,1)} %pad_maximum_fusion.14), channel_id=1, source_target_pairs={{0,2},{2,0},{1,3},{3,1},{4,6},{6,4},{5,7},{7,5},{8,10},{10,8},{9,1... | collective-permute-start | bytes 1572872 | tf_op jit(solution)/shard_map/ppermute | solution.py:297
  210.0 23.0 %collective-permute-start.29 = (bf16[2,4,64,1024]{3,2,1,0:T(8,128)(2,1)}, bf16[2,4,64,1024]{3,2,1,0:T(8,128)(2,1)S(1)}, u32[]{:S(2)}, u32[]{:S(2)}) collective-permute-start(bf16[2,4,64,1024]{3,2,1,0:T(8,128)(2,1)} %collective-permute-done.21.refs_1_.refs_10_.refs_8_), channel_id=1, source_target_pairs={{0,1},{1,0},{2,3},{3,2},{4,5},{5,4},{6,7},{7,6},{8,9},{9,8},{10,11... | collective-permute-start | bytes 3145736 | tf_op jit(solution)/shard_map/ppermute | solution.py:301
  210.0 23.1 %collective-permute-start.30 = (bf16[2,4,64,1024]{3,2,1,0:T(8,128)(2,1)}, bf16[2,4,64,1024]{3,2,1,0:T(8,128)(2,1)S(1)}, u32[]{:S(2)}, u32[]{:S(2)}) collective-permute-start(bf16[2,4,64,1024]{3,2,1,0:T(8,128)(2,1)} %collective-permute-done.22.refs_3_.refs_12_.refs_10_), channel_id=1, source_target_pairs={{0,1},{1,0},{2,3},{3,2},{4,5},{5,4},{6,7},{7,6},{8,9},{9,8},{10,11... | collective-permute-start | bytes 3145736 | tf_op jit(solution)/shard_map/ppermute | solution.py:301
  243.1 6.4 %collective-permute-start.37 = (bf16[512,1024]{1,0:T(8,128)(2,1)}, bf16[512,1024]{1,0:T(8,128)(2,1)S(1)}, u32[]{:S(2)}, u32[]{:S(2)}) collective-permute-start(bf16[512,1024]{1,0:T(8,128)(2,1)} %get-tuple-element.633.refs_0_), channel_id=1, source_target_pairs={{0,1},{1,0},{2,3},{3,2},{4,5},{5,4},{6,7},{7,6},{8,9},{9,8},{10,11... | collective-permute-start | bytes 3145736 | tf_op jit(solution)/shard_map/ppermute | solution.py:258
  243.2 7.4 %collective-permute-start.38 = (bf16[512,1024]{1,0:T(8,128)(2,1)}, bf16[512,1024]{1,0:T(8,128)(2,1)S(1)}, u32[]{:S(2)}, u32[]{:S(2)}) collective-permute-start(bf16[512,1024]{1,0:T(8,128)(2,1)} %get-tuple-element.635.refs_2_), channel_id=1, source_target_pairs={{0,1},{1,0},{2,3},{3,2},{4,5},{5,4},{6,7},{7,6},{8,9},{9,8},{10,11... | collective-permute-start | bytes 3145736 | tf_op jit(solution)/shard_map/ppermute | solution.py:258
  245.1 20.6 %copy-start.43 = (bf16[2,4,64,1024]{3,2,1,0:T(8,128)(2,1)}, bf16[2,4,64,1024]{3,2,1,0:T(8,128)(2,1)S(1)}, u32[]{:S(2)}) copy-start(bf16[2,4,64,1024]{3,2,1,0:T(8,128)(2,1)S(1)} %pad_maximum_fusion.6.refs_2_) | copy-start | bytes 3145732
  245.1 28.2 %collective-permute-start.36 = (bf16[2,4,64,1024]{3,2,1,0:T(8,128)(2,1)S(1)}, bf16[2,4,64,1024]{3,2,1,0:T(8,128)(2,1)}, u32[]{:S(2)}, u32[]{:S(2)}) collective-permute-start(bf16[2,4,64,1024]{3,2,1,0:T(8,128)(2,1)S(1)} %pad_maximum_fusion.6.refs_2_), channel_id=1, source_target_pairs={{0,1},{1,0},{2,3},{3,2},{4,5},{5,4},{6,7},{7,6},{8,9},{9,8},{10,11... | collective-permute-start | bytes 3145736 | tf_op jit(solution)/shard_map/ppermute | solution.py:301
  245.3 28.1 %collective-permute-start.34 = (bf16[2,4,64,1024]{3,2,1,0:T(8,128)(2,1)S(1)}, bf16[2,4,64,1024]{3,2,1,0:T(8,128)(2,1)}, u32[]{:S(2)}, u32[]{:S(2)}) collective-permute-start(bf16[2,4,64,1024]{3,2,1,0:T(8,128)(2,1)S(1)} %pad_maximum_fusion.6.refs_2_), channel_id=1, source_target_pairs={{0,4},{4,0},{8,12},{12,8},{16,20},{20,16},{24,28},{28,24},{1,5},{5... | collective-permute-start | bytes 3145736 | tf_op jit(solution)/shard_map/ppermute | solution.py:293
  249.4 24.0 %collective-permute-start.35 = (bf16[2,4,64,1024]{3,2,1,0:T(8,128)(2,1)}, bf16[2,4,64,1024]{3,2,1,0:T(8,128)(2,1)}, u32[]{:S(2)}, u32[]{:S(2)}) collective-permute-start(bf16[2,4,64,1024]{3,2,1,0:T(8,128)(2,1)} %pad_maximum_fusion.5.refs_0_), channel_id=1, source_target_pairs={{0,1},{1,0},{2,3},{3,2},{4,5},{5,4},{6,7},{7,6},{8,9},{9,8},{10,11... | collective-permute-start | bytes 3145736 | tf_op jit(solution)/shard_map/ppermute | solution.py:301
  249.6 25.7 %collective-permute-start.33 = (bf16[2,4,64,1024]{3,2,1,0:T(8,128)(2,1)}, bf16[2,4,64,1024]{3,2,1,0:T(8,128)(2,1)}, u32[]{:S(2)}, u32[]{:S(2)}) collective-permute-start(bf16[2,4,64,1024]{3,2,1,0:T(8,128)(2,1)} %pad_maximum_fusion.5.refs_0_), channel_id=1, source_target_pairs={{0,2},{2,0},{1,3},{3,1},{4,6},{6,4},{5,7},{7,5},{8,10},{10,8},{9,1... | collective-permute-start | bytes 3145736 | tf_op jit(solution)/shard_map/ppermute | solution.py:297
  251.6 21.7 %collective-permute-start = (bf16[256,1024]{1,0:T(8,128)(2,1)S(1)}, bf16[256,1024]{1,0:T(8,128)(2,1)}, u32[]{:S(2)}, u32[]{:S(2)}) collective-permute-start(bf16[256,1024]{1,0:T(8,128)(2,1)S(1)} %slice_bitcast_fusion.4), channel_id=1, source_target_pairs={{2,3},{3,2},{6,7},{7,6},{10,11},{11,10},{14,15},{15,14},{18,19},{1... | collective-permute-start | bytes 1572872 | tf_op jit(solution)/shard_map/ppermute | solution.py:215
  275.3 2.9 collective-permute-start.39
  275.3 4.4 collective-permute-start.40
  275.9 25.5 %collective-permute-start.41 = (bf16[256,1024]{1,0:T(8,128)(2,1)S(1)}, bf16[256,1024]{1,0:T(8,128)(2,1)}, u32[]{:S(2)}, u32[]{:S(2)}) collective-permute-start(bf16[256,1024]{1,0:T(8,128)(2,1)S(1)} %bitcast_select_fusion.1), channel_id=1, source_target_pairs={{0,2},{1,3},{2,1},{3,0},{4,6},{5,7},{6,5},{7,4},{8,10},{9,11},{10,... | collective-permute-start | bytes 1572872 | tf_op jit(solution)/shard_map/ppermute | solution.py:210
  303.3 28.8 %collective-permute-start.42 = (bf16[256,1024]{1,0:T(8,128)(2,1)S(1)}, bf16[256,1024]{1,0:T(8,128)(2,1)S(1)}, u32[]{:S(2)}, u32[]{:S(2)}) collective-permute-start(bf16[256,1024]{1,0:T(8,128)(2,1)S(1)} %broadcast_select_fusion.2), channel_id=1, source_target_pairs={{2,0},{3,1},{1,2},{0,3},{6,4},{7,5},{5,6},{4,7},{10,8},{11,9},{9,1... | collective-permute-start | bytes 1572872 | tf_op jit(solution)/shard_map/ppermute | solution.py:231
  333.0 19.4 %collective-permute-start.43 = (bf16[256,1024]{1,0:T(8,128)(2,1)}, bf16[256,1024]{1,0:T(8,128)(2,1)S(1)}, u32[]{:S(2)}, u32[]{:S(2)}) collective-permute-start(bf16[256,1024]{1,0:T(8,128)(2,1)} %get-tuple-element.735), channel_id=1, source_target_pairs={{3,2},{2,3},{7,6},{6,7},{11,10},{10,11},{15,14},{14,15},{19,18},{1... | collective-permute-start | bytes 1572872 | tf_op jit(solution)/shard_map/ppermute | solution.py:237
  352.4 18.3 %copy-start.64 = (bf16[256,1024]{1,0:T(8,128)(2,1)}, bf16[256,1024]{1,0:T(8,128)(2,1)S(1)}, u32[]{:S(2)}) copy-start(bf16[256,1024]{1,0:T(8,128)(2,1)S(1)} %collective-permute-done.43) | copy-start | bytes 1572868
  352.4 3.0 collective-permute-start.44
  352.9 4.0 collective-permute-start.45
  412.8 3.0 collective-permute-start.46
  413.3 4.0 collective-permute-start.47
  427.7 2.0 collective-permute-start.48
  430.7 34.1 %all-to-all-start.1 = ((bf16[16,16,1024]{2,1,0:T(8,128)(2,1)}), bf16[16,16,1024]{2,1,0:T(8,128)(2,1)S(1)}, u32[]{:S(2)}, u32[]{:S(2)}) async-start(bf16[16,16,1024]{2,1,0:T(8,128)(2,1)} %fusion), calls=%async_computation.1 | async-start | bytes 1048576 | tf_op jit(solution)/shard_map/all_to_all | solution.py:1205
  448.1 5.4 %collective-permute-start.50 = (bf16[256,1024]{1,0:T(8,128)(2,1)S(1)}, bf16[256,1024]{1,0:T(8,128)(2,1)S(1)}, u32[]{:S(2)}, u32[]{:S(2)}) collective-permute-start(bf16[256,1024]{1,0:T(8,128)(2,1)S(1)} %get-tuple-element.732), channel_id=1, source_target_pairs={{3,2},{2,3},{7,6},{6,7},{11,10},{10,11},{15,14},{14,15},{19,18},{1... | collective-permute-start | bytes 1572872 | tf_op jit(solution)/shard_map/ppermute | solution.py:237
  448.9 15.9 %collective-permute-start.49 = (bf16[256,1024]{1,0:T(8,128)(2,1)S(1)}, bf16[256,1024]{1,0:T(8,128)(2,1)}, u32[]{:S(2)}, u32[]{:S(2)}) collective-permute-start(bf16[256,1024]{1,0:T(8,128)(2,1)S(1)} %get-tuple-element.733), channel_id=1, source_target_pairs={{2,0},{3,1},{1,2},{0,3},{6,4},{7,5},{5,6},{4,7},{10,8},{11,9},{9,1... | collective-permute-start | bytes 1572872 | tf_op jit(solution)/shard_map/ppermute | solution.py:231
  452.2 12.5 %copy-start.50 = (bf16[512,1024]{1,0:T(8,128)(2,1)S(1)}, bf16[512,1024]{1,0:T(8,128)(2,1)}, u32[]{:S(2)}) copy-start(bf16[512,1024]{1,0:T(8,128)(2,1)} %get-tuple-element.702) | copy-start | bytes 3145732
  (78 other events, 335.9 us)
Sparse Core Ops, SparseCore 0:
  10.9 163.8 all-gather.5
  177.6 83.3 all-gather.3
